TPU v7x, 32 devices: a whole 2x2x4 slice. The times are simulated.
32 devices in a mesh: dp: 16 (over z, y, x), group: 2 (over core).
Axes of the slice: x: 2, y: 2, z: 4, core: 2. Of those that a mesh axis runs over, the one named last changes fastest.
Arguments:
- samples: bfloat16 [32, 2048, 512], P(('dp', 'group')), may hold values from -6 to 6
- mel: bfloat16 [32, 11, 80], P(('dp', 'group')), may hold values from -6 to 6
- lengths: int32 [32], P(('dp', 'group')), may hold values from 1024 to 2048, as said below
- hops: int32 [32], P(('dp', 'group')), may hold values from 200 to 300, as said below
- conv_weight: bfloat16 [2, 1024, 1024], P(None, None, ('dp', 'group')), may hold values from -0.1875 to 0.1875
- cond_weight: bfloat16 [2, 80, 1024], P(None, None, ('dp', 'group')), may hold values from -0.625 to 0.625
- conv_bias: bfloat16 [2, 1024], P(None, ('dp', 'group')), may hold values from -3 to 3
- out_weight: bfloat16 [2, 512, 1024], P(None, None, ('dp', 'group')), may hold values from -0.75 to 0.75
- out_bias: bfloat16 [2, 1024], P(None, ('dp', 'group')), may hold values from -3 to 3
- grad_out: bfloat16 [32, 2048, 512], P(('dp', 'group')), may hold values from -6 to 6
- grad_skip: bfloat16 [32, 2048, 512], P(('dp', 'group')), may hold values from -6 to 6
Outputs:
- residual_out: bfloat16 [32, 2048, 512], P(('dp', 'group'))
- skip_output_sum: bfloat16 [32, 2048, 512], P(('dp', 'group'))
- samples_grad: float32 [32, 2048, 512], P(('dp', 'group'))
- mel_grad: float32 [32, 11, 80], P(('dp', 'group'))
- conv_weight_grad: float32 [2, 1024, 1024], P(None, None, ('dp', 'group'))
- cond_weight_grad: float32 [2, 80, 1024], P(None, None, ('dp', 'group'))
- conv_bias_grad: float32 [2, 1024], P(None, ('dp', 'group'))
- out_weight_grad: float32 [2, 512, 1024], P(None, None, ('dp', 'group'))
- out_bias_grad: float32 [2, 1024], P(None, ('dp', 'group'))
Inputs may be any that keep to these rules, and one draw needn't show every extreme that they name: `lengths`: every clip uses at least 1024 samples, and some clip uses all 2048. `hops`: each clip's value is 200 or 300, both occur.
All inputs are finite; a program needn't handle non-finite values.
Results may differ from a plain program's by a relative error of at most 0.0074.
Values may be sent and summed in bfloat16 or wider, within the bound.
No kernel may reach another device: no remote copies, remote signals or barrier semaphores. Data moves between devices by JAX's collectives and lax.ppermute only.
A program may use at most 192 MiB of HBM per device.

v0:
```python
import jax
import jax.numpy as jnp
from jax import lax
from jax.sharding import PartitionSpec as P

FIRST_DILATION = 512


def contract_rows(left, right):
    return lax.dot_general(
        left, right, (((0,), (0,)), ((), ())), preferred_element_type=jnp.float32
    )


def contract_cols(left, right):
    return lax.dot_general(
        left, right, (((1,), (1,)), ((), ())), preferred_element_type=jnp.float32
    )


def fetch_forward(conv_w, cond_w, conv_b, out_w, out_b):
    return (
        lax.all_gather(conv_w, ("dp", "group"), axis=1, tiled=True),
        lax.all_gather(cond_w, ("dp", "group"), axis=1, tiled=True),
        lax.all_gather(conv_b, ("dp", "group"), axis=0, tiled=True),
        lax.all_gather(out_w, ("dp", "group"), axis=1, tiled=True),
        lax.all_gather(out_b, ("dp", "group"), axis=0, tiled=True),
    )


def fetch_backward(conv_w, cond_w, conv_b, out_w, out_b):
    return (
        lax.all_gather(conv_w, ("dp", "group"), axis=1, tiled=True),
        lax.all_gather(cond_w, ("dp", "group"), axis=1, tiled=True),
        lax.all_gather(conv_b, ("dp", "group"), axis=0, tiled=True),
        lax.all_gather(out_w, ("dp", "group"), axis=1, tiled=True),
        lax.all_gather(out_b, ("dp", "group"), axis=0, tiled=True),
    )


def layer_forward(hidden, conditioning, pad_mask, weights, dilation_factor):
    conv_w, cond_w, conv_b, out_w, out_b = weights
    channels = hidden.shape[1]
    sample_count = hidden.shape[0]
    hidden_low = hidden.astype(jnp.bfloat16)
    shifted = jnp.pad(hidden_low[: sample_count - dilation_factor], ((dilation_factor, 0), (0, 0)))
    preact = jnp.dot(shifted, conv_w[:channels], preferred_element_type=jnp.float32)
    preact = preact + jnp.dot(hidden_low, conv_w[channels:], preferred_element_type=jnp.float32)
    preact = (
        preact
        + jnp.dot(conditioning, cond_w, preferred_element_type=jnp.float32)
        + conv_b.astype(jnp.float32)
    )
    tangent = jnp.tanh(preact[:, :channels])
    sig_gate = jax.nn.sigmoid(preact[:, channels:])
    gated_out = (tangent * sig_gate).astype(jnp.bfloat16)
    projected = jnp.dot(gated_out, out_w, preferred_element_type=jnp.float32) + out_b.astype(
        jnp.float32
    )
    hidden_next = (hidden + projected[:, :channels]) * pad_mask
    skip_part = projected[:, channels:] * pad_mask
    return (hidden_next, skip_part, (hidden_low, shifted, tangent, sig_gate, gated_out))


def layer_backward(
    grad_next, skip_cot, pad_mask, conditioning, weights, kept_values, dilation_factor
):
    conv_w, cond_w, conv_b, out_w, out_b = weights
    hidden_low, shifted, tangent, sig_gate, gated_out = kept_values
    channels = tangent.shape[1]
    grad_proj = jnp.concatenate([grad_next * pad_mask, skip_cot], axis=1).astype(jnp.bfloat16)
    grad_out_w = contract_rows(gated_out, grad_proj)
    grad_out_b = jnp.sum(grad_proj, axis=0, dtype=jnp.float32)
    grad_gated = contract_cols(grad_proj, out_w)
    grad_tanh_part = grad_gated * sig_gate * (1.0 - tangent * tangent)
    grad_sig_part = grad_gated * tangent * sig_gate * (1.0 - sig_gate)
    grad_pre = jnp.concatenate([grad_tanh_part, grad_sig_part], axis=1).astype(jnp.bfloat16)
    grad_conv_w = jnp.concatenate(
        [contract_rows(shifted, grad_pre), contract_rows(hidden_low, grad_pre)], axis=0
    )
    grad_cond_w = contract_rows(conditioning, grad_pre)
    grad_conv_b = jnp.sum(grad_pre, axis=0, dtype=jnp.float32)
    grad_stack = contract_cols(grad_pre, conv_w)
    moved = jnp.pad(grad_stack[dilation_factor:, :channels], ((0, dilation_factor), (0, 0)))
    grad_hidden = grad_next * pad_mask + grad_stack[:, channels:] + moved
    grad_cond = contract_cols(grad_pre, cond_w)
    return (grad_hidden, grad_cond, (grad_conv_w, grad_cond_w, grad_conv_b, grad_out_w, grad_out_b))


def per_device(
    samples,
    mel,
    lengths,
    hops,
    conv_weight,
    cond_weight,
    conv_bias,
    out_weight,
    out_bias,
    grad_out,
    grad_skip,
):
    sample_count = samples.shape[1]
    frame_count = mel.shape[1]
    number_of_layers = conv_weight.shape[0]
    positions = jnp.arange(sample_count, dtype=jnp.int32)
    pad_mask = (positions < lengths[0]).astype(jnp.float32)[:, None]
    frame_table = (
        (positions // hops[0])[:, None] == jnp.arange(frame_count, dtype=jnp.int32)[None, :]
    ).astype(jnp.float32)
    conditioning = jnp.dot(
        frame_table.astype(jnp.bfloat16), mel[0], preferred_element_type=jnp.float32
    ).astype(jnp.bfloat16)
    dilation_factors = [
        FIRST_DILATION if layer_position == 0 else 1 for layer_position in range(number_of_layers)
    ]
    hidden = samples[0].astype(jnp.float32) * pad_mask
    skip_total = jnp.zeros(hidden.shape, jnp.float32)
    loaded_weights = []
    saved = []
    for layer_position in range(number_of_layers):
        weights = fetch_forward(
            conv_weight[layer_position],
            cond_weight[layer_position],
            conv_bias[layer_position],
            out_weight[layer_position],
            out_bias[layer_position],
        )
        loaded_weights.append(weights)
        hidden, skip_part, kept_values = layer_forward(
            hidden, conditioning, pad_mask, weights, dilation_factors[layer_position]
        )
        skip_total = skip_total + skip_part
        saved.append(kept_values)
    residual_out = hidden.astype(jnp.bfloat16)[None]
    skip_output_sum = skip_total.astype(jnp.bfloat16)[None]
    grad_hidden = grad_out[0].astype(jnp.float32)
    skip_cot = grad_skip[0].astype(jnp.float32) * pad_mask
    grad_cond_total = jnp.zeros((sample_count, mel.shape[2]), jnp.float32)
    layer_results = [None] * number_of_layers
    for layer_position in reversed(range(number_of_layers)):
        weights = fetch_backward(
            conv_weight[layer_position],
            cond_weight[layer_position],
            conv_bias[layer_position],
            out_weight[layer_position],
            out_bias[layer_position],
        )
        grad_hidden, grad_cond, grads_full = layer_backward(
            grad_hidden,
            skip_cot,
            pad_mask,
            conditioning,
            weights,
            saved[layer_position],
            dilation_factors[layer_position],
        )
        grad_cond_total = grad_cond_total + grad_cond
        layer_results[layer_position] = (
            lax.psum_scatter(grads_full[0], ("dp", "group"), scatter_dimension=1, tiled=True),
            lax.psum_scatter(grads_full[1], ("dp", "group"), scatter_dimension=1, tiled=True),
            lax.psum_scatter(grads_full[2], ("dp", "group"), scatter_dimension=0, tiled=True),
            lax.psum_scatter(grads_full[3], ("dp", "group"), scatter_dimension=1, tiled=True),
            lax.psum_scatter(grads_full[4], ("dp", "group"), scatter_dimension=0, tiled=True),
        )
    owned = tuple(
        (
            jnp.stack(
                [
                    layer_results[layer_position][member]
                    for layer_position in range(number_of_layers)
                ],
                axis=0,
            )
            for member in range(5)
        )
    )
    samples_grad = (grad_hidden * pad_mask)[None]
    mel_grad = lax.dot_general(
        frame_table,
        grad_cond_total,
        (((0,), (0,)), ((), ())),
        precision=lax.Precision.HIGHEST,
        preferred_element_type=jnp.float32,
    )[None]
    return (
        residual_out,
        skip_output_sum,
        samples_grad,
        mel_grad,
        owned[0],
        owned[1],
        owned[2],
        owned[3],
        owned[4],
    )


def solution(mesh):
    return jax.shard_map(
        per_device,
        mesh=mesh,
        in_specs=(
            P(("dp", "group"), None, None),
            P(("dp", "group"), None, None),
            P(("dp", "group")),
            P(("dp", "group")),
            P(None, None, ("dp", "group")),
            P(None, None, ("dp", "group")),
            P(None, ("dp", "group")),
            P(None, None, ("dp", "group")),
            P(None, ("dp", "group")),
            P(("dp", "group"), None, None),
            P(("dp", "group"), None, None),
        ),
        out_specs=(
            P(("dp", "group"), None, None),
            P(("dp", "group"), None, None),
            P(("dp", "group"), None, None),
            P(("dp", "group"), None, None),
            P(None, None, ("dp", "group")),
            P(None, None, ("dp", "group")),
            P(None, ("dp", "group")),
            P(None, None, ("dp", "group")),
            P(None, ("dp", "group")),
        ),
        check_vma=False,
    )
```

profile of v0, /device:TPU:0, one launch (start us, length us, event | category | flops | bytes accessed | tf_op | source)
XLA Modules:
  0.0 1076.1 jit_solution(2836372742262541758)
XLA Ops:
  15.2 42.2 %all-reduce.13 = (bf16[1024]{0:T(1024)(128)(2,1)S(1)}, bf16[1024]{0:T(1024)(128)(2,1)S(1)}, bf16[1024]{0:T(1024)(128)(2,1)S(1)}, bf16[1024]{0:T(1024)(128)(2,1)S(1)}) all-reduce(bf16[1024]{0:T(1024)(128)(2,1)S(1)} %dynamic-update-slice.3, bf16[1024]{0:T(1024)(128)(2,1)S(1)} %dynamic-update-slice.1, ...), channel_id=11, replica_groups=mesh['dp'=16,'group'=2] {'dp','group'}, use_global_device_ids=true, to_apply=%add.7 | all-reduce | flops 4096 | bytes 16384
  58.2 41.1 %all-gather.6 = bf16[1,80,1024]{1,2,0:T(8,128)(2,1)S(1)} all-gather(bf16[1,80,32]{1,2,0:T(8,128)(2,1)S(1)} %get-tuple-element.48), channel_id=8, replica_groups=mesh['dp'=16,'group'=2] {'dp','group'}, dimensions={2}, use_global_device_ids=true | all-gather | bytes 168960 | tf_op jit(solution)/shard_map/all_gather | solution.py:24
  99.2 37.7 %all-gather.1 = bf16[1,80,1024]{1,2,0:T(8,128)(2,1)S(1)} all-gather(bf16[1,80,32]{1,2,0:T(8,128)(2,1)S(1)} %get-tuple-element.49), channel_id=3, replica_groups=mesh['dp'=16,'group'=2] {'dp','group'}, dimensions={2}, use_global_device_ids=true | all-gather | bytes 168960 | tf_op jit(solution)/shard_map/all_gather | solution.py:24
  141.1 3.7 fusion.39
  148.6 3.3 copy-done.4
  154.9 4.4 broadcast_add_fusion.1
  159.3 3.3 copy-done.7
  162.6 3.7 fusion.17
  166.4 19.4 %all-gather.19.cloned.1.call-done = bf16[1,1024,1024]{1,2,0:T(8,128)(2,1)} async-done(((bf16[1,1024,32]{1,2,0:T(8,128)(2,1)}), bf16[1,1024,1024]{1,2,0:T(8,128)(2,1)}) %all-gather.19.cloned.1.call-update) | async-done | bytes 2097168 | tf_op jit(solution)/shard_map/all_gather | solution.py:23
  185.7 4.4 fusion.32
  192.5 4.6 add_add_fusion
  197.1 44.4 %all-gather.21.cloned.1.call-done = bf16[1,512,1024]{1,2,0:T(8,128)(2,1)} async-done(((bf16[1,512,32]{1,2,0:T(8,128)(2,1)}), bf16[1,512,1024]{1,2,0:T(8,128)(2,1)}) %all-gather.21.cloned.1.call-update) | async-done | bytes 1048592 | tf_op jit(solution)/shard_map/all_gather | solution.py:26
  241.6 8.6 multiply_convert_fusion.3
  254.2 7.5 fusion.28
  262.3 3.7 copy-done.5
  271.4 4.5 multiply_convert_fusion.1
  280.1 6.6 fusion.34
  286.7 6.5 fusion.36
  293.5 5.4 fusion.30
  303.8 5.4 copy.32
  309.3 5.2 fusion.20
  319.4 5.6 copy.30
  325.1 3.7 fusion.46
  332.0 4.6 fusion.26
  347.1 39.9 %all-reduce.12 = (f32[1024]{0:T(1024)S(1)}, f32[1024]{0:T(1024)S(1)}, f32[1024]{0:T(1024)S(1)}, f32[1024]{0:T(1024)S(1)}) all-reduce(f32[1024]{0:T(1024)S(1)} %convert_reduce_fusion.2, f32[1024]{0:T(1024)S(1)} %convert_reduce_fusion.3, f32[1024]{0:T(1024)S(1)} %get-tuple-element.28, ...), channel_id=17, replica_groups=mesh['dp'=16,'group'=2] {'dp','group'}, use_global_device_ids=true, to_apply=%region_7.8.clone | all-reduce | flops 4096 | bytes 32768
  388.3 7.7 broadcast_add_fusion
  396.0 14.7 %fusion.25 = (bf16[1,2048,512]{2,1,0:T(8,128)(2,1)}, bf16[1,2048,512]{2,1,0:T(8,128)(2,1)}, f32[1,2048,512]{2,1,0:T(8,128)}) fusion(f32[2048,1024]{1,0:T(8,128)} %broadcast_add_fusion, f32[2048,1024]{1,0:T(8,128)} %copy-done.7, f32[2048]{0:T(1024)S(1)} %fusion.51, bf16[1,2048,512]{2,1,0:T(8,128)(2,1)S(1)} %copy-done.6, f32[1536,512]{1,0:T(8,128)} %slice.139, ...), kind=kLoop, calls=%fused_computation.59 | loop fusion | flops 18874368 | bytes 45094912 | tf_op jit(solution)/shard_map/broadcast_in_dim | solution.py:136
  410.7 108.8 %reduce-scatter.11.cloned.1.call-done = f32[80,32]{0,1:T(8,128)} async-done(((f32[80,1024]{0,1:T(8,128)}), f32[80,32]{0,1:T(8,128)}) %reduce-scatter.11.cloned.1.call-update) | async-done | bytes 10256 | tf_op jit(solution)/shard_map/reduce_scatter | solution.py:161
  520.9 133.1 %reduce-scatter.17.cloned.1.call-done = f32[512,32]{0,1:T(8,128)} async-done(((f32[512,1024]{0,1:T(8,128)}), f32[512,32]{0,1:T(8,128)}) %reduce-scatter.17.cloned.1.call-update) | async-done | bytes 65552 | tf_op jit(solution)/shard_map/reduce_scatter | solution.py:163
  654.0 134.7 %reduce-scatter.15.cloned.1.call-done = f32[512,32]{0,1:T(8,128)} async-done(((f32[512,1024]{0,1:T(8,128)}), f32[512,32]{0,1:T(8,128)}) %reduce-scatter.15.cloned.1.call-update) | async-done | bytes 65552 | tf_op jit(solution)/shard_map/reduce_scatter | solution.py:163
  790.3 137.8 %reduce-scatter.21.cloned.1.call-done = f32[32,1024]{1,0:T(8,128)} async-done(((f32[1024,1024]{1,0:T(8,128)}), f32[32,1024]{1,0:T(8,128)}) %reduce-scatter.21.cloned.1.call-update) | async-done | bytes 131088
  929.4 137.6 %reduce-scatter.19.cloned.1.call-done = f32[32,1024]{1,0:T(8,128)} async-done(((f32[1024,1024]{1,0:T(8,128)}), f32[32,1024]{1,0:T(8,128)}) %reduce-scatter.19.cloned.1.call-update) | async-done | bytes 131088
  (155 shorter events, 66.0 us)
Async XLA Ops:
  7.2 133.3 %copy-start = (bf16[1,11,80]{2,1,0:T(8,128)(2,1)S(1)}, bf16[1,11,80]{2,1,0:T(8,128)(2,1)}, u32[]{:S(2)}) copy-start(bf16[1,11,80]{2,1,0:T(8,128)(2,1)} %param.12) | copy-start | bytes 5284
  7.2 133.9 %all-gather.15.cloned.1.call-start = ((), (), s32[]{:S(2)}) async-start(), calls=%async_computation.10 | async-start | bytes 2162688 | tf_op jit(solution)/shard_map/all_gather | solution.py:23
  8.8 146.1 %all-gather.17.cloned.1.call-start = ((), (), s32[]{:S(2)}) async-start(), calls=%async_computation.11 | async-start | bytes 1081344 | tf_op jit(solution)/shard_map/all_gather | solution.py:26
  10.3 175.4 %all-gather.19.cloned.1.call-start = ((), (), s32[]{:S(2)}) async-start(), calls=%async_computation.12 | async-start | bytes 2162688 | tf_op jit(solution)/shard_map/all_gather | solution.py:23
  11.0 230.5 %all-gather.21.cloned.1.call-start = ((), (), s32[]{:S(2)}) async-start(), calls=%async_computation.13 | async-start | bytes 1081344 | tf_op jit(solution)/shard_map/all_gather | solution.py:26
  11.6 399.1 %reduce-scatter.13.cloned.1.call-start = ((), (), s32[]{:S(2)}) async-start(), calls=%async_computation.7 | async-start | bytes 540672 | tf_op jit(solution)/shard_map/reduce_scatter | solution.py:161
  139.0 5.9 copy-start.17
  141.1 3.8 copy-start.34
  141.1 3.8 copy-start.35
  154.9 7.7 copy-start.6
  154.9 7.7 copy-start.8
  154.9 7.7 copy-start.31
  185.7 4.4 copy-start.32
  185.7 4.4 copy-start.37
  254.2 265.4 %reduce-scatter.11.cloned.1.call-start = ((), (), s32[]{:S(2)}) async-start(), calls=%async_computation.6 | async-start | bytes 540672 | tf_op jit(solution)/shard_map/reduce_scatter | solution.py:161
  261.8 4.3 copy-start.5
  261.8 6.4 copy-start.9
  261.8 7.6 slice-start
  271.4 4.5 copy-start.11
  280.0 374.0 %reduce-scatter.17.cloned.1.call-start = ((), (), s32[]{:S(2)}) async-start(), calls=%async_computation.9 | async-start | bytes 2162688 | tf_op jit(solution)/shard_map/reduce_scatter | solution.py:163
  286.7 502.1 %reduce-scatter.15.cloned.1.call-start = ((), (), s32[]{:S(2)}) async-start(), calls=%async_computation.8 | async-start | bytes 2162688 | tf_op jit(solution)/shard_map/reduce_scatter | solution.py:163
  293.3 634.9 %reduce-scatter.21.cloned.1.call-start = ((), (), s32[]{:S(2)}) async-start(), calls=%async_computation.15 | async-start | bytes 4325376
  293.5 5.4 copy-start.20
  293.5 5.4 copy-start.23
  293.5 5.4 copy-start.33
  309.2 757.8 %reduce-scatter.19.cloned.1.call-start = ((), (), s32[]{:S(2)}) async-start(), calls=%async_computation.14 | async-start | bytes 4325376
  309.3 5.2 copy-start.18
  309.3 5.2 copy-start.26
  309.3 5.2 copy-start.29
  388.3 7.7 copy-start.3
  388.3 7.7 copy-start.10
  396.0 673.0 %copy-start.1 = (bf16[1,11,80]{2,1,0:T(8,128)(2,1)S(1)}, bf16[1,11,80]{2,1,0:T(8,128)(2,1)}, u32[]{:S(2)}) copy-start(bf16[1,11,80]{2,1,0:T(8,128)(2,1)} %param.12) | copy-start | bytes 5284
  (19 other events, 50.2 us)
Sparse Core Ops, SparseCore 0:
  11.5 59.2 all-gather.14
  74.2 52.4 all-gather.16
  130.1 55.5 all-gather.18
  189.0 52.5 all-gather.20
  254.3 132.9 reduce-scatter.12
  389.4 130.0 reduce-scatter.10
  521.8 132.1 reduce-scatter.16
  656.4 132.3 reduce-scatter.14
  791.0 137.0 reduce-scatter.20
  930.3 136.6 reduce-scatter.18
where the time goes:
time: 1080 us
  waiting for transfers between devices  717 us (66%)
  blocking collectives  161 us (15%)
  matrix products  95.4 us (9%)
  local copies, waits for them, and re-layouts  48.9 us (5%)
  other arithmetic  36.8 us (3%)
  between operations  16.3 us (2%)
    unnamed x12, waiting for transfers between devices  277 us
    reduce_scatter x2, waiting for transfers between devices, per_device(): lax.psum_scatter(grads_full[3], ('dp', 'group'), scatter_dimension=1, til...  268 us
    reduce_scatter x2, waiting for transfers between devices, per_device(): lax.psum_scatter(grads_full[1], ('dp', 'group'), scatter_dimension=1, til...  109 us
    unnamed x2, blocking collectives  82.1 us
    all_gather x2, blocking collectives, fetch_forward(): lax.all_gather(cond_w, ('dp', 'group'), axis=1, tiled=True)  78.8 us
    all_gather x2, waiting for transfers between devices, fetch_forward(): lax.all_gather(out_w, ('dp', 'group'), axis=1, tiled=True)  44.4 us
    unnamed x97, local copies, waits for them, and re-layouts  40.8 us
    dot_general x8, matrix products, contract_rows(): lax.dot_general(left, right, (((0,), (0,)), ((), ())), preferred_element_...  32.6 us
  transfers between devices with their start and end apart: 10, of which 7 were waited for; matrix products, arithmetic and copies ran while one was open for 13% of the time, Pallas kernels for 0%

commit v1 on v0

v1 whole, which is shorter than its diff:
```python
import jax
import jax.numpy as jnp
from jax import lax
from jax.sharding import PartitionSpec as P

FIRST_DILATION = 512
AXES = ("dp", "group")
LANES = 128


def contract_rows(left, right):
    return lax.dot_general(
        left, right, (((0,), (0,)), ((), ())), preferred_element_type=jnp.float32
    )


def contract_cols(left, right):
    return lax.dot_general(
        left, right, (((1,), (1,)), ((), ())), preferred_element_type=jnp.float32
    )


class Wires:
    def __init__(self, dp, cores):
        assert dp % 4 == 0 and cores == 2
        self.rest = dp // 4
        self.devices = dp * 2
        me = lax.axis_index(AXES)
        self.core = me % 2
        self.a = (me // 2) % 2
        self.b = (me // 4) % 2
        self.alone = jnp.where(self.core == 0, self.a, self.b)
        self.core_pairs = [(i, i ^ 1) for i in range(self.devices)]
        self.alone_pairs = [(i, i ^ (2 if i % 2 == 0 else 4)) for i in range(self.devices)]
        groups = []
        for core in range(2):
            for fixed in range(2):
                members = []
                for rest in range(self.rest):
                    for varied in range(2):
                        b, a = (varied, fixed) if core == 0 else (fixed, varied)
                        members.append(((rest * 2 + b) * 2 + a) * 2 + core)
                groups.append(members)
        self.groups = groups

    def spread(self, blocks):
        return lax.all_to_all(blocks, AXES, 0, 0, tiled=True, axis_index_groups=self.groups)

    def gather(self, block):
        rows, depth = block.shape
        count = self.rest * 2
        mine = self.spread(jnp.broadcast_to(block[None], (count, rows, depth)))
        other = lax.ppermute(mine, AXES, self.alone_pairs)
        low = jnp.where(self.alone == 0, mine, other)
        high = jnp.where(self.alone == 0, other, mine)
        half = jnp.stack([low, high]).reshape(2, self.rest, 2, rows, depth)
        passed = lax.ppermute(half, AXES, self.core_pairs)
        first = jnp.where(self.core == 0, half, passed)
        second = jnp.where(self.core == 0, passed, half)
        whole = jnp.stack(
            [first.transpose(1, 2, 0, 3, 4), second.transpose(1, 0, 2, 3, 4)], axis=3
        )
        return whole.reshape(self.devices * rows, depth)

    def scatter_sum(self, full):
        depth = full.shape[1]
        rows = full.shape[0] // self.devices
        blocks = full.reshape(self.rest, 4, 2, rows, depth)
        away = lax.dynamic_index_in_dim(blocks, 1 - self.core, 2, keepdims=False)
        here = lax.dynamic_index_in_dim(blocks, self.core, 2, keepdims=False)
        came = lax.ppermute(away.astype(jnp.bfloat16), AXES, self.core_pairs)
        chip = here + came.astype(jnp.float32)

        def pick(side):
            places = [
                jnp.where(self.core == 0, step * 2 + side, side * 2 + step) for step in range(2)
            ]
            return jnp.stack(
                [lax.dynamic_index_in_dim(chip, place, 1, keepdims=False) for place in places],
                axis=1,
            )

        came = lax.ppermute(pick(1 - self.alone).astype(jnp.bfloat16), AXES, self.alone_pairs)
        pair = pick(self.alone) + came.astype(jnp.float32)
        parts = self.spread(pair.astype(jnp.bfloat16).reshape(self.rest * 2, rows, depth))
        return jnp.sum(parts.astype(jnp.float32), axis=0)


def layer_forward(hidden, conditioning, pad_mask, weights, dilation_factor):
    conv_t, cond_t, conv_b, out_t, out_b = weights
    channels = hidden.shape[1]
    sample_count = hidden.shape[0]
    hidden_low = hidden.astype(jnp.bfloat16)
    shifted = jnp.pad(hidden_low[: sample_count - dilation_factor], ((dilation_factor, 0), (0, 0)))
    taps = jnp.concatenate([shifted, hidden_low, conditioning], axis=1)
    preact = contract_cols(taps, jnp.concatenate([conv_t, cond_t], axis=1)) + conv_b
    tangent = jnp.tanh(preact[:, :channels])
    sig_gate = jax.nn.sigmoid(preact[:, channels:])
    gated_out = (tangent * sig_gate).astype(jnp.bfloat16)
    projected = contract_cols(gated_out, out_t) + out_b
    hidden_next = (hidden + projected[:, :channels]) * pad_mask
    skip_part = projected[:, channels:] * pad_mask
    return (hidden_next, skip_part, (hidden_low, shifted, tangent, sig_gate, gated_out))


def per_device(
    dp,
    cores,
    samples,
    mel,
    lengths,
    hops,
    conv_weight,
    cond_weight,
    conv_bias,
    out_weight,
    out_bias,
    grad_out,
    grad_skip,
):
    wires = Wires(dp, cores)
    sample_count, channels = samples.shape[1:]
    frame_count, mel_count = mel.shape[1:]
    number_of_layers = conv_weight.shape[0]
    conv_depth = conv_weight.shape[1]
    out_depth = out_weight.shape[1]
    positions = jnp.arange(sample_count, dtype=jnp.int32)
    pad_mask = (positions < lengths[0]).astype(jnp.float32)[:, None]
    frame_table = (
        (positions // hops[0])[:, None] == jnp.arange(frame_count, dtype=jnp.int32)[None, :]
    ).astype(jnp.bfloat16)
    conditioning = jnp.dot(
        frame_table, mel[0], preferred_element_type=jnp.float32
    ).astype(jnp.bfloat16)

    loaded = []
    for layer in range(number_of_layers):
        fill = -(mel_count + 2) % LANES
        conv_pack = jnp.concatenate(
            [
                conv_weight[layer],
                cond_weight[layer],
                conv_bias[layer][None],
                out_bias[layer][None],
                jnp.zeros((fill, conv_weight.shape[2]), jnp.bfloat16),
            ],
            axis=0,
        ).T
        conv_full = wires.gather(conv_pack)
        out_t = wires.gather(out_weight[layer].T)
        at = conv_depth + mel_count
        loaded.append(
            (
                conv_full[:, :conv_depth],
                conv_full[:, conv_depth:at],
                conv_full[:, at].astype(jnp.float32),
                out_t,
                conv_full[:, at + 1].astype(jnp.float32),
            )
        )

    hidden = samples[0].astype(jnp.float32) * pad_mask
    skip_total = jnp.zeros(hidden.shape, jnp.float32)
    saved = []
    for layer in range(number_of_layers):
        dilation = FIRST_DILATION if layer == 0 else 1
        hidden, skip_part, kept = layer_forward(
            hidden, conditioning, pad_mask, loaded[layer], dilation
        )
        skip_total = skip_total + skip_part
        saved.append(kept)
    residual_out = hidden.astype(jnp.bfloat16)[None]
    skip_output_sum = skip_total.astype(jnp.bfloat16)[None]

    grad_hidden = grad_out[0].astype(jnp.float32)
    skip_cot = grad_skip[0].astype(jnp.float32) * pad_mask
    mel_grad = jnp.zeros((frame_count, mel_count), jnp.float32)
    owned = [None] * number_of_layers
    exact = dict(precision=lax.Precision.HIGHEST, preferred_element_type=jnp.float32)
    for layer in reversed(range(number_of_layers)):
        dilation = FIRST_DILATION if layer == 0 else 1
        conv_t, cond_t, conv_b, out_t, out_b = loaded[layer]
        hidden_low, shifted, tangent, sig_gate, gated_out = saved[layer]
        masked = grad_hidden * pad_mask
        grad_proj = jnp.concatenate([masked, skip_cot], axis=1).astype(jnp.bfloat16)
        out_grad = contract_rows(grad_proj, gated_out)
        out_b_grad = jnp.sum(grad_proj, axis=0, dtype=jnp.float32)
        out_own = wires.scatter_sum(out_grad)
        grad_gated = jnp.dot(grad_proj, out_t, preferred_element_type=jnp.float32)
        grad_pre = jnp.concatenate(
            [
                grad_gated * sig_gate * (1.0 - tangent * tangent),
                grad_gated * tangent * sig_gate * (1.0 - sig_gate),
            ],
            axis=1,
        ).astype(jnp.bfloat16)
        conv_grad = contract_rows(grad_pre, jnp.concatenate([shifted, hidden_low], axis=1))
        frame_sums = contract_rows(grad_pre, frame_table)
        cond_grad = lax.dot_general(
            frame_sums, mel[0].astype(jnp.float32), (((1,), (0,)), ((), ())), **exact
        )
        mel_grad = mel_grad + lax.dot_general(
            frame_sums, cond_t.astype(jnp.float32), (((0,), (0,)), ((), ())), **exact
        )
        fill = jnp.zeros((conv_grad.shape[0], -(mel_count + 2) % LANES), jnp.float32)
        conv_own = wires.scatter_sum(
            jnp.concatenate(
                [
                    conv_grad,
                    cond_grad,
                    jnp.sum(frame_sums, axis=1, keepdims=True),
                    out_b_grad[:, None],
                    fill,
                ],
                axis=1,
            )
        )
        grad_stack = jnp.dot(grad_pre, conv_t, preferred_element_type=jnp.float32)
        moved = jnp.pad(grad_stack[dilation:, :channels], ((0, dilation), (0, 0)))
        grad_hidden = masked + grad_stack[:, channels:] + moved
        at = conv_depth + mel_count
        owned[layer] = (
            conv_own[:, :conv_depth].T,
            conv_own[:, conv_depth:at].T,
            conv_own[:, at],
            out_own.T,
            conv_own[:, at + 1],
        )
    samples_grad = (grad_hidden * pad_mask)[None]
    owned = [jnp.stack([part[member] for part in owned], axis=0) for member in range(5)]
    return (residual_out, skip_output_sum, samples_grad, mel_grad[None], *owned)


def solution(mesh):
    dp, cores = mesh.shape["dp"], mesh.shape["group"]

    def whole(*arrays):
        return per_device(dp, cores, *arrays)

    clips = P(AXES, None, None)
    columns = P(None, None, AXES)
    biases = P(None, AXES)
    return jax.shard_map(
        whole,
        mesh=mesh,
        in_specs=(
            clips, clips, P(AXES), P(AXES), columns, columns, biases, columns, biases, clips, clips,
        ),
        out_specs=(clips, clips, clips, clips, columns, columns, biases, columns, biases),
        check_vma=False,
    )
```

time: 1080 us -> 344 us (0.32)
  waiting for transfers between devices: 717 us -> 58.1 us
  blocking collectives: 161 us -> 0 us
  starting transfers between devices: 0.58 us -> 52.3 us
  local copies, waits for them, and re-layouts: 48.9 us -> 86.1 us
  other arithmetic: 36.8 us -> 57.3 us
  matrix products: 95.4 us -> 80.9 us
  between operations: 16.3 us -> 3.18 us
    reduce_scatter x4 -> x0, waiting for transfers between devices: 377 us -> none  [the longest x2 268 us: per_device(): lax.psum_scatter(grads_full[3], ('dp', 'group'), scatter_dimension=1, til...]
    unnamed x12 -> x0, waiting for transfers between devices: 277 us -> none
    unnamed x2 -> x0, blocking collectives: 82.1 us -> none
    all_gather x2 -> x0, blocking collectives: 78.8 us -> none  [fetch_forward(): lax.all_gather(cond_w, ('dp', 'group'), axis=1, tiled=True)]
    all_gather x4 -> x0, waiting for transfers between devices: 63.8 us -> none  [the longest x2 44.4 us: fetch_forward(): lax.all_gather(out_w, ('dp', 'group'), axis=1, tiled=True)]
    all_to_all x0 -> x8, waiting for transfers between devices: none -> 45.9 us  [spread(): lax.all_to_all(blocks, AXES, 0, 0, tiled=True, axis_index_groups=self.gro...]
    all_to_all x0 -> x8, starting transfers between devices: none -> 40.3 us  [spread(): lax.all_to_all(blocks, AXES, 0, 0, tiled=True, axis_index_groups=self.gro...]
    concatenate x0 -> x9, local copies, waits for them, and re-layouts: none -> 17.3 us  [the longest x7 17.1 us: per_device(): jnp.concatenate([conv_grad, cond_grad, jnp.sum(frame_sums, axis=1, keepdi...]
  transfers between devices with their start and end apart: 10 -> 24, of which waited for: 7 -> 10; matrix products, arithmetic and copies ran while one was open for 13% -> 32% of each run, Pallas kernels for 0% -> 0%
where the time goes in v1:
time: 344 us; the launch traced here: 338 us
  local copies, waits for them, and re-layouts  86.1 us (25%)
  matrix products  80.9 us (24%)
  waiting for transfers between devices  58.1 us (17%)
  other arithmetic  57.3 us (17%)
  starting transfers between devices  52.3 us (15%)
    all_to_all x8, waiting for transfers between devices, spread(): lax.all_to_all(blocks, AXES, 0, 0, tiled=True, axis_index_groups=self.gro...  45.9 us
    all_to_all x8, starting transfers between devices, spread(): lax.all_to_all(blocks, AXES, 0, 0, tiled=True, axis_index_groups=self.gro...  40.3 us
    unnamed x105, local copies, waits for them, and re-layouts  37.9 us
    dot_general x6, matrix products, contract_rows(): lax.dot_general(left, right, (((0,), (0,)), ((), ())), preferred_element_...  24.5 us
    dot_general x4, matrix products, contract_cols(): lax.dot_general(left, right, (((1,), (1,)), ((), ())), preferred_element_...  23.1 us
    concatenate x7, local copies, waits for them, and re-layouts, per_device(): jnp.concatenate([conv_grad, cond_grad, jnp.sum(frame_sums, axis=1, keepdi...  17.1 us
    dot_general x2, matrix products, per_device(): grad_gated = jnp.dot(grad_proj, out_t, preferred_element_type=jnp.float32)  14.4 us
    broadcast_in_dim x1, other arithmetic, per_device(): skip_output_sum = skip_total.astype(jnp.bfloat16)[None]  14.2 us
  transfers between devices with their start and end apart: 24, of which 10 were waited for; matrix products, arithmetic and copies ran while one was open for 32% of the time, Pallas kernels for 0%

profile of v1, /device:TPU:0, one launch (start us, length us, event | category | flops | bytes accessed | tf_op | source)
XLA Modules:
  0.0 337.9 jit_solution(10561249540913745730)
XLA Ops:
  2.2 7.3 %all-to-all-start.1 = ((bf16[8,32,512]{2,1,0:T(8,128)(2,1)}), bf16[8,32,512]{2,1,0:T(8,128)(2,1)S(1)}, u32[]{:S(2)}, u32[]{:S(2)}) async-start(bf16[8,32,512]{2,1,0:T(8,128)(2,1)} %broadcast_in_dim.17), calls=%async_computation.1 | async-start | bytes 524288 | tf_op jit(solution)/shard_map/all_to_all | solution.py:47
  10.2 8.2 %all-to-all-done.1 = bf16[8,32,512]{2,1,0:T(8,128)(2,1)S(1)} async-done(((bf16[8,32,512]{2,1,0:T(8,128)(2,1)}), bf16[8,32,512]{2,1,0:T(8,128)(2,1)S(1)}, u32[]{:S(2)}, u32[]{:S(2)}) %all-to-all-start.1) | async-done | bytes 262176 | tf_op jit(solution)/shard_map/all_to_all | solution.py:47
  25.2 6.2 %all-to-all-done.3 = bf16[8,32,512]{2,1,0:T(8,128)(2,1)S(1)} async-done(((bf16[8,32,512]{2,1,0:T(8,128)(2,1)}), bf16[8,32,512]{2,1,0:T(8,128)(2,1)S(1)}, u32[]{:S(2)}, u32[]{:S(2)}) %all-to-all-start.3) | async-done | bytes 262176 | tf_op jit(solution)/shard_map/all_to_all | solution.py:47
  32.3 4.2 %all-to-all-start = ((bf16[8,32,1152]{2,1,0:T(8,128)(2,1)}), bf16[8,32,1152]{2,1,0:T(8,128)(2,1)}, u32[]{:S(2)}, u32[]{:S(2)}) async-start(bf16[8,32,1152]{2,1,0:T(8,128)(2,1)} %broadcast_in_dim.16), calls=%async_computation | async-start | bytes 1179648 | tf_op jit(solution)/shard_map/all_to_all | solution.py:47
  36.8 14.3 %all-to-all-done = bf16[8,32,1152]{2,1,0:T(8,128)(2,1)} async-done(((bf16[8,32,1152]{2,1,0:T(8,128)(2,1)}), bf16[8,32,1152]{2,1,0:T(8,128)(2,1)}, u32[]{:S(2)}, u32[]{:S(2)}) %all-to-all-start) | async-done | bytes 589856 | tf_op jit(solution)/shard_map/all_to_all | solution.py:47
  51.9 4.2 %all-to-all-start.2 = ((bf16[8,32,1152]{2,1,0:T(8,128)(2,1)}), bf16[8,32,1152]{2,1,0:T(8,128)(2,1)}, u32[]{:S(2)}, u32[]{:S(2)}) async-start(bf16[8,32,1152]{2,1,0:T(8,128)(2,1)} %broadcast_in_dim.18), calls=%async_computation.2 | async-start | bytes 1179648 | tf_op jit(solution)/shard_map/all_to_all | solution.py:47
  76.8 4.0 %collective-permute-done.4 = bf16[8,32,1152]{2,1,0:T(8,128)(2,1)S(1)} collective-permute-done((bf16[8,32,1152]{2,1,0:T(8,128)(2,1)}, bf16[8,32,1152]{2,1,0:T(8,128)(2,1)S(1)}, u32[]{:S(2)}, u32[]{:S(2)}) %collective-permute-start.4) | collective-permute-done | bytes 589856 | tf_op jit(solution)/shard_map/ppermute | solution.py:53
  89.9 3.9 %copy.72 = bf16[1,2048,512]{1,2,0:T(8,128)(2,1)} copy(bf16[1,2048,512]{2,1,0:T(8,128)(2,1)} %param.20) | data formatting | bytes 4194304 | tf_op args[9]
  93.8 4.1 %copy.73 = bf16[1,2048,512]{1,2,0:T(8,128)(2,1)} copy(bf16[1,2048,512]{2,1,0:T(8,128)(2,1)} %param.21) | data formatting | bytes 4194304 | tf_op args[10]
  111.5 5.6 %fusion.9 = f32[2048,1024]{0,1:T(8,128)S(1)} fusion(bf16[2048,80]{0,1:T(8,128)(2,1)S(1)} %convolution_convert_fusion, bf16[2048,512]{0,1:T(8,128)(2,1)S(1)} %copy-done.20, bf16[2048,512]{0,1:T(8,128)(2,1)S(1)} %copy-done.31, f32[1024]{0:T(1024)S(1)} %get-tuple-element.29, bf16[1024,1152]{1,0:T(8,128)(2,1)S(1)} %bitcast.183), kind=kOutput, calls=%fused_computation.15 | convolution fusion | flops 4646174720 | bytes 15273984 | tf_op jit(solution)/shard_map/dot_general | solution.py:18
  124.1 4.7 %fusion.35 = (bf16[2048,512]{0,1:T(8,128)(2,1)S(1)}, bf16[2048,512]{0,1:T(8,128)(2,1)}, bf16[2048,512]{0,1:T(8,128)(2,1)}) fusion(bf16[1,2048,512]{1,2,0:T(8,128)(2,1)S(1)} %copy-done.3, f32[2048]{0:T(1024)S(1)} %fusion.75, f32[2048,1024]{0,1:T(8,128)S(1)} %broadcast_add_fusion.1, bf16[1,2048,512]{1,2,0:T(8,128)(2,1)S(1)} %copy.48, ...), kind=kLoop, calls=%fused_computation.54 | loop fusion | flops 11534336 | bytes 16785408 | tf_op jit(solution)/shard_map/convert.21
  128.9 4.0 %pad.17 = bf16[2048,512]{0,1:T(8,128)(2,1)S(1)} pad(bf16[2047,512]{0,1:T(8,128)(2,1)} %bitcast.181, bf16[]{:T(256)} %constant.114.clone.1), padding=1_0x0_0 | pad | bytes 4193282 | tf_op jit(solution)/shard_map/jit(_pad)/pad | solution.py:94
  132.9 9.6 %fusion.8 = f32[2048,1024]{0,1:T(8,128)} fusion(bf16[2048,80]{0,1:T(8,128)(2,1)S(1)} %copy-done.44, bf16[2048,512]{0,1:T(8,128)(2,1)S(1)} %copy-done.17, bf16[2048,512]{0,1:T(8,128)(2,1)S(1)} %pad.17, f32[1024]{0:T(1024)S(1)} %get-tuple-element.27, bf16[1024,1152]{1,0:T(8,128)(2,1)} %bitcast.187), kind=kOutput, calls=%fused_computation.14 | convolution fusion | flops 4646174720 | bytes 15273984 | tf_op jit(solution)/shard_map/dot_general | solution.py:18
  142.4 7.7 %multiply_convert_fusion.3 = (bf16[2048,512]{0,1:T(8,128)(2,1)S(1)}, bf16[2048,512]{0,1:T(8,128)(2,1)S(1)}, bf16[2048,512]{0,1:T(8,128)(2,1)}) fusion(f32[2048,1024]{0,1:T(8,128)} %fusion.8, bf16[1024,512]{1,0:T(8,128)(2,1)S(1)} %bitcast.208, bf16[2048,512]{0,1:T(8,128)(2,1)S(1)} %copy-done.16, bf16[2048,512]{0,1:T(8,128)(2,1)S(1)} %get-tuple-element.75), kind=kOutput, calls=%fused_computation.60 | convolution fusion | flops 2171600896 | bytes 19922944 | tf_op jit(solution)/shard_map/dot_general | solution.py:189
  150.1 6.6 %fusion.30 = f32[1024,1024]{1,0:T(8,128)} fusion(bf16[2048,512]{0,1:T(8,128)(2,1)S(1)} %copy-done.17, bf16[2048,512]{0,1:T(8,128)(2,1)S(1)} %pad.17, bf16[2048,512]{0,1:T(8,128)(2,1)S(1)} %get-tuple-element.42, bf16[2048,512]{0,1:T(8,128)(2,1)S(1)} %get-tuple-element.41), kind=kOutput, calls=%fused_computation.47 | convolution fusion | flops 4311744512 | bytes 12582912 | tf_op jit(solution)/shard_map/dot_general | solution.py:12
  158.4 6.6 %fusion.44 = f32[2048,1024]{0,1:T(8,128)S(1)} fusion(bf16[1024,1152]{1,0:T(8,128)(2,1)S(1)} %bitcast.189, bf16[2048,512]{0,1:T(8,128)(2,1)} %copy-done.46, bf16[2048,512]{0,1:T(8,128)(2,1)S(1)} %get-tuple-element.41), kind=kOutput, calls=%fused_computation.79 | convolution fusion | flops 4303355904 | bytes 14680064 | tf_op jit(solution)/shard_map/dot_general | solution.py:218
  170.4 6.7 %multiply_convert_fusion.1 = (bf16[2048,512]{0,1:T(8,128)(2,1)S(1)}, bf16[2048,512]{0,1:T(8,128)(2,1)S(1)}) fusion(f32[2048,1024]{0,1:T(8,128)} %copy-done.11, bf16[1024,512]{1,0:T(8,128)(2,1)S(1)} %bitcast.211, bf16[2048,512]{0,1:T(8,128)(2,1)S(1)} %copy-done.16, bf16[2048,512]{0,1:T(8,128)(2,1)S(1)} %fusion.92), kind=kOutput, calls=%fused_computation.58 | convolution fusion | flops 2169503744 | bytes 17825792 | tf_op jit(solution)/shard_map/dot_general | solution.py:189
  182.3 6.5 %fusion.26 = f32[1024,1024]{1,0:T(8,128)} fusion(bf16[2048,512]{0,1:T(8,128)(2,1)S(1)} %copy-done.21, bf16[2048,512]{0,1:T(8,128)(2,1)S(1)} %copy-done.32, bf16[2048,512]{0,1:T(8,128)(2,1)S(1)} %get-tuple-element.40, bf16[2048,512]{0,1:T(8,128)(2,1)S(1)} %get-tuple-element.39), kind=kOutput, calls=%fused_computation.43 | convolution fusion | flops 4311744512 | bytes 12582912 | tf_op jit(solution)/shard_map/dot_general | solution.py:12
  190.5 7.2 %fusion.42 = f32[2048,1024]{0,1:T(8,128)} fusion(bf16[1024,1152]{1,0:T(8,128)(2,1)S(1)} %bitcast.185, bf16[2048,512]{0,1:T(8,128)(2,1)S(1)} %get-tuple-element.40, bf16[2048,512]{0,1:T(8,128)(2,1)S(1)} %get-tuple-element.39), kind=kOutput, calls=%fused_computation.77 | convolution fusion | flops 4303355904 | bytes 14680064 | tf_op jit(solution)/shard_map/dot_general | solution.py:218
  199.7 5.2 %fusion.46 = f32[1024,512]{1,0:T(8,128)S(1)} fusion(bf16[2048,512]{0,1:T(8,128)(2,1)} %get-tuple-element.43, bf16[2048,512]{0,1:T(8,128)(2,1)} %get-tuple-element.77, bf16[2048,512]{0,1:T(8,128)(2,1)} %copy-done.14), kind=kOutput, calls=%fused_computation.81 | convolution fusion | flops 2155872256 | bytes 8388608 | tf_op jit(solution)/shard_map/dot_general | solution.py:12
  215.4 6.2 %concatenate.86 = f32[4,4,2,32,1152]{4,3,2,1,0:T(8,128)} concatenate(f32[4,4,2,32,1024]{4,3,2,1,0:T(8,128)} %bitcast.190, f32[4,4,2,32,80]{4,3,2,1,0:T(8,128)S(1)} %fusion.71, f32[4,4,2,32,1]{4,3,2,1,0:T(8,128)} %concatenate.89, f32[4,4,2,32,1]{4,3,2,1,0:T(8,128)} %concatenate.90, f32[4,4,2,32,46]{4,3,2,1,0:T(8,128)S(1)} %concatenate.80), dimensions={4} | concatenate | bytes 9437184 | tf_op jit(solution)/shard_map/concatenate | solution.py:207
  224.4 6.3 %concatenate.81 = f32[4,4,2,32,1152]{4,3,2,1,0:T(8,128)} concatenate(f32[4,4,2,32,1024]{4,3,2,1,0:T(8,128)} %bitcast.191, f32[4,4,2,32,80]{4,3,2,1,0:T(8,128)} %fusion.73, f32[4,4,2,32,1]{4,3,2,1,0:T(8,128)} %concatenate.87, f32[4,4,2,32,1]{4,3,2,1,0:T(8,128)} %concatenate.88, f32[4,4,2,32,46]{4,3,2,1,0:T(8,128)S(1)} %concatenate.80), dimensions={4} | concatenate | bytes 9437184 | tf_op jit(solution)/shard_map/concatenate | solution.py:207
  233.4 3.7 %slice.181 = f32[1536,512]{0,1:T(8,128)} slice(f32[2048,1024]{0,1:T(8,128)} %fusion.42), slice={[512:2048], [0:512]} | slice | bytes 6291456 | tf_op jit(solution)/shard_map/slice | solution.py:219
  237.1 5.6 %broadcast_add_fusion = f32[2048,1024]{0,1:T(8,128)} fusion(f32[1024]{0:T(1024)S(1)} %copy-done.42, bf16[1024,512]{1,0:T(8,128)(2,1)S(1)} %bitcast.209, bf16[2048,512]{0,1:T(8,128)(2,1)S(1)} %copy-done.45), kind=kOutput, calls=%fused_computation.61 | convolution fusion | flops 2149580800 | bytes 11538432 | tf_op jit(solution)/shard_map/dot_general | solution.py:18
  242.7 14.2 %fusion.41 = (bf16[1,2048,512]{1,2,0:T(8,128)(2,1)}, bf16[1,2048,512]{1,2,0:T(8,128)(2,1)}, f32[1,2048,512]{1,2,0:T(8,128)}) fusion(f32[2048,1024]{0,1:T(8,128)} %broadcast_add_fusion, f32[2048,1024]{0,1:T(8,128)} %copy-done.6, f32[2048]{0:T(1024)S(1)} %fusion.75, bf16[1,2048,512]{1,2,0:T(8,128)(2,1)S(1)} %copy.48, f32[1536,512]{0,1:T(8,128)} %slice.181, ...), kind=kLoop, calls=%fused_computation.76 | loop fusion | flops 18874368 | bytes 45094912 | tf_op jit(solution)/shard_map/broadcast_in_dim | solution.py:173
  266.0 5.7 %all-to-all-start.7 = ((bf16[8,32,512]{2,1,0:T(8,128)(2,1)}), bf16[8,32,512]{2,1,0:T(8,128)(2,1)S(1)}, u32[]{:S(2)}, u32[]{:S(2)}) async-start(bf16[8,32,512]{2,1,0:T(8,128)(2,1)} %bitcast.77), calls=%async_computation.7 | async-start | bytes 524288 | tf_op jit(solution)/shard_map/all_to_all | solution.py:47
  281.6 6.0 %all-to-all-start.6 = ((bf16[8,32,512]{2,1,0:T(8,128)(2,1)}), bf16[8,32,512]{2,1,0:T(8,128)(2,1)}, u32[]{:S(2)}, u32[]{:S(2)}) async-start(bf16[8,32,512]{2,1,0:T(8,128)(2,1)} %bitcast.71), calls=%async_computation.6 | async-start | bytes 524288 | tf_op jit(solution)/shard_map/all_to_all | solution.py:47
  290.6 5.3 %all-to-all-done.6 = bf16[8,32,512]{2,1,0:T(8,128)(2,1)} async-done(((bf16[8,32,512]{2,1,0:T(8,128)(2,1)}), bf16[8,32,512]{2,1,0:T(8,128)(2,1)}, u32[]{:S(2)}, u32[]{:S(2)}) %all-to-all-start.6) | async-done | bytes 262176 | tf_op jit(solution)/shard_map/all_to_all | solution.py:47
  302.5 3.9 %copy.83 = bf16[1,2048,512]{2,1,0:T(8,128)(2,1)} copy(bf16[1,2048,512]{1,2,0:T(8,128)(2,1)} %get-tuple-element.37) | data formatting | bytes 4194304
  308.9 5.5 %copy.84 = f32[1,2048,512]{2,1,0:T(8,128)} copy(f32[1,2048,512]{1,2,0:T(8,128)} %get-tuple-element.74) | data formatting | bytes 8388608
  316.6 5.9 %all-to-all-start.5 = ((bf16[8,32,1152]{2,1,0:T(8,128)(2,1)}), bf16[8,32,1152]{2,1,0:T(8,128)(2,1)S(1)}, u32[]{:S(2)}, u32[]{:S(2)}) async-start(bf16[8,32,1152]{2,1,0:T(8,128)(2,1)} %bitcast.61), calls=%async_computation.5 | async-start | bytes 1179648 | tf_op jit(solution)/shard_map/all_to_all | solution.py:47
  324.5 10.4 %all-to-all-done.5 = bf16[8,32,1152]{2,1,0:T(8,128)(2,1)S(1)} async-done(((bf16[8,32,1152]{2,1,0:T(8,128)(2,1)}), bf16[8,32,1152]{2,1,0:T(8,128)(2,1)S(1)}, u32[]{:S(2)}, u32[]{:S(2)}) %all-to-all-start.5) | async-done | bytes 589856 | tf_op jit(solution)/shard_map/all_to_all | solution.py:47
  (243 shorter events, 129.3 us)
Async XLA Ops:
  0.6 97.4 %copy-start = (bf16[1,11,80]{2,1,0:T(8,128)(2,1)S(1)}, bf16[1,11,80]{2,1,0:T(8,128)(2,1)}, u32[]{:S(2)}) copy-start(bf16[1,11,80]{2,1,0:T(8,128)(2,1)} %param.12) | copy-start | bytes 5284
  2.2 16.2 %all-to-all-start.1 = ((bf16[8,32,512]{2,1,0:T(8,128)(2,1)}), bf16[8,32,512]{2,1,0:T(8,128)(2,1)S(1)}, u32[]{:S(2)}, u32[]{:S(2)}) async-start(bf16[8,32,512]{2,1,0:T(8,128)(2,1)} %broadcast_in_dim.17), calls=%async_computation.1 | async-start | bytes 524288 | tf_op jit(solution)/shard_map/all_to_all | solution.py:47
  19.1 12.3 %all-to-all-start.3 = ((bf16[8,32,512]{2,1,0:T(8,128)(2,1)}), bf16[8,32,512]{2,1,0:T(8,128)(2,1)S(1)}, u32[]{:S(2)}, u32[]{:S(2)}) async-start(bf16[8,32,512]{2,1,0:T(8,128)(2,1)} %broadcast_in_dim.19), calls=%async_computation.3 | async-start | bytes 524288 | tf_op jit(solution)/shard_map/all_to_all | solution.py:47
  32.3 18.8 %all-to-all-start = ((bf16[8,32,1152]{2,1,0:T(8,128)(2,1)}), bf16[8,32,1152]{2,1,0:T(8,128)(2,1)}, u32[]{:S(2)}, u32[]{:S(2)}) async-start(bf16[8,32,1152]{2,1,0:T(8,128)(2,1)} %broadcast_in_dim.16), calls=%async_computation | async-start | bytes 1179648 | tf_op jit(solution)/shard_map/all_to_all | solution.py:47
  51.9 18.7 %all-to-all-start.2 = ((bf16[8,32,1152]{2,1,0:T(8,128)(2,1)}), bf16[8,32,1152]{2,1,0:T(8,128)(2,1)}, u32[]{:S(2)}, u32[]{:S(2)}) async-start(bf16[8,32,1152]{2,1,0:T(8,128)(2,1)} %broadcast_in_dim.18), calls=%async_computation.2 | async-start | bytes 1179648 | tf_op jit(solution)/shard_map/all_to_all | solution.py:47
  56.2 7.2 %collective-permute-start.2 = (bf16[8,32,512]{2,1,0:T(8,128)(2,1)S(1)}, bf16[8,32,512]{2,1,0:T(8,128)(2,1)S(1)}, u32[]{:S(2)}, u32[]{:S(2)}) collective-permute-start(bf16[8,32,512]{2,1,0:T(8,128)(2,1)S(1)} %all-to-all-done.1), channel_id=1, source_target_pairs={{0,2},{1,5},{2,0},{3,7},{4,6},{5,1},{6,4},{7,3},{8,10},{9,13},{10,... | collective-permute-start | bytes 786440 | tf_op jit(solution)/shard_map/ppermute | solution.py:53
  61.3 6.4 %collective-permute-start.6 = (bf16[8,32,512]{2,1,0:T(8,128)(2,1)S(1)}, bf16[8,32,512]{2,1,0:T(8,128)(2,1)S(1)}, u32[]{:S(2)}, u32[]{:S(2)}) collective-permute-start(bf16[8,32,512]{2,1,0:T(8,128)(2,1)S(1)} %all-to-all-done.3), channel_id=1, source_target_pairs={{0,2},{1,5},{2,0},{3,7},{4,6},{5,1},{6,4},{7,3},{8,10},{9,13},{10,... | collective-permute-start | bytes 786440 | tf_op jit(solution)/shard_map/ppermute | solution.py:53
  61.9 12.2 %collective-permute-start = (bf16[8,32,1152]{2,1,0:T(8,128)(2,1)}, bf16[8,32,1152]{2,1,0:T(8,128)(2,1)}, u32[]{:S(2)}, u32[]{:S(2)}) collective-permute-start(bf16[8,32,1152]{2,1,0:T(8,128)(2,1)} %all-to-all-done), channel_id=1, source_target_pairs={{0,2},{1,5},{2,0},{3,7},{4,6},{5,1},{6,4},{7,3},{8,10},{9,13},{10,... | collective-permute-start | bytes 1769480 | tf_op jit(solution)/shard_map/ppermute | solution.py:53
  68.7 29.9 %collective-permute-start.7 = (bf16[2,4,2,32,512]{4,3,2,1,0:T(8,128)(2,1)}, bf16[2,4,2,32,512]{4,3,2,1,0:T(8,128)(2,1)}, u32[]{:S(2)}, u32[]{:S(2)}) collective-permute-start(bf16[2,4,2,32,512]{4,3,2,1,0:T(8,128)(2,1)} %pad_maximum_fusion.31), channel_id=1, source_target_pairs={{0,1},{1,0},{2,3},{3,2},{4,5},{5,4},{6,7},{7,6},{8,9},{9,8},{10,11... | collective-permute-start | bytes 1572872 | tf_op jit(solution)/shard_map/ppermute | solution.py:57
  68.7 29.9 %collective-permute-start.3 = (bf16[2,4,2,32,512]{4,3,0,1,2:T(8,128)(2,1)}, bf16[2,4,2,32,512]{4,3,0,1,2:T(8,128)(2,1)}, u32[]{:S(2)}, u32[]{:S(2)}) collective-permute-start(bf16[2,4,2,32,512]{4,3,0,1,2:T(8,128)(2,1)} %copy.57), channel_id=1, source_target_pairs={{0,1},{1,0},{2,3},{3,2},{4,5},{5,4},{6,7},{7,6},{8,9},{9,8},{10,11... | collective-permute-start | bytes 1572872 | tf_op jit(solution)/shard_map/ppermute | solution.py:57
  70.7 10.1 %collective-permute-start.4 = (bf16[8,32,1152]{2,1,0:T(8,128)(2,1)}, bf16[8,32,1152]{2,1,0:T(8,128)(2,1)S(1)}, u32[]{:S(2)}, u32[]{:S(2)}) collective-permute-start(bf16[8,32,1152]{2,1,0:T(8,128)(2,1)} %all-to-all-done.2), channel_id=1, source_target_pairs={{0,2},{1,5},{2,0},{3,7},{4,6},{5,1},{6,4},{7,3},{8,10},{9,13},{10,... | collective-permute-start | bytes 1769480 | tf_op jit(solution)/shard_map/ppermute | solution.py:53
  84.0 18.4 %collective-permute-start.5 = (bf16[2,4,2,32,1152]{4,3,2,1,0:T(8,128)(2,1)}, bf16[2,4,2,32,1152]{4,3,2,1,0:T(8,128)(2,1)}, u32[]{:S(2)}, u32[]{:S(2)}) collective-permute-start(bf16[2,4,2,32,1152]{4,3,2,1,0:T(8,128)(2,1)} %pad_maximum_fusion.25), channel_id=1, source_target_pairs={{0,1},{1,0},{2,3},{3,2},{4,5},{5,4},{6,7},{7,6},{8,9},{9,8},{10,11... | collective-permute-start | bytes 3538952 | tf_op jit(solution)/shard_map/ppermute | solution.py:57
  84.0 18.4 %collective-permute-start.1 = (bf16[2,4,2,32,1152]{4,3,0,1,2:T(8,128)(2,1)}, bf16[2,4,2,32,1152]{4,3,0,1,2:T(8,128)(2,1)}, u32[]{:S(2)}, u32[]{:S(2)}) collective-permute-start(bf16[2,4,2,32,1152]{4,3,0,1,2:T(8,128)(2,1)} %copy.52), channel_id=1, source_target_pairs={{0,1},{1,0},{2,3},{3,2},{4,5},{5,4},{6,7},{7,6},{8,9},{9,8},{10,11... | collective-permute-start | bytes 3538952 | tf_op jit(solution)/shard_map/ppermute | solution.py:57
  98.6 10.9 %copy-start.43 = (bf16[2048,80]{0,1:T(8,128)(2,1)}, bf16[2048,80]{0,1:T(8,128)(2,1)S(1)}, u32[]{:S(2)}) copy-start(bf16[2048,80]{0,1:T(8,128)(2,1)S(1)} %convolution_convert_fusion) | copy-start | bytes 983044
  102.1 18.3 %copy-start.37 = (bf16[4,2,2,2,32,512]{5,4,3,2,1,0:T(8,128)(2,1)}, bf16[4,2,2,2,32,512]{5,4,3,2,1,0:T(8,128)(2,1)S(1)}, u32[]{:S(2)}) copy-start(bf16[4,2,2,2,32,512]{5,4,3,2,1,0:T(8,128)(2,1)S(1)} %copy.60) | copy-start | bytes 3145732
  102.3 40.1 %copy-start.35 = (bf16[4,2,2,2,32,512]{5,4,3,2,1,0:T(8,128)(2,1)}, bf16[4,2,2,2,32,512]{5,4,3,2,1,0:T(8,128)(2,1)S(1)}, u32[]{:S(2)}) copy-start(bf16[4,2,2,2,32,512]{5,4,3,2,1,0:T(8,128)(2,1)S(1)} %copy.70) | copy-start | bytes 3145732
  128.8 13.6 %copy-start.14 = (bf16[2048,512]{0,1:T(8,128)(2,1)}, bf16[2048,512]{0,1:T(8,128)(2,1)S(1)}, u32[]{:S(2)}) copy-start(bf16[2048,512]{0,1:T(8,128)(2,1)S(1)} %get-tuple-element.75) | copy-start | bytes 6291460
  158.4 39.3 %copy-start.40 = (f32[1024,11]{0,1:T(8,128)}, f32[1024,11]{0,1:T(8,128)S(1)}, u32[]{:S(2)}) copy-start(f32[1024,11]{0,1:T(8,128)S(1)} %get-tuple-element.83) | copy-start | bytes 135172
  190.5 17.7 %copy-start.41 = (f32[1024,11]{0,1:T(8,128)}, f32[1024,11]{0,1:T(8,128)S(1)}, u32[]{:S(2)}) copy-start(f32[1024,11]{0,1:T(8,128)S(1)} %get-tuple-element.85) | copy-start | bytes 135172
  207.1 49.8 %collective-permute-start.14 = (bf16[4,4,32,512]{3,2,1,0:T(8,128)(2,1)}, bf16[4,4,32,512]{3,2,1,0:T(8,128)(2,1)}, u32[]{:S(2)}, u32[]{:S(2)}) collective-permute-start(bf16[4,4,32,512]{3,2,1,0:T(8,128)(2,1)} %fusion.60), channel_id=1, source_target_pairs={{0,1},{1,0},{2,3},{3,2},{4,5},{5,4},{6,7},{7,6},{8,9},{9,8},{10,11... | collective-permute-start | bytes 1572872 | tf_op jit(solution)/shard_map/ppermute | solution.py:71
  215.3 45.0 %collective-permute-start.12 = (bf16[4,4,32,512]{3,2,1,0:T(8,128)(2,1)}, bf16[4,4,32,512]{3,2,1,0:T(8,128)(2,1)}, u32[]{:S(2)}, u32[]{:S(2)}) collective-permute-start(bf16[4,4,32,512]{3,2,1,0:T(8,128)(2,1)} %fusion.59), channel_id=1, source_target_pairs={{0,1},{1,0},{2,3},{3,2},{4,5},{5,4},{6,7},{7,6},{8,9},{9,8},{10,11... | collective-permute-start | bytes 1572872 | tf_op jit(solution)/shard_map/ppermute | solution.py:71
  232.7 39.8 %collective-permute-start.8 = (bf16[4,4,32,1152]{3,2,1,0:T(8,128)(2,1)S(1)}, bf16[4,4,32,1152]{3,2,1,0:T(8,128)(2,1)}, u32[]{:S(2)}, u32[]{:S(2)}) collective-permute-start(bf16[4,4,32,1152]{3,2,1,0:T(8,128)(2,1)S(1)} %fusion.52), channel_id=1, source_target_pairs={{0,1},{1,0},{2,3},{3,2},{4,5},{5,4},{6,7},{7,6},{8,9},{9,8},{10,11... | collective-permute-start | bytes 3538952 | tf_op jit(solution)/shard_map/ppermute | solution.py:71
  233.3 43.4 %collective-permute-start.10 = (bf16[4,4,32,1152]{3,2,1,0:T(8,128)(2,1)}, bf16[4,4,32,1152]{3,2,1,0:T(8,128)(2,1)}, u32[]{:S(2)}, u32[]{:S(2)}) collective-permute-start(bf16[4,4,32,1152]{3,2,1,0:T(8,128)(2,1)} %fusion.53), channel_id=1, source_target_pairs={{0,1},{1,0},{2,3},{3,2},{4,5},{5,4},{6,7},{7,6},{8,9},{9,8},{10,11... | collective-permute-start | bytes 3538952 | tf_op jit(solution)/shard_map/ppermute | solution.py:71
  258.8 6.4 %collective-permute-start.15 = (bf16[4,2,32,512]{3,2,1,0:T(8,128)(2,1)S(1)}, bf16[4,2,32,512]{3,2,1,0:T(8,128)(2,1)S(1)}, u32[]{:S(2)}, u32[]{:S(2)}) collective-permute-start(bf16[4,2,32,512]{3,2,1,0:T(8,128)(2,1)S(1)} %pad_maximum_fusion.34), channel_id=1, source_target_pairs={{0,2},{1,5},{2,0},{3,7},{4,6},{5,1},{6,4},{7,3},{8,10},{9,13},{10,... | collective-permute-start | bytes 786440 | tf_op jit(solution)/shard_map/ppermute | solution.py:83
  261.7 10.1 %collective-permute-start.13 = (bf16[4,2,32,512]{3,2,1,0:T(8,128)(2,1)S(1)}, bf16[4,2,32,512]{3,2,1,0:T(8,128)(2,1)S(1)}, u32[]{:S(2)}, u32[]{:S(2)}) collective-permute-start(bf16[4,2,32,512]{3,2,1,0:T(8,128)(2,1)S(1)} %pad_maximum_fusion.33), channel_id=1, source_target_pairs={{0,2},{1,5},{2,0},{3,7},{4,6},{5,1},{6,4},{7,3},{8,10},{9,13},{10,... | collective-permute-start | bytes 786440 | tf_op jit(solution)/shard_map/ppermute | solution.py:83
  266.0 15.6 %all-to-all-start.7 = ((bf16[8,32,512]{2,1,0:T(8,128)(2,1)}), bf16[8,32,512]{2,1,0:T(8,128)(2,1)S(1)}, u32[]{:S(2)}, u32[]{:S(2)}) async-start(bf16[8,32,512]{2,1,0:T(8,128)(2,1)} %bitcast.77), calls=%async_computation.7 | async-start | bytes 524288 | tf_op jit(solution)/shard_map/all_to_all | solution.py:47
  275.4 12.2 %collective-permute-start.9 = (bf16[4,2,32,1152]{3,2,1,0:T(8,128)(2,1)S(1)}, bf16[4,2,32,1152]{3,2,1,0:T(8,128)(2,1)S(1)}, u32[]{:S(2)}, u32[]{:S(2)}) collective-permute-start(bf16[4,2,32,1152]{3,2,1,0:T(8,128)(2,1)S(1)} %pad_maximum_fusion.28), channel_id=1, source_target_pairs={{0,2},{1,5},{2,0},{3,7},{4,6},{5,1},{6,4},{7,3},{8,10},{9,13},{10,... | collective-permute-start | bytes 1769480 | tf_op jit(solution)/shard_map/ppermute | solution.py:83
  280.6 33.9 %collective-permute-start.11 = (bf16[4,2,32,1152]{3,2,1,0:T(8,128)(2,1)}, bf16[4,2,32,1152]{3,2,1,0:T(8,128)(2,1)}, u32[]{:S(2)}, u32[]{:S(2)}) collective-permute-start(bf16[4,2,32,1152]{3,2,1,0:T(8,128)(2,1)} %pad_maximum_fusion.29), channel_id=1, source_target_pairs={{0,2},{1,5},{2,0},{3,7},{4,6},{5,1},{6,4},{7,3},{8,10},{9,13},{10,... | collective-permute-start | bytes 1769480 | tf_op jit(solution)/shard_map/ppermute | solution.py:83
  281.6 14.3 %all-to-all-start.6 = ((bf16[8,32,512]{2,1,0:T(8,128)(2,1)}), bf16[8,32,512]{2,1,0:T(8,128)(2,1)}, u32[]{:S(2)}, u32[]{:S(2)}) async-start(bf16[8,32,512]{2,1,0:T(8,128)(2,1)} %bitcast.71), calls=%async_computation.6 | async-start | bytes 524288 | tf_op jit(solution)/shard_map/all_to_all | solution.py:47
  288.4 18.0 %copy-start.12 = (bf16[1,2048,512]{1,2,0:T(8,128)(2,1)S(1)}, bf16[1,2048,512]{1,2,0:T(8,128)(2,1)}, u32[]{:S(2)}) copy-start(bf16[1,2048,512]{1,2,0:T(8,128)(2,1)} %get-tuple-element.38) | copy-start | bytes 6291460
  295.9 20.6 %all-to-all-start.4 = ((bf16[8,32,1152]{2,1,0:T(8,128)(2,1)}), bf16[8,32,1152]{2,1,0:T(8,128)(2,1)S(1)}, u32[]{:S(2)}, u32[]{:S(2)}) async-start(bf16[8,32,1152]{2,1,0:T(8,128)(2,1)} %bitcast.53), calls=%async_computation.4 | async-start | bytes 1179648 | tf_op jit(solution)/shard_map/all_to_all | solution.py:47
  316.6 18.3 %all-to-all-start.5 = ((bf16[8,32,1152]{2,1,0:T(8,128)(2,1)}), bf16[8,32,1152]{2,1,0:T(8,128)(2,1)S(1)}, u32[]{:S(2)}, u32[]{:S(2)}) async-start(bf16[8,32,1152]{2,1,0:T(8,128)(2,1)} %bitcast.61), calls=%async_computation.5 | async-start | bytes 1179648 | tf_op jit(solution)/shard_map/all_to_all | solution.py:47
  (42 other events, 157.5 us)

commit v2 on v1

v2 whole, which is shorter than its diff:
```python
import functools

import jax
import jax.numpy as jnp
from jax import lax
from jax.experimental import pallas as pl
from jax.experimental.pallas import tpu as pltpu
from jax.sharding import PartitionSpec as P

FIRST_DILATION = 512
AXES = ("dp", "group")
LANES = 128
TILE = 512
VMEM = 56 * 1024 * 1024
LOW = jnp.bfloat16
FULL = jnp.float32


def dot(left, right):
    return jnp.dot(left, right, preferred_element_type=FULL)


def dot_cols(left, right, **more):
    return lax.dot_general(
        left, right, (((1,), (1,)), ((), ())), preferred_element_type=FULL, **more
    )


def dot_rows(left, right, **more):
    return lax.dot_general(
        left, right, (((0,), (0,)), ((), ())), preferred_element_type=FULL, **more
    )


class Sizes:
    def __init__(self, channels, mel_count):
        self.channels = channels
        self.mel = mel_count
        self.taps = 2 * channels
        self.extra = -(-(mel_count + 2) // LANES) * LANES
        self.conv = self.taps + self.extra
        self.pack = self.conv + channels


def mask_of(info_ref, start, rows):
    places = start + lax.broadcasted_iota(jnp.int32, (rows, 1), 0)
    return (places < info_ref[0]).astype(FULL)


def frames_of(info_ref, start, rows):
    places = start + lax.broadcasted_iota(jnp.int32, (rows, LANES), 0)
    first = lax.broadcasted_iota(jnp.int32, (rows, LANES), 1) * info_ref[1]
    return ((places >= first) & (places < first + info_ref[1])).astype(FULL).astype(LOW)


def out_bias_row(size, w_ref, rows):
    column = lax.broadcasted_iota(jnp.int32, (8, size.extra), 1)
    pick = (column == size.mel + 1).astype(FULL).astype(LOW)
    return dot_cols(pick, w_ref[rows, size.taps : size.conv])[0:1]


def gates(taps, w_ref, size, side):
    channels = size.channels
    width = channels // 2
    low = slice(side * width, (side + 1) * width)
    high = slice(channels + side * width, channels + (side + 1) * width)
    tangent = jnp.tanh(dot_cols(taps, w_ref[low, : size.conv]))
    sig_gate = 0.5 * jnp.tanh(0.5 * dot_cols(taps, w_ref[high, : size.conv])) + 0.5
    gated = tangent * sig_gate
    return low, high, gated, sig_gate * (1.0 - tangent * tangent), gated * (1.0 - sig_gate)


def forward_0(size, info_ref, prev_ref, x_ref, w_ref, mel_ref, low0_ref, h1_ref, low1_ref, gated_ref, slope_ref):
    step = pl.program_id(0)
    rows, channels = x_ref.shape
    mask = mask_of(info_ref, step * rows, rows)
    hidden = x_ref[...].astype(FULL) * mask
    low = hidden.astype(LOW)
    low0_ref[...] = low
    prev_mask = mask_of(info_ref, (step - 1) * rows, rows) * (step > 0).astype(FULL)
    prev = (prev_ref[...].astype(FULL) * prev_mask).astype(LOW)
    cond = dot(frames_of(info_ref, step * rows, rows), mel_ref[...]).astype(LOW)
    taps = jnp.concatenate([prev, low, cond], axis=1)
    for side in range(2):
        first, second, gated, slope_a, slope_b = gates(taps, w_ref, size, side)
        gated_ref[:, first] = gated.astype(LOW)
        slope_ref[:, first] = slope_a.astype(LOW)
        slope_ref[:, second] = slope_b.astype(LOW)
    moved = dot_cols(gated_ref[...], w_ref[:channels, size.conv :])
    moved = moved + out_bias_row(size, w_ref, slice(0, channels))
    hidden = (hidden + moved) * mask
    h1_ref[...] = hidden
    low1_ref[...] = hidden.astype(LOW)


def forward_1(size, info_ref, low1_ref, w_ref, mel_ref, go_ref, gs_ref, prev_ref, gated_ref, pre_ref, proj_ref, carry_ref):
    step = pl.program_id(0)
    rows, channels = low1_ref.shape
    mask = mask_of(info_ref, step * rows, rows)
    low = low1_ref[...]
    wide = low.astype(FULL)

    @pl.when(step == 0)
    def _():
        carry_ref[...] = jnp.zeros_like(carry_ref)

    place = lax.broadcasted_iota(jnp.int32, (rows, 1), 0)
    prev = jnp.where(place == 0, carry_ref[7:8], pltpu.roll(wide, 1, 0)).astype(LOW)
    carry_ref[...] = wide[rows - 8 :]
    prev_ref[...] = prev
    cond = dot(frames_of(info_ref, step * rows, rows), mel_ref[...]).astype(LOW)
    taps = jnp.concatenate([prev, low, cond], axis=1)
    proj_ref[:, :channels] = (go_ref[...].astype(FULL) * mask).astype(LOW)
    proj_ref[:, channels:] = (gs_ref[...].astype(FULL) * mask).astype(LOW)
    grad_gated = dot(proj_ref[...], w_ref[:, size.conv :])
    for side in range(2):
        first, second, gated, slope_a, slope_b = gates(taps, w_ref, size, side)
        gated_ref[:, first] = gated.astype(LOW)
        pre_ref[:, first] = (grad_gated[:, first] * slope_a).astype(LOW)
        pre_ref[:, second] = (grad_gated[:, first] * slope_b).astype(LOW)


def weight_grads(size, shift, info_ref, pre_ref, proj_ref, low_ref, prev_ref, gated_ref, mel_ref, wc_ref, out_ref, melg_ref, frames_ref):
    step = pl.program_id(0)
    samples = low_ref.shape[0]

    @pl.when(step == 0)
    def _():
        frames_ref[...] = frames_of(info_ref, 0, samples)
        melg_ref[...] = jnp.zeros_like(melg_ref)

    pre = pre_ref[...]
    if shift % TILE == 0:
        early = dot_rows(pre[shift:], low_ref[: samples - shift])
    else:
        early = dot_rows(pre, prev_ref[...])
    out_ref[:, : size.channels] = early.astype(LOW)
    out_ref[:, size.channels : size.taps] = dot_rows(pre, low_ref[...]).astype(LOW)
    sums = dot_rows(pre, frames_ref[...])
    exact = dict(precision=lax.Precision.HIGHEST)
    extra = jnp.dot(sums, mel_ref[...].astype(FULL), preferred_element_type=FULL, **exact)
    melg_ref[...] += dot_rows(sums, wc_ref[...].astype(FULL), **exact)
    proj = proj_ref[...]
    bias = jnp.sum(dot_rows(proj, frames_ref[...]), axis=1, keepdims=True)
    column = lax.broadcasted_iota(jnp.int32, extra.shape, 1)
    extra = jnp.where(column == size.mel + 1, bias, extra)
    out_ref[:, size.taps : size.conv] = extra.astype(LOW)
    out_ref[:, size.conv :] = dot_rows(proj, gated_ref[...]).astype(LOW)


def backward_0(size, info_ref, pre1_ref, w1_ref, w0_ref, go_ref, gs_ref, slope_ref, gh_ref, proj_ref, pre0_ref, carry_ref):
    step = pl.program_id(0)
    rows, channels = go_ref.shape
    tile = pl.num_programs(0) - 1 - step
    mask = mask_of(info_ref, tile * rows, rows)

    @pl.when(step == 0)
    def _():
        carry_ref[...] = jnp.zeros_like(carry_ref)

    pre1 = pre1_ref[...]
    early = dot(pre1, w1_ref[:, :channels])
    place = lax.broadcasted_iota(jnp.int32, (rows, 1), 0)
    later = jnp.where(place == rows - 1, carry_ref[0:1], pltpu.roll(early, rows - 1, 0))
    carry_ref[...] = early[:8]
    now = dot(pre1, w1_ref[:, channels : size.taps])
    grad = (go_ref[...].astype(FULL) * mask + now + later) * mask
    gh_ref[...] = grad
    proj_ref[:, :channels] = grad.astype(LOW)
    proj_ref[:, channels:] = (gs_ref[...].astype(FULL) * mask).astype(LOW)
    grad_gated = dot(proj_ref[...], w0_ref[:, size.conv :])
    pre0_ref[:, :channels] = (grad_gated * slope_ref[:, :channels].astype(FULL)).astype(LOW)
    pre0_ref[:, channels:] = (grad_gated * slope_ref[:, channels:].astype(FULL)).astype(LOW)


def outputs(size, info_ref, gh_ref, pre_ref, next_ref, w0_ref, w1_ref, h1_ref, gated0_ref, gated1_ref, res_ref, skip_ref, sg_ref):
    step = pl.program_id(0)
    rows, channels = gh_ref.shape
    mask = mask_of(info_ref, step * rows, rows)
    grad = gh_ref[...] + dot(pre_ref[...], w0_ref[:, channels : size.taps])
    later = dot(next_ref[...], w0_ref[:, :channels])
    grad = grad + jnp.where(step < pl.num_programs(0) - 1, later, 0.0)
    sg_ref[...] = grad * mask
    gated1 = gated1_ref[...]
    res = dot_cols(gated1, w1_ref[:channels, size.conv :])
    res = res + out_bias_row(size, w1_ref, slice(0, channels))
    res_ref[...] = ((h1_ref[...] + res) * mask).astype(LOW)
    late = slice(channels, 2 * channels)
    skip = dot_cols(gated0_ref[...], w0_ref[late, size.conv :])
    skip = skip + dot_cols(gated1, w1_ref[late, size.conv :])
    skip = skip + out_bias_row(size, w0_ref, late) + out_bias_row(size, w1_ref, late)
    skip_ref[...] = (skip * mask).astype(LOW)


def call(kernel, grid, info, operands, specs, outs, out_specs, scratch, flops):
    moved = sum(x.size * x.dtype.itemsize for x in operands)
    moved += sum(x.size * x.dtype.itemsize for x in outs)
    return pl.pallas_call(
        kernel,
        grid_spec=pltpu.PrefetchScalarGridSpec(
            num_scalar_prefetch=1,
            grid=(grid,),
            in_specs=specs,
            out_specs=out_specs,
            scratch_shapes=scratch,
        ),
        out_shape=outs,
        compiler_params=pltpu.CompilerParams(
            vmem_limit_bytes=VMEM, dimension_semantics=("arbitrary",)
        ),
        cost_estimate=pl.CostEstimate(flops=flops, bytes_accessed=moved, transcendentals=0),
    )(info, *operands)


def shape_of(*shape, dtype=LOW):
    return jax.ShapeDtypeStruct(shape, dtype)


def tiled(width, place=lambda i: i):
    return pl.BlockSpec((TILE, width), lambda i, info: (place(i), 0))


def fixed(*shape):
    return pl.BlockSpec(shape, lambda i, info: (0,) * len(shape))


def put_together(rows, core_ref, *refs):
    pieces, out_ref, sems = refs[:4], refs[4], refs[5]
    core, a, b = core_ref[0], core_ref[1], core_ref[2]
    copies = []
    for index, piece in enumerate(pieces):
        source = core if index < 2 else 1 - core
        alone = jnp.where(source == 0, a, b)
        alone = alone if index % 2 == 0 else 1 - alone
        for block in range(piece.shape[0]):
            rest, varied = block // 2, block % 2
            at_b = jnp.where(source == 0, varied, alone)
            at_a = jnp.where(source == 0, alone, varied)
            place = ((rest * 2 + at_b) * 2 + at_a) * 2 + source
            copies.append(
                pltpu.make_async_copy(
                    piece.at[block],
                    out_ref.at[pl.ds(pl.multiple_of(place * rows, rows), rows)],
                    sems.at[index, block],
                )
            )
    for copy in copies:
        copy.start()
    for copy in copies:
        copy.wait()


class Wires:
    def __init__(self, dp, cores):
        assert dp % 4 == 0 and cores == 2
        self.rest = dp // 4
        self.devices = dp * 2
        me = lax.axis_index(AXES)
        self.core = me % 2
        self.a = (me // 2) % 2
        self.b = (me // 4) % 2
        self.alone = jnp.where(self.core == 0, self.a, self.b)
        self.core_pairs = [(i, i ^ 1) for i in range(self.devices)]
        self.alone_pairs = [(i, i ^ (2 if i % 2 == 0 else 4)) for i in range(self.devices)]
        groups = []
        for core in range(2):
            for still in range(2):
                members = []
                for rest in range(self.rest):
                    for varied in range(2):
                        b, a = (varied, still) if core == 0 else (still, varied)
                        members.append(((rest * 2 + b) * 2 + a) * 2 + core)
                groups.append(members)
        self.groups = groups

    def spread(self, blocks):
        return lax.all_to_all(blocks, AXES, 0, 0, tiled=True, axis_index_groups=self.groups)

    def gather(self, block):
        rows, depth = block.shape
        count = self.rest * 2
        mine = self.spread(jnp.broadcast_to(block[None], (count, rows, depth)))
        other = lax.ppermute(mine, AXES, self.alone_pairs)
        passed = lax.ppermute(mine, AXES, self.core_pairs)
        passed_other = lax.ppermute(other, AXES, self.core_pairs)
        pieces = (mine, other, passed, passed_other)
        if rows % 16:
            return self.put_in_order(pieces)
        return pl.pallas_call(
            functools.partial(put_together, rows),
            in_specs=[pl.BlockSpec(memory_space=pltpu.SMEM)]
            + [pl.BlockSpec(memory_space=pl.ANY)] * 4,
            out_specs=pl.BlockSpec(memory_space=pl.ANY),
            out_shape=shape_of(self.devices * rows, depth),
            scratch_shapes=[pltpu.SemaphoreType.DMA((4, count))],
        )(jnp.stack([self.core, self.a, self.b]).astype(jnp.int32), *pieces)

    def put_in_order(self, pieces):
        mine, other, passed, passed_other = pieces
        count, rows, depth = mine.shape
        sibling = jnp.where(self.core == 0, self.b, self.a)

        def ordered(own, away, alone):
            low = jnp.where(alone == 0, own, away)
            high = jnp.where(alone == 0, away, own)
            return jnp.stack([low, high]).reshape(2, self.rest, 2, rows, depth)

        half = ordered(mine, other, self.alone)
        half_passed = ordered(passed, passed_other, sibling)
        first = jnp.where(self.core == 0, half, half_passed)
        second = jnp.where(self.core == 0, half_passed, half)
        whole = jnp.stack(
            [first.transpose(1, 2, 0, 3, 4), second.transpose(1, 0, 2, 3, 4)], axis=3
        )
        return whole.reshape(self.devices * rows, depth)

    def scatter_sum(self, full):
        depth = full.shape[1]
        rows = full.shape[0] // self.devices
        blocks = full.reshape(self.rest, 4, 2, rows, depth)
        away = lax.dynamic_index_in_dim(blocks, 1 - self.core, 2, keepdims=False)
        here = lax.dynamic_index_in_dim(blocks, self.core, 2, keepdims=False)
        came = lax.ppermute(away, AXES, self.core_pairs)
        chip = (here.astype(FULL) + came.astype(FULL)).astype(LOW)

        def pick(side):
            places = [
                jnp.where(self.core == 0, step * 2 + side, side * 2 + step) for step in range(2)
            ]
            return jnp.stack(
                [lax.dynamic_index_in_dim(chip, place, 1, keepdims=False) for place in places],
                axis=1,
            )

        came = lax.ppermute(pick(1 - self.alone), AXES, self.alone_pairs)
        pair = pick(self.alone).astype(FULL) + came.astype(FULL)
        parts = self.spread(pair.astype(LOW).reshape(self.rest * 2, rows, depth))
        return jnp.sum(parts.astype(FULL), axis=0)


def per_device(
    dp,
    cores,
    samples,
    mel,
    lengths,
    hops,
    conv_weight,
    cond_weight,
    conv_bias,
    out_weight,
    out_bias,
    grad_out,
    grad_skip,
):
    wires = Wires(dp, cores)
    sample_count, channels = samples.shape[1:]
    frame_count, mel_count = mel.shape[1:]
    layers = conv_weight.shape[0]
    size = Sizes(channels, mel_count)
    gate = 2 * channels
    assert layers == 2 and sample_count % TILE == 0 and TILE == FIRST_DILATION
    steps = sample_count // TILE
    info = jnp.concatenate([lengths, hops])
    x, go, gs = samples[0], grad_out[0], grad_skip[0]
    mel_table = jnp.zeros((LANES, size.extra), LOW)
    mel_table = mel_table.at[:frame_count, :mel_count].set(mel[0])
    mel_table = mel_table.at[:frame_count, mel_count].set(1.0)

    packs = []
    for layer in range(layers):
        fill = jnp.zeros((size.extra - mel_count - 2, conv_weight.shape[2]), LOW)
        pack = jnp.concatenate(
            [
                conv_weight[layer],
                cond_weight[layer],
                conv_bias[layer][None],
                out_bias[layer][None],
                fill,
                out_weight[layer],
            ],
            axis=0,
        ).T
        packs.append(wires.gather(pack))
    w0, w1 = packs

    weights = fixed(gate, size.pack)
    table = fixed(LANES, size.extra)
    macs = sample_count * channels * channels

    low0, h1, low1, gated0, slope0 = call(
        functools.partial(forward_0, size),
        steps,
        info,
        (x, x, w0, mel_table),
        [tiled(channels, lambda i: jnp.maximum(i - 1, 0)), tiled(channels), weights, table],
        (
            shape_of(sample_count, channels),
            shape_of(sample_count, channels, dtype=FULL),
            shape_of(sample_count, channels),
            shape_of(sample_count, channels),
            shape_of(sample_count, gate),
        ),
        [tiled(channels), tiled(channels), tiled(channels), tiled(channels), tiled(gate)],
        [],
        10 * macs,
    )
    prev1, gated1, pre1, proj1 = call(
        functools.partial(forward_1, size),
        steps,
        info,
        (low1, w1, mel_table, go, gs),
        [tiled(channels), weights, table, tiled(channels), tiled(channels)],
        (
            shape_of(sample_count, channels),
            shape_of(sample_count, channels),
            shape_of(sample_count, gate),
            shape_of(sample_count, gate),
        ),
        [tiled(channels), tiled(channels), tiled(gate), tiled(gate)],
        [pltpu.VMEM((8, channels), FULL)],
        12 * macs,
    )

    part = gate // 4
    columns = pl.BlockSpec((sample_count, part), lambda i, info: (0, i))
    whole = fixed(sample_count, channels)

    def weight_part(shift, pre, proj, low, prev, gated, w):
        cond_columns = pl.BlockSpec(
            (part, size.extra), lambda i, info: (i, size.taps // size.extra)
        )
        return call(
            functools.partial(weight_grads, size, shift),
            4,
            info,
            (pre, proj, low, prev, gated, mel_table, w),
            [columns, columns, whole, whole, whole, table, cond_columns],
            (shape_of(gate, size.pack), shape_of(LANES, size.extra, dtype=FULL)),
            [
                pl.BlockSpec((part, size.pack), lambda i, info: (i, 0)),
                fixed(LANES, size.extra),
            ],
            [pltpu.VMEM((sample_count, LANES), LOW)],
            12 * macs,
        )

    grads1, melg1 = weight_part(1, pre1, proj1, low1, prev1, gated1, w1)
    own1 = wires.scatter_sum(grads1)

    backwards = lambda i: steps - 1 - i
    gh1, proj0, pre0 = call(
        functools.partial(backward_0, size),
        steps,
        info,
        (pre1, w1, w0, go, gs, slope0),
        [
            tiled(gate, backwards),
            weights,
            weights,
            tiled(channels, backwards),
            tiled(channels, backwards),
            tiled(gate, backwards),
        ],
        (
            shape_of(sample_count, channels, dtype=FULL),
            shape_of(sample_count, gate),
            shape_of(sample_count, gate),
        ),
        [tiled(channels, backwards), tiled(gate, backwards), tiled(gate, backwards)],
        [pltpu.VMEM((8, channels), FULL)],
        12 * macs,
    )
    grads0, melg0 = weight_part(FIRST_DILATION, pre0, proj0, low0, low0, gated0, w0)
    own0 = wires.scatter_sum(grads0)

    residual_out, skip_output_sum, samples_grad = call(
        functools.partial(outputs, size),
        steps,
        info,
        (gh1, pre0, pre0, w0, w1, h1, gated0, gated1),
        [
            tiled(channels),
            tiled(gate),
            tiled(gate, lambda i: jnp.minimum(i + 1, steps - 1)),
            weights,
            weights,
            tiled(channels),
            tiled(channels),
            tiled(channels),
        ],
        (
            shape_of(sample_count, channels),
            shape_of(sample_count, channels),
            shape_of(sample_count, channels, dtype=FULL),
        ),
        [tiled(channels), tiled(channels), tiled(channels)],
        [],
        14 * macs,
    )
    mel_grad = (melg0 + melg1)[:frame_count, :mel_count]
    own = jnp.stack([own0, own1]).transpose(0, 2, 1)
    at = size.taps + mel_count
    return (
        residual_out[None],
        skip_output_sum[None],
        samples_grad[None],
        mel_grad[None],
        own[:, : size.taps],
        own[:, size.taps : at],
        own[:, at],
        own[:, size.conv :],
        own[:, at + 1],
    )


def solution(mesh):
    dp, cores = mesh.shape["dp"], mesh.shape["group"]

    def everything(*arrays):
        return per_device(dp, cores, *arrays)

    clips = P(AXES, None, None)
    columns = P(None, None, AXES)
    biases = P(None, AXES)
    return jax.shard_map(
        everything,
        mesh=mesh,
        in_specs=(
            clips, clips, P(AXES), P(AXES), columns, columns, biases, columns, biases, clips, clips,
        ),
        out_specs=(clips, clips, clips, clips, columns, columns, biases, columns, biases),
        check_vma=False,
    )
```

time: 344 us -> 446 us (1.30); the launches traced: 338 us -> 445 us
  Pallas kernels: 0 us -> 303 us
  matrix products: 80.9 us -> 0 us
  local copies, waits for them, and re-layouts: 86.1 us -> 18.2 us
  other arithmetic: 57.3 us -> 11.1 us
  waiting for transfers between devices: 58.1 us -> 85.3 us
  starting transfers between devices: 52.3 us -> 25.2 us
    pallas_call x0 -> x8, Pallas kernels: none -> 303 us  [the longest x2 211 us: gather(): pl.pallas_call(functools.partial(put_together, rows), in_specs=[pl.BlockS...]
    dot_general x19 -> x0, matrix products: 80.9 us -> none  [the longest x6 24.5 us: contract_rows(): lax.dot_general(left, right, (((0,), (0,)), ((), ())), preferred_element_...]
    unnamed x105 -> x19, local copies, waits for them, and re-layouts: 37.9 us -> 0.64 us
    ppermute x12 -> x8, waiting for transfers between devices: 2.89 us -> 27.7 us  [the longest x2 25.9 us: scatter_sum(): came = lax.ppermute(pick(1 - self.alone), AXES, self.alone_pairs)]
    all_to_all x8 -> x4, starting transfers between devices: 40.3 us -> 18.1 us  [spread(): lax.all_to_all(blocks, AXES, 0, 0, tiled=True, axis_index_groups=self.gro...]
    concatenate x7 -> x0, local copies, waits for them, and re-layouts: 17.1 us -> none  [per_device(): jnp.concatenate([conv_grad, cond_grad, jnp.sum(frame_sums, axis=1, keepdi...]
    another operation x19 -> x4, other arithmetic: 19 us -> 3.26 us  [the longest x8 7.63 us: gather(): jnp.stack([first.transpose(1, 2, 0, 3, 4), second.transpose(1, 0, 2, 3, 4...]
    broadcast_in_dim x1, other arithmetic: 14.2 us -> 0.72 us  [per_device(): mel_grad[None]]
  transfers between devices with their start and end apart: 24 -> 14, of which waited for: 10 -> 8; matrix products, arithmetic and copies ran while one was open for 32% -> 3% of each run, Pallas kernels for 0% -> 37%
where the time goes in v2:
time: 446 us; the launch traced here: 445 us
  Pallas kernels  303 us (68%)
  waiting for transfers between devices  85.3 us (19%)
  starting transfers between devices  25.2 us (6%)
  local copies, waits for them, and re-layouts  18.2 us (4%)
  other arithmetic  11.1 us (2%)
    pallas_call x2, Pallas kernels, gather(): pl.pallas_call(functools.partial(put_together, rows), in_specs=[pl.BlockS...  211 us
    pallas_call x6, Pallas kernels, call(): pl.pallas_call(kernel, grid_spec=pltpu.PrefetchScalarGridSpec(num_scalar_...  92.3 us
    all_to_all x4, waiting for transfers between devices, spread(): lax.all_to_all(blocks, AXES, 0, 0, tiled=True, axis_index_groups=self.gro...  47.7 us
    ppermute x2, waiting for transfers between devices, scatter_sum(): came = lax.ppermute(pick(1 - self.alone), AXES, self.alone_pairs)  25.9 us
    all_to_all x4, starting transfers between devices, spread(): lax.all_to_all(blocks, AXES, 0, 0, tiled=True, axis_index_groups=self.gro...  18.1 us
    ppermute x2, waiting for transfers between devices, gather(): other = lax.ppermute(mine, AXES, self.alone_pairs)  9.99 us
  transfers between devices with their start and end apart: 14, of which 8 were waited for; matrix products, arithmetic and copies ran while one was open for 3% of the time, Pallas kernels for 37%

profile of v2, /device:TPU:0, one launch (start us, length us, event | category | flops | bytes accessed | tf_op | source)
XLA Modules:
  0.0 444.9 jit_solution(9140043997254501969)
XLA Ops:
  5.8 7.4 %all-to-all-start = ((bf16[8,32,1664]{2,1,0:T(8,128)(2,1)}), bf16[8,32,1664]{2,1,0:T(8,128)(2,1)S(1)}, u32[]{:S(2)}, u32[]{:S(2)}) async-start(bf16[8,32,1664]{2,1,0:T(8,128)(2,1)} %broadcast_in_dim.12), calls=%async_computation | async-start | bytes 1703936 | tf_op jit(solution)/shard_map/all_to_all | solution.py:277
  13.5 21.3 %all-to-all-done.refs_0_ = bf16[8,32,1664]{2,1,0:T(8,128)(2,1)S(1)} async-done(((bf16[8,32,1664]{2,1,0:T(8,128)(2,1)}), bf16[8,32,1664]{2,1,0:T(8,128)(2,1)S(1)}, u32[]{:S(2)}, u32[]{:S(2)}) %all-to-all-start) | async-done | bytes 852000 | tf_op jit(solution)/shard_map/all_to_all | solution.py:277
  35.9 3.6 all-to-all-start.1
  39.4 1.5 collective-permute-start
  40.9 20.2 %all-to-all-done.1.refs_0_ = bf16[8,32,1664]{2,1,0:T(8,128)(2,1)S(1)} async-done(((bf16[8,32,1664]{2,1,0:T(8,128)(2,1)}), bf16[8,32,1664]{2,1,0:T(8,128)(2,1)S(1)}, u32[]{:S(2)}, u32[]{:S(2)}) %all-to-all-start.1) | async-done | bytes 852000 | tf_op jit(solution)/shard_map/all_to_all | solution.py:277
  61.1 1.4 collective-permute-start.3
  63.9 10.0 %collective-permute-done.3.refs_1_ = bf16[8,32,1664]{2,1,0:T(8,128)(2,1)S(1)} collective-permute-done((bf16[8,32,1664]{2,1,0:T(8,128)(2,1)S(1)}, bf16[8,32,1664]{2,1,0:T(8,128)(2,1)S(1)}, u32[]{:S(2)}, u32[]{:S(2)}) %collective-permute-start.3) | collective-permute-done | bytes 852000 | tf_op jit(solution)/shard_map/ppermute | solution.py:283
  75.9 2.0 fusion.3
  77.9 1.7 scatter.9.mel_ref
  80.8 105.3 %shard_map.178.w_ref.w0_ref.wc_ref = bf16[1024,1664]{1,0:T(8,128)(2,1)} custom-call(s32[3]{0:T(128)} %pad_add_fusion.1.core_ref, bf16[8,32,1664]{2,1,0:T(8,128)(2,1)} %copy-done.2, bf16[8,32,1664]{2,1,0:T(8,128)(2,1)} %copy-done.5, bf16[8,32,1664]{2,1,0:T(8,128)(2,1)} %collective-permute-done.1.refs_2_, bf16[8,32,1664]{2,1,0:T(8,128)(2,1)} %collective-permute-done.2.refs_3_), custom_call_target="tpu_custom_call" | custom-call | tf_op jit(solution)/shard_map/pallas_call | solution.py:289
  186.1 12.5 %shard_map.179 = (bf16[2048,512]{1,0:T(8,128)(2,1)}, f32[2048,512]{1,0:T(8,128)}, bf16[2048,512]{1,0:T(8,128)(2,1)}, bf16[2048,512]{1,0:T(8,128)(2,1)}, bf16[2048,1024]{1,0:T(8,128)(2,1)}) custom-call(s32[2]{0:T(128)} %pad_add_fusion.info_ref, bf16[2048,512]{1,0:T(8,128)(2,1)} %bitcast.56, bf16[2048,512]{1,0:T(8,128)(2,1)} %bitcast.57, ...), custom_call_target="tpu_custom_call" | custom-call | flops 5368709120 | bytes 22315008 | tf_op jit(solution)/shard_map/pallas_call | solution.py:198
  198.7 105.3 %shard_map.180.w_ref.w1_ref.wc_ref = bf16[1024,1664]{1,0:T(8,128)(2,1)} custom-call(s32[3]{0:T(128)} %pad_add_fusion.1.core_ref, bf16[8,32,1664]{2,1,0:T(8,128)(2,1)} %copy-done.3, bf16[8,32,1664]{2,1,0:T(8,128)(2,1)} %copy-done.4, bf16[8,32,1664]{2,1,0:T(8,128)(2,1)} %collective-permute-done.4.refs_2_, bf16[8,32,1664]{2,1,0:T(8,128)(2,1)} %collective-permute-done.5.refs_3_), custom_call_target="tpu_custom_call" | custom-call | tf_op jit(solution)/shard_map/pallas_call | solution.py:289
  304.0 14.4 %shard_map.181 = (bf16[2048,512]{1,0:T(8,128)(2,1)}, bf16[2048,512]{1,0:T(8,128)(2,1)}, bf16[2048,1024]{1,0:T(8,128)(2,1)}, bf16[2048,1024]{1,0:T(8,128)(2,1)}) custom-call(s32[2]{0:T(128)} %pad_add_fusion.info_ref, bf16[2048,512]{1,0:T(8,128)(2,1)} %get-tuple-element.52.low1_ref.low_ref, bf16[1024,1664]{1,0:T(8,128)(2,1)} %shard_map.180.w_ref.w1_ref.wc_ref, ...), custom_call_target="tpu_custom_call" | custom-call | flops 6442450944 | bytes 22315008 | tf_op jit(solution)/shard_map/pallas_call | solution.py:198
  318.4 16.7 %shard_map.185 = (bf16[1024,1664]{1,0:T(8,128)(2,1)}, f32[128,128]{1,0:T(8,128)}) custom-call(s32[2]{0:T(128)} %pad_add_fusion.info_ref, bf16[2048,1024]{1,0:T(8,128)(2,1)} %get-tuple-element.53.pre1_ref.pre_ref, bf16[2048,1024]{1,0:T(8,128)(2,1)} %get-tuple-element.66.proj_ref, bf16[2048,512]{1,0:T(8,128)(2,1)} %get-tuple-element.52.low1_ref.low_ref, ...), custom_call_target="tpu_custom_call" | custom-call | flops 6442450944 | bytes 21594112 | tf_op jit(solution)/shard_map/pallas_call | solution.py:198
  335.1 2.8 dynamic-slice_bitcast_fusion
  338.3 14.4 %shard_map.182 = (f32[2048,512]{1,0:T(8,128)}, bf16[2048,1024]{1,0:T(8,128)(2,1)}, bf16[2048,1024]{1,0:T(8,128)(2,1)}) custom-call(s32[2]{0:T(128)} %pad_add_fusion.info_ref, bf16[2048,1024]{1,0:T(8,128)(2,1)} %get-tuple-element.53.pre1_ref.pre_ref, bf16[1024,1664]{1,0:T(8,128)(2,1)} %shard_map.180.w_ref.w1_ref.wc_ref, ...), custom_call_target="tpu_custom_call" | custom-call | flops 6442450944 | bytes 31981568 | tf_op jit(solution)/shard_map/pallas_call | solution.py:198
  352.6 16.2 %shard_map.184 = (bf16[1024,1664]{1,0:T(8,128)(2,1)}, f32[128,128]{1,0:T(8,128)}) custom-call(s32[2]{0:T(128)} %pad_add_fusion.info_ref, bf16[2048,1024]{1,0:T(8,128)(2,1)} %get-tuple-element.56.pre_ref.next_ref, bf16[2048,1024]{1,0:T(8,128)(2,1)} %get-tuple-element.63.proj_ref, bf16[2048,512]{1,0:T(8,128)(2,1)} %get-tuple-element.64.low_ref.prev_ref, ...), custom_call_target="tpu_custom_call" | custom-call | flops 6442450944 | bytes 21594112 | tf_op jit(solution)/shard_map/pallas_call | solution.py:198
  368.8 2.9 dynamic-slice_bitcast_fusion.1
  371.9 2.0 fusion
  373.9 1.8 collective-permute-done.6
  375.7 1.9 fusion.1
  377.9 1.5 collective-permute-start.7
  379.4 11.3 %collective-permute-done.7 = bf16[4,2,32,1664]{3,2,1,0:T(8,128)(2,1)S(1)} collective-permute-done((bf16[4,2,32,1664]{3,2,1,0:T(8,128)(2,1)S(1)}, bf16[4,2,32,1664]{3,2,1,0:T(8,128)(2,1)S(1)}, u32[]{:S(2)}, u32[]{:S(2)}) %collective-permute-start.7) | collective-permute-done | bytes 852000 | tf_op jit(solution)/shard_map/ppermute | solution.py:335
  390.7 1.1 add_convert_fusion.1
  391.8 3.6 all-to-all-start.2
  395.5 1.6 collective-permute-start.9
  397.1 14.6 %collective-permute-done.9 = bf16[4,2,32,1664]{3,2,1,0:T(8,128)(2,1)S(1)} collective-permute-done((bf16[4,2,32,1664]{3,2,1,0:T(8,128)(2,1)S(1)}, bf16[4,2,32,1664]{3,2,1,0:T(8,128)(2,1)S(1)}, u32[]{:S(2)}, u32[]{:S(2)}) %collective-permute-start.9) | collective-permute-done | bytes 852000 | tf_op jit(solution)/shard_map/ppermute | solution.py:335
  411.7 1.1 add_convert_fusion
  412.8 4.0 all-to-all-done.2
  416.8 3.5 all-to-all-start.3
  421.7 18.1 %shard_map.183 = (bf16[2048,512]{1,0:T(8,128)(2,1)}, bf16[2048,512]{1,0:T(8,128)(2,1)}, f32[2048,512]{1,0:T(8,128)}) custom-call(s32[2]{0:T(128)} %pad_add_fusion.info_ref, f32[2048,512]{1,0:T(8,128)} %get-tuple-element.55.gh_ref, bf16[2048,1024]{1,0:T(8,128)(2,1)} %get-tuple-element.56.pre_ref.next_ref, ...), custom_call_target="tpu_custom_call" | custom-call | flops 7516192768 | bytes 36175872 | tf_op jit(solution)/shard_map/pallas_call | solution.py:198
  439.9 2.1 all-to-all-done.3
  (62 shorter events, 15.0 us)
Async XLA Ops:
  5.8 57.3 %copy-start.8 = (s32[2]{0:T(128)S(1)}, s32[2]{0:T(128)}, u32[]{:S(2)}) copy-start(s32[2]{0:T(128)} %constant.133.clone.1) | copy-start | bytes 28
  5.8 70.0 %copy-start.7 = (bf16[1,11,80]{2,1,0:T(8,128)(2,1)S(1)}, bf16[1,11,80]{2,1,0:T(8,128)(2,1)}, u32[]{:S(2)}) copy-start(bf16[1,11,80]{2,1,0:T(8,128)(2,1)} %param.16) | copy-start | bytes 5284
  5.8 29.0 %all-to-all-start = ((bf16[8,32,1664]{2,1,0:T(8,128)(2,1)}), bf16[8,32,1664]{2,1,0:T(8,128)(2,1)S(1)}, u32[]{:S(2)}, u32[]{:S(2)}) async-start(bf16[8,32,1664]{2,1,0:T(8,128)(2,1)} %broadcast_in_dim.12), calls=%async_computation | async-start | bytes 1703936 | tf_op jit(solution)/shard_map/all_to_all | solution.py:277
  34.8 45.9 %copy-start.2 = (bf16[8,32,1664]{2,1,0:T(8,128)(2,1)}, bf16[8,32,1664]{2,1,0:T(8,128)(2,1)S(1)}, u32[]{:S(2)}) copy-start(bf16[8,32,1664]{2,1,0:T(8,128)(2,1)S(1)} %all-to-all-done.refs_0_) | copy-start | bytes 2555908
  35.9 25.2 %all-to-all-start.1 = ((bf16[8,32,1664]{2,1,0:T(8,128)(2,1)}), bf16[8,32,1664]{2,1,0:T(8,128)(2,1)S(1)}, u32[]{:S(2)}, u32[]{:S(2)}) async-start(bf16[8,32,1664]{2,1,0:T(8,128)(2,1)} %broadcast_in_dim.26), calls=%async_computation.1 | async-start | bytes 1703936 | tf_op jit(solution)/shard_map/all_to_all | solution.py:277
  39.4 23.1 %collective-permute-start = (bf16[8,32,1664]{2,1,0:T(8,128)(2,1)S(1)}, bf16[8,32,1664]{2,1,0:T(8,128)(2,1)S(1)}, u32[]{:S(2)}, u32[]{:S(2)}) collective-permute-start(bf16[8,32,1664]{2,1,0:T(8,128)(2,1)S(1)} %all-to-all-done.refs_0_), channel_id=1, source_target_pairs={{0,2},{1,5},{2,0},{3,7},{4,6},{5,1},{6,4},{7,3},{8,10},{9,13},{10,... | collective-permute-start | bytes 2555912 | tf_op jit(solution)/shard_map/ppermute | solution.py:283
  61.1 124.9 %copy-start.3 = (bf16[8,32,1664]{2,1,0:T(8,128)(2,1)}, bf16[8,32,1664]{2,1,0:T(8,128)(2,1)S(1)}, u32[]{:S(2)}) copy-start(bf16[8,32,1664]{2,1,0:T(8,128)(2,1)S(1)} %all-to-all-done.1.refs_0_) | copy-start | bytes 2555908
  61.1 12.7 %collective-permute-start.3 = (bf16[8,32,1664]{2,1,0:T(8,128)(2,1)S(1)}, bf16[8,32,1664]{2,1,0:T(8,128)(2,1)S(1)}, u32[]{:S(2)}, u32[]{:S(2)}) collective-permute-start(bf16[8,32,1664]{2,1,0:T(8,128)(2,1)S(1)} %all-to-all-done.1.refs_0_), channel_id=1, source_target_pairs={{0,2},{1,5},{2,0},{3,7},{4,6},{5,1},{6,4},{7,3},{8,10},{9,13},{10,... | collective-permute-start | bytes 2555912 | tf_op jit(solution)/shard_map/ppermute | solution.py:283
  62.5 18.2 %collective-permute-start.1 = (bf16[8,32,1664]{2,1,0:T(8,128)(2,1)S(1)}, bf16[8,32,1664]{2,1,0:T(8,128)(2,1)}, u32[]{:S(2)}, u32[]{:S(2)}) collective-permute-start(bf16[8,32,1664]{2,1,0:T(8,128)(2,1)S(1)} %all-to-all-done.refs_0_), channel_id=1, source_target_pairs={{0,1},{1,0},{2,3},{3,2},{4,5},{5,4},{6,7},{7,6},{8,9},{9,8},{10,11... | collective-permute-start | bytes 2555912 | tf_op jit(solution)/shard_map/ppermute | solution.py:284
  62.6 18.2 %copy-start.5 = (bf16[8,32,1664]{2,1,0:T(8,128)(2,1)}, bf16[8,32,1664]{2,1,0:T(8,128)(2,1)S(1)}, u32[]{:S(2)}) copy-start(bf16[8,32,1664]{2,1,0:T(8,128)(2,1)S(1)} %collective-permute-done.refs_1_) | copy-start | bytes 2555908
  62.6 18.2 %collective-permute-start.2 = (bf16[8,32,1664]{2,1,0:T(8,128)(2,1)S(1)}, bf16[8,32,1664]{2,1,0:T(8,128)(2,1)}, u32[]{:S(2)}, u32[]{:S(2)}) collective-permute-start(bf16[8,32,1664]{2,1,0:T(8,128)(2,1)S(1)} %collective-permute-done.refs_1_), channel_id=1, source_target_pairs={{0,1},{1,0},{2,3},{3,2},{4,5},{5,4},{6,7},{7,6},{8,9},{9,8},{10,11... | collective-permute-start | bytes 2555912 | tf_op jit(solution)/shard_map/ppermute | solution.py:285
  63.7 134.9 %collective-permute-start.4 = (bf16[8,32,1664]{2,1,0:T(8,128)(2,1)S(1)}, bf16[8,32,1664]{2,1,0:T(8,128)(2,1)}, u32[]{:S(2)}, u32[]{:S(2)}) collective-permute-start(bf16[8,32,1664]{2,1,0:T(8,128)(2,1)S(1)} %all-to-all-done.1.refs_0_), channel_id=1, source_target_pairs={{0,1},{1,0},{2,3},{3,2},{4,5},{5,4},{6,7},{7,6},{8,9},{9,8},{10,11... | collective-permute-start | bytes 2555912 | tf_op jit(solution)/shard_map/ppermute | solution.py:284
  73.8 112.3 %copy-start.4 = (bf16[8,32,1664]{2,1,0:T(8,128)(2,1)}, bf16[8,32,1664]{2,1,0:T(8,128)(2,1)S(1)}, u32[]{:S(2)}) copy-start(bf16[8,32,1664]{2,1,0:T(8,128)(2,1)S(1)} %collective-permute-done.3.refs_1_) | copy-start | bytes 2555908
  73.8 124.8 %collective-permute-start.5 = (bf16[8,32,1664]{2,1,0:T(8,128)(2,1)S(1)}, bf16[8,32,1664]{2,1,0:T(8,128)(2,1)}, u32[]{:S(2)}, u32[]{:S(2)}) collective-permute-start(bf16[8,32,1664]{2,1,0:T(8,128)(2,1)S(1)} %collective-permute-done.3.refs_1_), channel_id=1, source_target_pairs={{0,1},{1,0},{2,3},{3,2},{4,5},{5,4},{6,7},{7,6},{8,9},{9,8},{10,11... | collective-permute-start | bytes 2555912 | tf_op jit(solution)/shard_map/ppermute | solution.py:285
  79.6 106.5 %copy-start.6 = (bf16[128,128]{1,0:T(8,128)(2,1)}, bf16[128,128]{1,0:T(8,128)(2,1)S(1)}, u32[]{:S(2)}) copy-start(bf16[128,128]{1,0:T(8,128)(2,1)S(1)} %scatter.9.mel_ref) | copy-start | bytes 98308
  337.8 34.0 %collective-permute-start.8 = (bf16[4,4,32,1664]{3,2,1,0:T(8,128)(2,1)}, bf16[4,4,32,1664]{3,2,1,0:T(8,128)(2,1)}, u32[]{:S(2)}, u32[]{:S(2)}) collective-permute-start(bf16[4,4,32,1664]{3,2,1,0:T(8,128)(2,1)} %dynamic-slice_bitcast_fusion), channel_id=1, source_target_pairs={{0,1},{1,0},{2,3},{3,2},{4,5},{5,4},{6,7},{7,6},{8,9},{9,8},{10,11... | collective-permute-start | bytes 5111816 | tf_op jit(solution)/shard_map/ppermute | solution.py:323
  368.8 3.1 copy-start
  371.7 3.9 collective-permute-start.6
  371.8 3.8 copy-start.1
  377.9 12.8 %collective-permute-start.7 = (bf16[4,2,32,1664]{3,2,1,0:T(8,128)(2,1)S(1)}, bf16[4,2,32,1664]{3,2,1,0:T(8,128)(2,1)S(1)}, u32[]{:S(2)}, u32[]{:S(2)}) collective-permute-start(bf16[4,2,32,1664]{3,2,1,0:T(8,128)(2,1)S(1)} %pad_maximum_fusion), channel_id=1, source_target_pairs={{0,2},{1,5},{2,0},{3,7},{4,6},{5,1},{6,4},{7,3},{8,10},{9,13},{10,... | collective-permute-start | bytes 2555912 | tf_op jit(solution)/shard_map/ppermute | solution.py:335
  391.8 24.9 %all-to-all-start.2 = ((bf16[8,32,1664]{2,1,0:T(8,128)(2,1)}), bf16[8,32,1664]{2,1,0:T(8,128)(2,1)S(1)}, u32[]{:S(2)}, u32[]{:S(2)}) async-start(bf16[8,32,1664]{2,1,0:T(8,128)(2,1)} %bitcast.24), calls=%async_computation.2 | async-start | bytes 1703936 | tf_op jit(solution)/shard_map/all_to_all | solution.py:277
  395.5 16.2 %collective-permute-start.9 = (bf16[4,2,32,1664]{3,2,1,0:T(8,128)(2,1)S(1)}, bf16[4,2,32,1664]{3,2,1,0:T(8,128)(2,1)S(1)}, u32[]{:S(2)}, u32[]{:S(2)}) collective-permute-start(bf16[4,2,32,1664]{3,2,1,0:T(8,128)(2,1)S(1)} %pad_maximum_fusion.1), channel_id=1, source_target_pairs={{0,2},{1,5},{2,0},{3,7},{4,6},{5,1},{6,4},{7,3},{8,10},{9,13},{10,... | collective-permute-start | bytes 2555912 | tf_op jit(solution)/shard_map/ppermute | solution.py:335
  416.8 25.2 %all-to-all-start.3 = ((bf16[8,32,1664]{2,1,0:T(8,128)(2,1)}), bf16[8,32,1664]{2,1,0:T(8,128)(2,1)S(1)}, u32[]{:S(2)}, u32[]{:S(2)}) async-start(bf16[8,32,1664]{2,1,0:T(8,128)(2,1)} %bitcast.29), calls=%async_computation.3 | async-start | bytes 1703936 | tf_op jit(solution)/shard_map/all_to_all | solution.py:277

commit v3 on v2

v3 whole, which is shorter than its diff:
```python
import functools

import jax
import jax.numpy as jnp
from jax import lax
from jax.experimental import pallas as pl
from jax.experimental.pallas import tpu as pltpu
from jax.sharding import PartitionSpec as P

FIRST_DILATION = 512
AXES = ("dp", "group")
LANES = 128
TILE = 512
VMEM = 56 * 1024 * 1024
LOW = jnp.bfloat16
FULL = jnp.float32


def dot(left, right):
    return jnp.dot(left, right, preferred_element_type=FULL)


def dot_cols(left, right, **more):
    return lax.dot_general(
        left, right, (((1,), (1,)), ((), ())), preferred_element_type=FULL, **more
    )


def dot_rows(left, right, **more):
    return lax.dot_general(
        left, right, (((0,), (0,)), ((), ())), preferred_element_type=FULL, **more
    )


class Sizes:
    def __init__(self, channels, mel_count):
        self.channels = channels
        self.gate = 2 * channels
        self.mel = mel_count
        self.early = channels
        self.now = 2 * channels
        self.extra = 3 * channels
        self.extra_width = -(-(mel_count + 2) // LANES) * LANES
        self.pack = self.extra + self.extra_width


def mask_of(info_ref, start, rows):
    places = start + lax.broadcasted_iota(jnp.int32, (rows, 1), 0)
    return (places < info_ref[0]).astype(FULL)


def frames_of(info_ref, start, rows):
    places = start + lax.broadcasted_iota(jnp.int32, (rows, LANES), 0)
    first = lax.broadcasted_iota(jnp.int32, (rows, LANES), 1) * info_ref[1]
    return ((places >= first) & (places < first + info_ref[1])).astype(FULL).astype(LOW)


def masked(ref, mask):
    return (ref[...].astype(FULL) * mask).astype(LOW)


def out_bias_row(size, extra):
    column = lax.broadcasted_iota(jnp.int32, (8, size.extra_width), 1)
    pick = (column == size.mel + 1).astype(FULL).astype(LOW)
    return dot_cols(pick, extra)[0:1]


def gates(taps, w_ref, size, side):
    channels = size.channels
    width = channels // 2
    low = slice(side * width, (side + 1) * width)
    high = slice(channels + side * width, channels + (side + 1) * width)
    tangent = jnp.tanh(dot_cols(taps, w_ref[low, size.early :]))
    sig_gate = 0.5 * jnp.tanh(0.5 * dot_cols(taps, w_ref[high, size.early :])) + 0.5
    gated = tangent * sig_gate
    return low, high, gated, sig_gate * (1.0 - tangent * tangent), gated * (1.0 - sig_gate)


def forward_0(size, wires, info_ref, x_ref, mel_ref, *refs):
    pieces, refs = refs[: wires.pieces], refs[wires.pieces :]
    low1_ref, gated_ref, slope_ref, whole_ref, w_ref, prev_ref, sems, out_sem = refs
    step = pl.program_id(0)
    rows, channels = x_ref.shape

    @pl.when(step == 0)
    def _():
        wires.put_together(info_ref, pieces, w_ref, sems)
        pltpu.make_async_copy(w_ref, whole_ref, out_sem).start()
        prev_ref[...] = jnp.zeros_like(prev_ref)

    mask = mask_of(info_ref, step * rows, rows)
    hidden = x_ref[...].astype(FULL) * mask
    low = hidden.astype(LOW)
    cond = dot(frames_of(info_ref, step * rows, rows), mel_ref[...]).astype(LOW)
    taps = jnp.concatenate([prev_ref[...], low, cond], axis=1)
    for side in range(2):
        first, second, gated, slope_a, slope_b = gates(taps, w_ref, size, side)
        gated_ref[:, first] = gated.astype(LOW)
        slope_ref[:, first] = slope_a.astype(LOW)
        slope_ref[:, second] = slope_b.astype(LOW)
    prev_ref[...] = low
    moved = dot_cols(gated_ref[...], w_ref[:channels, :channels])
    moved = moved + out_bias_row(size, w_ref[:channels, size.extra :])
    low1_ref[...] = ((hidden + moved) * mask).astype(LOW)

    @pl.when(step == pl.num_programs(0) - 1)
    def _():
        pltpu.make_async_copy(w_ref, whole_ref, out_sem).wait()


def layer_1(size, wires, steps, info_ref, low1_ref, mel_ref, go_ref, gs_ref, *refs):
    pieces, refs = refs[: wires.pieces], refs[wires.pieces :]
    gated_ref, pre_ref, here_ref, away_ref, melg_ref, whole_ref, *scratch = refs
    w_ref, prev_s, low_s, gated_s, pre_s, proj_s, frames_s, part_s, carry_ref, sems, out_sem = scratch
    step = pl.program_id(0)
    rows, channels = low1_ref.shape

    @pl.when(step == 0)
    def _():
        wires.put_together(info_ref, pieces, w_ref, sems)
        pltpu.make_async_copy(w_ref, whole_ref, out_sem).start()
        carry_ref[...] = jnp.zeros_like(carry_ref)
        melg_ref[...] = jnp.zeros_like(melg_ref)

    @pl.when(step < steps)
    def _():
        tile = pl.ds(pl.multiple_of(step * rows, rows), rows)
        mask = mask_of(info_ref, step * rows, rows)
        low = low1_ref[...]
        wide = low.astype(FULL)
        place = lax.broadcasted_iota(jnp.int32, (rows, 1), 0)
        prev = jnp.where(place == 0, carry_ref[7:8], pltpu.roll(wide, 1, 0)).astype(LOW)
        carry_ref[...] = wide[rows - 8 :]
        frames = frames_of(info_ref, step * rows, rows)
        cond = dot(frames, mel_ref[...]).astype(LOW)
        taps = jnp.concatenate([prev, low, cond], axis=1)
        proj = jnp.concatenate([masked(go_ref, mask), masked(gs_ref, mask)], axis=1)
        prev_s[tile] = prev
        low_s[tile] = low
        frames_s[tile] = frames
        proj_s[tile] = proj
        grad_gated = dot(proj, w_ref[:, :channels])
        for side in range(2):
            first, second, gated, slope_a, slope_b = gates(taps, w_ref, size, side)
            gated_ref[:, first] = gated.astype(LOW)
            pre_ref[:, first] = (grad_gated[:, first] * slope_a).astype(LOW)
            pre_ref[:, second] = (grad_gated[:, first] * slope_b).astype(LOW)
        gated_s[tile] = gated_ref[...]
        pre_s[tile] = pre_ref[...]

    @pl.when(step >= steps)
    def _():
        width = part_s.shape[0]
        part = pl.ds(pl.multiple_of((step - steps) * width, width), width)
        pre = pre_s[:, part]
        part_s[:, size.early : size.now] = dot_rows(pre, prev_s[...]).astype(LOW)
        part_s[:, size.now : size.extra] = dot_rows(pre, low_s[...]).astype(LOW)
        finish_part(size, pre, proj_s[:, part], frames_s, gated_s, mel_ref, w_ref[part, size.extra :], melg_ref, part_s)
        wires.put_apart(info_ref, part_s, here_ref, away_ref)

    @pl.when(step == pl.num_programs(0) - 1)
    def _():
        pltpu.make_async_copy(w_ref, whole_ref, out_sem).wait()


def finish_part(size, pre, proj, frames_ref, gated_ref, mel_ref, cond_weight, melg_ref, part_ref):
    exact = dict(precision=lax.Precision.HIGHEST)
    sums = dot_rows(pre, frames_ref[...])
    extra = jnp.dot(sums, mel_ref[...].astype(FULL), preferred_element_type=FULL, **exact)
    melg_ref[...] += dot_rows(sums, cond_weight.astype(FULL), **exact)
    total = jnp.sum(proj.astype(FULL), axis=0, keepdims=True)
    bias = jnp.broadcast_to(total, (LANES, total.shape[1])).T[:, 0:1]
    column = lax.broadcasted_iota(jnp.int32, extra.shape, 1)
    part_ref[:, size.extra :] = jnp.where(column == size.mel + 1, bias, extra).astype(LOW)
    part_ref[:, : size.channels] = dot_rows(proj, gated_ref[...]).astype(LOW)


def backward_0(size, info_ref, pre1_ref, early1_ref, now1_ref, out0_ref, go_ref, gs_ref, slope_ref, res_ref, pre0_ref, carry_ref):
    step = pl.program_id(0)
    rows, channels = go_ref.shape
    tile = pl.num_programs(0) - 1 - step
    mask = mask_of(info_ref, tile * rows, rows)

    @pl.when(step == 0)
    def _():
        carry_ref[...] = jnp.zeros_like(carry_ref)

    pre1 = pre1_ref[...]
    early = dot(pre1, early1_ref[...])
    place = lax.broadcasted_iota(jnp.int32, (rows, 1), 0)
    later = jnp.where(place == rows - 1, carry_ref[0:1], pltpu.roll(early, rows - 1, 0))
    carry_ref[...] = early[:8]
    now = dot(pre1, now1_ref[...])
    res = ((go_ref[...].astype(FULL) * mask + now + later) * mask).astype(LOW)
    res_ref[...] = res
    proj = jnp.concatenate([res, masked(gs_ref, mask)], axis=1)
    grad_gated = dot(proj, out0_ref[...])
    pre0_ref[:, :channels] = (grad_gated * slope_ref[:, :channels].astype(FULL)).astype(LOW)
    pre0_ref[:, channels:] = (grad_gated * slope_ref[:, channels:].astype(FULL)).astype(LOW)


def weights_0(size, wires, info_ref, pre_ref, res_ref, gs_ref, x_ref, gated_ref, mel_ref, wc_ref, here_ref, away_ref, melg_ref, frames_s, proj_s, part_s):
    step = pl.program_id(0)
    samples = x_ref.shape[0]

    @pl.when(step == 0)
    def _():
        frames_s[...] = frames_of(info_ref, 0, samples)
        melg_ref[...] = jnp.zeros_like(melg_ref)

    half = pl.num_programs(0) // 2

    @pl.when(step < half)
    def _():
        proj_s[...] = res_ref[...]

    @pl.when(step >= half)
    def _():
        proj_s[...] = masked(gs_ref, mask_of(info_ref, 0, samples))

    pre = pre_ref[...]
    shift = FIRST_DILATION
    early = dot_rows(pre[shift:], x_ref[: samples - shift])
    part_s[:, size.early : size.now] = early.astype(LOW)
    part_s[:, size.now : size.extra] = dot_rows(pre, x_ref[...]).astype(LOW)
    finish_part(size, pre, proj_s[...], frames_s, gated_ref, mel_ref, wc_ref[...], melg_ref, part_s)
    wires.put_apart(info_ref, part_s, here_ref, away_ref)


def outputs(size, info_ref, x_ref, res_ref, pre_ref, next_ref, gated0_ref, gated1_ref, w0_ref, out1_ref, extra1_ref, out_ref, skip_ref, sg_ref):
    step = pl.program_id(0)
    rows, channels = x_ref.shape
    mask = mask_of(info_ref, step * rows, rows)
    grad = res_ref[...].astype(FULL) + dot(pre_ref[...], w0_ref[:, size.now : size.extra])
    later = dot(next_ref[...], w0_ref[:, size.early : size.now])
    grad = grad + jnp.where(step < pl.num_programs(0) - 1, later, 0.0)
    sg_ref[...] = grad * mask
    gated0, gated1 = gated0_ref[...], gated1_ref[...]
    gated = jnp.concatenate([gated0, gated1], axis=1)

    def projected(rows):
        both = jnp.concatenate([w0_ref[rows, :channels], out1_ref[rows]], axis=1)
        bias = out_bias_row(size, w0_ref[rows, size.extra :]) + out_bias_row(size, extra1_ref[rows])
        return dot_cols(gated, both) + bias

    res = projected(slice(0, channels))
    out_ref[...] = ((x_ref[...].astype(FULL) + res) * mask).astype(LOW)
    skip_ref[...] = (projected(slice(channels, 2 * channels)) * mask).astype(LOW)


def call(kernel, grid, info, operands, specs, outs, out_specs, scratch, flops):
    moved = sum(x.size * x.dtype.itemsize for x in operands)
    moved += sum(x.size * x.dtype.itemsize for x in outs)
    return pl.pallas_call(
        kernel,
        grid_spec=pltpu.PrefetchScalarGridSpec(
            num_scalar_prefetch=1,
            grid=(grid,),
            in_specs=specs,
            out_specs=out_specs,
            scratch_shapes=scratch,
        ),
        out_shape=outs,
        compiler_params=pltpu.CompilerParams(
            vmem_limit_bytes=VMEM, dimension_semantics=("arbitrary",)
        ),
        cost_estimate=pl.CostEstimate(flops=flops, bytes_accessed=moved, transcendentals=0),
    )(info, *operands)


def shape_of(*shape, dtype=LOW):
    return jax.ShapeDtypeStruct(shape, dtype)


def tiled(width, place=lambda i: i):
    return pl.BlockSpec((TILE, width), lambda i, info: (place(i), 0))


def fixed(*shape, at=(0, 0)):
    return pl.BlockSpec(shape, lambda i, info: at)


ANYWHERE = pl.BlockSpec(memory_space=pl.ANY)


class Wires:
    def __init__(self, dp, cores, channels):
        assert dp % 4 == 0 and cores == 2
        self.rest = dp // 4
        self.devices = dp * 2
        self.rows = channels // self.devices
        self.direct = self.rows % 16 == 0
        self.pieces = 8 if self.direct else 1
        me = lax.axis_index(AXES)
        self.core = me % 2
        self.a = (me // 2) % 2
        self.b = (me // 4) % 2
        every = range(self.devices)
        self.sibling = [(i, i ^ 1) for i in every]
        self.first = [(i, i ^ (4 if i % 2 else 2)) for i in every]
        self.second = [(i, i ^ (2 if i % 2 else 4)) for i in every]
        self.columns = [[rest * 8 + low for rest in range(self.rest)] for low in range(8)]

    def place(self):
        return jnp.stack([self.core, self.a, self.b]).astype(jnp.int32)

    def hop(self, value, pairs):
        return lax.ppermute(value, AXES, pairs)

    def swap_rest(self, blocks):
        return lax.all_to_all(blocks, AXES, 0, 0, tiled=True, axis_index_groups=self.columns)

    def gather(self, block):
        mine = self.swap_rest(jnp.broadcast_to(block[None], (self.rest,) + block.shape))
        one = self.hop(mine, self.first)
        two = self.hop(mine, self.second)
        far = self.hop(one, self.second)
        pieces = [mine, one, two, far]
        pieces += [self.hop(piece, self.sibling) for piece in pieces]
        return pieces if self.direct else [self.put_in_order(pieces)]

    def put_in_order(self, pieces):
        whole = jnp.zeros((self.rest, 2, 2, 2) + pieces[0].shape[1:], LOW)
        for index, piece in enumerate(pieces):
            source = self.core if index < 4 else 1 - self.core
            first, second = index % 2, (index // 2) % 2
            at_a = self.a ^ jnp.where(source == 0, first, second)
            at_b = self.b ^ jnp.where(source == 0, second, first)
            whole = lax.dynamic_update_slice(
                whole, piece[:, None, None, None], (0, at_b, at_a, source, 0, 0)
            )
        return whole.reshape(-1, pieces[0].shape[2])

    def put_together(self, info_ref, pieces, w_ref, sems):
        if not self.direct:
            copy = pltpu.make_async_copy(pieces[0], w_ref, sems.at[0, 0])
            copy.start()
            copy.wait()
            return
        core, a, b = info_ref[2], info_ref[3], info_ref[4]
        copies = []
        for index, piece in enumerate(pieces):
            source = core if index < 4 else 1 - core
            first, second = index % 2, (index // 2) % 2
            at_a = a ^ jnp.where(source == 0, first, second)
            at_b = b ^ jnp.where(source == 0, second, first)
            for rest in range(self.rest):
                place = ((rest * 2 + at_b) * 2 + at_a) * 2 + source
                rows = pl.ds(pl.multiple_of(place * self.rows, self.rows), self.rows)
                copies.append(
                    pltpu.make_async_copy(piece.at[rest], w_ref.at[rows], sems.at[index, rest])
                )
        for copy in copies:
            copy.start()
        for copy in copies:
            copy.wait()

    def put_apart(self, info_ref, part_ref, here_ref, away_ref):
        if not self.direct:
            here_ref[...] = part_ref[...]
            return
        core, a, b = info_ref[2], info_ref[3], info_ref[4]
        for block in range(part_ref.shape[0] // self.rows):
            at_b, at_a, owner = (block // 4) % 2, (block // 2) % 2, block % 2
            value = part_ref[block * self.rows : (block + 1) * self.rows]
            first, second = at_a ^ a, at_b ^ b
            if owner:
                first, second = second, first

            @pl.when(core == owner)
            def _():
                here_ref[first, second, block // 8] = value

            @pl.when(core != owner)
            def _():
                away_ref[first, second, block // 8] = value

    def apart_specs(self, parts, width, pack, step):
        if not self.direct:
            spec = pl.BlockSpec((width, pack), lambda i, info: (step(i), 0))
            none = pl.BlockSpec((8, LANES), lambda i, info: (0, 0))
            return (shape_of(parts * width, pack), shape_of(8, LANES)), [spec, none]
        shape = shape_of(2, 2, self.rest, self.rows, pack)
        spec = pl.BlockSpec(
            (2, 2, self.rest // parts, self.rows, pack), lambda i, info: (0, 0, step(i), 0, 0)
        )
        return (shape, shape), [spec, spec]

    def by_distance(self, full):
        rows = full.shape[0] // self.devices
        blocks = full.reshape(self.rest, 2, 2, 2, rows, full.shape[1])
        parts = []
        for away in range(2):
            source = self.core ^ away
            for first in range(2):
                for second in range(2):
                    at_a = self.a ^ jnp.where(source == 0, first, second)
                    at_b = self.b ^ jnp.where(source == 0, second, first)
                    parts.append(
                        lax.dynamic_slice(
                            blocks,
                            (0, at_b, at_a, source, 0, 0),
                            (self.rest, 1, 1, 1, rows, full.shape[1]),
                        )[:, 0, 0, 0]
                    )
        return jnp.stack(parts).reshape(2, 2, 2, self.rest, rows, full.shape[1])

    def chip_sum(self, here, away):
        return add_low(here, self.hop(away, self.sibling))

    def pair_sum(self, chip):
        return add_low(chip[0], self.hop(chip[1], self.first))

    def four_sum(self, pair):
        return add_low(pair[0], self.hop(pair[1], self.second))

    def rest_sum(self, four):
        return jnp.sum(self.swap_rest(four).astype(FULL), axis=0)


def add_low(left, right):
    return (left.astype(FULL) + right.astype(FULL)).astype(LOW)


def per_device(
    dp,
    cores,
    samples,
    mel,
    lengths,
    hops,
    conv_weight,
    cond_weight,
    conv_bias,
    out_weight,
    out_bias,
    grad_out,
    grad_skip,
):
    sample_count, channels = samples.shape[1:]
    frame_count, mel_count = mel.shape[1:]
    layers = conv_weight.shape[0]
    size = Sizes(channels, mel_count)
    gate = size.gate
    wires = Wires(dp, cores, gate)
    assert layers == 2 and sample_count % TILE == 0 and TILE == FIRST_DILATION
    steps = sample_count // TILE
    info = jnp.concatenate([lengths, hops, wires.place()])
    x, go, gs = samples[0], grad_out[0], grad_skip[0]
    mel_table = jnp.concatenate([mel[0], jnp.ones((frame_count, 1), LOW)], axis=1)
    mel_table = jnp.pad(
        mel_table, ((0, LANES - frame_count), (0, size.extra_width - mel_count - 1))
    )

    packs = []
    for layer in range(layers):
        fill = jnp.zeros((size.extra_width - mel_count - 2, conv_weight.shape[2]), LOW)
        pack = jnp.concatenate(
            [
                out_weight[layer],
                conv_weight[layer],
                cond_weight[layer],
                conv_bias[layer][None],
                out_bias[layer][None],
                fill,
            ],
            axis=0,
        ).T
        packs.append(wires.gather(pack))

    table = fixed(LANES, size.extra_width)
    macs = sample_count * channels * channels
    whole_w = shape_of(gate, size.pack)
    weights = pltpu.VMEM((gate, size.pack), LOW)
    sems = pltpu.SemaphoreType.DMA((8, wires.rest))
    one_sem = pltpu.SemaphoreType.DMA

    low1, gated0, slope0, w0 = call(
        functools.partial(forward_0, size, wires),
        steps,
        info,
        (x, mel_table, *packs[0]),
        [tiled(channels), table] + [ANYWHERE] * wires.pieces,
        (
            shape_of(sample_count, channels),
            shape_of(sample_count, channels),
            shape_of(sample_count, gate),
            whole_w,
        ),
        [tiled(channels), tiled(channels), tiled(gate), ANYWHERE],
        [weights, pltpu.VMEM((TILE, channels), LOW), sems, one_sem],
        10 * macs,
    )

    parts = 4
    width = gate // parts
    late = lambda i: jnp.minimum(i, steps - 1)
    apart, apart_specs = wires.apart_specs(
        parts, width, size.pack, lambda i: jnp.maximum(i - steps, 0)
    )
    melg = shape_of(LANES, size.extra_width, dtype=FULL)
    gated1, pre1, here1, away1, melg1, w1 = call(
        functools.partial(layer_1, size, wires, steps),
        steps + parts,
        info,
        (low1, mel_table, go, gs, *packs[1]),
        [tiled(channels, late), table, tiled(channels, late), tiled(channels, late)]
        + [ANYWHERE] * wires.pieces,
        (shape_of(sample_count, channels), shape_of(sample_count, gate), *apart, melg, whole_w),
        [tiled(channels, late), tiled(gate, late), *apart_specs, table, ANYWHERE],
        [
            weights,
            pltpu.VMEM((sample_count, channels), LOW),
            pltpu.VMEM((sample_count, channels), LOW),
            pltpu.VMEM((sample_count, channels), LOW),
            pltpu.VMEM((sample_count, gate), LOW),
            pltpu.VMEM((sample_count, gate), LOW),
            pltpu.VMEM((sample_count, LANES), LOW),
            pltpu.VMEM((width, size.pack), LOW),
            pltpu.VMEM((8, channels), FULL),
            sems,
            one_sem,
        ],
        24 * macs,
    )
    if not wires.direct:
        here1, away1 = wires.by_distance(here1)

    backwards = lambda i: steps - 1 - i
    tap = lambda at: fixed(gate, channels, at=(0, at))
    res0, pre0 = call(
        functools.partial(backward_0, size),
        steps,
        info,
        (pre1, w1, w1, w0, go, gs, slope0),
        [
            tiled(gate, backwards),
            tap(1),
            tap(2),
            tap(0),
            tiled(channels, backwards),
            tiled(channels, backwards),
            tiled(gate, backwards),
        ],
        (shape_of(sample_count, channels), shape_of(sample_count, gate)),
        [tiled(channels, backwards), tiled(gate, backwards)],
        [pltpu.VMEM((8, channels), FULL)],
        12 * macs,
    )
    chip1 = wires.chip_sum(here1, away1)
    pre0, chip1 = lax.optimization_barrier((pre0, chip1))

    half = parts // 2
    apart, apart_specs = wires.apart_specs(parts, width, size.pack, lambda i: i)
    columns = lambda place: pl.BlockSpec((sample_count, width), lambda i, info: (0, place(i)))
    here0, away0, melg0 = call(
        functools.partial(weights_0, size, wires),
        parts,
        info,
        (pre0, res0, gs, x, gated0, mel_table, w0),
        [
            columns(lambda i: i),
            columns(lambda i: jnp.minimum(i, half - 1)),
            columns(lambda i: jnp.maximum(i - half, 0)),
            fixed(sample_count, channels),
            fixed(sample_count, channels),
            table,
            pl.BlockSpec(
                (width, size.extra_width), lambda i, info: (i, size.extra // size.extra_width)
            ),
        ],
        (*apart, melg),
        [*apart_specs, table],
        [
            pltpu.VMEM((sample_count, LANES), LOW),
            pltpu.VMEM((sample_count, width), LOW),
            pltpu.VMEM((width, size.pack), LOW),
        ],
        12 * macs,
    )
    if not wires.direct:
        here0, away0 = wires.by_distance(here0)
    pair1 = wires.pair_sum(chip1)
    chip0 = wires.chip_sum(here0, away0)
    four1 = wires.four_sum(pair1)
    pair0 = wires.pair_sum(chip0)
    own1 = wires.rest_sum(four1)
    four0 = wires.four_sum(pair0)
    own0 = wires.rest_sum(four0)

    residual_out, skip_output_sum, samples_grad = call(
        functools.partial(outputs, size),
        steps,
        info,
        (x, res0, pre0, pre0, gated0, gated1, w0, w1, w1),
        [
            tiled(channels),
            tiled(channels),
            tiled(gate),
            tiled(gate, lambda i: jnp.minimum(i + 1, steps - 1)),
            tiled(channels),
            tiled(channels),
            fixed(gate, size.pack),
            tap(0),
            fixed(gate, size.extra_width, at=(0, size.extra // size.extra_width)),
        ],
        (
            shape_of(sample_count, channels),
            shape_of(sample_count, channels),
            shape_of(sample_count, channels, dtype=FULL),
        ),
        [tiled(channels), tiled(channels), tiled(channels)],
        [],
        16 * macs,
    )
    mel_grad = (melg0 + melg1)[:frame_count, :mel_count]
    own = jnp.stack([own0, own1]).transpose(0, 2, 1)
    at = size.extra + mel_count
    return (
        residual_out[None],
        skip_output_sum[None],
        samples_grad[None],
        mel_grad[None],
        own[:, size.early : size.extra],
        own[:, size.extra : at],
        own[:, at],
        own[:, : size.channels],
        own[:, at + 1],
    )


def solution(mesh):
    dp, cores = mesh.shape["dp"], mesh.shape["group"]

    def everything(*arrays):
        return per_device(dp, cores, *arrays)

    clips = P(AXES, None, None)
    columns = P(None, None, AXES)
    biases = P(None, AXES)
    return jax.shard_map(
        everything,
        mesh=mesh,
        in_specs=(
            clips, clips, P(AXES), P(AXES), columns, columns, biases, columns, biases, clips, clips,
        ),
        out_specs=(clips, clips, clips, clips, columns, columns, biases, columns, biases),
        check_vma=False,
    )
```

time: 446 us -> 202 us (0.45)
  Pallas kernels: 303 us -> 86.2 us
  waiting for transfers between devices: 85.3 us -> 63.2 us
  starting transfers between devices: 25.2 us -> 33.5 us
  local copies, waits for them, and re-layouts: 18.2 us -> 11.4 us
  other arithmetic: 11.1 us -> 4.44 us
    pallas_call x2 -> x0, Pallas kernels: 211 us -> none  [gather(): pl.pallas_call(functools.partial(put_together, rows), in_specs=[pl.BlockS...]
    all_to_all x4, waiting for transfers between devices: 47.7 us -> 29.6 us  [swap_rest(): lax.all_to_all(blocks, AXES, 0, 0, tiled=True, axis_index_groups=self.col...]
    ppermute x10 -> x20, starting transfers between devices: 7.1 us -> 16.8 us  [hop(): return lax.ppermute(value, AXES, pairs)]
    pallas_call x6 -> x5, Pallas kernels: 92.3 us -> 86.2 us  [call(): pl.pallas_call(kernel, grid_spec=pltpu.PrefetchScalarGridSpec(num_scalar_...]
    squeeze x2 -> x4, local copies, waits for them, and re-layouts: 5.73 us -> 0.19 us  [the longest x2 0.13 us: pair_sum(): return add_low(chip[0], self.hop(chip[1], self.first))]
    ppermute x10 -> x20, waiting for transfers between devices: 37.7 us -> 33.6 us  [hop(): return lax.ppermute(value, AXES, pairs)]
  transfers between devices with their start and end apart: 14 -> 24, of which waited for: 8 -> 9; matrix products, arithmetic and copies ran while one was open for 3% -> 3% of each run, Pallas kernels for 37% -> 21%
where the time goes in v3:
time: 202 us; the launch traced here: 201 us
  Pallas kernels  86.2 us (43%)
  waiting for transfers between devices  63.2 us (31%)
  starting transfers between devices  33.5 us (17%)
  local copies, waits for them, and re-layouts  11.4 us (6%)
  other arithmetic  4.44 us (2%)
  between operations  2.26 us (1%)
    pallas_call x5, Pallas kernels, call(): pl.pallas_call(kernel, grid_spec=pltpu.PrefetchScalarGridSpec(num_scalar_...  86.2 us
    ppermute x20, waiting for transfers between devices, hop(): return lax.ppermute(value, AXES, pairs)  33.6 us
    all_to_all x4, waiting for transfers between devices, swap_rest(): lax.all_to_all(blocks, AXES, 0, 0, tiled=True, axis_index_groups=self.col...  29.6 us
    ppermute x20, starting transfers between devices, hop(): return lax.ppermute(value, AXES, pairs)  16.8 us
    all_to_all x4, starting transfers between devices, swap_rest(): lax.all_to_all(blocks, AXES, 0, 0, tiled=True, axis_index_groups=self.col...  16.7 us
  transfers between devices with their start and end apart: 24, of which 9 were waited for; matrix products, arithmetic and copies ran while one was open for 3% of the time, Pallas kernels for 21%

profile of v3, /device:TPU:0, one launch (start us, length us, event | category | flops | bytes accessed | tf_op | source)
XLA Modules:
  0.0 201.0 jit_solution(14829390329554411309)
XLA Ops:
  0.6 0.9 slice_bitcast_fusion.7
  4.8 0.8 broadcast_in_dim.24
  5.6 6.3 %all-to-all-start = ((bf16[4,32,1664]{2,1,0:T(8,128)(2,1)}), bf16[4,32,1664]{2,1,0:T(8,128)(2,1)S(1)}, u32[]{:S(2)}, u32[]{:S(2)}) async-start(bf16[4,32,1664]{2,1,0:T(8,128)(2,1)} %broadcast_in_dim.24), calls=%async_computation | async-start | bytes 851968 | tf_op jit(solution)/shard_map/all_to_all | solution.py:311
  12.2 12.1 %all-to-all-done.refs_0_ = bf16[4,32,1664]{2,1,0:T(8,128)(2,1)S(1)} async-done(((bf16[4,32,1664]{2,1,0:T(8,128)(2,1)}), bf16[4,32,1664]{2,1,0:T(8,128)(2,1)S(1)}, u32[]{:S(2)}, u32[]{:S(2)}) %all-to-all-start) | async-done | bytes 426016 | tf_op jit(solution)/shard_map/all_to_all | solution.py:311
  24.3 0.8 broadcast_in_dim.25
  25.1 3.5 %all-to-all-start.1 = ((bf16[4,32,1664]{2,1,0:T(8,128)(2,1)}), bf16[4,32,1664]{2,1,0:T(8,128)(2,1)S(1)}, u32[]{:S(2)}, u32[]{:S(2)}) async-start(bf16[4,32,1664]{2,1,0:T(8,128)(2,1)} %broadcast_in_dim.25), calls=%async_computation.1 | async-start | bytes 851968 | tf_op jit(solution)/shard_map/all_to_all | solution.py:311
  28.6 1.6 collective-permute-start
  30.2 1.5 collective-permute-start.1
  31.7 8.8 %all-to-all-done.1.refs_0_ = bf16[4,32,1664]{2,1,0:T(8,128)(2,1)S(1)} async-done(((bf16[4,32,1664]{2,1,0:T(8,128)(2,1)}), bf16[4,32,1664]{2,1,0:T(8,128)(2,1)S(1)}, u32[]{:S(2)}, u32[]{:S(2)}) %all-to-all-start.1) | async-done | bytes 426016 | tf_op jit(solution)/shard_map/all_to_all | solution.py:311
  40.5 1.5 collective-permute-start.7
  42.0 1.5 collective-permute-start.2
  44.5 8.6 %collective-permute-done.7.refs_1_ = bf16[4,32,1664]{2,1,0:T(8,128)(2,1)S(1)} collective-permute-done((bf16[4,32,1664]{2,1,0:T(8,128)(2,1)S(1)}, bf16[4,32,1664]{2,1,0:T(8,128)(2,1)S(1)}, u32[]{:S(2)}, u32[]{:S(2)}) %collective-permute-start.7) | collective-permute-done | bytes 426016 | tf_op jit(solution)/shard_map/ppermute | solution.py:308
  53.1 1.6 collective-permute-start.9
  58.3 2.9 %collective-permute-done.9.refs_3_ = bf16[4,32,1664]{2,1,0:T(8,128)(2,1)S(1)} collective-permute-done((bf16[4,32,1664]{2,1,0:T(8,128)(2,1)S(1)}, bf16[4,32,1664]{2,1,0:T(8,128)(2,1)S(1)}, u32[]{:S(2)}, u32[]{:S(2)}) %collective-permute-start.9) | collective-permute-done | bytes 426016 | tf_op jit(solution)/shard_map/ppermute | solution.py:308
  61.5 13.3 %shard_map.178 = (bf16[2048,512]{1,0:T(8,128)(2,1)}, bf16[2048,512]{1,0:T(8,128)(2,1)}, bf16[2048,1024]{1,0:T(8,128)(2,1)}, bf16[1024,1664]{1,0:T(8,128)(2,1)}) custom-call(s32[5]{0:T(128)} %concatenate.12.info_ref, bf16[2048,512]{1,0:T(8,128)(2,1)} %bitcast.66, bf16[128,128]{1,0:T(8,128)(2,1)} %fusion.6.mel_ref, bf16[4,32,1664]{2,1,0:T(8,128)(2,1)} %copy-done.2, ...), custom_call_target="tpu_custom_call" | custom-call | flops 5368709120 | bytes 17334272 | tf_op jit(solution)/shard_map/pallas_call | solution.py:254
  76.0 26.9 %shard_map.179 = (bf16[2048,512]{1,0:T(8,128)(2,1)}, bf16[2048,1024]{1,0:T(8,128)(2,1)}, bf16[2,2,4,32,1664]{4,3,2,1,0:T(8,128)(2,1)}, bf16[2,2,4,32,1664]{4,3,2...) custom-call(s32[5]{0:T(128)} %concatenate.12.info_ref, bf16[2048,512]{1,0:T(8,128)(2,1)} %get-tuple-element.29.low1_ref, ...), custom_call_target="tpu_custom_call" | custom-call | flops 12884901888 | bytes 22904832 | tf_op jit(solution)/shard_map/pallas_call | solution.py:254
  103.4 12.9 %shard_map.180 = (bf16[2048,512]{1,0:T(8,128)(2,1)}, bf16[2048,1024]{1,0:T(8,128)(2,1)}) custom-call(s32[5]{0:T(128)} %concatenate.12.info_ref, bf16[2048,1024]{1,0:T(8,128)(2,1)} %get-tuple-element.30.pre1_ref, bf16[1024,1664]{1,0:T(8,128)(2,1)} %get-tuple-element.31.early1_ref.now1_ref.out1_ref.extra1_ref, ...), custom_call_target="tpu_custom_call" | custom-call | flops 6442450944 | bytes 29097984 | tf_op jit(solution)/shard_map/pallas_call | solution.py:254
  116.7 16.2 %shard_map.182 = (bf16[2,2,4,32,1664]{4,3,2,1,0:T(8,128)(2,1)}, bf16[2,2,4,32,1664]{4,3,2,1,0:T(8,128)(2,1)}, f32[128,128]{1,0:T(8,128)}) custom-call(s32[5]{0:T(128)} %concatenate.12.info_ref, bf16[2048,1024]{1,0:T(8,128)(2,1)} %get-tuple-element.38.pre_ref.next_ref, bf16[2048,512]{1,0:T(8,128)(2,1)} %get-tuple-element.34.res_ref, ...), custom_call_target="tpu_custom_call" | custom-call | flops 6442450944 | bytes 19496960 | tf_op jit(solution)/shard_map/pallas_call | solution.py:254
  133.3 1.6 collective-permute-start.18
  134.9 2.0 collective-permute-done.15
  137.4 1.6 collective-permute-start.16
  138.9 7.2 %collective-permute-done.18 = bf16[2,4,32,1664]{3,2,1,0:T(8,128)(2,1)S(1)} collective-permute-done((bf16[2,4,32,1664]{3,2,1,0:T(8,128)(2,1)S(1)}, bf16[2,4,32,1664]{3,2,1,0:T(8,128)(2,1)S(1)}, u32[]{:S(2)}, u32[]{:S(2)}) %collective-permute-start.18) | collective-permute-done | bytes 852000 | tf_op jit(solution)/shard_map/ppermute | solution.py:308
  146.3 1.6 collective-permute-start.19
  147.9 11.9 %collective-permute-done.16 = bf16[2,4,32,1664]{3,2,1,0:T(8,128)(2,1)S(1)} collective-permute-done((bf16[2,4,32,1664]{3,2,1,0:T(8,128)(2,1)S(1)}, bf16[2,4,32,1664]{3,2,1,0:T(8,128)(2,1)S(1)}, u32[]{:S(2)}, u32[]{:S(2)}) %collective-permute-start.16) | collective-permute-done | bytes 852000 | tf_op jit(solution)/shard_map/ppermute | solution.py:308
  160.0 1.6 collective-permute-start.17
  161.6 0.9 fusion.2
  162.5 3.5 %all-to-all-start.3 = ((bf16[4,32,1664]{2,1,0:T(8,128)(2,1)}), bf16[4,32,1664]{2,1,0:T(8,128)(2,1)S(1)}, u32[]{:S(2)}, u32[]{:S(2)}) async-start(bf16[4,32,1664]{2,1,0:T(8,128)(2,1)} %fusion.2), calls=%async_computation.3 | async-start | bytes 851968 | tf_op jit(solution)/shard_map/all_to_all | solution.py:311
  167.3 1.0 collective-permute-done.17
  168.2 0.9 fusion.3
  169.1 8.8 %all-to-all-done.3 = bf16[4,32,1664]{2,1,0:T(8,128)(2,1)S(1)} async-done(((bf16[4,32,1664]{2,1,0:T(8,128)(2,1)}), bf16[4,32,1664]{2,1,0:T(8,128)(2,1)S(1)}, u32[]{:S(2)}, u32[]{:S(2)}) %all-to-all-start.3) | async-done | bytes 426016 | tf_op jit(solution)/shard_map/all_to_all | solution.py:311
  177.9 3.5 %all-to-all-start.2 = ((bf16[4,32,1664]{2,1,0:T(8,128)(2,1)}), bf16[4,32,1664]{2,1,0:T(8,128)(2,1)S(1)}, u32[]{:S(2)}, u32[]{:S(2)}) async-start(bf16[4,32,1664]{2,1,0:T(8,128)(2,1)} %fusion.3), calls=%async_computation.2 | async-start | bytes 851968 | tf_op jit(solution)/shard_map/all_to_all | solution.py:311
  181.3 16.8 %shard_map.181 = (bf16[2048,512]{1,0:T(8,128)(2,1)}, bf16[2048,512]{1,0:T(8,128)(2,1)}, f32[2048,512]{1,0:T(8,128)}) custom-call(s32[5]{0:T(128)} %concatenate.12.info_ref, bf16[2048,512]{1,0:T(8,128)(2,1)} %bitcast.68, bf16[2048,512]{1,0:T(8,128)(2,1)} %get-tuple-element.34.res_ref, bf16[2048,1024]{1,0:T(8,128)(2,1)} %get-tuple-element.38.pre_ref.next_ref, ...), custom_call_target="tpu_custom_call" | custom-call | flops 8589934592 | bytes 35389440 | tf_op jit(solution)/shard_map/pallas_call | solution.py:254
  (86 shorter events, 14.6 us)
Async XLA Ops:
  4.7 52.0 %copy-start.4 = (bf16[1,11,80]{2,1,0:T(8,128)(2,1)S(1)}, bf16[1,11,80]{2,1,0:T(8,128)(2,1)}, u32[]{:S(2)}) copy-start(bf16[1,11,80]{2,1,0:T(8,128)(2,1)} %param.12) | copy-start | bytes 5284
  5.6 18.7 %all-to-all-start = ((bf16[4,32,1664]{2,1,0:T(8,128)(2,1)}), bf16[4,32,1664]{2,1,0:T(8,128)(2,1)S(1)}, u32[]{:S(2)}, u32[]{:S(2)}) async-start(bf16[4,32,1664]{2,1,0:T(8,128)(2,1)} %broadcast_in_dim.24), calls=%async_computation | async-start | bytes 851968 | tf_op jit(solution)/shard_map/all_to_all | solution.py:311
  24.3 37.1 %copy-start.2 = (bf16[4,32,1664]{2,1,0:T(8,128)(2,1)}, bf16[4,32,1664]{2,1,0:T(8,128)(2,1)S(1)}, u32[]{:S(2)}) copy-start(bf16[4,32,1664]{2,1,0:T(8,128)(2,1)S(1)} %all-to-all-done.refs_0_) | copy-start | bytes 1277956
  25.1 15.3 %all-to-all-start.1 = ((bf16[4,32,1664]{2,1,0:T(8,128)(2,1)}), bf16[4,32,1664]{2,1,0:T(8,128)(2,1)S(1)}, u32[]{:S(2)}, u32[]{:S(2)}) async-start(bf16[4,32,1664]{2,1,0:T(8,128)(2,1)} %broadcast_in_dim.25), calls=%async_computation.1 | async-start | bytes 851968 | tf_op jit(solution)/shard_map/all_to_all | solution.py:311
  28.6 13.4 %collective-permute-start = (bf16[4,32,1664]{2,1,0:T(8,128)(2,1)S(1)}, bf16[4,32,1664]{2,1,0:T(8,128)(2,1)S(1)}, u32[]{:S(2)}, u32[]{:S(2)}) collective-permute-start(bf16[4,32,1664]{2,1,0:T(8,128)(2,1)S(1)} %all-to-all-done.refs_0_), channel_id=1, source_target_pairs={{0,2},{1,5},{2,0},{3,7},{4,6},{5,1},{6,4},{7,3},{8,10},{9,13},{10,... | collective-permute-start | bytes 1277960 | tf_op jit(solution)/shard_map/ppermute | solution.py:308
  30.2 13.8 %collective-permute-start.1 = (bf16[4,32,1664]{2,1,0:T(8,128)(2,1)S(1)}, bf16[4,32,1664]{2,1,0:T(8,128)(2,1)S(1)}, u32[]{:S(2)}, u32[]{:S(2)}) collective-permute-start(bf16[4,32,1664]{2,1,0:T(8,128)(2,1)S(1)} %all-to-all-done.refs_0_), channel_id=1, source_target_pairs={{0,4},{1,3},{2,6},{3,1},{4,0},{5,7},{6,2},{7,5},{8,12},{9,11},{10,... | collective-permute-start | bytes 1277960 | tf_op jit(solution)/shard_map/ppermute | solution.py:308
  31.7 12.3 %collective-permute-start.3 = (bf16[4,32,1664]{2,1,0:T(8,128)(2,1)S(1)}, bf16[4,32,1664]{2,1,0:T(8,128)(2,1)S(1)}, u32[]{:S(2)}, u32[]{:S(2)}) collective-permute-start(bf16[4,32,1664]{2,1,0:T(8,128)(2,1)S(1)} %all-to-all-done.refs_0_), channel_id=1, source_target_pairs={{0,1},{1,0},{2,3},{3,2},{4,5},{5,4},{6,7},{7,6},{8,9},{9,8},{10,11... | collective-permute-start | bytes 1277960 | tf_op jit(solution)/shard_map/ppermute | solution.py:308
  40.5 34.3 %copy-start.3 = (bf16[4,32,1664]{2,1,0:T(8,128)(2,1)}, bf16[4,32,1664]{2,1,0:T(8,128)(2,1)S(1)}, u32[]{:S(2)}) copy-start(bf16[4,32,1664]{2,1,0:T(8,128)(2,1)S(1)} %all-to-all-done.1.refs_0_) | copy-start | bytes 1277956
  40.5 12.6 %collective-permute-start.7 = (bf16[4,32,1664]{2,1,0:T(8,128)(2,1)S(1)}, bf16[4,32,1664]{2,1,0:T(8,128)(2,1)S(1)}, u32[]{:S(2)}, u32[]{:S(2)}) collective-permute-start(bf16[4,32,1664]{2,1,0:T(8,128)(2,1)S(1)} %all-to-all-done.1.refs_0_), channel_id=1, source_target_pairs={{0,2},{1,5},{2,0},{3,7},{4,6},{5,1},{6,4},{7,3},{8,10},{9,13},{10,... | collective-permute-start | bytes 1277960 | tf_op jit(solution)/shard_map/ppermute | solution.py:308
  42.0 19.5 %copy-start.6 = (bf16[4,32,1664]{2,1,0:T(8,128)(2,1)}, bf16[4,32,1664]{2,1,0:T(8,128)(2,1)S(1)}, u32[]{:S(2)}) copy-start(bf16[4,32,1664]{2,1,0:T(8,128)(2,1)S(1)} %collective-permute-done.refs_1_) | copy-start | bytes 1277956
  42.0 12.8 %collective-permute-start.2 = (bf16[4,32,1664]{2,1,0:T(8,128)(2,1)S(1)}, bf16[4,32,1664]{2,1,0:T(8,128)(2,1)}, u32[]{:S(2)}, u32[]{:S(2)}) collective-permute-start(bf16[4,32,1664]{2,1,0:T(8,128)(2,1)S(1)} %collective-permute-done.refs_1_), channel_id=1, source_target_pairs={{0,4},{1,3},{2,6},{3,1},{4,0},{5,7},{6,2},{7,5},{8,12},{9,11},{10,... | collective-permute-start | bytes 1277960 | tf_op jit(solution)/shard_map/ppermute | solution.py:308
  43.5 13.8 %collective-permute-start.8 = (bf16[4,32,1664]{2,1,0:T(8,128)(2,1)S(1)}, bf16[4,32,1664]{2,1,0:T(8,128)(2,1)S(1)}, u32[]{:S(2)}, u32[]{:S(2)}) collective-permute-start(bf16[4,32,1664]{2,1,0:T(8,128)(2,1)S(1)} %all-to-all-done.1.refs_0_), channel_id=1, source_target_pairs={{0,4},{1,3},{2,6},{3,1},{4,0},{5,7},{6,2},{7,5},{8,12},{9,11},{10,... | collective-permute-start | bytes 1277960 | tf_op jit(solution)/shard_map/ppermute | solution.py:308
  44.0 17.5 %copy-start.8 = (bf16[4,32,1664]{2,1,0:T(8,128)(2,1)}, bf16[4,32,1664]{2,1,0:T(8,128)(2,1)S(1)}, u32[]{:S(2)}) copy-start(bf16[4,32,1664]{2,1,0:T(8,128)(2,1)S(1)} %collective-permute-done.1.refs_2_) | copy-start | bytes 1277956
  44.0 13.8 %collective-permute-start.4 = (bf16[4,32,1664]{2,1,0:T(8,128)(2,1)S(1)}, bf16[4,32,1664]{2,1,0:T(8,128)(2,1)}, u32[]{:S(2)}, u32[]{:S(2)}) collective-permute-start(bf16[4,32,1664]{2,1,0:T(8,128)(2,1)S(1)} %collective-permute-done.refs_1_), channel_id=1, source_target_pairs={{0,1},{1,0},{2,3},{3,2},{4,5},{5,4},{6,7},{7,6},{8,9},{9,8},{10,11... | collective-permute-start | bytes 1277960 | tf_op jit(solution)/shard_map/ppermute | solution.py:308
  44.0 17.4 %copy-start.9 = (bf16[4,32,1664]{2,1,0:T(8,128)(2,1)}, bf16[4,32,1664]{2,1,0:T(8,128)(2,1)S(1)}, u32[]{:S(2)}) copy-start(bf16[4,32,1664]{2,1,0:T(8,128)(2,1)S(1)} %collective-permute-done.3.refs_4_) | copy-start | bytes 1277956
  44.0 13.9 %collective-permute-start.5 = (bf16[4,32,1664]{2,1,0:T(8,128)(2,1)S(1)}, bf16[4,32,1664]{2,1,0:T(8,128)(2,1)}, u32[]{:S(2)}, u32[]{:S(2)}) collective-permute-start(bf16[4,32,1664]{2,1,0:T(8,128)(2,1)S(1)} %collective-permute-done.1.refs_2_), channel_id=1, source_target_pairs={{0,1},{1,0},{2,3},{3,2},{4,5},{5,4},{6,7},{7,6},{8,9},{9,8},{10,11... | collective-permute-start | bytes 1277960 | tf_op jit(solution)/shard_map/ppermute | solution.py:308
  53.1 21.6 %copy-start.5 = (bf16[4,32,1664]{2,1,0:T(8,128)(2,1)}, bf16[4,32,1664]{2,1,0:T(8,128)(2,1)S(1)}, u32[]{:S(2)}) copy-start(bf16[4,32,1664]{2,1,0:T(8,128)(2,1)S(1)} %collective-permute-done.7.refs_1_) | copy-start | bytes 1277956
  53.1 8.1 %collective-permute-start.9 = (bf16[4,32,1664]{2,1,0:T(8,128)(2,1)S(1)}, bf16[4,32,1664]{2,1,0:T(8,128)(2,1)S(1)}, u32[]{:S(2)}, u32[]{:S(2)}) collective-permute-start(bf16[4,32,1664]{2,1,0:T(8,128)(2,1)S(1)} %collective-permute-done.7.refs_1_), channel_id=1, source_target_pairs={{0,4},{1,3},{2,6},{3,1},{4,0},{5,7},{6,2},{7,5},{8,12},{9,11},{10,... | collective-permute-start | bytes 1277960 | tf_op jit(solution)/shard_map/ppermute | solution.py:308
  54.7 6.7 %collective-permute-start.6 = (bf16[4,32,1664]{2,1,0:T(8,128)(2,1)}, bf16[4,32,1664]{2,1,0:T(8,128)(2,1)}, u32[]{:S(2)}, u32[]{:S(2)}) collective-permute-start(bf16[4,32,1664]{2,1,0:T(8,128)(2,1)} %collective-permute-done.2.refs_3_), channel_id=1, source_target_pairs={{0,1},{1,0},{2,3},{3,2},{4,5},{5,4},{6,7},{7,6},{8,9},{9,8},{10,11... | collective-permute-start | bytes 1277960 | tf_op jit(solution)/shard_map/ppermute | solution.py:308
  57.3 17.5 %copy-start.7 = (bf16[4,32,1664]{2,1,0:T(8,128)(2,1)}, bf16[4,32,1664]{2,1,0:T(8,128)(2,1)S(1)}, u32[]{:S(2)}) copy-start(bf16[4,32,1664]{2,1,0:T(8,128)(2,1)S(1)} %collective-permute-done.8.refs_2_) | copy-start | bytes 1277956
  57.3 17.5 %collective-permute-start.10 = (bf16[4,32,1664]{2,1,0:T(8,128)(2,1)S(1)}, bf16[4,32,1664]{2,1,0:T(8,128)(2,1)S(1)}, u32[]{:S(2)}, u32[]{:S(2)}) collective-permute-start(bf16[4,32,1664]{2,1,0:T(8,128)(2,1)S(1)} %all-to-all-done.1.refs_0_), channel_id=1, source_target_pairs={{0,1},{1,0},{2,3},{3,2},{4,5},{5,4},{6,7},{7,6},{8,9},{9,8},{10,11... | collective-permute-start | bytes 1277960 | tf_op jit(solution)/shard_map/ppermute | solution.py:308
  57.8 17.0 %collective-permute-start.11 = (bf16[4,32,1664]{2,1,0:T(8,128)(2,1)S(1)}, bf16[4,32,1664]{2,1,0:T(8,128)(2,1)S(1)}, u32[]{:S(2)}, u32[]{:S(2)}) collective-permute-start(bf16[4,32,1664]{2,1,0:T(8,128)(2,1)S(1)} %collective-permute-done.7.refs_1_), channel_id=1, source_target_pairs={{0,1},{1,0},{2,3},{3,2},{4,5},{5,4},{6,7},{7,6},{8,9},{9,8},{10,11... | collective-permute-start | bytes 1277960 | tf_op jit(solution)/shard_map/ppermute | solution.py:308
  57.9 16.9 %collective-permute-start.12 = (bf16[4,32,1664]{2,1,0:T(8,128)(2,1)S(1)}, bf16[4,32,1664]{2,1,0:T(8,128)(2,1)S(1)}, u32[]{:S(2)}, u32[]{:S(2)}) collective-permute-start(bf16[4,32,1664]{2,1,0:T(8,128)(2,1)S(1)} %collective-permute-done.8.refs_2_), channel_id=1, source_target_pairs={{0,1},{1,0},{2,3},{3,2},{4,5},{5,4},{6,7},{7,6},{8,9},{9,8},{10,11... | collective-permute-start | bytes 1277960 | tf_op jit(solution)/shard_map/ppermute | solution.py:308
  61.2 13.6 %collective-permute-start.13 = (bf16[4,32,1664]{2,1,0:T(8,128)(2,1)S(1)}, bf16[4,32,1664]{2,1,0:T(8,128)(2,1)S(1)}, u32[]{:S(2)}, u32[]{:S(2)}) collective-permute-start(bf16[4,32,1664]{2,1,0:T(8,128)(2,1)S(1)} %collective-permute-done.9.refs_3_), channel_id=1, source_target_pairs={{0,1},{1,0},{2,3},{3,2},{4,5},{5,4},{6,7},{7,6},{8,9},{9,8},{10,11... | collective-permute-start | bytes 1277960 | tf_op jit(solution)/shard_map/ppermute | solution.py:308
  103.0 13.3 %collective-permute-start.14 = (bf16[2,2,4,32,1664]{4,3,2,1,0:T(8,128)(2,1)}, bf16[2,2,4,32,1664]{4,3,2,1,0:T(8,128)(2,1)S(1)}, u32[]{:S(2)}, u32[]{:S(2)}) collective-permute-start(bf16[2,2,4,32,1664]{4,3,2,1,0:T(8,128)(2,1)} %get-tuple-element.37), channel_id=1, source_target_pairs={{0,1},{1,0},{2,3},{3,2},{4,5},{5,4},{6,7},{7,6},{8,9},{9,8},{10,11... | collective-permute-start | bytes 5111816 | tf_op jit(solution)/shard_map/ppermute | solution.py:308
  133.0 3.9 %collective-permute-start.15 = (bf16[2,2,4,32,1664]{4,3,2,1,0:T(8,128)(2,1)}, bf16[2,2,4,32,1664]{4,3,2,1,0:T(8,128)(2,1)S(1)}, u32[]{:S(2)}, u32[]{:S(2)}) collective-permute-start(bf16[2,2,4,32,1664]{4,3,2,1,0:T(8,128)(2,1)} %get-tuple-element.47), channel_id=1, source_target_pairs={{0,1},{1,0},{2,3},{3,2},{4,5},{5,4},{6,7},{7,6},{8,9},{9,8},{10,11... | collective-permute-start | bytes 5111816 | tf_op jit(solution)/shard_map/ppermute | solution.py:308
  133.3 12.8 %collective-permute-start.18 = (bf16[2,4,32,1664]{3,2,1,0:T(8,128)(2,1)S(1)}, bf16[2,4,32,1664]{3,2,1,0:T(8,128)(2,1)S(1)}, u32[]{:S(2)}, u32[]{:S(2)}) collective-permute-start(bf16[2,4,32,1664]{3,2,1,0:T(8,128)(2,1)S(1)} %slice_bitcast_fusion.2), channel_id=1, source_target_pairs={{0,2},{1,5},{2,0},{3,7},{4,6},{5,1},{6,4},{7,3},{8,10},{9,13},{10,... | collective-permute-start | bytes 2555912 | tf_op jit(solution)/shard_map/ppermute | solution.py:308
  137.4 22.4 %collective-permute-start.16 = (bf16[2,4,32,1664]{3,2,1,0:T(8,128)(2,1)S(1)}, bf16[2,4,32,1664]{3,2,1,0:T(8,128)(2,1)S(1)}, u32[]{:S(2)}, u32[]{:S(2)}) collective-permute-start(bf16[2,4,32,1664]{3,2,1,0:T(8,128)(2,1)S(1)} %slice_bitcast_fusion), channel_id=1, source_target_pairs={{0,2},{1,5},{2,0},{3,7},{4,6},{5,1},{6,4},{7,3},{8,10},{9,13},{10,... | collective-permute-start | bytes 2555912 | tf_op jit(solution)/shard_map/ppermute | solution.py:308
  146.3 15.3 %collective-permute-start.19 = (bf16[4,32,1664]{2,1,0:T(8,128)(2,1)S(1)}, bf16[4,32,1664]{2,1,0:T(8,128)(2,1)S(1)}, u32[]{:S(2)}, u32[]{:S(2)}) collective-permute-start(bf16[4,32,1664]{2,1,0:T(8,128)(2,1)S(1)} %slice_bitcast_fusion.3), channel_id=1, source_target_pairs={{0,4},{1,3},{2,6},{3,1},{4,0},{5,7},{6,2},{7,5},{8,12},{9,11},{10,... | collective-permute-start | bytes 1277960 | tf_op jit(solution)/shard_map/ppermute | solution.py:308
  160.0 8.2 %collective-permute-start.17 = (bf16[4,32,1664]{2,1,0:T(8,128)(2,1)S(1)}, bf16[4,32,1664]{2,1,0:T(8,128)(2,1)S(1)}, u32[]{:S(2)}, u32[]{:S(2)}) collective-permute-start(bf16[4,32,1664]{2,1,0:T(8,128)(2,1)S(1)} %slice_bitcast_fusion.5), channel_id=1, source_target_pairs={{0,4},{1,3},{2,6},{3,1},{4,0},{5,7},{6,2},{7,5},{8,12},{9,11},{10,... | collective-permute-start | bytes 1277960 | tf_op jit(solution)/shard_map/ppermute | solution.py:308
  162.5 15.4 %all-to-all-start.3 = ((bf16[4,32,1664]{2,1,0:T(8,128)(2,1)}), bf16[4,32,1664]{2,1,0:T(8,128)(2,1)S(1)}, u32[]{:S(2)}, u32[]{:S(2)}) async-start(bf16[4,32,1664]{2,1,0:T(8,128)(2,1)} %fusion.2), calls=%async_computation.3 | async-start | bytes 851968 | tf_op jit(solution)/shard_map/all_to_all | solution.py:311
  177.9 20.3 %all-to-all-start.2 = ((bf16[4,32,1664]{2,1,0:T(8,128)(2,1)}), bf16[4,32,1664]{2,1,0:T(8,128)(2,1)S(1)}, u32[]{:S(2)}, u32[]{:S(2)}) async-start(bf16[4,32,1664]{2,1,0:T(8,128)(2,1)} %fusion.3), calls=%async_computation.2 | async-start | bytes 851968 | tf_op jit(solution)/shard_map/all_to_all | solution.py:311
  (7 other events, 34.3 us)

commit v4 on v3

v4 whole, which is shorter than its diff:
```python
import functools

import jax
import jax.numpy as jnp
from jax import lax
from jax.experimental import pallas as pl
from jax.experimental.pallas import tpu as pltpu
from jax.sharding import PartitionSpec as P

FIRST_DILATION = 512
AXES = ("dp", "group")
LANES = 128
TILE = 512
MIB = 1024 * 1024
ROOM_0, ROOM_1, ROOM_2, ROOM_3, ROOM_4, ROOM_5, ROOM_SMALL = 8, 13, 6, 8, 8, 8, 12
LOW = jnp.bfloat16
FULL = jnp.float32


def dot(left, right):
    return jnp.dot(left, right, preferred_element_type=FULL)


def dot_cols(left, right, **more):
    return lax.dot_general(
        left, right, (((1,), (1,)), ((), ())), preferred_element_type=FULL, **more
    )


def dot_rows(left, right, **more):
    return lax.dot_general(
        left, right, (((0,), (0,)), ((), ())), preferred_element_type=FULL, **more
    )


class Sizes:
    def __init__(self, channels, mel_count):
        self.channels = channels
        self.gate = 2 * channels
        self.mel = mel_count
        self.early = channels
        self.now = 2 * channels
        self.extra = 3 * channels
        self.extra_width = -(-(mel_count + 2) // LANES) * LANES
        self.pack = self.extra + self.extra_width


def mask_of(info_ref, start, rows):
    places = start + lax.broadcasted_iota(jnp.int32, (rows, 1), 0)
    return (places < info_ref[0]).astype(FULL)


def frames_of(info_ref, start, rows):
    places = start + lax.broadcasted_iota(jnp.int32, (rows, LANES), 0)
    first = lax.broadcasted_iota(jnp.int32, (rows, LANES), 1) * info_ref[1]
    return ((places >= first) & (places < first + info_ref[1])).astype(FULL).astype(LOW)


def masked(value, mask):
    return (value.astype(FULL) * mask).astype(LOW)


def out_bias_row(size, extra):
    column = lax.broadcasted_iota(jnp.int32, (8, size.extra_width), 1)
    pick = (column == size.mel + 1).astype(FULL).astype(LOW)
    return dot_cols(pick, extra)[0:1]


def gates(taps, w_ref, size, side):
    channels = size.channels
    width = channels // 2
    low = slice(side * width, (side + 1) * width)
    high = slice(channels + side * width, channels + (side + 1) * width)
    tangent = jnp.tanh(dot_cols(taps, w_ref[low, size.early :]))
    sig_gate = 0.5 * jnp.tanh(0.5 * dot_cols(taps, w_ref[high, size.early :])) + 0.5
    gated = tangent * sig_gate
    return low, high, gated, sig_gate * (1.0 - tangent * tangent), gated * (1.0 - sig_gate)


def rows_of(step, rows):
    return pl.ds(pl.multiple_of(step * rows, rows), rows)


def forward_0(size, wires, info_ref, x_ref, mel_ref, *refs):
    pieces, refs = refs[: wires.pieces], refs[wires.pieces :]
    low1_ref, gated_ref, slope_ref, w_ref = refs
    step = pl.program_id(0)
    channels = size.channels

    @pl.when(step == 0)
    def _():
        wires.put_together(info_ref, pieces, w_ref)

    tile = rows_of(step, TILE)
    mask = mask_of(info_ref, step * TILE, TILE)
    hidden = x_ref[tile].astype(FULL) * mask
    low = hidden.astype(LOW)
    prev_mask = mask_of(info_ref, (step - 1) * TILE, TILE) * (step > 0).astype(FULL)
    prev = x_ref[rows_of(jnp.maximum(step - 1, 0), TILE)].astype(FULL) * prev_mask
    cond = dot(frames_of(info_ref, step * TILE, TILE), mel_ref[...]).astype(LOW)
    taps = jnp.concatenate([prev.astype(LOW), low, cond], axis=1)
    for side in range(2):
        first, second, gated, slope_a, slope_b = gates(taps, w_ref, size, side)
        gated_ref[tile, first] = gated.astype(LOW)
        slope_ref[tile, first] = slope_a.astype(LOW)
        slope_ref[tile, second] = slope_b.astype(LOW)
    moved = dot_cols(gated_ref[tile], w_ref[:channels, :channels])
    moved = moved + out_bias_row(size, w_ref[:channels, size.extra :])
    low1_ref[tile] = ((hidden + moved) * mask).astype(LOW)


def layer_1(size, wires, steps, info_ref, low1_ref, mel_ref, go_ref, gs_ref, *refs):
    pieces, refs = refs[: wires.pieces], refs[wires.pieces :]
    gated_ref, pre_ref, w_ref, here_ref, away_ref, melg_ref, *scratch = refs
    prev_s, proj_s, frames_s, part_s = scratch
    step = pl.program_id(0)
    channels = size.channels

    @pl.when(step == 0)
    def _():
        wires.put_together(info_ref, pieces, w_ref)
        melg_ref[...] = jnp.zeros_like(melg_ref)

    @pl.when(step < steps)
    def _():
        tile = rows_of(step, TILE)
        mask = mask_of(info_ref, step * TILE, TILE)
        low = low1_ref[tile]
        before = pl.ds(pl.multiple_of(jnp.maximum(step * TILE - 16, 0), 16), 16)
        last = low1_ref[before].astype(FULL)[15:16] * (step > 0).astype(FULL)
        place = lax.broadcasted_iota(jnp.int32, (TILE, 1), 0)
        prev = jnp.where(place == 0, last, pltpu.roll(low.astype(FULL), 1, 0)).astype(LOW)
        frames = frames_of(info_ref, step * TILE, TILE)
        cond = dot(frames, mel_ref[...]).astype(LOW)
        taps = jnp.concatenate([prev, low, cond], axis=1)
        proj = jnp.concatenate([masked(go_ref[tile], mask), masked(gs_ref[tile], mask)], axis=1)
        prev_s[tile] = prev
        frames_s[tile] = frames
        grad_gated = dot(proj, w_ref[:, :channels])
        for side in range(2):
            first, second, gated, slope_a, slope_b = gates(taps, w_ref, size, side)
            gated_ref[tile, first] = gated.astype(LOW)
            pre_ref[tile, first] = (grad_gated[:, first] * slope_a).astype(LOW)
            pre_ref[tile, second] = (grad_gated[:, first] * slope_b).astype(LOW)

    @pl.when(step >= steps)
    def _():
        width = part_s.shape[0]
        part = rows_of(step - steps, width)
        half = channels // width
        mask = mask_of(info_ref, 0, low1_ref.shape[0])

        @pl.when(step < steps + half)
        def _():
            columns = rows_of(jnp.clip(step - steps, 0, half - 1), width)
            proj_s[...] = masked(go_ref[:, columns], mask)

        @pl.when(step >= steps + half)
        def _():
            columns = rows_of(jnp.maximum(step - steps - half, 0), width)
            proj_s[...] = masked(gs_ref[:, columns], mask)

        pre = pre_ref[:, part]
        part_s[:, size.early : size.now] = dot_rows(pre, prev_s[...]).astype(LOW)
        part_s[:, size.now : size.extra] = dot_rows(pre, low1_ref[...]).astype(LOW)
        finish_part(size, pre, proj_s[...], frames_s, gated_ref, mel_ref, w_ref[part, size.extra :], melg_ref, part_s)
        wires.put_apart(info_ref, step - steps, part_s, here_ref, away_ref)

def in_two(value):
    high = value.astype(LOW)
    return high, (value - high.astype(FULL)).astype(LOW)


def finish_part(size, pre, proj, frames_ref, gated_ref, mel_ref, cond_weight, melg_ref, part_ref):
    sums = in_two(dot_rows(frames_ref[...], pre))
    extra = sum(dot_rows(half, mel_ref[...]) for half in sums)
    melg_ref[...] += sum(dot(half, cond_weight) for half in sums)
    total = jnp.sum(proj.astype(FULL), axis=0, keepdims=True)
    bias = jnp.broadcast_to(total, (LANES, total.shape[1])).T[:, 0:1]
    column = lax.broadcasted_iota(jnp.int32, extra.shape, 1)
    part_ref[:, size.extra :] = jnp.where(column == size.mel + 1, bias, extra).astype(LOW)
    part_ref[:, : size.channels] = dot_rows(proj, gated_ref[...]).astype(LOW)


def backward_0(size, info_ref, pre1_ref, w1_ref, w0_ref, go_ref, gs_ref, slope_ref, res_ref, pre0_ref, carry_ref):
    step = pl.program_id(0)
    channels = size.channels
    index = pl.num_programs(0) - 1 - step
    tile = rows_of(index, TILE)
    mask = mask_of(info_ref, index * TILE, TILE)

    @pl.when(step == 0)
    def _():
        carry_ref[...] = jnp.zeros_like(carry_ref)

    pre1 = pre1_ref[tile]
    early = dot(pre1, w1_ref[:, size.early : size.now])
    place = lax.broadcasted_iota(jnp.int32, (TILE, 1), 0)
    later = jnp.where(place == TILE - 1, carry_ref[0:1], pltpu.roll(early, TILE - 1, 0))
    carry_ref[...] = early[:8]
    now = dot(pre1, w1_ref[:, size.now : size.extra])
    res = ((go_ref[tile].astype(FULL) * mask + now + later) * mask).astype(LOW)
    res_ref[tile] = res
    proj = jnp.concatenate([res, masked(gs_ref[tile], mask)], axis=1)
    grad_gated = dot(proj, w0_ref[:, :channels])
    for half in (slice(0, channels), slice(channels, 2 * channels)):
        pre0_ref[tile, half] = (grad_gated * slope_ref[tile, half].astype(FULL)).astype(LOW)


def weights_0(size, wires, info_ref, pre_ref, res_ref, gs_ref, x_ref, gated_ref, mel_ref, w_ref, here_ref, away_ref, melg_ref, frames_s, proj_s, part_s):
    step = pl.program_id(0)
    samples = x_ref.shape[0]

    @pl.when(step == 0)
    def _():
        frames_s[...] = frames_of(info_ref, 0, samples)
        melg_ref[...] = jnp.zeros_like(melg_ref)

    width = part_s.shape[0]
    half = pl.num_programs(0) // 2
    part = rows_of(step, width)

    @pl.when(step < half)
    def _():
        proj_s[...] = res_ref[:, rows_of(jnp.minimum(step, half - 1), width)]

    @pl.when(step >= half)
    def _():
        proj_s[...] = masked(
            gs_ref[:, rows_of(jnp.maximum(step - half, 0), width)], mask_of(info_ref, 0, samples)
        )

    pre = pre_ref[:, part]
    shift = FIRST_DILATION
    early = dot_rows(pre[shift:], x_ref[: samples - shift])
    part_s[:, size.early : size.now] = early.astype(LOW)
    part_s[:, size.now : size.extra] = dot_rows(pre, x_ref[...]).astype(LOW)
    finish_part(size, pre, proj_s[...], frames_s, gated_ref, mel_ref, w_ref[part, size.extra :], melg_ref, part_s)
    wires.put_apart(info_ref, step, part_s, here_ref, away_ref)


def samples_gradient(size, info_ref, res_ref, pre_ref, w0_ref, sg_ref):
    step = pl.program_id(0)
    tile = rows_of(step, TILE)
    grad = res_ref[tile].astype(FULL) + dot(pre_ref[tile], w0_ref[:, size.now : size.extra])
    after = rows_of(jnp.minimum(step + 1, pl.num_programs(0) - 1), TILE)
    later = dot(pre_ref[after], w0_ref[:, size.early : size.now])
    grad = grad + jnp.where(step < pl.num_programs(0) - 1, later, 0.0)
    sg_ref[...] = grad * mask_of(info_ref, step * TILE, TILE)


def forward_outputs(size, info_ref, x_ref, gated0_ref, gated1_ref, w0_ref, w1_ref, res_ref, skip_ref):
    step = pl.program_id(0)
    tile = rows_of(step, TILE)
    mask = mask_of(info_ref, step * TILE, TILE)
    channels = size.channels
    gated = jnp.concatenate([gated0_ref[tile], gated1_ref[tile]], axis=1)

    def projected(rows):
        both = jnp.concatenate([w0_ref[rows, :channels], w1_ref[rows, :channels]], axis=1)
        bias = out_bias_row(size, w0_ref[rows, size.extra :])
        return dot_cols(gated, both) + bias + out_bias_row(size, w1_ref[rows, size.extra :])

    res = projected(slice(0, channels))
    res_ref[...] = ((x_ref[tile].astype(FULL) + res) * mask).astype(LOW)
    skip_ref[...] = (projected(slice(channels, 2 * channels)) * mask).astype(LOW)


def add_and_part(left_ref, right_ref, stay_ref, go_ref):
    stay_ref[...] = add_low(left_ref[0], right_ref[0])
    go_ref[...] = add_low(left_ref[1], right_ref[1])


def pack_layers(layers, copies, conv_ref, cond_ref, conv_b_ref, out_ref, out_b_ref, *refs):
    rows = conv_ref.shape[1]
    same = lax.broadcasted_iota(jnp.int32, (rows, rows), 0)
    same = (same == lax.broadcasted_iota(jnp.int32, (rows, rows), 1)).astype(FULL).astype(LOW)
    for layer in range(layers):
        to_ref = refs[layer]
        early, extra = out_ref.shape[2], out_ref.shape[2] + conv_ref.shape[2]
        mel = cond_ref.shape[2]
        width = to_ref.shape[2] - extra
        biases = dot_cols(same, jnp.concatenate([conv_b_ref[...], out_b_ref[...]], axis=0))
        place = lax.broadcasted_iota(jnp.int32, (rows, width), 1)
        cond = jnp.concatenate(
            [cond_ref[layer].astype(FULL), jnp.zeros((rows, width - mel), FULL)], axis=1
        )
        cond = jnp.where(place == mel, biases[:, layer : layer + 1], cond)
        cond = jnp.where(place == mel + 1, biases[:, layers + layer : layers + layer + 1], cond)
        cond = cond.astype(LOW)
        for copy in range(copies):
            to_ref[copy, :, :early] = out_ref[layer]
            to_ref[copy, :, early:extra] = conv_ref[layer]
            to_ref[copy, :, extra:] = cond


def unpack_layers(layers, mel, *refs):
    conv_ref, cond_ref, conv_b_ref, out_ref, out_b_ref = refs[layers:]
    rows = conv_ref.shape[1]
    same = lax.broadcasted_iota(jnp.int32, (rows, rows), 0)
    same = (same == lax.broadcasted_iota(jnp.int32, (rows, rows), 1)).astype(FULL)
    early, extra = out_ref.shape[2], out_ref.shape[2] + conv_ref.shape[2]
    for layer in range(layers):
        total = jnp.sum(refs[layer][...].astype(FULL), axis=0)
        out_ref[layer] = total[:, :early]
        conv_ref[layer] = total[:, early:extra]
        cond_ref[layer] = total[:, extra : extra + mel]
        biases = dot_rows(total[:, extra:], same, precision=lax.Precision.HIGHEST)
        conv_b_ref[layer : layer + 1] = biases[mel : mel + 1]
        out_b_ref[layer : layer + 1] = biases[mel + 1 : mel + 2]


def plain(kernel, operands, outs):
    return pl.pallas_call(
        kernel,
        out_shape=outs,
        compiler_params=pltpu.CompilerParams(vmem_limit_bytes=ROOM_SMALL * MIB),
    )(*operands)


def call(kernel, grid, info, operands, outs, scratch, flops, room):
    arrays = [x if spec else pltpu.with_memory_space_constraint(x, pltpu.VMEM) for x, spec in operands]
    shapes = [x if spec else pltpu.VMEM(x.shape, x.dtype) for x, spec in outs]
    moved = sum(x.size * x.dtype.itemsize for x, spec in (*operands, *outs) if spec)
    return pl.pallas_call(
        kernel,
        grid_spec=pltpu.PrefetchScalarGridSpec(
            num_scalar_prefetch=1,
            grid=(grid,),
            in_specs=[spec or KEPT for _, spec in operands],
            out_specs=[spec or KEPT for _, spec in outs],
            scratch_shapes=scratch,
        ),
        out_shape=shapes,
        compiler_params=pltpu.CompilerParams(
            vmem_limit_bytes=room * MIB, dimension_semantics=("arbitrary",)
        ),
        cost_estimate=pl.CostEstimate(flops=flops, bytes_accessed=moved, transcendentals=0),
    )(info, *arrays)


def shape_of(*shape, dtype=LOW):
    return jax.ShapeDtypeStruct(shape, dtype)


def tiled(width, place=lambda i: i):
    return pl.BlockSpec((TILE, width), lambda i, info: (place(i), 0))


def fixed(*shape, at=(0, 0)):
    return pl.BlockSpec(shape, lambda i, info: at)


KEPT = pl.BlockSpec(memory_space=pltpu.VMEM)


class Wires:
    def __init__(self, dp, cores, channels):
        assert dp % 4 == 0 and cores == 2
        self.rest = dp // 4
        self.devices = dp * 2
        self.rows = channels // self.devices
        self.direct = self.rows % 16 == 0
        self.pieces = 8 if self.direct else 1
        me = lax.axis_index(AXES)
        self.core = me % 2
        self.a = (me // 2) % 2
        self.b = (me // 4) % 2
        every = range(self.devices)
        self.sibling = [(i, i ^ 1) for i in every]
        self.first = [(i, i ^ (4 if i % 2 else 2)) for i in every]
        self.second = [(i, i ^ (2 if i % 2 else 4)) for i in every]
        self.columns = [[rest * 8 + low for rest in range(self.rest)] for low in range(8)]

    def place(self):
        return jnp.stack([self.core, self.a, self.b]).astype(jnp.int32)

    def hop(self, value, pairs):
        return lax.ppermute(value, AXES, pairs)

    def swap_rest(self, blocks):
        return lax.all_to_all(blocks, AXES, 0, 0, tiled=True, axis_index_groups=self.columns)

    def far_hops(self, mine, one, two):
        pieces = [mine, one, two, self.hop(one, self.second)]
        pieces += [self.hop(piece, self.sibling) for piece in pieces]
        return pieces if self.direct else [self.put_in_order(pieces)]

    def put_in_order(self, pieces):
        whole = jnp.zeros((self.rest, 2, 2, 2) + pieces[0].shape[1:], LOW)
        for index, piece in enumerate(pieces):
            source = self.core if index < 4 else 1 - self.core
            first, second = index % 2, (index // 2) % 2
            at_a = self.a ^ jnp.where(source == 0, first, second)
            at_b = self.b ^ jnp.where(source == 0, second, first)
            whole = lax.dynamic_update_slice(
                whole, piece[:, None, None, None], (0, at_b, at_a, source, 0, 0)
            )
        return whole.reshape(-1, pieces[0].shape[2])

    def put_together(self, info_ref, pieces, w_ref):
        if not self.direct:
            w_ref[...] = pieces[0][...]
            return
        core, a, b = info_ref[2], info_ref[3], info_ref[4]
        for index, piece in enumerate(pieces):
            source = core if index < 4 else 1 - core
            first, second = index % 2, (index // 2) % 2
            at_a = a ^ jnp.where(source == 0, first, second)
            at_b = b ^ jnp.where(source == 0, second, first)
            for rest in range(self.rest):
                place = ((rest * 2 + at_b) * 2 + at_a) * 2 + source
                w_ref[rows_of(place, self.rows)] = piece[rest]

    def put_apart(self, info_ref, step, part_ref, here_ref, away_ref):
        if not self.direct:
            here_ref[rows_of(step, part_ref.shape[0])] = part_ref[...]
            return
        core, a, b = info_ref[2], info_ref[3], info_ref[4]
        blocks = part_ref.shape[0] // self.rows
        for block in range(blocks):
            at_b, at_a, owner = (block // 4) % 2, (block // 2) % 2, block % 2
            value = part_ref[block * self.rows : (block + 1) * self.rows]
            first, second = at_a ^ a, at_b ^ b
            if owner:
                first, second = second, first
            rest = step * (blocks // 8) + block // 8

            @pl.when(core == owner)
            def _():
                here_ref[first, second, rest] = value

            @pl.when(core != owner)
            def _():
                away_ref[first, second, rest] = value

    def apart(self, depth):
        if not self.direct:
            return [(shape_of(self.devices * self.rows, depth), None), (shape_of(16, LANES), None)]
        return [(shape_of(2, 2, self.rest, self.rows, depth), None)] * 2

    def by_distance(self, full):
        rows = full.shape[0] // self.devices
        blocks = full.reshape(self.rest, 2, 2, 2, rows, full.shape[1])
        parts = []
        for away in range(2):
            source = self.core ^ away
            for first in range(2):
                for second in range(2):
                    at_a = self.a ^ jnp.where(source == 0, first, second)
                    at_b = self.b ^ jnp.where(source == 0, second, first)
                    parts.append(
                        lax.dynamic_slice(
                            blocks,
                            (0, at_b, at_a, source, 0, 0),
                            (self.rest, 1, 1, 1, rows, full.shape[1]),
                        )[:, 0, 0, 0]
                    )
        return jnp.stack(parts).reshape(2, 2, 2, self.rest, rows, full.shape[1])


def add_low(left, right):
    return (left.astype(FULL) + right.astype(FULL)).astype(LOW)


def per_device(
    dp,
    cores,
    samples,
    mel,
    lengths,
    hops,
    conv_weight,
    cond_weight,
    conv_bias,
    out_weight,
    out_bias,
    grad_out,
    grad_skip,
):
    sample_count, channels = samples.shape[1:]
    frame_count, mel_count = mel.shape[1:]
    layers = conv_weight.shape[0]
    size = Sizes(channels, mel_count)
    gate = size.gate
    wires = Wires(dp, cores, gate)
    assert layers == 2 and sample_count % TILE == 0 and TILE == FIRST_DILATION
    steps = sample_count // TILE
    info = jnp.concatenate([lengths, hops, wires.place()])
    x, go, gs = samples[0], grad_out[0], grad_skip[0]
    mel_table = jnp.concatenate([mel[0], jnp.ones((frame_count, 1), LOW)], axis=1)
    mel_table = jnp.pad(
        mel_table, ((0, LANES - frame_count), (0, size.extra_width - mel_count - 1))
    )

    conv_t, cond_t, out_t = (
        w.swapaxes(1, 2) for w in (conv_weight, cond_weight, out_weight)
    )
    rows = conv_t.shape[1]
    own = plain(
        functools.partial(pack_layers, layers, wires.rest),
        (conv_t, cond_t, conv_bias, out_t, out_bias),
        [shape_of(wires.rest, rows, size.pack)] * layers,
    )
    mine0 = wires.swap_rest(own[0])
    one0, two0 = wires.hop(mine0, wires.first), wires.hop(mine0, wires.second)
    pieces0 = wires.far_hops(mine0, one0, two0)
    mine1 = wires.swap_rest(own[1])
    mine1, *pieces0 = lax.optimization_barrier((mine1, *pieces0))
    one1, two1 = wires.hop(mine1, wires.first), wires.hop(mine1, wires.second)

    table = fixed(LANES, size.extra_width)
    macs = sample_count * channels * channels
    kept = lambda *columns: [(shape_of(sample_count, c), None) for c in columns]
    whole_w = (shape_of(gate, size.pack), None)
    parts = 4
    width = gate // parts
    melg = (shape_of(LANES, size.extra_width, dtype=FULL), table)
    scratch = lambda *shape: pltpu.VMEM(shape, LOW)

    blocked = (shape_of(sample_count, channels), tiled(channels))
    keep = lambda *values: [(value, None) for value in values]

    low1, gated0, slope0, w0 = call(
        functools.partial(forward_0, size, wires),
        steps,
        info,
        [(x, None), (mel_table, table), *keep(*pieces0)],
        [*kept(channels, channels, gate), whole_w],
        [],
        10 * macs,
        ROOM_0,
    )
    one1, two1, low1 = lax.optimization_barrier((one1, two1, low1))
    gated1, pre1, w1, here1, away1, melg1 = call(
        functools.partial(layer_1, size, wires, steps),
        steps + parts,
        info,
        [(low1, None), (mel_table, table), (go, None), (gs, None)]
        + keep(*wires.far_hops(mine1, one1, two1)),
        [
            *kept(channels, gate),
            whole_w,
            *wires.apart(size.pack),
            melg,
        ],
        [
            scratch(sample_count, channels),
            scratch(sample_count, width),
            scratch(sample_count, LANES),
            scratch(width, size.pack),
        ],
        24 * macs,
        ROOM_1,
    )
    if not wires.direct:
        here1, away1 = wires.by_distance(here1)
    came1 = wires.hop(away1, wires.sibling)

    res0, pre0 = call(
        functools.partial(backward_0, size),
        steps,
        info,
        keep(pre1, w1, w0, go, gs, slope0),
        kept(channels, gate),
        [pltpu.VMEM((8, channels), FULL)],
        12 * macs,
        ROOM_2,
    )
    half_shape = shape_of(2, wires.rest, rows, size.pack)
    last_shape = shape_of(wires.rest, rows, size.pack)
    stay1, leave1 = plain(add_and_part, (here1, came1), [half_shape] * 2)
    pre0, stay1, leave1 = lax.optimization_barrier((pre0, stay1, leave1))
    came1 = wires.hop(leave1, wires.first)

    here0, away0, melg0 = call(
        functools.partial(weights_0, size, wires),
        parts,
        info,
        [*keep(pre0, res0, gs, x, gated0), (mel_table, table), (w0, None)],
        [*wires.apart(size.pack), melg],
        [
            scratch(sample_count, LANES),
            scratch(sample_count, width),
            scratch(width, size.pack),
        ],
        12 * macs,
        ROOM_3,
    )
    if not wires.direct:
        here0, away0 = wires.by_distance(here0)
    away0, came1 = lax.optimization_barrier((away0, came1))
    came0 = wires.hop(away0, wires.sibling)
    stay1, leave1 = plain(add_and_part, (stay1, came1), [last_shape] * 2)
    came1 = wires.hop(leave1, wires.second)
    came0, leave1 = lax.optimization_barrier((came0, leave1))
    stay0, leave0 = plain(add_and_part, (here0, came0), [half_shape] * 2)
    pre0, stay0, leave0 = lax.optimization_barrier((pre0, stay0, leave0))
    came0 = wires.hop(leave0, wires.first)

    (samples_grad,) = call(
        functools.partial(samples_gradient, size),
        steps,
        info,
        keep(res0, pre0, w0),
        [(shape_of(sample_count, channels, dtype=FULL), tiled(channels))],
        [],
        8 * macs,
        ROOM_4,
    )
    came1, samples_grad = lax.optimization_barrier((came1, samples_grad))
    parts1 = wires.swap_rest(add_low(stay1, came1))
    stay0, leave0 = plain(add_and_part, (stay0, came0), [last_shape] * 2)
    x, stay0, leave0 = lax.optimization_barrier((x, stay0, leave0))
    came0 = wires.hop(leave0, wires.second)
    residual_out, skip_output_sum = call(
        functools.partial(forward_outputs, size),
        steps,
        info,
        keep(x, gated0, gated1, w0, w1),
        [blocked, blocked],
        [],
        8 * macs,
        ROOM_5,
    )
    came0, residual_out = lax.optimization_barrier((came0, residual_out))
    parts0 = wires.swap_rest(add_low(stay0, came0))
    grads = plain(
        functools.partial(unpack_layers, layers, mel_count),
        (parts0, parts1),
        [
            shape_of(layers, rows, 2 * channels, dtype=FULL),
            shape_of(layers, rows, mel_count, dtype=FULL),
            shape_of(layers, rows, dtype=FULL),
            shape_of(layers, rows, channels, dtype=FULL),
            shape_of(layers, rows, dtype=FULL),
        ],
    )
    mel_grad = (melg0 + melg1)[:frame_count, :mel_count]
    conv_grad, cond_grad, conv_b_grad, out_grad, out_b_grad = grads
    return (
        residual_out[None],
        skip_output_sum[None],
        samples_grad[None],
        mel_grad[None],
        conv_grad.swapaxes(1, 2),
        cond_grad.swapaxes(1, 2),
        conv_b_grad,
        out_grad.swapaxes(1, 2),
        out_b_grad,
    )


def solution(mesh):
    dp, cores = mesh.shape["dp"], mesh.shape["group"]

    def everything(*arrays):
        return per_device(dp, cores, *arrays)

    clips = P(AXES, None, None)
    columns = P(None, None, AXES)
    biases = P(None, AXES)
    return jax.shard_map(
        everything,
        mesh=mesh,
        in_specs=(
            clips, clips, P(AXES), P(AXES), columns, columns, biases, columns, biases, clips, clips,
        ),
        out_specs=(clips, clips, clips, clips, columns, columns, biases, columns, biases),
        check_vma=False,
    )
```

time: 202 us -> 183 us (0.906)
  blocking collectives: 0 us -> 18.5 us
  Pallas kernels: 86.2 us -> 71.5 us
  waiting for transfers between devices: 63.2 us -> 48.8 us
  starting transfers between devices: 33.5 us -> 22.8 us
  local copies, waits for them, and re-layouts: 11.4 us -> 15.1 us
    all_to_all x0 -> x1, blocking collectives: none -> 18.5 us  [swap_rest(): lax.all_to_all(blocks, AXES, 0, 0, tiled=True, axis_index_groups=self.col...]
    pallas_call x5 -> x6, Pallas kernels: 86.2 us -> 68.3 us  [call(): pl.pallas_call(kernel, grid_spec=pltpu.PrefetchScalarGridSpec(num_scalar_...]
    all_to_all x4 -> x3, waiting for transfers between devices: 29.6 us -> 13.8 us  [swap_rest(): lax.all_to_all(blocks, AXES, 0, 0, tiled=True, axis_index_groups=self.col...]
    unnamed x31 -> x35, local copies, waits for them, and re-layouts: 1.83 us -> 15 us
    ppermute x20, starting transfers between devices: 16.8 us -> 10.9 us  [hop(): return lax.ppermute(value, AXES, pairs)]
    all_to_all x4 -> x3, starting transfers between devices: 16.7 us -> 12 us  [swap_rest(): lax.all_to_all(blocks, AXES, 0, 0, tiled=True, axis_index_groups=self.col...]
    slice x10 -> x0, local copies, waits for them, and re-layouts: 4.61 us -> none  [the longest x3 0.94 us: per_device(): out_bias[layer][None]]
    pallas_call x0 -> x6, Pallas kernels: none -> 3.25 us  [plain(): pl.pallas_call(kernel, out_shape=outs, compiler_params=pltpu.CompilerPara...]
  transfers between devices with their start and end apart: 24 -> 23, of which waited for: 9 -> 10; matrix products, arithmetic and copies ran while one was open for 3% -> 2% of each run, Pallas kernels for 21% -> 25%
where the time goes in v4:
time: 183 us; the launch traced here: 182 us
  Pallas kernels  71.5 us (39%)
  waiting for transfers between devices  48.8 us (27%)
  starting transfers between devices  22.8 us (12%)
  blocking collectives  18.5 us (10%)
  local copies, waits for them, and re-layouts  15.1 us (8%)
  other arithmetic  3.48 us (2%)
  between operations  2.18 us (1%)
    pallas_call x6, Pallas kernels, call(): pl.pallas_call(kernel, grid_spec=pltpu.PrefetchScalarGridSpec(num_scalar_...  68.3 us
    ppermute x20, waiting for transfers between devices, hop(): return lax.ppermute(value, AXES, pairs)  35 us
    all_to_all x1, blocking collectives, swap_rest(): lax.all_to_all(blocks, AXES, 0, 0, tiled=True, axis_index_groups=self.col...  18.5 us
    unnamed x35, local copies, waits for them, and re-layouts  15 us
    all_to_all x3, waiting for transfers between devices, swap_rest(): lax.all_to_all(blocks, AXES, 0, 0, tiled=True, axis_index_groups=self.col...  13.8 us
    all_to_all x3, starting transfers between devices, swap_rest(): lax.all_to_all(blocks, AXES, 0, 0, tiled=True, axis_index_groups=self.col...  12 us
    ppermute x20, starting transfers between devices, hop(): return lax.ppermute(value, AXES, pairs)  10.9 us
  transfers between devices with their start and end apart: 23, of which 10 were waited for; matrix products, arithmetic and copies ran while one was open for 2% of the time, Pallas kernels for 25%

profile of v4, /device:TPU:0, one launch (start us, length us, event | category | flops | bytes accessed | tf_op | source)
XLA Modules:
  0.0 182.4 jit_solution(198919780663680170)
XLA Ops:
  4.4 1.0 shard_map.178
  5.4 18.5 %all_to_all.20.refs_0_ = bf16[4,32,1664]{2,1,0:T(8,128)(2,1)S(1)} all-to-all(bf16[4,32,1664]{2,1,0:T(8,128)(2,1)S(1)} %get-tuple-element.70), channel_id=1, replica_groups={{0,8,16,24},{1,9,17,25},{2,10,18,26},{3,11,19,27},{4,12,20,28},{5,13,21..., dimensions={0} | all-to-all | bytes 851968 | tf_op jit(solution)/shard_map/all_to_all | solution.py:382
  23.9 1.5 collective-permute-start
  25.4 1.5 collective-permute-start.1
  26.9 9.6 %collective-permute-done.refs_1_ = bf16[4,32,1664]{2,1,0:T(8,128)(2,1)S(1)} collective-permute-done((bf16[4,32,1664]{2,1,0:T(8,128)(2,1)S(1)}, bf16[4,32,1664]{2,1,0:T(8,128)(2,1)S(1)}, u32[]{:S(2)}, u32[]{:S(2)}) %collective-permute-start) | collective-permute-done | bytes 426016 | tf_op jit(solution)/shard_map/ppermute | solution.py:379
  36.6 3.5 %all-to-all-start = ((bf16[4,32,1664]{2,1,0:T(8,128)(2,1)}), bf16[4,32,1664]{2,1,0:T(8,128)(2,1)S(1)}, u32[]{:S(2)}, u32[]{:S(2)}) async-start(bf16[4,32,1664]{2,1,0:T(8,128)(2,1)} %get-tuple-element.69), calls=%async_computation | async-start | bytes 851968 | tf_op jit(solution)/shard_map/all_to_all | solution.py:382
  40.8 3.9 %collective-permute-done.2.refs_3_ = bf16[4,32,1664]{2,1,0:T(8,128)(2,1)S(1)} collective-permute-done((bf16[4,32,1664]{2,1,0:T(8,128)(2,1)S(1)}, bf16[4,32,1664]{2,1,0:T(8,128)(2,1)S(1)}, u32[]{:S(2)}, u32[]{:S(2)}) %collective-permute-start.2) | collective-permute-done | bytes 426016 | tf_op jit(solution)/shard_map/ppermute | solution.py:379
  46.8 2.9 %all-to-all-done.refs_0_ = bf16[4,32,1664]{2,1,0:T(8,128)(2,1)S(1)} async-done(((bf16[4,32,1664]{2,1,0:T(8,128)(2,1)}), bf16[4,32,1664]{2,1,0:T(8,128)(2,1)S(1)}, u32[]{:S(2)}, u32[]{:S(2)}) %all-to-all-start) | async-done | bytes 426016 | tf_op jit(solution)/shard_map/all_to_all | solution.py:382
  49.6 1.1 collective-permute-start.7
  50.8 2.0 %collective-permute-start.8 = (bf16[4,32,1664]{2,1,0:T(8,128)(2,1)S(1)}, bf16[4,32,1664]{2,1,0:T(8,128)(2,1)S(1)}, u32[]{:S(2)}, u32[]{:S(2)}) collective-permute-start(bf16[4,32,1664]{2,1,0:T(8,128)(2,1)S(1)} %all-to-all-done.refs_0_), channel_id=1, source_target_pairs={{0,4},{1,3},{2,6},{3,1},{4,0},{5,7},{6,2},{7,5},{8,12},{9,11},{10,... | collective-permute-start | bytes 1277960 | tf_op jit(solution)/shard_map/ppermute | solution.py:379
  52.8 1.6 copy-done.7
  54.4 10.3 %shard_map.179 = (bf16[2048,512]{1,0:T(8,128)(2,1)S(1)}, bf16[2048,512]{1,0:T(8,128)(2,1)S(1)}, bf16[2048,1024]{1,0:T(8,128)(2,1)S(1)}, bf16[1024,1664]{1,0:T(8,128)(2,1)S(1)}) custom-call(s32[5]{0:T(128)S(1)} %concatenate.6.info_ref, bf16[2048,512]{1,0:T(8,128)(2,1)S(1)} %bitcast.26, bf16[128,128]{1,0:T(8,128)(2,1)S(1)} %fusion.2.mel_ref, ...), custom_call_target="tpu_custom_call" | custom-call | flops 5368709120 | bytes 32768 | tf_op jit(solution)/shard_map/pallas_call | solution.py:325
  65.5 7.5 %collective-permute-done.9.refs_3_ = bf16[4,32,1664]{2,1,0:T(8,128)(2,1)S(1)} collective-permute-done((bf16[4,32,1664]{2,1,0:T(8,128)(2,1)S(1)}, bf16[4,32,1664]{2,1,0:T(8,128)(2,1)S(1)}, u32[]{:S(2)}, u32[]{:S(2)}) %collective-permute-start.9) | collective-permute-done | bytes 426016 | tf_op jit(solution)/shard_map/ppermute | solution.py:379
  73.0 1.7 collective-permute-done.13.refs_7_
  74.8 22.5 %shard_map.180 = (bf16[2048,512]{1,0:T(8,128)(2,1)S(1)}, bf16[2048,1024]{1,0:T(8,128)(2,1)S(1)}, bf16[1024,1664]{1,0:T(8,128)(2,1)S(1)}, bf16[2,2,4,32,1664]{4,3...) custom-call(s32[5]{0:T(128)S(1)} %concatenate.6.info_ref, ...), custom_call_target="tpu_custom_call" | custom-call | flops 12884901888 | bytes 98304 | tf_op jit(solution)/shard_map/pallas_call | solution.py:325
  97.3 1.3 copy-done.15
  98.7 8.4 %shard_map.181 = (bf16[2048,512]{1,0:T(8,128)(2,1)S(1)}, bf16[2048,1024]{1,0:T(8,128)(2,1)S(1)}) custom-call(s32[5]{0:T(128)S(1)} %concatenate.6.info_ref, bf16[2048,1024]{1,0:T(8,128)(2,1)S(1)} %get-tuple-element.84.pre1_ref, bf16[1024,1664]{1,0:T(8,128)(2,1)S(1)} %get-tuple-element.85.w1_ref, bf16[1024,1664]{1,0:T(8,128)(2,1)S(1)} %get-tuple-element.86.w0_ref.w_ref, ...), custom_call_target="tpu_custom_call" | custom-call | flops 6442450944 | tf_op jit(solution)/shard_map/pallas_call | solution.py:325
  108.8 11.4 %shard_map.183 = (bf16[2,2,4,32,1664]{4,3,2,1,0:T(8,128)(2,1)S(1)}, bf16[2,2,4,32,1664]{4,3,2,1,0:T(8,128)(2,1)S(1)}, f32[128,128]{1,0:T(8,128)S(1)}) custom-call(s32[5]{0:T(128)S(1)} %concatenate.6.info_ref, bf16[2048,1024]{1,0:T(8,128)(2,1)S(1)} %get-tuple-element.116.pre_ref, bf16[2048,512]{1,0:T(8,128)(2,1)S(1)} %get-tuple-element.94.res_ref, ...), custom_call_target="tpu_custom_call" | custom-call | flops 6442450944 | bytes 98304 | tf_op jit(solution)/shard_map/pallas_call | solution.py:325
  120.9 3.1 %collective-permute-done.16.right_ref = bf16[2,2,4,32,1664]{4,3,2,1,0:T(8,128)(2,1)S(1)} collective-permute-done((bf16[2,2,4,32,1664]{4,3,2,1,0:T(8,128)(2,1)S(1)}, bf16[2,2,4,32,1664]{4,3,2,1,0:T(8,128)(2,1)S(1)}, u32[]{:S(2)}, u32[]{:S(2)}) %collective-permute-start.16) | collective-permute-done | bytes 1703968 | tf_op jit(solution)/shard_map/ppermute | solution.py:379
  125.5 6.8 %shard_map.188 = f32[2048,512]{1,0:T(8,128)} custom-call(s32[5]{0:T(128)S(1)} %concatenate.6.info_ref, bf16[2048,512]{1,0:T(8,128)(2,1)S(1)} %get-tuple-element.94.res_ref, bf16[2048,1024]{1,0:T(8,128)(2,1)S(1)} %get-tuple-element.116.pre_ref, bf16[1024,1664]{1,0:T(8,128)(2,1)S(1)} %get-tuple-element.86.w0_ref.w_ref), custom_call_target="tpu_custom_call" | custom-call | flops 4294967296 | bytes 4194304 | tf_op jit(solution)/shard_map/pallas_call | solution.py:325
  132.4 5.7 %collective-permute-done.19 = bf16[4,32,1664]{2,1,0:T(8,128)(2,1)S(1)} collective-permute-done((bf16[4,32,1664]{2,1,0:T(8,128)(2,1)S(1)}, bf16[4,32,1664]{2,1,0:T(8,128)(2,1)S(1)}, u32[]{:S(2)}, u32[]{:S(2)}) %collective-permute-start.19) | collective-permute-done | bytes 426016 | tf_op jit(solution)/shard_map/ppermute | solution.py:379
  138.1 3.3 %collective-permute-done.17.right_ref = bf16[2,4,32,1664]{3,2,1,0:T(8,128)(2,1)S(1)} collective-permute-done((bf16[2,4,32,1664]{3,2,1,0:T(8,128)(2,1)S(1)}, bf16[2,4,32,1664]{3,2,1,0:T(8,128)(2,1)S(1)}, u32[]{:S(2)}, u32[]{:S(2)}) %collective-permute-start.17) | collective-permute-done | bytes 852000 | tf_op jit(solution)/shard_map/ppermute | solution.py:379
  143.5 3.5 %all-to-all-start.3 = ((bf16[4,32,1664]{2,1,0:T(8,128)(2,1)}), bf16[4,32,1664]{2,1,0:T(8,128)(2,1)S(1)}, u32[]{:S(2)}, u32[]{:S(2)}) async-start(bf16[4,32,1664]{2,1,0:T(8,128)(2,1)} %add_convert_fusion), calls=%async_computation.3 | async-start | bytes 851968 | tf_op jit(solution)/shard_map/all_to_all | solution.py:382
  146.9 2.0 %copy-done.10 = bf16[1024,1664]{1,0:T(8,128)(2,1)S(1)} copy-done((bf16[1024,1664]{1,0:T(8,128)(2,1)S(1)}, bf16[1024,1664]{1,0:T(8,128)(2,1)}, u32[]{:S(2)}) %copy-start.10) | copy-done | bytes 3407896
  148.9 2.0 %copy-done.12 = bf16[1024,1664]{1,0:T(8,128)(2,1)S(1)} copy-done((bf16[1024,1664]{1,0:T(8,128)(2,1)S(1)}, bf16[1024,1664]{1,0:T(8,128)(2,1)}, u32[]{:S(2)}) %copy-start.12) | copy-done | bytes 3407896
  150.9 1.6 copy-done.14
  152.5 1.6 copy-done.16
  154.0 8.8 %shard_map.187 = (bf16[2048,512]{1,0:T(8,128)(2,1)}, bf16[2048,512]{1,0:T(8,128)(2,1)}) custom-call(s32[5]{0:T(128)S(1)} %concatenate.6.info_ref, bf16[2048,512]{1,0:T(8,128)(2,1)S(1)} %bitcast.28, bf16[2048,512]{1,0:T(8,128)(2,1)S(1)} %copy-done.14, bf16[2048,512]{1,0:T(8,128)(2,1)S(1)} %copy-done.16, bf16[1024,1664]{1,0:T(8,128)(2,1)S(1)} %copy-done.10, ...), custom_call_target="tpu_custom_call" | custom-call | flops 4294967296 | bytes 4194304 | tf_op jit(solution)/shard_map/pallas_call | solution.py:325
  162.8 1.9 %add_convert_fusion.1 = bf16[4,32,1664]{2,1,0:T(8,128)(2,1)} fusion(bf16[4,32,1664]{2,1,0:T(8,128)(2,1)} %collective-permute-done.18, bf16[4,32,1664]{2,1,0:T(8,128)(2,1)S(1)} %get-tuple-element.120), kind=kLoop, calls=%fused_computation.1 | loop fusion | flops 851968 | bytes 1277952 | tf_op jit(solution)/shard_map/convert_element_type | solution.py:463
  164.7 5.1 %all-to-all-start.2 = ((bf16[4,32,1664]{2,1,0:T(8,128)(2,1)}), bf16[4,32,1664]{2,1,0:T(8,128)(2,1)S(1)}, u32[]{:S(2)}, u32[]{:S(2)}) async-start(bf16[4,32,1664]{2,1,0:T(8,128)(2,1)} %add_convert_fusion.1), calls=%async_computation.2 | async-start | bytes 851968 | tf_op jit(solution)/shard_map/all_to_all | solution.py:382
  170.4 10.9 %all-to-all-done.2.refs_0_ = bf16[4,32,1664]{2,1,0:T(8,128)(2,1)S(1)} async-done(((bf16[4,32,1664]{2,1,0:T(8,128)(2,1)}), bf16[4,32,1664]{2,1,0:T(8,128)(2,1)S(1)}, u32[]{:S(2)}, u32[]{:S(2)}) %all-to-all-start.2) | async-done | bytes 426016 | tf_op jit(solution)/shard_map/all_to_all | solution.py:382
  181.3 1.1 shard_map.189
  (67 shorter events, 12.7 us)
Async XLA Ops:
  23.9 12.6 %collective-permute-start = (bf16[4,32,1664]{2,1,0:T(8,128)(2,1)S(1)}, bf16[4,32,1664]{2,1,0:T(8,128)(2,1)S(1)}, u32[]{:S(2)}, u32[]{:S(2)}) collective-permute-start(bf16[4,32,1664]{2,1,0:T(8,128)(2,1)S(1)} %all_to_all.20.refs_0_), channel_id=1, source_target_pairs={{0,2},{1,5},{2,0},{3,7},{4,6},{5,1},{6,4},{7,3},{8,10},{9,13},{10,... | collective-permute-start | bytes 1277960 | tf_op jit(solution)/shard_map/ppermute | solution.py:379
  25.4 15.3 %collective-permute-start.1 = (bf16[4,32,1664]{2,1,0:T(8,128)(2,1)S(1)}, bf16[4,32,1664]{2,1,0:T(8,128)(2,1)S(1)}, u32[]{:S(2)}, u32[]{:S(2)}) collective-permute-start(bf16[4,32,1664]{2,1,0:T(8,128)(2,1)S(1)} %all_to_all.20.refs_0_), channel_id=1, source_target_pairs={{0,4},{1,3},{2,6},{3,1},{4,0},{5,7},{6,2},{7,5},{8,12},{9,11},{10,... | collective-permute-start | bytes 1277960 | tf_op jit(solution)/shard_map/ppermute | solution.py:379
  36.5 8.1 %collective-permute-start.2 = (bf16[4,32,1664]{2,1,0:T(8,128)(2,1)S(1)}, bf16[4,32,1664]{2,1,0:T(8,128)(2,1)S(1)}, u32[]{:S(2)}, u32[]{:S(2)}) collective-permute-start(bf16[4,32,1664]{2,1,0:T(8,128)(2,1)S(1)} %collective-permute-done.refs_1_), channel_id=1, source_target_pairs={{0,4},{1,3},{2,6},{3,1},{4,0},{5,7},{6,2},{7,5},{8,12},{9,11},{10,... | collective-permute-start | bytes 1277960 | tf_op jit(solution)/shard_map/ppermute | solution.py:379
  36.6 13.0 %all-to-all-start = ((bf16[4,32,1664]{2,1,0:T(8,128)(2,1)}), bf16[4,32,1664]{2,1,0:T(8,128)(2,1)S(1)}, u32[]{:S(2)}, u32[]{:S(2)}) async-start(bf16[4,32,1664]{2,1,0:T(8,128)(2,1)} %get-tuple-element.69), calls=%async_computation | async-start | bytes 851968 | tf_op jit(solution)/shard_map/all_to_all | solution.py:382
  40.1 9.5 %collective-permute-start.3 = (bf16[4,32,1664]{2,1,0:T(8,128)(2,1)S(1)}, bf16[4,32,1664]{2,1,0:T(8,128)(2,1)S(1)}, u32[]{:S(2)}, u32[]{:S(2)}) collective-permute-start(bf16[4,32,1664]{2,1,0:T(8,128)(2,1)S(1)} %all_to_all.20.refs_0_), channel_id=1, source_target_pairs={{0,1},{1,0},{2,3},{3,2},{4,5},{5,4},{6,7},{7,6},{8,9},{9,8},{10,11... | collective-permute-start | bytes 1277960 | tf_op jit(solution)/shard_map/ppermute | solution.py:379
  40.2 9.4 %collective-permute-start.4 = (bf16[4,32,1664]{2,1,0:T(8,128)(2,1)S(1)}, bf16[4,32,1664]{2,1,0:T(8,128)(2,1)S(1)}, u32[]{:S(2)}, u32[]{:S(2)}) collective-permute-start(bf16[4,32,1664]{2,1,0:T(8,128)(2,1)S(1)} %collective-permute-done.refs_1_), channel_id=1, source_target_pairs={{0,1},{1,0},{2,3},{3,2},{4,5},{5,4},{6,7},{7,6},{8,9},{9,8},{10,11... | collective-permute-start | bytes 1277960 | tf_op jit(solution)/shard_map/ppermute | solution.py:379
  40.7 8.9 %collective-permute-start.5 = (bf16[4,32,1664]{2,1,0:T(8,128)(2,1)S(1)}, bf16[4,32,1664]{2,1,0:T(8,128)(2,1)}, u32[]{:S(2)}, u32[]{:S(2)}) collective-permute-start(bf16[4,32,1664]{2,1,0:T(8,128)(2,1)S(1)} %collective-permute-done.1.refs_2_), channel_id=1, source_target_pairs={{0,1},{1,0},{2,3},{3,2},{4,5},{5,4},{6,7},{7,6},{8,9},{9,8},{10,11... | collective-permute-start | bytes 1277960 | tf_op jit(solution)/shard_map/ppermute | solution.py:379
  44.7 5.0 %collective-permute-start.6 = (bf16[4,32,1664]{2,1,0:T(8,128)(2,1)S(1)}, bf16[4,32,1664]{2,1,0:T(8,128)(2,1)}, u32[]{:S(2)}, u32[]{:S(2)}) collective-permute-start(bf16[4,32,1664]{2,1,0:T(8,128)(2,1)S(1)} %collective-permute-done.2.refs_3_), channel_id=1, source_target_pairs={{0,1},{1,0},{2,3},{3,2},{4,5},{5,4},{6,7},{7,6},{8,9},{9,8},{10,11... | collective-permute-start | bytes 1277960 | tf_op jit(solution)/shard_map/ppermute | solution.py:379
  49.6 15.1 %collective-permute-start.7 = (bf16[4,32,1664]{2,1,0:T(8,128)(2,1)S(1)}, bf16[4,32,1664]{2,1,0:T(8,128)(2,1)S(1)}, u32[]{:S(2)}, u32[]{:S(2)}) collective-permute-start(bf16[4,32,1664]{2,1,0:T(8,128)(2,1)S(1)} %all-to-all-done.refs_0_), channel_id=1, source_target_pairs={{0,2},{1,5},{2,0},{3,7},{4,6},{5,1},{6,4},{7,3},{8,10},{9,13},{10,... | collective-permute-start | bytes 1277960 | tf_op jit(solution)/shard_map/ppermute | solution.py:379
  50.8 14.0 %collective-permute-start.8 = (bf16[4,32,1664]{2,1,0:T(8,128)(2,1)S(1)}, bf16[4,32,1664]{2,1,0:T(8,128)(2,1)S(1)}, u32[]{:S(2)}, u32[]{:S(2)}) collective-permute-start(bf16[4,32,1664]{2,1,0:T(8,128)(2,1)S(1)} %all-to-all-done.refs_0_), channel_id=1, source_target_pairs={{0,4},{1,3},{2,6},{3,1},{4,0},{5,7},{6,2},{7,5},{8,12},{9,11},{10,... | collective-permute-start | bytes 1277960 | tf_op jit(solution)/shard_map/ppermute | solution.py:379
  52.8 1.6 copy-start.7
  54.4 20.4 %copy-start.5 = (bf16[1,2048,512]{2,1,0:T(8,128)(2,1)S(1)}, bf16[1,2048,512]{2,1,0:T(8,128)(2,1)}, u32[]{:S(2)}) copy-start(bf16[1,2048,512]{2,1,0:T(8,128)(2,1)} %param.20) | copy-start | bytes 6291460
  54.4 20.4 %copy-start.6 = (bf16[1,2048,512]{2,1,0:T(8,128)(2,1)S(1)}, bf16[1,2048,512]{2,1,0:T(8,128)(2,1)}, u32[]{:S(2)}) copy-start(bf16[1,2048,512]{2,1,0:T(8,128)(2,1)} %param.21) | copy-start | bytes 6291460
  64.8 43.4 %copy-start.13 = (bf16[2048,512]{1,0:T(8,128)(2,1)}, bf16[2048,512]{1,0:T(8,128)(2,1)S(1)}, u32[]{:S(2)}) copy-start(bf16[2048,512]{1,0:T(8,128)(2,1)S(1)} %get-tuple-element.95.gated_ref.gated0_ref) | copy-start | bytes 6291460
  64.8 60.8 %copy-start.9 = (bf16[1024,1664]{1,0:T(8,128)(2,1)}, bf16[1024,1664]{1,0:T(8,128)(2,1)S(1)}, u32[]{:S(2)}) copy-start(bf16[1024,1664]{1,0:T(8,128)(2,1)S(1)} %get-tuple-element.86.w0_ref.w_ref) | copy-start | bytes 10223620
  64.8 8.2 %collective-permute-start.9 = (bf16[4,32,1664]{2,1,0:T(8,128)(2,1)S(1)}, bf16[4,32,1664]{2,1,0:T(8,128)(2,1)S(1)}, u32[]{:S(2)}, u32[]{:S(2)}) collective-permute-start(bf16[4,32,1664]{2,1,0:T(8,128)(2,1)S(1)} %collective-permute-done.7.refs_1_), channel_id=1, source_target_pairs={{0,4},{1,3},{2,6},{3,1},{4,0},{5,7},{6,2},{7,5},{8,12},{9,11},{10,... | collective-permute-start | bytes 1277960 | tf_op jit(solution)/shard_map/ppermute | solution.py:379
  64.9 8.1 %collective-permute-start.10 = (bf16[4,32,1664]{2,1,0:T(8,128)(2,1)S(1)}, bf16[4,32,1664]{2,1,0:T(8,128)(2,1)S(1)}, u32[]{:S(2)}, u32[]{:S(2)}) collective-permute-start(bf16[4,32,1664]{2,1,0:T(8,128)(2,1)S(1)} %all-to-all-done.refs_0_), channel_id=1, source_target_pairs={{0,1},{1,0},{2,3},{3,2},{4,5},{5,4},{6,7},{7,6},{8,9},{9,8},{10,11... | collective-permute-start | bytes 1277960 | tf_op jit(solution)/shard_map/ppermute | solution.py:379
  65.0 8.0 %collective-permute-start.11 = (bf16[4,32,1664]{2,1,0:T(8,128)(2,1)S(1)}, bf16[4,32,1664]{2,1,0:T(8,128)(2,1)S(1)}, u32[]{:S(2)}, u32[]{:S(2)}) collective-permute-start(bf16[4,32,1664]{2,1,0:T(8,128)(2,1)S(1)} %collective-permute-done.7.refs_1_), channel_id=1, source_target_pairs={{0,1},{1,0},{2,3},{3,2},{4,5},{5,4},{6,7},{7,6},{8,9},{9,8},{10,11... | collective-permute-start | bytes 1277960 | tf_op jit(solution)/shard_map/ppermute | solution.py:379
  65.5 7.6 %collective-permute-start.12 = (bf16[4,32,1664]{2,1,0:T(8,128)(2,1)S(1)}, bf16[4,32,1664]{2,1,0:T(8,128)(2,1)S(1)}, u32[]{:S(2)}, u32[]{:S(2)}) collective-permute-start(bf16[4,32,1664]{2,1,0:T(8,128)(2,1)S(1)} %collective-permute-done.8.refs_2_), channel_id=1, source_target_pairs={{0,1},{1,0},{2,3},{3,2},{4,5},{5,4},{6,7},{7,6},{8,9},{9,8},{10,11... | collective-permute-start | bytes 1277960 | tf_op jit(solution)/shard_map/ppermute | solution.py:379
  73.0 1.8 collective-permute-start.13
  98.6 8.6 %copy-start.11 = (bf16[1024,1664]{1,0:T(8,128)(2,1)}, bf16[1024,1664]{1,0:T(8,128)(2,1)S(1)}, u32[]{:S(2)}) copy-start(bf16[1024,1664]{1,0:T(8,128)(2,1)S(1)} %get-tuple-element.85.w1_ref) | copy-start | bytes 10223620
  98.6 8.6 %collective-permute-start.14 = (bf16[2,2,4,32,1664]{4,3,2,1,0:T(8,128)(2,1)S(1)}, bf16[2,2,4,32,1664]{4,3,2,1,0:T(8,128)(2,1)S(1)}, u32[]{:S(2)}, u32[]{:S(2)}) collective-permute-start(bf16[2,2,4,32,1664]{4,3,2,1,0:T(8,128)(2,1)S(1)} %get-tuple-element.90), channel_id=1, source_target_pairs={{0,1},{1,0},{2,3},{3,2},{4,5},{5,4},{6,7},{7,6},{8,9},{9,8},{10,11... | collective-permute-start | bytes 5111816 | tf_op jit(solution)/shard_map/ppermute | solution.py:379
  107.2 1.6 copy-start.8
  107.6 12.8 %collective-permute-start.15 = (bf16[2,4,32,1664]{3,2,1,0:T(8,128)(2,1)S(1)}, bf16[2,4,32,1664]{3,2,1,0:T(8,128)(2,1)S(1)}, u32[]{:S(2)}, u32[]{:S(2)}) collective-permute-start(bf16[2,4,32,1664]{3,2,1,0:T(8,128)(2,1)S(1)} %get-tuple-element.98), channel_id=1, source_target_pairs={{0,2},{1,5},{2,0},{3,7},{4,6},{5,1},{6,4},{7,3},{8,10},{9,13},{10,... | collective-permute-start | bytes 2555912 | tf_op jit(solution)/shard_map/ppermute | solution.py:379
  120.4 3.6 %collective-permute-start.16 = (bf16[2,2,4,32,1664]{4,3,2,1,0:T(8,128)(2,1)S(1)}, bf16[2,2,4,32,1664]{4,3,2,1,0:T(8,128)(2,1)S(1)}, u32[]{:S(2)}, u32[]{:S(2)}) collective-permute-start(bf16[2,2,4,32,1664]{4,3,2,1,0:T(8,128)(2,1)S(1)} %get-tuple-element.99), channel_id=1, source_target_pairs={{0,1},{1,0},{2,3},{3,2},{4,5},{5,4},{6,7},{7,6},{8,9},{9,8},{10,11... | collective-permute-start | bytes 5111816 | tf_op jit(solution)/shard_map/ppermute | solution.py:379
  124.3 17.0 %collective-permute-start.17 = (bf16[2,4,32,1664]{3,2,1,0:T(8,128)(2,1)S(1)}, bf16[2,4,32,1664]{3,2,1,0:T(8,128)(2,1)S(1)}, u32[]{:S(2)}, u32[]{:S(2)}) collective-permute-start(bf16[2,4,32,1664]{3,2,1,0:T(8,128)(2,1)S(1)} %get-tuple-element.107), channel_id=1, source_target_pairs={{0,2},{1,5},{2,0},{3,7},{4,6},{5,1},{6,4},{7,3},{8,10},{9,13},{10,... | collective-permute-start | bytes 2555912 | tf_op jit(solution)/shard_map/ppermute | solution.py:379
  125.3 12.8 %collective-permute-start.19 = (bf16[4,32,1664]{2,1,0:T(8,128)(2,1)S(1)}, bf16[4,32,1664]{2,1,0:T(8,128)(2,1)S(1)}, u32[]{:S(2)}, u32[]{:S(2)}) collective-permute-start(bf16[4,32,1664]{2,1,0:T(8,128)(2,1)S(1)} %get-tuple-element.102), channel_id=1, source_target_pairs={{0,4},{1,3},{2,6},{3,1},{4,0},{5,7},{6,2},{7,5},{8,12},{9,11},{10,... | collective-permute-start | bytes 1277960 | tf_op jit(solution)/shard_map/ppermute | solution.py:379
  141.6 21.2 %collective-permute-start.18 = (bf16[4,32,1664]{2,1,0:T(8,128)(2,1)S(1)}, bf16[4,32,1664]{2,1,0:T(8,128)(2,1)}, u32[]{:S(2)}, u32[]{:S(2)}) collective-permute-start(bf16[4,32,1664]{2,1,0:T(8,128)(2,1)S(1)} %get-tuple-element.110), channel_id=1, source_target_pairs={{0,4},{1,3},{2,6},{3,1},{4,0},{5,7},{6,2},{7,5},{8,12},{9,11},{10,... | collective-permute-start | bytes 1277960 | tf_op jit(solution)/shard_map/ppermute | solution.py:379
  143.5 21.3 %all-to-all-start.3 = ((bf16[4,32,1664]{2,1,0:T(8,128)(2,1)}), bf16[4,32,1664]{2,1,0:T(8,128)(2,1)S(1)}, u32[]{:S(2)}, u32[]{:S(2)}) async-start(bf16[4,32,1664]{2,1,0:T(8,128)(2,1)} %add_convert_fusion), calls=%async_computation.3 | async-start | bytes 851968 | tf_op jit(solution)/shard_map/all_to_all | solution.py:382
  146.9 2.0 %copy-start.10 = (bf16[1024,1664]{1,0:T(8,128)(2,1)S(1)}, bf16[1024,1664]{1,0:T(8,128)(2,1)}, u32[]{:S(2)}) copy-start(bf16[1024,1664]{1,0:T(8,128)(2,1)} %copy-done.9) | copy-start | bytes 10223620
  148.9 2.0 %copy-start.12 = (bf16[1024,1664]{1,0:T(8,128)(2,1)S(1)}, bf16[1024,1664]{1,0:T(8,128)(2,1)}, u32[]{:S(2)}) copy-start(bf16[1024,1664]{1,0:T(8,128)(2,1)} %copy-done.11) | copy-start | bytes 10223620
  164.7 16.6 %all-to-all-start.2 = ((bf16[4,32,1664]{2,1,0:T(8,128)(2,1)}), bf16[4,32,1664]{2,1,0:T(8,128)(2,1)S(1)}, u32[]{:S(2)}, u32[]{:S(2)}) async-start(bf16[4,32,1664]{2,1,0:T(8,128)(2,1)} %add_convert_fusion.1), calls=%async_computation.2 | async-start | bytes 851968 | tf_op jit(solution)/shard_map/all_to_all | solution.py:382
  (8 other events, 8.3 us)

commit v5 on v4

--- a/solution.py
+++ b/solution.py
@@ -12,6 +12,7 @@
 LANES = 128
 TILE = 512
 MIB = 1024 * 1024
+HINT = 4
 ROOM_0, ROOM_1, ROOM_2, ROOM_3, ROOM_4, ROOM_5, ROOM_SMALL = 8, 13, 6, 8, 8, 8, 12
 LOW = jnp.bfloat16
 FULL = jnp.float32
@@ -82,7 +83,8 @@
 
 
 def forward_0(size, wires, info_ref, x_ref, mel_ref, *refs):
-    pieces, refs = refs[: wires.pieces], refs[wires.pieces :]
+    count = 8 if wires.direct else 1
+    pieces, refs = refs[:count], refs[count:]
     low1_ref, gated_ref, slope_ref, w_ref = refs
     step = pl.program_id(0)
     channels = size.channels
@@ -110,7 +112,8 @@
 
 
 def layer_1(size, wires, steps, info_ref, low1_ref, mel_ref, go_ref, gs_ref, *refs):
-    pieces, refs = refs[: wires.pieces], refs[wires.pieces :]
+    count = 8 if wires.direct else 1
+    pieces, refs = refs[:count], refs[count:]
     gated_ref, pre_ref, w_ref, here_ref, away_ref, melg_ref, *scratch = refs
     prev_s, proj_s, frames_s, part_s = scratch
     step = pl.program_id(0)
@@ -266,42 +269,56 @@
     skip_ref[...] = (projected(slice(channels, 2 * channels)) * mask).astype(LOW)
 
 
-def add_and_part(left_ref, right_ref, stay_ref, go_ref):
-    stay_ref[...] = add_low(left_ref[0], right_ref[0])
-    go_ref[...] = add_low(left_ref[1], right_ref[1])
-
-
-def pack_layers(layers, copies, conv_ref, cond_ref, conv_b_ref, out_ref, out_b_ref, *refs):
+def add_and_part(left_ref, right_ref, *refs):
+    for index, ref in enumerate(refs):
+        ref[...] = add_low(left_ref[index], right_ref[index])
+
+
+def put_side_by_side(*refs):
+    for index, ref in enumerate(refs[:-1]):
+        refs[-1][index] = ref[...]
+
+
+def pack_layers(layers, *refs):
+    sources, packs, kept = refs[:5], refs[5 : 5 + layers], refs[5 + layers : 10 + layers]
+    sems = refs[-1]
+    copies = [
+        pltpu.make_async_copy(source, to, sems.at[index])
+        for index, (source, to) in enumerate(zip(sources, kept))
+    ]
+    for copy in copies:
+        copy.start()
+    for copy in copies:
+        copy.wait()
+    conv_ref, cond_ref, conv_b_ref, out_ref, out_b_ref = kept
     rows = conv_ref.shape[1]
     same = lax.broadcasted_iota(jnp.int32, (rows, rows), 0)
     same = (same == lax.broadcasted_iota(jnp.int32, (rows, rows), 1)).astype(FULL).astype(LOW)
-    for layer in range(layers):
-        to_ref = refs[layer]
-        early, extra = out_ref.shape[2], out_ref.shape[2] + conv_ref.shape[2]
-        mel = cond_ref.shape[2]
-        width = to_ref.shape[2] - extra
-        biases = dot_cols(same, jnp.concatenate([conv_b_ref[...], out_b_ref[...]], axis=0))
+    biases = dot_cols(same, jnp.concatenate([conv_b_ref[...], out_b_ref[...]], axis=0))
+    early, extra = out_ref.shape[2], out_ref.shape[2] + conv_ref.shape[2]
+    mel = cond_ref.shape[2]
+    for layer, to_ref in enumerate(packs):
+        width = to_ref.shape[1] - extra
         place = lax.broadcasted_iota(jnp.int32, (rows, width), 1)
         cond = jnp.concatenate(
             [cond_ref[layer].astype(FULL), jnp.zeros((rows, width - mel), FULL)], axis=1
         )
         cond = jnp.where(place == mel, biases[:, layer : layer + 1], cond)
         cond = jnp.where(place == mel + 1, biases[:, layers + layer : layers + layer + 1], cond)
-        cond = cond.astype(LOW)
-        for copy in range(copies):
-            to_ref[copy, :, :early] = out_ref[layer]
-            to_ref[copy, :, early:extra] = conv_ref[layer]
-            to_ref[copy, :, extra:] = cond
+        to_ref[:, :early] = out_ref[layer]
+        to_ref[:, early:extra] = conv_ref[layer]
+        to_ref[:, extra:] = cond.astype(LOW)
 
 
 def unpack_layers(layers, mel, *refs):
-    conv_ref, cond_ref, conv_b_ref, out_ref, out_b_ref = refs[layers:]
+    conv_ref, cond_ref, conv_b_ref, out_ref, out_b_ref = refs[-5:]
+    count = (len(refs) - 5) // layers
     rows = conv_ref.shape[1]
     same = lax.broadcasted_iota(jnp.int32, (rows, rows), 0)
     same = (same == lax.broadcasted_iota(jnp.int32, (rows, rows), 1)).astype(FULL)
     early, extra = out_ref.shape[2], out_ref.shape[2] + conv_ref.shape[2]
     for layer in range(layers):
-        total = jnp.sum(refs[layer][...].astype(FULL), axis=0)
+        total = sum(ref[...].astype(FULL) for ref in refs[layer * count : (layer + 1) * count])
         out_ref[layer] = total[:, :early]
         conv_ref[layer] = total[:, early:extra]
         cond_ref[layer] = total[:, extra : extra + mel]
@@ -335,7 +352,7 @@
         compiler_params=pltpu.CompilerParams(
             vmem_limit_bytes=room * MIB, dimension_semantics=("arbitrary",)
         ),
-        cost_estimate=pl.CostEstimate(flops=flops, bytes_accessed=moved, transcendentals=0),
+        cost_estimate=pl.CostEstimate(flops=flops // HINT, bytes_accessed=moved // HINT, transcendentals=0),
     )(info, *arrays)
 
 
@@ -356,30 +373,28 @@
 
 class Wires:
     def __init__(self, dp, cores, channels):
-        assert dp % 4 == 0 and cores == 2
         self.rest = dp // 4
+        assert dp == self.rest * 4 and self.rest & (self.rest - 1) == 0 and cores == 2
         self.devices = dp * 2
         self.rows = channels // self.devices
         self.direct = self.rows % 16 == 0
-        self.pieces = 8 if self.direct else 1
-        me = lax.axis_index(AXES)
-        self.core = me % 2
-        self.a = (me // 2) % 2
-        self.b = (me // 4) % 2
+        self.dp = lax.axis_index(AXES[0])
+        self.core = lax.axis_index(AXES[1])
         every = range(self.devices)
         self.sibling = [(i, i ^ 1) for i in every]
         self.first = [(i, i ^ (4 if i % 2 else 2)) for i in every]
         self.second = [(i, i ^ (2 if i % 2 else 4)) for i in every]
-        self.columns = [[rest * 8 + low for rest in range(self.rest)] for low in range(8)]
-
-    def place(self):
-        return jnp.stack([self.core, self.a, self.b]).astype(jnp.int32)
+
+    def along_rest(self, distance):
+        return [(i, i ^ (8 * distance)) for i in range(self.devices)]
 
     def hop(self, value, pairs):
         return lax.ppermute(value, AXES, pairs)
 
-    def swap_rest(self, blocks):
-        return lax.all_to_all(blocks, AXES, 0, 0, tiled=True, axis_index_groups=self.columns)
+    def spread(self, blocks):
+        return [blocks[0]] + [
+            self.hop(blocks[k], self.along_rest(k)) for k in range(1, self.rest)
+        ]
 
     def far_hops(self, mine, one, two):
         pieces = [mine, one, two, self.hop(one, self.second)]
@@ -388,13 +403,12 @@
 
     def put_in_order(self, pieces):
         whole = jnp.zeros((self.rest, 2, 2, 2) + pieces[0].shape[1:], LOW)
+        order = jnp.arange(self.rest) ^ (self.dp >> 2)
         for index, piece in enumerate(pieces):
-            source = self.core if index < 4 else 1 - self.core
-            first, second = index % 2, (index // 2) % 2
-            at_a = self.a ^ jnp.where(source == 0, first, second)
-            at_b = self.b ^ jnp.where(source == 0, second, first)
+            source = self.core ^ (index // 4)
+            at_a, at_b = turned(self.dp, source, index % 2, (index // 2) % 2)
             whole = lax.dynamic_update_slice(
-                whole, piece[:, None, None, None], (0, at_b, at_a, source, 0, 0)
+                whole, piece[order][:, None, None, None], (0, at_b, at_a, source, 0, 0)
             )
         return whole.reshape(-1, pieces[0].shape[2])
 
@@ -402,37 +416,35 @@
         if not self.direct:
             w_ref[...] = pieces[0][...]
             return
-        core, a, b = info_ref[2], info_ref[3], info_ref[4]
+        dp, core = info_ref[2], info_ref[3]
         for index, piece in enumerate(pieces):
-            source = core if index < 4 else 1 - core
-            first, second = index % 2, (index // 2) % 2
-            at_a = a ^ jnp.where(source == 0, first, second)
-            at_b = b ^ jnp.where(source == 0, second, first)
-            for rest in range(self.rest):
-                place = ((rest * 2 + at_b) * 2 + at_a) * 2 + source
-                w_ref[rows_of(place, self.rows)] = piece[rest]
+            source = core ^ (index // 4)
+            at_a, at_b = turned(dp, source, index % 2, (index // 2) % 2)
+            for distance in range(self.rest):
+                place = ((((dp >> 2) ^ distance) * 2 + at_b) * 2 + at_a) * 2 + source
+                w_ref[rows_of(place, self.rows)] = piece[distance]
 
     def put_apart(self, info_ref, step, part_ref, here_ref, away_ref):
         if not self.direct:
             here_ref[rows_of(step, part_ref.shape[0])] = part_ref[...]
             return
-        core, a, b = info_ref[2], info_ref[3], info_ref[4]
+        dp, core = info_ref[2], info_ref[3]
         blocks = part_ref.shape[0] // self.rows
         for block in range(blocks):
             at_b, at_a, owner = (block // 4) % 2, (block // 2) % 2, block % 2
             value = part_ref[block * self.rows : (block + 1) * self.rows]
-            first, second = at_a ^ a, at_b ^ b
+            first, second = at_a ^ (dp & 1), at_b ^ ((dp >> 1) & 1)
             if owner:
                 first, second = second, first
-            rest = step * (blocks // 8) + block // 8
+            distance = (step * (blocks // 8) + block // 8) ^ (dp >> 2)
 
             @pl.when(core == owner)
             def _():
-                here_ref[first, second, rest] = value
+                here_ref[first, second, distance] = value
 
             @pl.when(core != owner)
             def _():
-                away_ref[first, second, rest] = value
+                away_ref[first, second, distance] = value
 
     def apart(self, depth):
         if not self.direct:
@@ -442,13 +454,13 @@
     def by_distance(self, full):
         rows = full.shape[0] // self.devices
         blocks = full.reshape(self.rest, 2, 2, 2, rows, full.shape[1])
+        blocks = blocks[jnp.arange(self.rest) ^ (self.dp >> 2)]
         parts = []
         for away in range(2):
             source = self.core ^ away
             for first in range(2):
                 for second in range(2):
-                    at_a = self.a ^ jnp.where(source == 0, first, second)
-                    at_b = self.b ^ jnp.where(source == 0, second, first)
+                    at_a, at_b = turned(self.dp, source, first, second)
                     parts.append(
                         lax.dynamic_slice(
                             blocks,
@@ -457,6 +469,12 @@
                         )[:, 0, 0, 0]
                     )
         return jnp.stack(parts).reshape(2, 2, 2, self.rest, rows, full.shape[1])
+
+
+def turned(dp, owner, first, second):
+    along_a = jnp.where(owner == 0, first, second)
+    along_b = jnp.where(owner == 0, second, first)
+    return (dp & 1) ^ along_a, ((dp >> 1) & 1) ^ along_b
 
 
 def add_low(left, right):
@@ -486,7 +504,8 @@
     wires = Wires(dp, cores, gate)
     assert layers == 2 and sample_count % TILE == 0 and TILE == FIRST_DILATION
     steps = sample_count // TILE
-    info = jnp.concatenate([lengths, hops, wires.place()])
+    where = jnp.stack([wires.dp, wires.core]).astype(jnp.int32)
+    info = jnp.concatenate([lengths, hops, where])
     x, go, gs = samples[0], grad_out[0], grad_skip[0]
     mel_table = jnp.concatenate([mel[0], jnp.ones((frame_count, 1), LOW)], axis=1)
     mel_table = jnp.pad(
@@ -497,16 +516,26 @@
         w.swapaxes(1, 2) for w in (conv_weight, cond_weight, out_weight)
     )
     rows = conv_t.shape[1]
-    own = plain(
-        functools.partial(pack_layers, layers, wires.rest),
-        (conv_t, cond_t, conv_bias, out_t, out_bias),
-        [shape_of(wires.rest, rows, size.pack)] * layers,
-    )
-    mine0 = wires.swap_rest(own[0])
+    sources = (conv_t, cond_t, conv_bias, out_t, out_bias)
+    own = pl.pallas_call(
+        functools.partial(pack_layers, layers),
+        in_specs=[pl.BlockSpec(memory_space=pl.ANY)] * len(sources),
+        out_shape=[shape_of(rows, size.pack)] * layers,
+        scratch_shapes=[pltpu.VMEM(source.shape, LOW) for source in sources]
+        + [pltpu.SemaphoreType.DMA((len(sources),))],
+        compiler_params=pltpu.CompilerParams(vmem_limit_bytes=ROOM_SMALL * MIB),
+    )(*(pltpu.with_memory_space_constraint(source, pltpu.HBM) for source in sources))
+    last_shape = shape_of(wires.rest, rows, size.pack)
+    half_shape = shape_of(2, wires.rest, rows, size.pack)
+    blocks_shape = [shape_of(rows, size.pack)] * wires.rest
+    side_by_side = lambda blocks: plain(put_side_by_side, blocks, [last_shape])[0]
+    near0 = wires.spread([own[0]] * wires.rest)
+    near1 = wires.spread([own[1]] * wires.rest)
+    mine0 = side_by_side(near0)
     one0, two0 = wires.hop(mine0, wires.first), wires.hop(mine0, wires.second)
+    one0, two0, *near1 = lax.optimization_barrier((one0, two0, *near1))
     pieces0 = wires.far_hops(mine0, one0, two0)
-    mine1 = wires.swap_rest(own[1])
-    mine1, *pieces0 = lax.optimization_barrier((mine1, *pieces0))
+    mine1 = side_by_side(near1)
     one1, two1 = wires.hop(mine1, wires.first), wires.hop(mine1, wires.second)
 
     table = fixed(LANES, size.extra_width)
@@ -567,8 +596,6 @@
         12 * macs,
         ROOM_2,
     )
-    half_shape = shape_of(2, wires.rest, rows, size.pack)
-    last_shape = shape_of(wires.rest, rows, size.pack)
     stay1, leave1 = plain(add_and_part, (here1, came1), [half_shape] * 2)
     pre0, stay1, leave1 = lax.optimization_barrier((pre0, stay1, leave1))
     came1 = wires.hop(leave1, wires.first)
@@ -608,8 +635,8 @@
         8 * macs,
         ROOM_4,
     )
-    came1, samples_grad = lax.optimization_barrier((came1, samples_grad))
-    parts1 = wires.swap_rest(add_low(stay1, came1))
+    came0, came1, samples_grad = lax.optimization_barrier((came0, came1, samples_grad))
+    parts1 = wires.spread(plain(add_and_part, (stay1, came1), blocks_shape))
     stay0, leave0 = plain(add_and_part, (stay0, came0), [last_shape] * 2)
     x, stay0, leave0 = lax.optimization_barrier((x, stay0, leave0))
     came0 = wires.hop(leave0, wires.second)
@@ -624,10 +651,10 @@
         ROOM_5,
     )
     came0, residual_out = lax.optimization_barrier((came0, residual_out))
-    parts0 = wires.swap_rest(add_low(stay0, came0))
+    parts0 = wires.spread(plain(add_and_part, (stay0, came0), blocks_shape))
     grads = plain(
         functools.partial(unpack_layers, layers, mel_count),
-        (parts0, parts1),
+        (*parts0, *parts1),
         [
             shape_of(layers, rows, 2 * channels, dtype=FULL),
             shape_of(layers, rows, mel_count, dtype=FULL),

time: 183 us -> 157 us (0.86)
  blocking collectives: 18.5 us -> 0 us
  local copies, waits for them, and re-layouts: 15.1 us -> 2.2 us
  starting transfers between devices: 22.8 us -> 32 us
  other arithmetic: 3.48 us -> 0.78 us
  waiting for transfers between devices: 48.8 us -> 46.9 us
    ppermute x20 -> x32, starting transfers between devices: 10.9 us -> 32 us  [hop(): return lax.ppermute(value, AXES, pairs)]
    all_to_all x1 -> x0, blocking collectives: 18.5 us -> none  [swap_rest(): lax.all_to_all(blocks, AXES, 0, 0, tiled=True, axis_index_groups=self.col...]
    all_to_all x3 -> x0, waiting for transfers between devices: 13.8 us -> none  [swap_rest(): lax.all_to_all(blocks, AXES, 0, 0, tiled=True, axis_index_groups=self.col...]
    unnamed x35 -> x9, local copies, waits for them, and re-layouts: 15 us -> 2.2 us
    all_to_all x3 -> x0, starting transfers between devices: 12 us -> none  [swap_rest(): lax.all_to_all(blocks, AXES, 0, 0, tiled=True, axis_index_groups=self.col...]
    ppermute x20 -> x32, waiting for transfers between devices: 35 us -> 46.9 us  [hop(): return lax.ppermute(value, AXES, pairs)]
    convert_element_type x2 -> x0, other arithmetic: 2.78 us -> none  [add_low(): return (left.astype(FULL) + right.astype(FULL)).astype(LOW)]
  transfers between devices with their start and end apart: 23 -> 32, of which waited for: 10 -> 11; matrix products, arithmetic and copies ran while one was open for 2% -> 1% of each run, Pallas kernels for 25% -> 29%
where the time goes in v5:
time: 157 us
  Pallas kernels  72.9 us (46%)
  waiting for transfers between devices  46.9 us (30%)
  starting transfers between devices  32 us (20%)
  local copies, waits for them, and re-layouts  2.2 us (1%)
  between operations  2.13 us (1%)
    pallas_call x6, Pallas kernels, call(): pl.pallas_call(kernel, grid_spec=pltpu.PrefetchScalarGridSpec(num_scalar_...  68.4 us
    ppermute x32, waiting for transfers between devices, hop(): return lax.ppermute(value, AXES, pairs)  46.9 us
    ppermute x32, starting transfers between devices, hop(): return lax.ppermute(value, AXES, pairs)  32 us
    pallas_call x9, Pallas kernels, plain(): pl.pallas_call(kernel, out_shape=outs, compiler_params=pltpu.CompilerPara...  3.3 us
  transfers between devices with their start and end apart: 32, of which 11 were waited for; matrix products, arithmetic and copies ran while one was open for 1% of the time, Pallas kernels for 29%

profile of v5, /device:TPU:0, one launch (start us, length us, event | category | flops | bytes accessed | tf_op | source)
XLA Modules:
  0.0 156.9 jit_solution(13869542559592085325)
XLA Ops:
  1.8 3.1 %collective-permute-start = (bf16[32,1664]{1,0:T(8,128)(2,1)S(1)}, bf16[32,1664]{1,0:T(8,128)(2,1)S(1)}, u32[]{:S(2)}, u32[]{:S(2)}) collective-permute-start(bf16[32,1664]{1,0:T(8,128)(2,1)S(1)} %get-tuple-element.75.refs_0_), channel_id=1, source_target_pairs={{0,8},{1,9},{2,10},{3,11},{4,12},{5,13},{6,14},{7,15},{8,0},{9,1},... | collective-permute-start | bytes 319496 | tf_op jit(solution)/shard_map/ppermute | solution.py:392
  4.9 2.6 %collective-permute-start.1 = (bf16[32,1664]{1,0:T(8,128)(2,1)S(1)}, bf16[32,1664]{1,0:T(8,128)(2,1)S(1)}, u32[]{:S(2)}, u32[]{:S(2)}) collective-permute-start(bf16[32,1664]{1,0:T(8,128)(2,1)S(1)} %get-tuple-element.75.refs_0_), channel_id=1, source_target_pairs={{0,16},{1,17},{2,18},{3,19},{4,20},{5,21},{6,22},{7,23},{8,24},{9,... | collective-permute-start | bytes 319496 | tf_op jit(solution)/shard_map/ppermute | solution.py:392
  7.9 8.1 %collective-permute-done.1.refs_2_ = bf16[32,1664]{1,0:T(8,128)(2,1)S(1)} collective-permute-done((bf16[32,1664]{1,0:T(8,128)(2,1)S(1)}, bf16[32,1664]{1,0:T(8,128)(2,1)S(1)}, u32[]{:S(2)}, u32[]{:S(2)}) %collective-permute-start.1) | collective-permute-done | bytes 106528 | tf_op jit(solution)/shard_map/ppermute | solution.py:392
  16.0 1.6 %collective-permute-start.3 = (bf16[4,32,1664]{2,1,0:T(8,128)(2,1)S(1)}, bf16[4,32,1664]{2,1,0:T(8,128)(2,1)S(1)}, u32[]{:S(2)}, u32[]{:S(2)}) collective-permute-start(bf16[4,32,1664]{2,1,0:T(8,128)(2,1)S(1)} %shard_map.179.refs_0_), channel_id=1, source_target_pairs={{0,2},{1,5},{2,0},{3,7},{4,6},{5,1},{6,4},{7,3},{8,10},{9,13},{10,... | collective-permute-start | bytes 1277960 | tf_op jit(solution)/shard_map/ppermute | solution.py:392
  17.6 1.5 collective-permute-start.4
  19.1 1.7 %collective-permute-start.5 = (bf16[32,1664]{1,0:T(8,128)(2,1)S(1)}, bf16[32,1664]{1,0:T(8,128)(2,1)S(1)}, u32[]{:S(2)}, u32[]{:S(2)}) collective-permute-start(bf16[32,1664]{1,0:T(8,128)(2,1)S(1)} %get-tuple-element.77.refs_0_), channel_id=1, source_target_pairs={{0,8},{1,9},{2,10},{3,11},{4,12},{5,13},{6,14},{7,15},{8,0},{9,1},... | collective-permute-start | bytes 319496 | tf_op jit(solution)/shard_map/ppermute | solution.py:392
  20.8 1.3 collective-permute-start.6
  22.1 1.3 collective-permute-start.7
  24.3 5.7 %collective-permute-done.6.refs_2_ = bf16[32,1664]{1,0:T(8,128)(2,1)S(1)} collective-permute-done((bf16[32,1664]{1,0:T(8,128)(2,1)S(1)}, bf16[32,1664]{1,0:T(8,128)(2,1)S(1)}, u32[]{:S(2)}, u32[]{:S(2)}) %collective-permute-start.6) | collective-permute-done | bytes 106528 | tf_op jit(solution)/shard_map/ppermute | solution.py:392
  31.1 7.1 %collective-permute-done.10.refs_3_ = bf16[4,32,1664]{2,1,0:T(8,128)(2,1)S(1)} collective-permute-done((bf16[4,32,1664]{2,1,0:T(8,128)(2,1)S(1)}, bf16[4,32,1664]{2,1,0:T(8,128)(2,1)S(1)}, u32[]{:S(2)}, u32[]{:S(2)}) %collective-permute-start.10) | collective-permute-done | bytes 426016 | tf_op jit(solution)/shard_map/ppermute | solution.py:392
  42.2 1.6 %copy-done = bf16[1,2048,512]{2,1,0:T(8,128)(2,1)S(1)} copy-done((bf16[1,2048,512]{2,1,0:T(8,128)(2,1)S(1)}, bf16[1,2048,512]{2,1,0:T(8,128)(2,1)}, u32[]{:S(2)}) %copy-start) | copy-done | bytes 2097176
  43.7 9.0 %shard_map.181 = (bf16[2048,512]{1,0:T(8,128)(2,1)S(1)}, bf16[2048,512]{1,0:T(8,128)(2,1)S(1)}, bf16[2048,1024]{1,0:T(8,128)(2,1)S(1)}, bf16[1024,1664]{1,0:T(8,128)(2,1)S(1)}) custom-call(s32[4]{0:T(128)S(1)} %pad_add_fusion.info_ref, bf16[2048,512]{1,0:T(8,128)(2,1)S(1)} %bitcast.17, bf16[128,128]{1,0:T(8,128)(2,1)S(1)} %fusion.2.mel_ref, ...), custom_call_target="tpu_custom_call" | custom-call | flops 1342177280 | bytes 8192 | tf_op jit(solution)/shard_map/pallas_call | solution.py:342
  52.7 1.6 %collective-permute-start.15 = (bf16[4,32,1664]{2,1,0:T(8,128)(2,1)}, bf16[4,32,1664]{2,1,0:T(8,128)(2,1)S(1)}, u32[]{:S(2)}, u32[]{:S(2)}) collective-permute-start(bf16[4,32,1664]{2,1,0:T(8,128)(2,1)} %collective-permute-done.8.refs_1_), channel_id=1, source_target_pairs={{0,4},{1,3},{2,6},{3,1},{4,0},{5,7},{6,2},{7,5},{8,12},{9,11},{10,... | collective-permute-start | bytes 1277960 | tf_op jit(solution)/shard_map/ppermute | solution.py:392
  54.9 6.3 %collective-permute-done.15.refs_3_ = bf16[4,32,1664]{2,1,0:T(8,128)(2,1)S(1)} collective-permute-done((bf16[4,32,1664]{2,1,0:T(8,128)(2,1)}, bf16[4,32,1664]{2,1,0:T(8,128)(2,1)S(1)}, u32[]{:S(2)}, u32[]{:S(2)}) %collective-permute-start.15) | collective-permute-done | bytes 426016 | tf_op jit(solution)/shard_map/ppermute | solution.py:392
  61.2 1.7 %collective-permute-done.19.refs_7_ = bf16[4,32,1664]{2,1,0:T(8,128)(2,1)S(1)} collective-permute-done((bf16[4,32,1664]{2,1,0:T(8,128)(2,1)S(1)}, bf16[4,32,1664]{2,1,0:T(8,128)(2,1)S(1)}, u32[]{:S(2)}, u32[]{:S(2)}) %collective-permute-start.19) | collective-permute-done | bytes 426016 | tf_op jit(solution)/shard_map/ppermute | solution.py:392
  62.9 23.9 %shard_map.182 = (bf16[2048,512]{1,0:T(8,128)(2,1)S(1)}, bf16[2048,1024]{1,0:T(8,128)(2,1)S(1)}, bf16[1024,1664]{1,0:T(8,128)(2,1)S(1)}, bf16[2,2,4,32,1664]{4,3...) custom-call(s32[4]{0:T(128)S(1)} %pad_add_fusion.info_ref, ...), custom_call_target="tpu_custom_call" | custom-call | flops 3221225472 | bytes 24576 | tf_op jit(solution)/shard_map/pallas_call | solution.py:342
  87.0 8.4 %shard_map.183 = (bf16[2048,512]{1,0:T(8,128)(2,1)S(1)}, bf16[2048,1024]{1,0:T(8,128)(2,1)S(1)}) custom-call(s32[4]{0:T(128)S(1)} %pad_add_fusion.info_ref, bf16[2048,1024]{1,0:T(8,128)(2,1)S(1)} %get-tuple-element.87.pre1_ref, bf16[1024,1664]{1,0:T(8,128)(2,1)S(1)} %get-tuple-element.88.w1_ref, bf16[1024,1664]{1,0:T(8,128)(2,1)S(1)} %get-tuple-element.89.w0_ref.w_ref, ...), custom_call_target="tpu_custom_call" | custom-call | flops 1610612736 | tf_op jit(solution)/shard_map/pallas_call | solution.py:342
  95.9 1.6 %collective-permute-start.21 = (bf16[2,4,32,1664]{3,2,1,0:T(8,128)(2,1)S(1)}, bf16[2,4,32,1664]{3,2,1,0:T(8,128)(2,1)S(1)}, u32[]{:S(2)}, u32[]{:S(2)}) collective-permute-start(bf16[2,4,32,1664]{3,2,1,0:T(8,128)(2,1)S(1)} %get-tuple-element.101), channel_id=1, source_target_pairs={{0,2},{1,5},{2,0},{3,7},{4,6},{5,1},{6,4},{7,3},{8,10},{9,13},{10,... | collective-permute-start | bytes 2555912 | tf_op jit(solution)/shard_map/ppermute | solution.py:392
  97.5 11.5 %shard_map.185 = (bf16[2,2,4,32,1664]{4,3,2,1,0:T(8,128)(2,1)S(1)}, bf16[2,2,4,32,1664]{4,3,2,1,0:T(8,128)(2,1)S(1)}, f32[128,128]{1,0:T(8,128)S(1)}) custom-call(s32[4]{0:T(128)S(1)} %pad_add_fusion.info_ref, bf16[2048,1024]{1,0:T(8,128)(2,1)S(1)} %get-tuple-element.111.pre_ref, bf16[2048,512]{1,0:T(8,128)(2,1)S(1)} %get-tuple-element.97.res_ref, ...), custom_call_target="tpu_custom_call" | custom-call | flops 1610612736 | bytes 24576 | tf_op jit(solution)/shard_map/pallas_call | solution.py:342
  109.3 3.3 %collective-permute-done.22.right_ref = bf16[2,2,4,32,1664]{4,3,2,1,0:T(8,128)(2,1)S(1)} collective-permute-done((bf16[2,2,4,32,1664]{4,3,2,1,0:T(8,128)(2,1)S(1)}, bf16[2,2,4,32,1664]{4,3,2,1,0:T(8,128)(2,1)S(1)}, u32[]{:S(2)}, u32[]{:S(2)}) %collective-permute-start.22) | collective-permute-done | bytes 1703968 | tf_op jit(solution)/shard_map/ppermute | solution.py:392
  113.0 1.3 collective-permute-start.23
  114.3 1.4 collective-permute-start.24
  115.7 6.8 %shard_map.188 = f32[2048,512]{1,0:T(8,128)} custom-call(s32[4]{0:T(128)S(1)} %pad_add_fusion.info_ref, bf16[2048,512]{1,0:T(8,128)(2,1)S(1)} %get-tuple-element.97.res_ref, bf16[2048,1024]{1,0:T(8,128)(2,1)S(1)} %get-tuple-element.111.pre_ref, bf16[1024,1664]{1,0:T(8,128)(2,1)S(1)} %get-tuple-element.89.w0_ref.w_ref), custom_call_target="tpu_custom_call" | custom-call | flops 1073741824 | bytes 1048576 | tf_op jit(solution)/shard_map/pallas_call | solution.py:342
  122.5 4.5 %collective-permute-done.24.right_ref = bf16[4,32,1664]{2,1,0:T(8,128)(2,1)S(1)} collective-permute-done((bf16[4,32,1664]{2,1,0:T(8,128)(2,1)S(1)}, bf16[4,32,1664]{2,1,0:T(8,128)(2,1)S(1)}, u32[]{:S(2)}, u32[]{:S(2)}) %collective-permute-start.24) | collective-permute-done | bytes 426016 | tf_op jit(solution)/shard_map/ppermute | solution.py:392
  127.1 3.2 %collective-permute-done.23.right_ref = bf16[2,4,32,1664]{3,2,1,0:T(8,128)(2,1)S(1)} collective-permute-done((bf16[2,4,32,1664]{3,2,1,0:T(8,128)(2,1)S(1)}, bf16[2,4,32,1664]{3,2,1,0:T(8,128)(2,1)S(1)}, u32[]{:S(2)}, u32[]{:S(2)}) %collective-permute-start.23) | collective-permute-done | bytes 852000 | tf_op jit(solution)/shard_map/ppermute | solution.py:392
  131.6 1.7 %collective-permute-start.29 = (bf16[32,1664]{1,0:T(8,128)(2,1)S(1)}, bf16[32,1664]{1,0:T(8,128)(2,1)S(1)}, u32[]{:S(2)}, u32[]{:S(2)}) collective-permute-start(bf16[32,1664]{1,0:T(8,128)(2,1)S(1)} %get-tuple-element.133), channel_id=1, source_target_pairs={{0,8},{1,9},{2,10},{3,11},{4,12},{5,13},{6,14},{7,15},{8,0},{9,1},... | collective-permute-start | bytes 319496 | tf_op jit(solution)/shard_map/ppermute | solution.py:392
  133.3 1.3 collective-permute-start.30
  134.6 1.5 collective-permute-start.31
  136.1 8.9 %shard_map.190 = (bf16[2048,512]{1,0:T(8,128)(2,1)}, bf16[2048,512]{1,0:T(8,128)(2,1)}) custom-call(s32[4]{0:T(128)S(1)} %pad_add_fusion.info_ref, bf16[2048,512]{1,0:T(8,128)(2,1)S(1)} %bitcast.19, bf16[2048,512]{1,0:T(8,128)(2,1)S(1)} %get-tuple-element.98.gated_ref.gated0_ref, bf16[2048,512]{1,0:T(8,128)(2,1)S(1)} %get-tuple-element.117.gated1_ref, ...), custom_call_target="tpu_custom_call" | custom-call | flops 1073741824 | bytes 1048576 | tf_op jit(solution)/shard_map/pallas_call | solution.py:342
  145.9 2.2 %collective-permute-start.27 = (bf16[32,1664]{1,0:T(8,128)(2,1)S(1)}, bf16[32,1664]{1,0:T(8,128)(2,1)S(1)}, u32[]{:S(2)}, u32[]{:S(2)}) collective-permute-start(bf16[32,1664]{1,0:T(8,128)(2,1)S(1)} %get-tuple-element.128), channel_id=1, source_target_pairs={{0,16},{1,17},{2,18},{3,19},{4,20},{5,21},{6,22},{7,23},{8,24},{9,... | collective-permute-start | bytes 319496 | tf_op jit(solution)/shard_map/ppermute | solution.py:392
  148.0 1.5 collective-permute-start.28
  150.1 5.7 %collective-permute-done.27.refs_2_ = bf16[32,1664]{1,0:T(8,128)(2,1)S(1)} collective-permute-done((bf16[32,1664]{1,0:T(8,128)(2,1)S(1)}, bf16[32,1664]{1,0:T(8,128)(2,1)S(1)}, u32[]{:S(2)}, u32[]{:S(2)}) %collective-permute-start.27) | collective-permute-done | bytes 106528 | tf_op jit(solution)/shard_map/ppermute | solution.py:392
  (60 shorter events, 12.0 us)
Async XLA Ops:
  1.8 6.1 %collective-permute-start = (bf16[32,1664]{1,0:T(8,128)(2,1)S(1)}, bf16[32,1664]{1,0:T(8,128)(2,1)S(1)}, u32[]{:S(2)}, u32[]{:S(2)}) collective-permute-start(bf16[32,1664]{1,0:T(8,128)(2,1)S(1)} %get-tuple-element.75.refs_0_), channel_id=1, source_target_pairs={{0,8},{1,9},{2,10},{3,11},{4,12},{5,13},{6,14},{7,15},{8,0},{9,1},... | collective-permute-start | bytes 319496 | tf_op jit(solution)/shard_map/ppermute | solution.py:392
  4.9 11.0 %collective-permute-start.1 = (bf16[32,1664]{1,0:T(8,128)(2,1)S(1)}, bf16[32,1664]{1,0:T(8,128)(2,1)S(1)}, u32[]{:S(2)}, u32[]{:S(2)}) collective-permute-start(bf16[32,1664]{1,0:T(8,128)(2,1)S(1)} %get-tuple-element.75.refs_0_), channel_id=1, source_target_pairs={{0,16},{1,17},{2,18},{3,19},{4,20},{5,21},{6,22},{7,23},{8,24},{9,... | collective-permute-start | bytes 319496 | tf_op jit(solution)/shard_map/ppermute | solution.py:392
  7.5 8.4 %collective-permute-start.2 = (bf16[32,1664]{1,0:T(8,128)(2,1)S(1)}, bf16[32,1664]{1,0:T(8,128)(2,1)S(1)}, u32[]{:S(2)}, u32[]{:S(2)}) collective-permute-start(bf16[32,1664]{1,0:T(8,128)(2,1)S(1)} %get-tuple-element.75.refs_0_), channel_id=1, source_target_pairs={{0,24},{1,25},{2,26},{3,27},{4,28},{5,29},{6,30},{7,31},{8,16},{9,... | collective-permute-start | bytes 319496 | tf_op jit(solution)/shard_map/ppermute | solution.py:392
  16.0 14.0 %collective-permute-start.3 = (bf16[4,32,1664]{2,1,0:T(8,128)(2,1)S(1)}, bf16[4,32,1664]{2,1,0:T(8,128)(2,1)S(1)}, u32[]{:S(2)}, u32[]{:S(2)}) collective-permute-start(bf16[4,32,1664]{2,1,0:T(8,128)(2,1)S(1)} %shard_map.179.refs_0_), channel_id=1, source_target_pairs={{0,2},{1,5},{2,0},{3,7},{4,6},{5,1},{6,4},{7,3},{8,10},{9,13},{10,... | collective-permute-start | bytes 1277960 | tf_op jit(solution)/shard_map/ppermute | solution.py:392
  17.6 12.5 %collective-permute-start.4 = (bf16[4,32,1664]{2,1,0:T(8,128)(2,1)S(1)}, bf16[4,32,1664]{2,1,0:T(8,128)(2,1)S(1)}, u32[]{:S(2)}, u32[]{:S(2)}) collective-permute-start(bf16[4,32,1664]{2,1,0:T(8,128)(2,1)S(1)} %shard_map.179.refs_0_), channel_id=1, source_target_pairs={{0,4},{1,3},{2,6},{3,1},{4,0},{5,7},{6,2},{7,5},{8,12},{9,11},{10,... | collective-permute-start | bytes 1277960 | tf_op jit(solution)/shard_map/ppermute | solution.py:392
  19.1 5.2 %collective-permute-start.5 = (bf16[32,1664]{1,0:T(8,128)(2,1)S(1)}, bf16[32,1664]{1,0:T(8,128)(2,1)S(1)}, u32[]{:S(2)}, u32[]{:S(2)}) collective-permute-start(bf16[32,1664]{1,0:T(8,128)(2,1)S(1)} %get-tuple-element.77.refs_0_), channel_id=1, source_target_pairs={{0,8},{1,9},{2,10},{3,11},{4,12},{5,13},{6,14},{7,15},{8,0},{9,1},... | collective-permute-start | bytes 319496 | tf_op jit(solution)/shard_map/ppermute | solution.py:392
  20.8 9.2 %collective-permute-start.6 = (bf16[32,1664]{1,0:T(8,128)(2,1)S(1)}, bf16[32,1664]{1,0:T(8,128)(2,1)S(1)}, u32[]{:S(2)}, u32[]{:S(2)}) collective-permute-start(bf16[32,1664]{1,0:T(8,128)(2,1)S(1)} %get-tuple-element.77.refs_0_), channel_id=1, source_target_pairs={{0,16},{1,17},{2,18},{3,19},{4,20},{5,21},{6,22},{7,23},{8,24},{9,... | collective-permute-start | bytes 319496 | tf_op jit(solution)/shard_map/ppermute | solution.py:392
  22.1 7.9 %collective-permute-start.7 = (bf16[32,1664]{1,0:T(8,128)(2,1)S(1)}, bf16[32,1664]{1,0:T(8,128)(2,1)S(1)}, u32[]{:S(2)}, u32[]{:S(2)}) collective-permute-start(bf16[32,1664]{1,0:T(8,128)(2,1)S(1)} %get-tuple-element.77.refs_0_), channel_id=1, source_target_pairs={{0,24},{1,25},{2,26},{3,27},{4,28},{5,29},{6,30},{7,31},{8,16},{9,... | collective-permute-start | bytes 319496 | tf_op jit(solution)/shard_map/ppermute | solution.py:392
  30.0 8.2 %collective-permute-start.10 = (bf16[4,32,1664]{2,1,0:T(8,128)(2,1)S(1)}, bf16[4,32,1664]{2,1,0:T(8,128)(2,1)S(1)}, u32[]{:S(2)}, u32[]{:S(2)}) collective-permute-start(bf16[4,32,1664]{2,1,0:T(8,128)(2,1)S(1)} %collective-permute-done.3.refs_1_), channel_id=1, source_target_pairs={{0,4},{1,3},{2,6},{3,1},{4,0},{5,7},{6,2},{7,5},{8,12},{9,11},{10,... | collective-permute-start | bytes 1277960 | tf_op jit(solution)/shard_map/ppermute | solution.py:392
  30.6 9.0 %collective-permute-start.11 = (bf16[4,32,1664]{2,1,0:T(8,128)(2,1)S(1)}, bf16[4,32,1664]{2,1,0:T(8,128)(2,1)S(1)}, u32[]{:S(2)}, u32[]{:S(2)}) collective-permute-start(bf16[4,32,1664]{2,1,0:T(8,128)(2,1)S(1)} %shard_map.179.refs_0_), channel_id=1, source_target_pairs={{0,1},{1,0},{2,3},{3,2},{4,5},{5,4},{6,7},{7,6},{8,9},{9,8},{10,11... | collective-permute-start | bytes 1277960 | tf_op jit(solution)/shard_map/ppermute | solution.py:392
  30.6 11.5 %collective-permute-start.12 = (bf16[4,32,1664]{2,1,0:T(8,128)(2,1)S(1)}, bf16[4,32,1664]{2,1,0:T(8,128)(2,1)S(1)}, u32[]{:S(2)}, u32[]{:S(2)}) collective-permute-start(bf16[4,32,1664]{2,1,0:T(8,128)(2,1)S(1)} %collective-permute-done.3.refs_1_), channel_id=1, source_target_pairs={{0,1},{1,0},{2,3},{3,2},{4,5},{5,4},{6,7},{7,6},{8,9},{9,8},{10,11... | collective-permute-start | bytes 1277960 | tf_op jit(solution)/shard_map/ppermute | solution.py:392
  31.1 11.0 %collective-permute-start.13 = (bf16[4,32,1664]{2,1,0:T(8,128)(2,1)S(1)}, bf16[4,32,1664]{2,1,0:T(8,128)(2,1)S(1)}, u32[]{:S(2)}, u32[]{:S(2)}) collective-permute-start(bf16[4,32,1664]{2,1,0:T(8,128)(2,1)S(1)} %collective-permute-done.4.refs_2_), channel_id=1, source_target_pairs={{0,1},{1,0},{2,3},{3,2},{4,5},{5,4},{6,7},{7,6},{8,9},{9,8},{10,11... | collective-permute-start | bytes 1277960 | tf_op jit(solution)/shard_map/ppermute | solution.py:392
  38.2 3.9 %collective-permute-start.14 = (bf16[4,32,1664]{2,1,0:T(8,128)(2,1)S(1)}, bf16[4,32,1664]{2,1,0:T(8,128)(2,1)S(1)}, u32[]{:S(2)}, u32[]{:S(2)}) collective-permute-start(bf16[4,32,1664]{2,1,0:T(8,128)(2,1)S(1)} %collective-permute-done.10.refs_3_), channel_id=1, source_target_pairs={{0,1},{1,0},{2,3},{3,2},{4,5},{5,4},{6,7},{7,6},{8,9},{9,8},{10,11... | collective-permute-start | bytes 1277960 | tf_op jit(solution)/shard_map/ppermute | solution.py:392
  39.0 13.7 %collective-permute-start.8 = (bf16[4,32,1664]{2,1,0:T(8,128)(2,1)}, bf16[4,32,1664]{2,1,0:T(8,128)(2,1)}, u32[]{:S(2)}, u32[]{:S(2)}) collective-permute-start(bf16[4,32,1664]{2,1,0:T(8,128)(2,1)} %shard_map.180.refs_0_), channel_id=1, source_target_pairs={{0,2},{1,5},{2,0},{3,7},{4,6},{5,1},{6,4},{7,3},{8,10},{9,13},{10,... | collective-permute-start | bytes 1277960 | tf_op jit(solution)/shard_map/ppermute | solution.py:392
  39.6 13.2 %collective-permute-start.9 = (bf16[4,32,1664]{2,1,0:T(8,128)(2,1)}, bf16[4,32,1664]{2,1,0:T(8,128)(2,1)}, u32[]{:S(2)}, u32[]{:S(2)}) collective-permute-start(bf16[4,32,1664]{2,1,0:T(8,128)(2,1)} %shard_map.180.refs_0_), channel_id=1, source_target_pairs={{0,4},{1,3},{2,6},{3,1},{4,0},{5,7},{6,2},{7,5},{8,12},{9,11},{10,... | collective-permute-start | bytes 1277960 | tf_op jit(solution)/shard_map/ppermute | solution.py:392
  52.7 8.4 %collective-permute-start.15 = (bf16[4,32,1664]{2,1,0:T(8,128)(2,1)}, bf16[4,32,1664]{2,1,0:T(8,128)(2,1)S(1)}, u32[]{:S(2)}, u32[]{:S(2)}) collective-permute-start(bf16[4,32,1664]{2,1,0:T(8,128)(2,1)} %collective-permute-done.8.refs_1_), channel_id=1, source_target_pairs={{0,4},{1,3},{2,6},{3,1},{4,0},{5,7},{6,2},{7,5},{8,12},{9,11},{10,... | collective-permute-start | bytes 1277960 | tf_op jit(solution)/shard_map/ppermute | solution.py:392
  54.4 6.8 %collective-permute-start.16 = (bf16[4,32,1664]{2,1,0:T(8,128)(2,1)}, bf16[4,32,1664]{2,1,0:T(8,128)(2,1)S(1)}, u32[]{:S(2)}, u32[]{:S(2)}) collective-permute-start(bf16[4,32,1664]{2,1,0:T(8,128)(2,1)} %shard_map.180.refs_0_), channel_id=1, source_target_pairs={{0,1},{1,0},{2,3},{3,2},{4,5},{5,4},{6,7},{7,6},{8,9},{9,8},{10,11... | collective-permute-start | bytes 1277960 | tf_op jit(solution)/shard_map/ppermute | solution.py:392
  54.4 6.8 %collective-permute-start.17 = (bf16[4,32,1664]{2,1,0:T(8,128)(2,1)}, bf16[4,32,1664]{2,1,0:T(8,128)(2,1)S(1)}, u32[]{:S(2)}, u32[]{:S(2)}) collective-permute-start(bf16[4,32,1664]{2,1,0:T(8,128)(2,1)} %collective-permute-done.8.refs_1_), channel_id=1, source_target_pairs={{0,1},{1,0},{2,3},{3,2},{4,5},{5,4},{6,7},{7,6},{8,9},{9,8},{10,11... | collective-permute-start | bytes 1277960 | tf_op jit(solution)/shard_map/ppermute | solution.py:392
  54.9 6.3 %collective-permute-start.18 = (bf16[4,32,1664]{2,1,0:T(8,128)(2,1)}, bf16[4,32,1664]{2,1,0:T(8,128)(2,1)S(1)}, u32[]{:S(2)}, u32[]{:S(2)}) collective-permute-start(bf16[4,32,1664]{2,1,0:T(8,128)(2,1)} %collective-permute-done.9.refs_2_), channel_id=1, source_target_pairs={{0,1},{1,0},{2,3},{3,2},{4,5},{5,4},{6,7},{7,6},{8,9},{9,8},{10,11... | collective-permute-start | bytes 1277960 | tf_op jit(solution)/shard_map/ppermute | solution.py:392
  61.1 1.8 %collective-permute-start.19 = (bf16[4,32,1664]{2,1,0:T(8,128)(2,1)S(1)}, bf16[4,32,1664]{2,1,0:T(8,128)(2,1)S(1)}, u32[]{:S(2)}, u32[]{:S(2)}) collective-permute-start(bf16[4,32,1664]{2,1,0:T(8,128)(2,1)S(1)} %collective-permute-done.15.refs_3_), channel_id=1, source_target_pairs={{0,1},{1,0},{2,3},{3,2},{4,5},{5,4},{6,7},{7,6},{8,9},{9,8},{10,11... | collective-permute-start | bytes 1277960 | tf_op jit(solution)/shard_map/ppermute | solution.py:392
  86.8 8.7 %collective-permute-start.20 = (bf16[2,2,4,32,1664]{4,3,2,1,0:T(8,128)(2,1)S(1)}, bf16[2,2,4,32,1664]{4,3,2,1,0:T(8,128)(2,1)S(1)}, u32[]{:S(2)}, u32[]{:S(2)}) collective-permute-start(bf16[2,2,4,32,1664]{4,3,2,1,0:T(8,128)(2,1)S(1)} %get-tuple-element.93), channel_id=1, source_target_pairs={{0,1},{1,0},{2,3},{3,2},{4,5},{5,4},{6,7},{7,6},{8,9},{9,8},{10,11... | collective-permute-start | bytes 5111816 | tf_op jit(solution)/shard_map/ppermute | solution.py:392
  95.9 13.1 %collective-permute-start.21 = (bf16[2,4,32,1664]{3,2,1,0:T(8,128)(2,1)S(1)}, bf16[2,4,32,1664]{3,2,1,0:T(8,128)(2,1)S(1)}, u32[]{:S(2)}, u32[]{:S(2)}) collective-permute-start(bf16[2,4,32,1664]{3,2,1,0:T(8,128)(2,1)S(1)} %get-tuple-element.101), channel_id=1, source_target_pairs={{0,2},{1,5},{2,0},{3,7},{4,6},{5,1},{6,4},{7,3},{8,10},{9,13},{10,... | collective-permute-start | bytes 2555912 | tf_op jit(solution)/shard_map/ppermute | solution.py:392
  108.9 3.7 %collective-permute-start.22 = (bf16[2,2,4,32,1664]{4,3,2,1,0:T(8,128)(2,1)S(1)}, bf16[2,2,4,32,1664]{4,3,2,1,0:T(8,128)(2,1)S(1)}, u32[]{:S(2)}, u32[]{:S(2)}) collective-permute-start(bf16[2,2,4,32,1664]{4,3,2,1,0:T(8,128)(2,1)S(1)} %get-tuple-element.102), channel_id=1, source_target_pairs={{0,1},{1,0},{2,3},{3,2},{4,5},{5,4},{6,7},{7,6},{8,9},{9,8},{10,11... | collective-permute-start | bytes 5111816 | tf_op jit(solution)/shard_map/ppermute | solution.py:392
  113.0 17.3 %collective-permute-start.23 = (bf16[2,4,32,1664]{3,2,1,0:T(8,128)(2,1)S(1)}, bf16[2,4,32,1664]{3,2,1,0:T(8,128)(2,1)S(1)}, u32[]{:S(2)}, u32[]{:S(2)}) collective-permute-start(bf16[2,4,32,1664]{3,2,1,0:T(8,128)(2,1)S(1)} %get-tuple-element.110), channel_id=1, source_target_pairs={{0,2},{1,5},{2,0},{3,7},{4,6},{5,1},{6,4},{7,3},{8,10},{9,13},{10,... | collective-permute-start | bytes 2555912 | tf_op jit(solution)/shard_map/ppermute | solution.py:392
  114.3 12.8 %collective-permute-start.24 = (bf16[4,32,1664]{2,1,0:T(8,128)(2,1)S(1)}, bf16[4,32,1664]{2,1,0:T(8,128)(2,1)S(1)}, u32[]{:S(2)}, u32[]{:S(2)}) collective-permute-start(bf16[4,32,1664]{2,1,0:T(8,128)(2,1)S(1)} %get-tuple-element.105), channel_id=1, source_target_pairs={{0,4},{1,3},{2,6},{3,1},{4,0},{5,7},{6,2},{7,5},{8,12},{9,11},{10,... | collective-permute-start | bytes 1277960 | tf_op jit(solution)/shard_map/ppermute | solution.py:392
  130.5 14.4 %collective-permute-start.25 = (bf16[4,32,1664]{2,1,0:T(8,128)(2,1)S(1)}, bf16[4,32,1664]{2,1,0:T(8,128)(2,1)S(1)}, u32[]{:S(2)}, u32[]{:S(2)}) collective-permute-start(bf16[4,32,1664]{2,1,0:T(8,128)(2,1)S(1)} %get-tuple-element.115), channel_id=1, source_target_pairs={{0,4},{1,3},{2,6},{3,1},{4,0},{5,7},{6,2},{7,5},{8,12},{9,11},{10,... | collective-permute-start | bytes 1277960 | tf_op jit(solution)/shard_map/ppermute | solution.py:392
  131.6 16.4 %collective-permute-start.29 = (bf16[32,1664]{1,0:T(8,128)(2,1)S(1)}, bf16[32,1664]{1,0:T(8,128)(2,1)S(1)}, u32[]{:S(2)}, u32[]{:S(2)}) collective-permute-start(bf16[32,1664]{1,0:T(8,128)(2,1)S(1)} %get-tuple-element.133), channel_id=1, source_target_pairs={{0,8},{1,9},{2,10},{3,11},{4,12},{5,13},{6,14},{7,15},{8,0},{9,1},... | collective-permute-start | bytes 319496 | tf_op jit(solution)/shard_map/ppermute | solution.py:392
  133.3 16.8 %collective-permute-start.30 = (bf16[32,1664]{1,0:T(8,128)(2,1)S(1)}, bf16[32,1664]{1,0:T(8,128)(2,1)S(1)}, u32[]{:S(2)}, u32[]{:S(2)}) collective-permute-start(bf16[32,1664]{1,0:T(8,128)(2,1)S(1)} %get-tuple-element.134), channel_id=1, source_target_pairs={{0,16},{1,17},{2,18},{3,19},{4,20},{5,21},{6,22},{7,23},{8,24},{9,... | collective-permute-start | bytes 319496 | tf_op jit(solution)/shard_map/ppermute | solution.py:392
  134.6 15.5 %collective-permute-start.31 = (bf16[32,1664]{1,0:T(8,128)(2,1)S(1)}, bf16[32,1664]{1,0:T(8,128)(2,1)S(1)}, u32[]{:S(2)}, u32[]{:S(2)}) collective-permute-start(bf16[32,1664]{1,0:T(8,128)(2,1)S(1)} %get-tuple-element.135), channel_id=1, source_target_pairs={{0,24},{1,25},{2,26},{3,27},{4,28},{5,29},{6,30},{7,31},{8,16},{9,... | collective-permute-start | bytes 319496 | tf_op jit(solution)/shard_map/ppermute | solution.py:392
  145.1 5.1 %collective-permute-start.26 = (bf16[32,1664]{1,0:T(8,128)(2,1)S(1)}, bf16[32,1664]{1,0:T(8,128)(2,1)S(1)}, u32[]{:S(2)}, u32[]{:S(2)}) collective-permute-start(bf16[32,1664]{1,0:T(8,128)(2,1)S(1)} %get-tuple-element.127), channel_id=1, source_target_pairs={{0,8},{1,9},{2,10},{3,11},{4,12},{5,13},{6,14},{7,15},{8,0},{9,1},... | collective-permute-start | bytes 319496 | tf_op jit(solution)/shard_map/ppermute | solution.py:392
  145.9 9.9 %collective-permute-start.27 = (bf16[32,1664]{1,0:T(8,128)(2,1)S(1)}, bf16[32,1664]{1,0:T(8,128)(2,1)S(1)}, u32[]{:S(2)}, u32[]{:S(2)}) collective-permute-start(bf16[32,1664]{1,0:T(8,128)(2,1)S(1)} %get-tuple-element.128), channel_id=1, source_target_pairs={{0,16},{1,17},{2,18},{3,19},{4,20},{5,21},{6,22},{7,23},{8,24},{9,... | collective-permute-start | bytes 319496 | tf_op jit(solution)/shard_map/ppermute | solution.py:392
  148.0 7.8 %collective-permute-start.28 = (bf16[32,1664]{1,0:T(8,128)(2,1)S(1)}, bf16[32,1664]{1,0:T(8,128)(2,1)S(1)}, u32[]{:S(2)}, u32[]{:S(2)}) collective-permute-start(bf16[32,1664]{1,0:T(8,128)(2,1)S(1)} %get-tuple-element.129), channel_id=1, source_target_pairs={{0,24},{1,25},{2,26},{3,27},{4,28},{5,29},{6,30},{7,31},{8,16},{9,... | collective-permute-start | bytes 319496 | tf_op jit(solution)/shard_map/ppermute | solution.py:392
  (4 other events, 42.0 us)

commit v6 on v5

--- a/solution.py
+++ b/solution.py
@@ -11,6 +11,7 @@
 AXES = ("dp", "group")
 LANES = 128
 TILE = 512
+PART = 256
 MIB = 1024 * 1024
 HINT = 4
 ROOM_0, ROOM_1, ROOM_2, ROOM_3, ROOM_4, ROOM_5, ROOM_SMALL = 8, 13, 6, 8, 8, 8, 12
@@ -82,40 +83,55 @@
     return pl.ds(pl.multiple_of(step * rows, rows), rows)
 
 
-def forward_0(size, wires, info_ref, x_ref, mel_ref, *refs):
+def prepare(size, info_ref, x_ref, go_ref, gs_ref, mel_ref, low0_ref, cond_ref, frames_ref, proj1_ref):
+    step = pl.program_id(0)
+    tile = rows_of(step, TILE)
+    mask = mask_of(info_ref, step * TILE, TILE)
+    low0_ref[tile] = masked(x_ref[...], mask)
+    proj1_ref[tile, : size.channels] = masked(go_ref[...], mask)
+    proj1_ref[tile, size.channels :] = masked(gs_ref[...], mask)
+    frames = frames_of(info_ref, step * TILE, TILE)
+    frames_ref[tile] = frames
+    cond_ref[tile] = dot(frames, mel_ref[...]).astype(LOW)
+
+
+def forward_0(size, wires, info_ref, low0_ref, cond_ref, *refs):
     count = 8 if wires.direct else 1
     pieces, refs = refs[:count], refs[count:]
-    low1_ref, gated_ref, slope_ref, w_ref = refs
+    low1_ref, prev1_ref, gated_ref, slope_ref, w_ref, bias_s, carry_s = refs
     step = pl.program_id(0)
     channels = size.channels
 
     @pl.when(step == 0)
     def _():
         wires.put_together(info_ref, pieces, w_ref)
+        bias_s[...] = out_bias_row(size, w_ref[:channels, size.extra :])
+        carry_s[...] = jnp.zeros_like(carry_s)
 
     tile = rows_of(step, TILE)
     mask = mask_of(info_ref, step * TILE, TILE)
-    hidden = x_ref[tile].astype(FULL) * mask
-    low = hidden.astype(LOW)
-    prev_mask = mask_of(info_ref, (step - 1) * TILE, TILE) * (step > 0).astype(FULL)
-    prev = x_ref[rows_of(jnp.maximum(step - 1, 0), TILE)].astype(FULL) * prev_mask
-    cond = dot(frames_of(info_ref, step * TILE, TILE), mel_ref[...]).astype(LOW)
-    taps = jnp.concatenate([prev.astype(LOW), low, cond], axis=1)
+    low = low0_ref[tile]
+    before = low0_ref[rows_of(jnp.maximum(step - 1, 0), TILE)]
+    prev = jnp.where(step > 0, before, jnp.zeros_like(before))
+    taps = jnp.concatenate([prev, low, cond_ref[tile]], axis=1)
     for side in range(2):
         first, second, gated, slope_a, slope_b = gates(taps, w_ref, size, side)
         gated_ref[tile, first] = gated.astype(LOW)
         slope_ref[tile, first] = slope_a.astype(LOW)
         slope_ref[tile, second] = slope_b.astype(LOW)
     moved = dot_cols(gated_ref[tile], w_ref[:channels, :channels])
-    moved = moved + out_bias_row(size, w_ref[:channels, size.extra :])
-    low1_ref[tile] = ((hidden + moved) * mask).astype(LOW)
-
-
-def layer_1(size, wires, steps, info_ref, low1_ref, mel_ref, go_ref, gs_ref, *refs):
+    low = ((low.astype(FULL) + moved + bias_s[...]) * mask).astype(LOW)
+    low1_ref[tile] = low
+    wide = low.astype(FULL)
+    place = lax.broadcasted_iota(jnp.int32, (TILE, 1), 0)
+    prev1_ref[tile] = jnp.where(place == 0, carry_s[7:8], pltpu.roll(wide, 1, 0)).astype(LOW)
+    carry_s[...] = wide[TILE - 8 :]
+
+
+def layer_1(size, wires, steps, info_ref, low_ref, prev_ref, cond_ref, frames_ref, proj_ref, mel_ref, *refs):
     count = 8 if wires.direct else 1
     pieces, refs = refs[:count], refs[count:]
-    gated_ref, pre_ref, w_ref, here_ref, away_ref, melg_ref, *scratch = refs
-    prev_s, proj_s, frames_s, part_s = scratch
+    gated_ref, pre_ref, w_ref, here_ref, away_ref, melg_ref = refs
     step = pl.program_id(0)
     channels = size.channels
 
@@ -127,19 +143,8 @@
     @pl.when(step < steps)
     def _():
         tile = rows_of(step, TILE)
-        mask = mask_of(info_ref, step * TILE, TILE)
-        low = low1_ref[tile]
-        before = pl.ds(pl.multiple_of(jnp.maximum(step * TILE - 16, 0), 16), 16)
-        last = low1_ref[before].astype(FULL)[15:16] * (step > 0).astype(FULL)
-        place = lax.broadcasted_iota(jnp.int32, (TILE, 1), 0)
-        prev = jnp.where(place == 0, last, pltpu.roll(low.astype(FULL), 1, 0)).astype(LOW)
-        frames = frames_of(info_ref, step * TILE, TILE)
-        cond = dot(frames, mel_ref[...]).astype(LOW)
-        taps = jnp.concatenate([prev, low, cond], axis=1)
-        proj = jnp.concatenate([masked(go_ref[tile], mask), masked(gs_ref[tile], mask)], axis=1)
-        prev_s[tile] = prev
-        frames_s[tile] = frames
-        grad_gated = dot(proj, w_ref[:, :channels])
+        taps = jnp.concatenate([prev_ref[tile], low_ref[tile], cond_ref[tile]], axis=1)
+        grad_gated = dot(proj_ref[tile], w_ref[:, :channels])
         for side in range(2):
             first, second, gated, slope_a, slope_b = gates(taps, w_ref, size, side)
             gated_ref[tile, first] = gated.astype(LOW)
@@ -148,44 +153,34 @@
 
     @pl.when(step >= steps)
     def _():
-        width = part_s.shape[0]
-        part = rows_of(step - steps, width)
-        half = channels // width
-        mask = mask_of(info_ref, 0, low1_ref.shape[0])
-
-        @pl.when(step < steps + half)
-        def _():
-            columns = rows_of(jnp.clip(step - steps, 0, half - 1), width)
-            proj_s[...] = masked(go_ref[:, columns], mask)
-
-        @pl.when(step >= steps + half)
-        def _():
-            columns = rows_of(jnp.maximum(step - steps - half, 0), width)
-            proj_s[...] = masked(gs_ref[:, columns], mask)
-
+        part = rows_of(step - steps, PART)
         pre = pre_ref[:, part]
-        part_s[:, size.early : size.now] = dot_rows(pre, prev_s[...]).astype(LOW)
-        part_s[:, size.now : size.extra] = dot_rows(pre, low1_ref[...]).astype(LOW)
-        finish_part(size, pre, proj_s[...], frames_s, gated_ref, mel_ref, w_ref[part, size.extra :], melg_ref, part_s)
-        wires.put_apart(info_ref, step - steps, part_s, here_ref, away_ref)
+        proj = proj_ref[:, part]
+        grads = [
+            dot_rows(proj, gated_ref[...]),
+            dot_rows(pre, prev_ref[...]),
+            dot_rows(pre, low_ref[...]),
+            extra_grads(size, pre, proj, frames_ref, mel_ref, w_ref[part, size.extra :], melg_ref),
+        ]
+        wires.put_apart(info_ref, step - steps, grads, here_ref, away_ref)
+
 
 def in_two(value):
     high = value.astype(LOW)
     return high, (value - high.astype(FULL)).astype(LOW)
 
 
-def finish_part(size, pre, proj, frames_ref, gated_ref, mel_ref, cond_weight, melg_ref, part_ref):
-    sums = in_two(dot_rows(frames_ref[...], pre))
-    extra = sum(dot_rows(half, mel_ref[...]) for half in sums)
-    melg_ref[...] += sum(dot(half, cond_weight) for half in sums)
+def extra_grads(size, pre, proj, frames_ref, mel_ref, cond_weight, melg_ref):
+    sums = in_two(dot_rows(pre, frames_ref[...]))
+    extra = sum(dot(half, mel_ref[...]) for half in sums)
+    melg_ref[...] += sum(dot_rows(half, cond_weight) for half in sums)
     total = jnp.sum(proj.astype(FULL), axis=0, keepdims=True)
     bias = jnp.broadcast_to(total, (LANES, total.shape[1])).T[:, 0:1]
     column = lax.broadcasted_iota(jnp.int32, extra.shape, 1)
-    part_ref[:, size.extra :] = jnp.where(column == size.mel + 1, bias, extra).astype(LOW)
-    part_ref[:, : size.channels] = dot_rows(proj, gated_ref[...]).astype(LOW)
-
-
-def backward_0(size, info_ref, pre1_ref, w1_ref, w0_ref, go_ref, gs_ref, slope_ref, res_ref, pre0_ref, carry_ref):
+    return jnp.where(column == size.mel + 1, bias, extra)
+
+
+def backward_0(size, info_ref, pre1_ref, w1_ref, w0_ref, proj1_ref, slope_ref, proj_ref, pre0_ref, carry_ref):
     step = pl.program_id(0)
     channels = size.channels
     index = pl.num_programs(0) - 1 - step
@@ -202,76 +197,73 @@
     later = jnp.where(place == TILE - 1, carry_ref[0:1], pltpu.roll(early, TILE - 1, 0))
     carry_ref[...] = early[:8]
     now = dot(pre1, w1_ref[:, size.now : size.extra])
-    res = ((go_ref[tile].astype(FULL) * mask + now + later) * mask).astype(LOW)
-    res_ref[tile] = res
-    proj = jnp.concatenate([res, masked(gs_ref[tile], mask)], axis=1)
+    res = ((proj1_ref[tile, :channels].astype(FULL) + now + later) * mask).astype(LOW)
+    proj = jnp.concatenate([res, proj1_ref[tile, channels:]], axis=1)
+    proj_ref[tile] = proj
     grad_gated = dot(proj, w0_ref[:, :channels])
     for half in (slice(0, channels), slice(channels, 2 * channels)):
         pre0_ref[tile, half] = (grad_gated * slope_ref[tile, half].astype(FULL)).astype(LOW)
 
 
-def weights_0(size, wires, info_ref, pre_ref, res_ref, gs_ref, x_ref, gated_ref, mel_ref, w_ref, here_ref, away_ref, melg_ref, frames_s, proj_s, part_s):
+def weights_0(size, wires, info_ref, pre_ref, proj_ref, x_ref, gated_ref, frames_ref, mel_ref, w_ref, here_ref, away_ref, melg_ref):
     step = pl.program_id(0)
-    samples = x_ref.shape[0]
 
     @pl.when(step == 0)
     def _():
-        frames_s[...] = frames_of(info_ref, 0, samples)
         melg_ref[...] = jnp.zeros_like(melg_ref)
 
-    width = part_s.shape[0]
-    half = pl.num_programs(0) // 2
-    part = rows_of(step, width)
-
-    @pl.when(step < half)
-    def _():
-        proj_s[...] = res_ref[:, rows_of(jnp.minimum(step, half - 1), width)]
-
-    @pl.when(step >= half)
-    def _():
-        proj_s[...] = masked(
-            gs_ref[:, rows_of(jnp.maximum(step - half, 0), width)], mask_of(info_ref, 0, samples)
-        )
-
+    part = rows_of(step, PART)
     pre = pre_ref[:, part]
+    proj = proj_ref[:, part]
     shift = FIRST_DILATION
-    early = dot_rows(pre[shift:], x_ref[: samples - shift])
-    part_s[:, size.early : size.now] = early.astype(LOW)
-    part_s[:, size.now : size.extra] = dot_rows(pre, x_ref[...]).astype(LOW)
-    finish_part(size, pre, proj_s[...], frames_s, gated_ref, mel_ref, w_ref[part, size.extra :], melg_ref, part_s)
-    wires.put_apart(info_ref, step, part_s, here_ref, away_ref)
-
-
-def samples_gradient(size, info_ref, res_ref, pre_ref, w0_ref, sg_ref):
+    grads = [
+        dot_rows(proj, gated_ref[...]),
+        dot_rows(pre[shift:], x_ref[: x_ref.shape[0] - shift]),
+        dot_rows(pre, x_ref[...]),
+        extra_grads(size, pre, proj, frames_ref, mel_ref, w_ref[part, size.extra :], melg_ref),
+    ]
+    wires.put_apart(info_ref, step, grads, here_ref, away_ref)
+
+
+def samples_gradient(size, info_ref, proj_ref, pre_ref, w0_ref, sg_ref):
     step = pl.program_id(0)
     tile = rows_of(step, TILE)
-    grad = res_ref[tile].astype(FULL) + dot(pre_ref[tile], w0_ref[:, size.now : size.extra])
+    grad = proj_ref[tile, : size.channels].astype(FULL) + dot(pre_ref[tile], w0_ref[:, size.now : size.extra])
     after = rows_of(jnp.minimum(step + 1, pl.num_programs(0) - 1), TILE)
     later = dot(pre_ref[after], w0_ref[:, size.early : size.now])
     grad = grad + jnp.where(step < pl.num_programs(0) - 1, later, 0.0)
     sg_ref[...] = grad * mask_of(info_ref, step * TILE, TILE)
 
 
-def forward_outputs(size, info_ref, x_ref, gated0_ref, gated1_ref, w0_ref, w1_ref, res_ref, skip_ref):
+def forward_outputs(size, info_ref, low1_ref, gated0_ref, gated1_ref, w0_ref, w1_ref, res_ref, skip_ref, bias_s):
     step = pl.program_id(0)
+    channels = size.channels
+
+    @pl.when(step == 0)
+    def _():
+        bias_s[...] = out_bias_row(size, w1_ref[:, size.extra :])
+        bias_s[:, channels:] += out_bias_row(size, w0_ref[channels:, size.extra :])
+
     tile = rows_of(step, TILE)
     mask = mask_of(info_ref, step * TILE, TILE)
-    channels = size.channels
-    gated = jnp.concatenate([gated0_ref[tile], gated1_ref[tile]], axis=1)
-
-    def projected(rows):
-        both = jnp.concatenate([w0_ref[rows, :channels], w1_ref[rows, :channels]], axis=1)
-        bias = out_bias_row(size, w0_ref[rows, size.extra :])
-        return dot_cols(gated, both) + bias + out_bias_row(size, w1_ref[rows, size.extra :])
-
-    res = projected(slice(0, channels))
-    res_ref[...] = ((x_ref[tile].astype(FULL) + res) * mask).astype(LOW)
-    skip_ref[...] = (projected(slice(channels, 2 * channels)) * mask).astype(LOW)
+    res = dot_cols(gated1_ref[tile], w1_ref[:channels, :channels]) + bias_s[:, :channels]
+    res_ref[...] = ((low1_ref[tile].astype(FULL) + res) * mask).astype(LOW)
+    skip = dot_cols(gated0_ref[tile], w0_ref[channels:, :channels])
+    skip = skip + dot_cols(gated1_ref[tile], w1_ref[channels:, :channels])
+    skip_ref[...] = ((skip + bias_s[:, channels:]) * mask).astype(LOW)
 
 
 def add_and_part(left_ref, right_ref, *refs):
     for index, ref in enumerate(refs):
         ref[...] = add_low(left_ref[index], right_ref[index])
+
+
+def mel_rows(mel_ref, table_ref, wide_s):
+    frames, mel = mel_ref.shape
+    wide_s[...] = jnp.zeros_like(wide_s)
+    wide_s[:frames, :mel] = mel_ref[...].astype(FULL)
+    wide_s[:frames, mel : mel + 1] = jnp.ones((frames, 1), FULL)
+    table_ref[...] = wide_s[...].astype(LOW)
 
 
 def put_side_by_side(*refs):
@@ -356,6 +348,10 @@
     )(info, *arrays)
 
 
+def at_home(value):
+    return pltpu.with_memory_space_constraint(value, pltpu.HBM)
+
+
 def shape_of(*shape, dtype=LOW):
     return jax.ShapeDtypeStruct(shape, dtype)
 
@@ -396,9 +392,8 @@
             self.hop(blocks[k], self.along_rest(k)) for k in range(1, self.rest)
         ]
 
-    def far_hops(self, mine, one, two):
-        pieces = [mine, one, two, self.hop(one, self.second)]
-        pieces += [self.hop(piece, self.sibling) for piece in pieces]
+    def passed(self, *pieces):
+        pieces = [*pieces, *(self.hop(piece, self.sibling) for piece in pieces)]
         return pieces if self.direct else [self.put_in_order(pieces)]
 
     def put_in_order(self, pieces):
@@ -424,27 +419,25 @@
                 place = ((((dp >> 2) ^ distance) * 2 + at_b) * 2 + at_a) * 2 + source
                 w_ref[rows_of(place, self.rows)] = piece[distance]
 
-    def put_apart(self, info_ref, step, part_ref, here_ref, away_ref):
-        if not self.direct:
-            here_ref[rows_of(step, part_ref.shape[0])] = part_ref[...]
-            return
-        dp, core = info_ref[2], info_ref[3]
-        blocks = part_ref.shape[0] // self.rows
-        for block in range(blocks):
-            at_b, at_a, owner = (block // 4) % 2, (block // 2) % 2, block % 2
-            value = part_ref[block * self.rows : (block + 1) * self.rows]
-            first, second = at_a ^ (dp & 1), at_b ^ ((dp >> 1) & 1)
-            if owner:
-                first, second = second, first
-            distance = (step * (blocks // 8) + block // 8) ^ (dp >> 2)
-
-            @pl.when(core == owner)
-            def _():
-                here_ref[first, second, distance] = value
-
-            @pl.when(core != owner)
-            def _():
-                away_ref[first, second, distance] = value
+    def put_apart(self, info_ref, step, grads, here_ref, away_ref):
+        start = 0
+        for value in (grad.astype(LOW) for grad in grads):
+            columns = slice(start, start + value.shape[1])
+            start += value.shape[1]
+            if not self.direct:
+                here_ref[rows_of(step, value.shape[0]), columns] = value
+                continue
+            dp, core = info_ref[2], info_ref[3]
+            blocks = value.shape[0] // self.rows
+            for block in range(0, blocks, 2):
+                at_b, at_a = (block // 4) % 2, (block // 2) % 2
+                distance = (step * (blocks // 8) + block // 8) ^ (dp >> 2)
+                on_a, on_b = at_a ^ (dp & 1), at_b ^ ((dp >> 1) & 1)
+                even = value[block * self.rows : (block + 1) * self.rows]
+                odd = value[(block + 1) * self.rows : (block + 2) * self.rows]
+                first, second = jnp.where(core == 0, on_a, on_b), jnp.where(core == 0, on_b, on_a)
+                here_ref[first, second, distance, :, columns] = jnp.where(core == 0, even, odd)
+                away_ref[second, first, distance, :, columns] = jnp.where(core == 0, odd, even)
 
     def apart(self, depth):
         if not self.direct:
@@ -507,11 +500,6 @@
     where = jnp.stack([wires.dp, wires.core]).astype(jnp.int32)
     info = jnp.concatenate([lengths, hops, where])
     x, go, gs = samples[0], grad_out[0], grad_skip[0]
-    mel_table = jnp.concatenate([mel[0], jnp.ones((frame_count, 1), LOW)], axis=1)
-    mel_table = jnp.pad(
-        mel_table, ((0, LANES - frame_count), (0, size.extra_width - mel_count - 1))
-    )
-
     conv_t, cond_t, out_t = (
         w.swapaxes(1, 2) for w in (conv_weight, cond_weight, out_weight)
     )
@@ -524,61 +512,71 @@
         scratch_shapes=[pltpu.VMEM(source.shape, LOW) for source in sources]
         + [pltpu.SemaphoreType.DMA((len(sources),))],
         compiler_params=pltpu.CompilerParams(vmem_limit_bytes=ROOM_SMALL * MIB),
-    )(*(pltpu.with_memory_space_constraint(source, pltpu.HBM) for source in sources))
+    )(*map(at_home, sources))
     last_shape = shape_of(wires.rest, rows, size.pack)
     half_shape = shape_of(2, wires.rest, rows, size.pack)
     blocks_shape = [shape_of(rows, size.pack)] * wires.rest
     side_by_side = lambda blocks: plain(put_side_by_side, blocks, [last_shape])[0]
+    table = fixed(LANES, size.extra_width)
+    macs = sample_count * channels * channels
+    assert gate % PART == 0
+    kept = lambda *columns: [(shape_of(sample_count, c), None) for c in columns]
+    whole_w = (shape_of(gate, size.pack), None)
+    parts = gate // PART
+    melg = (shape_of(LANES, size.extra_width, dtype=FULL), table)
+    scratch = lambda *shape: pltpu.VMEM(shape, LOW)
+
+    blocked = (shape_of(sample_count, channels), tiled(channels))
+    keep = lambda *values: [(value, None) for value in values]
+
     near0 = wires.spread([own[0]] * wires.rest)
-    near1 = wires.spread([own[1]] * wires.rest)
     mine0 = side_by_side(near0)
     one0, two0 = wires.hop(mine0, wires.first), wires.hop(mine0, wires.second)
-    one0, two0, *near1 = lax.optimization_barrier((one0, two0, *near1))
-    pieces0 = wires.far_hops(mine0, one0, two0)
+    mel_late, _ = lax.optimization_barrier((mel[0], mine0))
+    mel_table = pl.pallas_call(
+        mel_rows,
+        out_shape=shape_of(LANES, size.extra_width),
+        scratch_shapes=[pltpu.VMEM((LANES, size.extra_width), FULL)],
+        compiler_params=pltpu.CompilerParams(vmem_limit_bytes=ROOM_SMALL * MIB),
+    )(mel_late)
+    own1, mel_table = lax.optimization_barrier((own[1], mel_table))
+    near1 = wires.spread([own1] * wires.rest)
+    mel_table, *near1 = lax.optimization_barrier((mel_table, *near1))
     mine1 = side_by_side(near1)
+    low0, cond, frames, proj1 = call(
+        functools.partial(prepare, size),
+        steps,
+        info,
+        [*((at_home(value), tiled(channels)) for value in (x, go, gs)), (mel_table, table)],
+        kept(channels, LANES, LANES, gate),
+        [],
+        macs,
+        ROOM_0,
+    )
+    one0, two0, mine1 = lax.optimization_barrier((one0, two0, mine1))
+    far0 = wires.hop(one0, wires.second)
     one1, two1 = wires.hop(mine1, wires.first), wires.hop(mine1, wires.second)
-
-    table = fixed(LANES, size.extra_width)
-    macs = sample_count * channels * channels
-    kept = lambda *columns: [(shape_of(sample_count, c), None) for c in columns]
-    whole_w = (shape_of(gate, size.pack), None)
-    parts = 4
-    width = gate // parts
-    melg = (shape_of(LANES, size.extra_width, dtype=FULL), table)
-    scratch = lambda *shape: pltpu.VMEM(shape, LOW)
-
-    blocked = (shape_of(sample_count, channels), tiled(channels))
-    keep = lambda *values: [(value, None) for value in values]
-
-    low1, gated0, slope0, w0 = call(
+    far0, one1, two1, low0 = lax.optimization_barrier((far0, one1, two1, low0))
+    low1, prev1, gated0, slope0, w0 = call(
         functools.partial(forward_0, size, wires),
         steps,
         info,
-        [(x, None), (mel_table, table), *keep(*pieces0)],
-        [*kept(channels, channels, gate), whole_w],
-        [],
+        keep(low0, cond, *wires.passed(mine0, one0, two0, far0)),
+        [*kept(channels, channels, channels, gate), whole_w],
+        [pltpu.VMEM((1, channels), FULL), pltpu.VMEM((8, channels), FULL)],
         10 * macs,
         ROOM_0,
     )
-    one1, two1, low1 = lax.optimization_barrier((one1, two1, low1))
+    far1 = wires.hop(one1, wires.second)
+    far1, low1 = lax.optimization_barrier((far1, low1))
     gated1, pre1, w1, here1, away1, melg1 = call(
         functools.partial(layer_1, size, wires, steps),
         steps + parts,
         info,
-        [(low1, None), (mel_table, table), (go, None), (gs, None)]
-        + keep(*wires.far_hops(mine1, one1, two1)),
-        [
-            *kept(channels, gate),
-            whole_w,
-            *wires.apart(size.pack),
-            melg,
-        ],
-        [
-            scratch(sample_count, channels),
-            scratch(sample_count, width),
-            scratch(sample_count, LANES),
-            scratch(width, size.pack),
-        ],
+        [*keep(low1, prev1, cond, frames, proj1), (mel_table, table)]
+        + keep(*wires.passed(mine1, one1, two1, far1)),
+        [*kept(channels, gate), whole_w, *wires.apart(size.pack), melg],
+        [],
         24 * macs,
         ROOM_1,
     )
@@ -586,12 +584,12 @@
         here1, away1 = wires.by_distance(here1)
     came1 = wires.hop(away1, wires.sibling)
 
-    res0, pre0 = call(
+    proj0, pre0 = call(
         functools.partial(backward_0, size),
         steps,
         info,
-        keep(pre1, w1, w0, go, gs, slope0),
-        kept(channels, gate),
+        keep(pre1, w1, w0, proj1, slope0),
+        kept(gate, gate),
         [pltpu.VMEM((8, channels), FULL)],
         12 * macs,
         ROOM_2,
@@ -604,13 +602,9 @@
         functools.partial(weights_0, size, wires),
         parts,
         info,
-        [*keep(pre0, res0, gs, x, gated0), (mel_table, table), (w0, None)],
+        [*keep(pre0, proj0, low0, gated0, frames), (mel_table, table), (w0, None)],
         [*wires.apart(size.pack), melg],
-        [
-            scratch(sample_count, LANES),
-            scratch(sample_count, width),
-            scratch(width, size.pack),
-        ],
+        [],
         12 * macs,
         ROOM_3,
     )
@@ -629,7 +623,7 @@
         functools.partial(samples_gradient, size),
         steps,
         info,
-        keep(res0, pre0, w0),
+        keep(proj0, pre0, w0),
         [(shape_of(sample_count, channels, dtype=FULL), tiled(channels))],
         [],
         8 * macs,
@@ -638,15 +632,15 @@
     came0, came1, samples_grad = lax.optimization_barrier((came0, came1, samples_grad))
     parts1 = wires.spread(plain(add_and_part, (stay1, came1), blocks_shape))
     stay0, leave0 = plain(add_and_part, (stay0, came0), [last_shape] * 2)
-    x, stay0, leave0 = lax.optimization_barrier((x, stay0, leave0))
+    low1, stay0, leave0 = lax.optimization_barrier((low1, stay0, leave0))
     came0 = wires.hop(leave0, wires.second)
     residual_out, skip_output_sum = call(
         functools.partial(forward_outputs, size),
         steps,
         info,
-        keep(x, gated0, gated1, w0, w1),
+        keep(low1, gated0, gated1, w0, w1),
         [blocked, blocked],
-        [],
+        [pltpu.VMEM((1, gate), FULL)],
         8 * macs,
         ROOM_5,
     )

time: 157 us -> 147 us (0.936)
  waiting for transfers between devices: 46.9 us -> 41.1 us
  Pallas kernels: 72.9 us -> 68.8 us
  starting transfers between devices: 32 us -> 33.8 us
    ppermute x32, waiting for transfers between devices: 46.9 us -> 41.1 us  [hop(): return lax.ppermute(value, AXES, pairs)]
    pallas_call x6 -> x7, Pallas kernels: 68.4 us -> 65 us  [call(): pl.pallas_call(kernel, grid_spec=pltpu.PrefetchScalarGridSpec(num_scalar_...]
    ppermute x32, starting transfers between devices: 32 us -> 33.8 us  [hop(): return lax.ppermute(value, AXES, pairs)]
  transfers between devices with their start and end apart: 32 -> 32, of which waited for: 11 -> 12; matrix products, arithmetic and copies ran while one was open for 1% -> 0% of each run, Pallas kernels for 29% -> 31%
where the time goes in v6:
time: 147 us
  Pallas kernels  68.8 us (47%)
  waiting for transfers between devices  41.1 us (28%)
  starting transfers between devices  33.8 us (23%)
  between operations  2.1 us (1%)
    pallas_call x7, Pallas kernels, call(): pl.pallas_call(kernel, grid_spec=pltpu.PrefetchScalarGridSpec(num_scalar_...  65 us
    ppermute x32, waiting for transfers between devices, hop(): return lax.ppermute(value, AXES, pairs)  41.1 us
    ppermute x32, starting transfers between devices, hop(): return lax.ppermute(value, AXES, pairs)  33.8 us
  transfers between devices with their start and end apart: 32, of which 12 were waited for; matrix products, arithmetic and copies ran while one was open for 0% of the time, Pallas kernels for 31%

profile of v6, /device:TPU:0, one launch (start us, length us, event | category | flops | bytes accessed | tf_op | source)
XLA Modules:
  0.0 147.2 jit_solution(6982509755312691058)
XLA Ops:
  0.6 1.2 shard_map.178
  1.8 3.1 %collective-permute-start = (bf16[32,1664]{1,0:T(8,128)(2,1)S(1)}, bf16[32,1664]{1,0:T(8,128)(2,1)S(1)}, u32[]{:S(2)}, u32[]{:S(2)}) collective-permute-start(bf16[32,1664]{1,0:T(8,128)(2,1)S(1)} %get-tuple-element.88.refs_0_), channel_id=1, source_target_pairs={{0,8},{1,9},{2,10},{3,11},{4,12},{5,13},{6,14},{7,15},{8,0},{9,1},... | collective-permute-start | bytes 319496 | tf_op jit(solution)/shard_map/ppermute | solution.py:388
  4.9 2.6 %collective-permute-start.1 = (bf16[32,1664]{1,0:T(8,128)(2,1)S(1)}, bf16[32,1664]{1,0:T(8,128)(2,1)S(1)}, u32[]{:S(2)}, u32[]{:S(2)}) collective-permute-start(bf16[32,1664]{1,0:T(8,128)(2,1)S(1)} %get-tuple-element.88.refs_0_), channel_id=1, source_target_pairs={{0,16},{1,17},{2,18},{3,19},{4,20},{5,21},{6,22},{7,23},{8,24},{9,... | collective-permute-start | bytes 319496 | tf_op jit(solution)/shard_map/ppermute | solution.py:388
  7.9 8.1 %collective-permute-done.1.refs_2_ = bf16[32,1664]{1,0:T(8,128)(2,1)S(1)} collective-permute-done((bf16[32,1664]{1,0:T(8,128)(2,1)S(1)}, bf16[32,1664]{1,0:T(8,128)(2,1)S(1)}, u32[]{:S(2)}, u32[]{:S(2)}) %collective-permute-start.1) | collective-permute-done | bytes 106528 | tf_op jit(solution)/shard_map/ppermute | solution.py:388
  16.0 1.6 %collective-permute-start.3 = (bf16[4,32,1664]{2,1,0:T(8,128)(2,1)S(1)}, bf16[4,32,1664]{2,1,0:T(8,128)(2,1)S(1)}, u32[]{:S(2)}, u32[]{:S(2)}) collective-permute-start(bf16[4,32,1664]{2,1,0:T(8,128)(2,1)S(1)} %shard_map.179.refs_0_), channel_id=1, source_target_pairs={{0,2},{1,5},{2,0},{3,7},{4,6},{5,1},{6,4},{7,3},{8,10},{9,13},{10,... | collective-permute-start | bytes 1277960 | tf_op jit(solution)/shard_map/ppermute | solution.py:388
  17.6 1.5 %collective-permute-start.4 = (bf16[4,32,1664]{2,1,0:T(8,128)(2,1)S(1)}, bf16[4,32,1664]{2,1,0:T(8,128)(2,1)S(1)}, u32[]{:S(2)}, u32[]{:S(2)}) collective-permute-start(bf16[4,32,1664]{2,1,0:T(8,128)(2,1)S(1)} %shard_map.179.refs_0_), channel_id=1, source_target_pairs={{0,4},{1,3},{2,6},{3,1},{4,0},{5,7},{6,2},{7,5},{8,12},{9,11},{10,... | collective-permute-start | bytes 1277960 | tf_op jit(solution)/shard_map/ppermute | solution.py:388
  19.8 1.8 %collective-permute-start.5 = (bf16[32,1664]{1,0:T(8,128)(2,1)S(1)}, bf16[32,1664]{1,0:T(8,128)(2,1)S(1)}, u32[]{:S(2)}, u32[]{:S(2)}) collective-permute-start(bf16[32,1664]{1,0:T(8,128)(2,1)S(1)} %get-tuple-element.93.refs_0_), channel_id=1, source_target_pairs={{0,8},{1,9},{2,10},{3,11},{4,12},{5,13},{6,14},{7,15},{8,0},{9,1},... | collective-permute-start | bytes 319496 | tf_op jit(solution)/shard_map/ppermute | solution.py:388
  21.6 1.3 collective-permute-start.6
  22.9 1.3 collective-permute-start.7
  25.1 5.7 %collective-permute-done.6.refs_2_ = bf16[32,1664]{1,0:T(8,128)(2,1)S(1)} collective-permute-done((bf16[32,1664]{1,0:T(8,128)(2,1)S(1)}, bf16[32,1664]{1,0:T(8,128)(2,1)S(1)}, u32[]{:S(2)}, u32[]{:S(2)}) %collective-permute-start.6) | collective-permute-done | bytes 106528 | tf_op jit(solution)/shard_map/ppermute | solution.py:388
  31.4 1.5 %collective-permute-start.8 = (bf16[4,32,1664]{2,1,0:T(8,128)(2,1)S(1)}, bf16[4,32,1664]{2,1,0:T(8,128)(2,1)S(1)}, u32[]{:S(2)}, u32[]{:S(2)}) collective-permute-start(bf16[4,32,1664]{2,1,0:T(8,128)(2,1)S(1)} %collective-permute-done.3.refs_1_), channel_id=1, source_target_pairs={{0,4},{1,3},{2,6},{3,1},{4,0},{5,7},{6,2},{7,5},{8,12},{9,11},{10,... | collective-permute-start | bytes 1277960 | tf_op jit(solution)/shard_map/ppermute | solution.py:388
  34.9 4.7 %shard_map.182 = (bf16[2048,512]{1,0:T(8,128)(2,1)S(1)}, bf16[2048,128]{1,0:T(8,128)(2,1)S(1)}, bf16[2048,128]{1,0:T(8,128)(2,1)S(1)}, bf16[2048,1024]{1,0:T(8,128)(2,1)S(1)}) custom-call(s32[4]{0:T(128)S(1)} %pad_add_fusion.info_ref, bf16[2048,512]{1,0:T(8,128)(2,1)} %bitcast.19, bf16[2048,512]{1,0:T(8,128)(2,1)} %bitcast.20, bf16[2048,512]{1,0:T(8,128)(2,1)} %bitcast.21, ...), custom_call_target="tpu_custom_call" | custom-call | flops 134217728 | bytes 1581056 | tf_op jit(solution)/shard_map/pallas_call | solution.py:334
  40.3 4.1 %collective-permute-done.8.refs_3_ = bf16[4,32,1664]{2,1,0:T(8,128)(2,1)S(1)} collective-permute-done((bf16[4,32,1664]{2,1,0:T(8,128)(2,1)S(1)}, bf16[4,32,1664]{2,1,0:T(8,128)(2,1)S(1)}, u32[]{:S(2)}, u32[]{:S(2)}) %collective-permute-start.8) | collective-permute-done | bytes 426016 | tf_op jit(solution)/shard_map/ppermute | solution.py:388
  46.2 9.5 %shard_map.183 = (bf16[2048,512]{1,0:T(8,128)(2,1)S(1)}, bf16[2048,512]{1,0:T(8,128)(2,1)S(1)}, bf16[2048,512]{1,0:T(8,128)(2,1)S(1)}, bf16[2048,1024]{1,0:T(8,128)(2,1)S(1)}, bf16[1024,1664]{1,0:T(8,128)(2,1)S(1)}) custom-call(s32[4]{0:T(128)S(1)} %pad_add_fusion.info_ref, bf16[2048,512]{1,0:T(8,128)(2,1)S(1)} %get-tuple-element.102.low0_ref.x_ref, ...), custom_call_target="tpu_custom_call" | custom-call | flops 1342177280 | tf_op jit(solution)/shard_map/pallas_call | solution.py:334
  55.9 1.6 %collective-permute-done.19.refs_7_ = bf16[4,32,1664]{2,1,0:T(8,128)(2,1)S(1)} collective-permute-done((bf16[4,32,1664]{2,1,0:T(8,128)(2,1)S(1)}, bf16[4,32,1664]{2,1,0:T(8,128)(2,1)S(1)}, u32[]{:S(2)}, u32[]{:S(2)}) %collective-permute-start.19) | collective-permute-done | bytes 426016 | tf_op jit(solution)/shard_map/ppermute | solution.py:388
  57.6 20.0 %shard_map.184 = (bf16[2048,512]{1,0:T(8,128)(2,1)S(1)}, bf16[2048,1024]{1,0:T(8,128)(2,1)S(1)}, bf16[1024,1664]{1,0:T(8,128)(2,1)S(1)}, bf16[2,2,4,32,1664]{4,3...) custom-call(s32[4]{0:T(128)S(1)} %pad_add_fusion.info_ref, ...), custom_call_target="tpu_custom_call" | custom-call | flops 3221225472 | bytes 24576 | tf_op jit(solution)/shard_map/pallas_call | solution.py:334
  77.7 8.4 %shard_map.185 = (bf16[2048,1024]{1,0:T(8,128)(2,1)S(1)}, bf16[2048,1024]{1,0:T(8,128)(2,1)S(1)}) custom-call(s32[4]{0:T(128)S(1)} %pad_add_fusion.info_ref, bf16[2048,1024]{1,0:T(8,128)(2,1)S(1)} %get-tuple-element.113.pre1_ref, bf16[1024,1664]{1,0:T(8,128)(2,1)S(1)} %get-tuple-element.114.w1_ref, bf16[1024,1664]{1,0:T(8,128)(2,1)S(1)} %get-tuple-element.115.w0_ref.w_ref, ...), custom_call_target="tpu_custom_call" | custom-call | flops 1610612736 | tf_op jit(solution)/shard_map/pallas_call | solution.py:334
  86.5 1.1 collective-permute-start.21
  87.6 9.5 %shard_map.187 = (bf16[2,2,4,32,1664]{4,3,2,1,0:T(8,128)(2,1)S(1)}, bf16[2,2,4,32,1664]{4,3,2,1,0:T(8,128)(2,1)S(1)}, f32[128,128]{1,0:T(8,128)S(1)}) custom-call(s32[4]{0:T(128)S(1)} %pad_add_fusion.info_ref, bf16[2048,1024]{1,0:T(8,128)(2,1)S(1)} %get-tuple-element.137.pre_ref, bf16[2048,1024]{1,0:T(8,128)(2,1)S(1)} %get-tuple-element.123.proj_ref, ...), custom_call_target="tpu_custom_call" | custom-call | flops 1610612736 | bytes 24576 | tf_op jit(solution)/shard_map/pallas_call | solution.py:334
  97.1 2.2 %collective-permute-done.21.right_ref = bf16[2,4,32,1664]{3,2,1,0:T(8,128)(2,1)S(1)} collective-permute-done((bf16[2,4,32,1664]{3,2,1,0:T(8,128)(2,1)S(1)}, bf16[2,4,32,1664]{3,2,1,0:T(8,128)(2,1)S(1)}, u32[]{:S(2)}, u32[]{:S(2)}) %collective-permute-start.21) | collective-permute-done | bytes 852000 | tf_op jit(solution)/shard_map/ppermute | solution.py:388
  99.5 3.4 %collective-permute-done.22.right_ref = bf16[2,2,4,32,1664]{4,3,2,1,0:T(8,128)(2,1)S(1)} collective-permute-done((bf16[2,2,4,32,1664]{4,3,2,1,0:T(8,128)(2,1)S(1)}, bf16[2,2,4,32,1664]{4,3,2,1,0:T(8,128)(2,1)S(1)}, u32[]{:S(2)}, u32[]{:S(2)}) %collective-permute-start.22) | collective-permute-done | bytes 1703968 | tf_op jit(solution)/shard_map/ppermute | solution.py:388
  103.3 1.1 collective-permute-start.23
  105.0 7.0 %shard_map.190 = f32[2048,512]{1,0:T(8,128)} custom-call(s32[4]{0:T(128)S(1)} %pad_add_fusion.info_ref, bf16[2048,1024]{1,0:T(8,128)(2,1)S(1)} %get-tuple-element.123.proj_ref, bf16[2048,1024]{1,0:T(8,128)(2,1)S(1)} %get-tuple-element.137.pre_ref, bf16[1024,1664]{1,0:T(8,128)(2,1)S(1)} %get-tuple-element.115.w0_ref.w_ref), custom_call_target="tpu_custom_call" | custom-call | flops 1073741824 | bytes 1048576 | tf_op jit(solution)/shard_map/pallas_call | solution.py:334
  112.0 5.1 %collective-permute-done.24.right_ref = bf16[4,32,1664]{2,1,0:T(8,128)(2,1)S(1)} collective-permute-done((bf16[4,32,1664]{2,1,0:T(8,128)(2,1)S(1)}, bf16[4,32,1664]{2,1,0:T(8,128)(2,1)S(1)}, u32[]{:S(2)}, u32[]{:S(2)}) %collective-permute-start.24) | collective-permute-done | bytes 426016 | tf_op jit(solution)/shard_map/ppermute | solution.py:388
  117.1 3.5 %collective-permute-done.23.right_ref = bf16[2,4,32,1664]{3,2,1,0:T(8,128)(2,1)S(1)} collective-permute-done((bf16[2,4,32,1664]{3,2,1,0:T(8,128)(2,1)S(1)}, bf16[2,4,32,1664]{3,2,1,0:T(8,128)(2,1)S(1)}, u32[]{:S(2)}, u32[]{:S(2)}) %collective-permute-start.23) | collective-permute-done | bytes 852000 | tf_op jit(solution)/shard_map/ppermute | solution.py:388
  121.9 4.5 %collective-permute-start.29 = (bf16[32,1664]{1,0:T(8,128)(2,1)S(1)}, bf16[32,1664]{1,0:T(8,128)(2,1)S(1)}, u32[]{:S(2)}, u32[]{:S(2)}) collective-permute-start(bf16[32,1664]{1,0:T(8,128)(2,1)S(1)} %get-tuple-element.159), channel_id=1, source_target_pairs={{0,8},{1,9},{2,10},{3,11},{4,12},{5,13},{6,14},{7,15},{8,0},{9,1},... | collective-permute-start | bytes 319496 | tf_op jit(solution)/shard_map/ppermute | solution.py:388
  126.5 1.5 %collective-permute-start.30 = (bf16[32,1664]{1,0:T(8,128)(2,1)S(1)}, bf16[32,1664]{1,0:T(8,128)(2,1)S(1)}, u32[]{:S(2)}, u32[]{:S(2)}) collective-permute-start(bf16[32,1664]{1,0:T(8,128)(2,1)S(1)} %get-tuple-element.160), channel_id=1, source_target_pairs={{0,16},{1,17},{2,18},{3,19},{4,20},{5,21},{6,22},{7,23},{8,24},{9,... | collective-permute-start | bytes 319496 | tf_op jit(solution)/shard_map/ppermute | solution.py:388
  128.0 1.4 collective-permute-start.31
  129.4 5.9 %shard_map.192 = (bf16[2048,512]{1,0:T(8,128)(2,1)}, bf16[2048,512]{1,0:T(8,128)(2,1)}) custom-call(s32[4]{0:T(128)S(1)} %pad_add_fusion.info_ref, bf16[2048,512]{1,0:T(8,128)(2,1)S(1)} %get-tuple-element.142.low_ref.low1_ref, bf16[2048,512]{1,0:T(8,128)(2,1)S(1)} %get-tuple-element.124.gated_ref.gated0_ref, ...), custom_call_target="tpu_custom_call" | custom-call | flops 1073741824 | bytes 1048576 | tf_op jit(solution)/shard_map/pallas_call | solution.py:334
  136.0 2.4 %collective-permute-start.27 = (bf16[32,1664]{1,0:T(8,128)(2,1)S(1)}, bf16[32,1664]{1,0:T(8,128)(2,1)S(1)}, u32[]{:S(2)}, u32[]{:S(2)}) collective-permute-start(bf16[32,1664]{1,0:T(8,128)(2,1)S(1)} %get-tuple-element.154), channel_id=1, source_target_pairs={{0,16},{1,17},{2,18},{3,19},{4,20},{5,21},{6,22},{7,23},{8,24},{9,... | collective-permute-start | bytes 319496 | tf_op jit(solution)/shard_map/ppermute | solution.py:388
  138.4 1.4 collective-permute-start.28
  140.4 5.7 %collective-permute-done.27.refs_2_ = bf16[32,1664]{1,0:T(8,128)(2,1)S(1)} collective-permute-done((bf16[32,1664]{1,0:T(8,128)(2,1)S(1)}, bf16[32,1664]{1,0:T(8,128)(2,1)S(1)}, u32[]{:S(2)}, u32[]{:S(2)}) %collective-permute-start.27) | collective-permute-done | bytes 106528 | tf_op jit(solution)/shard_map/ppermute | solution.py:388
  (55 shorter events, 11.4 us)
Async XLA Ops:
  1.8 6.1 %collective-permute-start = (bf16[32,1664]{1,0:T(8,128)(2,1)S(1)}, bf16[32,1664]{1,0:T(8,128)(2,1)S(1)}, u32[]{:S(2)}, u32[]{:S(2)}) collective-permute-start(bf16[32,1664]{1,0:T(8,128)(2,1)S(1)} %get-tuple-element.88.refs_0_), channel_id=1, source_target_pairs={{0,8},{1,9},{2,10},{3,11},{4,12},{5,13},{6,14},{7,15},{8,0},{9,1},... | collective-permute-start | bytes 319496 | tf_op jit(solution)/shard_map/ppermute | solution.py:388
  4.9 11.0 %collective-permute-start.1 = (bf16[32,1664]{1,0:T(8,128)(2,1)S(1)}, bf16[32,1664]{1,0:T(8,128)(2,1)S(1)}, u32[]{:S(2)}, u32[]{:S(2)}) collective-permute-start(bf16[32,1664]{1,0:T(8,128)(2,1)S(1)} %get-tuple-element.88.refs_0_), channel_id=1, source_target_pairs={{0,16},{1,17},{2,18},{3,19},{4,20},{5,21},{6,22},{7,23},{8,24},{9,... | collective-permute-start | bytes 319496 | tf_op jit(solution)/shard_map/ppermute | solution.py:388
  7.5 8.4 %collective-permute-start.2 = (bf16[32,1664]{1,0:T(8,128)(2,1)S(1)}, bf16[32,1664]{1,0:T(8,128)(2,1)S(1)}, u32[]{:S(2)}, u32[]{:S(2)}) collective-permute-start(bf16[32,1664]{1,0:T(8,128)(2,1)S(1)} %get-tuple-element.88.refs_0_), channel_id=1, source_target_pairs={{0,24},{1,25},{2,26},{3,27},{4,28},{5,29},{6,30},{7,31},{8,16},{9,... | collective-permute-start | bytes 319496 | tf_op jit(solution)/shard_map/ppermute | solution.py:388
  16.0 14.8 %collective-permute-start.3 = (bf16[4,32,1664]{2,1,0:T(8,128)(2,1)S(1)}, bf16[4,32,1664]{2,1,0:T(8,128)(2,1)S(1)}, u32[]{:S(2)}, u32[]{:S(2)}) collective-permute-start(bf16[4,32,1664]{2,1,0:T(8,128)(2,1)S(1)} %shard_map.179.refs_0_), channel_id=1, source_target_pairs={{0,2},{1,5},{2,0},{3,7},{4,6},{5,1},{6,4},{7,3},{8,10},{9,13},{10,... | collective-permute-start | bytes 1277960 | tf_op jit(solution)/shard_map/ppermute | solution.py:388
  17.6 13.3 %collective-permute-start.4 = (bf16[4,32,1664]{2,1,0:T(8,128)(2,1)S(1)}, bf16[4,32,1664]{2,1,0:T(8,128)(2,1)S(1)}, u32[]{:S(2)}, u32[]{:S(2)}) collective-permute-start(bf16[4,32,1664]{2,1,0:T(8,128)(2,1)S(1)} %shard_map.179.refs_0_), channel_id=1, source_target_pairs={{0,4},{1,3},{2,6},{3,1},{4,0},{5,7},{6,2},{7,5},{8,12},{9,11},{10,... | collective-permute-start | bytes 1277960 | tf_op jit(solution)/shard_map/ppermute | solution.py:388
  19.8 5.3 %collective-permute-start.5 = (bf16[32,1664]{1,0:T(8,128)(2,1)S(1)}, bf16[32,1664]{1,0:T(8,128)(2,1)S(1)}, u32[]{:S(2)}, u32[]{:S(2)}) collective-permute-start(bf16[32,1664]{1,0:T(8,128)(2,1)S(1)} %get-tuple-element.93.refs_0_), channel_id=1, source_target_pairs={{0,8},{1,9},{2,10},{3,11},{4,12},{5,13},{6,14},{7,15},{8,0},{9,1},... | collective-permute-start | bytes 319496 | tf_op jit(solution)/shard_map/ppermute | solution.py:388
  21.6 9.2 %collective-permute-start.6 = (bf16[32,1664]{1,0:T(8,128)(2,1)S(1)}, bf16[32,1664]{1,0:T(8,128)(2,1)S(1)}, u32[]{:S(2)}, u32[]{:S(2)}) collective-permute-start(bf16[32,1664]{1,0:T(8,128)(2,1)S(1)} %get-tuple-element.93.refs_0_), channel_id=1, source_target_pairs={{0,16},{1,17},{2,18},{3,19},{4,20},{5,21},{6,22},{7,23},{8,24},{9,... | collective-permute-start | bytes 319496 | tf_op jit(solution)/shard_map/ppermute | solution.py:388
  22.9 7.9 %collective-permute-start.7 = (bf16[32,1664]{1,0:T(8,128)(2,1)S(1)}, bf16[32,1664]{1,0:T(8,128)(2,1)S(1)}, u32[]{:S(2)}, u32[]{:S(2)}) collective-permute-start(bf16[32,1664]{1,0:T(8,128)(2,1)S(1)} %get-tuple-element.93.refs_0_), channel_id=1, source_target_pairs={{0,24},{1,25},{2,26},{3,27},{4,28},{5,29},{6,30},{7,31},{8,16},{9,... | collective-permute-start | bytes 319496 | tf_op jit(solution)/shard_map/ppermute | solution.py:388
  30.9 9.3 %collective-permute-start.10 = (bf16[4,32,1664]{2,1,0:T(8,128)(2,1)S(1)}, bf16[4,32,1664]{2,1,0:T(8,128)(2,1)S(1)}, u32[]{:S(2)}, u32[]{:S(2)}) collective-permute-start(bf16[4,32,1664]{2,1,0:T(8,128)(2,1)S(1)} %shard_map.181.refs_0_), channel_id=1, source_target_pairs={{0,4},{1,3},{2,6},{3,1},{4,0},{5,7},{6,2},{7,5},{8,12},{9,11},{10,... | collective-permute-start | bytes 1277960 | tf_op jit(solution)/shard_map/ppermute | solution.py:388
  31.4 13.0 %collective-permute-start.8 = (bf16[4,32,1664]{2,1,0:T(8,128)(2,1)S(1)}, bf16[4,32,1664]{2,1,0:T(8,128)(2,1)S(1)}, u32[]{:S(2)}, u32[]{:S(2)}) collective-permute-start(bf16[4,32,1664]{2,1,0:T(8,128)(2,1)S(1)} %collective-permute-done.3.refs_1_), channel_id=1, source_target_pairs={{0,4},{1,3},{2,6},{3,1},{4,0},{5,7},{6,2},{7,5},{8,12},{9,11},{10,... | collective-permute-start | bytes 1277960 | tf_op jit(solution)/shard_map/ppermute | solution.py:388
  32.9 11.5 %collective-permute-start.9 = (bf16[4,32,1664]{2,1,0:T(8,128)(2,1)S(1)}, bf16[4,32,1664]{2,1,0:T(8,128)(2,1)S(1)}, u32[]{:S(2)}, u32[]{:S(2)}) collective-permute-start(bf16[4,32,1664]{2,1,0:T(8,128)(2,1)S(1)} %shard_map.181.refs_0_), channel_id=1, source_target_pairs={{0,2},{1,5},{2,0},{3,7},{4,6},{5,1},{6,4},{7,3},{8,10},{9,13},{10,... | collective-permute-start | bytes 1277960 | tf_op jit(solution)/shard_map/ppermute | solution.py:388
  34.9 10.1 %collective-permute-start.12 = (bf16[4,32,1664]{2,1,0:T(8,128)(2,1)S(1)}, bf16[4,32,1664]{2,1,0:T(8,128)(2,1)S(1)}, u32[]{:S(2)}, u32[]{:S(2)}) collective-permute-start(bf16[4,32,1664]{2,1,0:T(8,128)(2,1)S(1)} %shard_map.179.refs_0_), channel_id=1, source_target_pairs={{0,1},{1,0},{2,3},{3,2},{4,5},{5,4},{6,7},{7,6},{8,9},{9,8},{10,11... | collective-permute-start | bytes 1277960 | tf_op jit(solution)/shard_map/ppermute | solution.py:388
  39.6 5.6 %collective-permute-start.13 = (bf16[4,32,1664]{2,1,0:T(8,128)(2,1)S(1)}, bf16[4,32,1664]{2,1,0:T(8,128)(2,1)S(1)}, u32[]{:S(2)}, u32[]{:S(2)}) collective-permute-start(bf16[4,32,1664]{2,1,0:T(8,128)(2,1)S(1)} %collective-permute-done.3.refs_1_), channel_id=1, source_target_pairs={{0,1},{1,0},{2,3},{3,2},{4,5},{5,4},{6,7},{7,6},{8,9},{9,8},{10,11... | collective-permute-start | bytes 1277960 | tf_op jit(solution)/shard_map/ppermute | solution.py:388
  40.2 5.3 %collective-permute-start.14 = (bf16[4,32,1664]{2,1,0:T(8,128)(2,1)S(1)}, bf16[4,32,1664]{2,1,0:T(8,128)(2,1)S(1)}, u32[]{:S(2)}, u32[]{:S(2)}) collective-permute-start(bf16[4,32,1664]{2,1,0:T(8,128)(2,1)S(1)} %collective-permute-done.4.refs_2_), channel_id=1, source_target_pairs={{0,1},{1,0},{2,3},{3,2},{4,5},{5,4},{6,7},{7,6},{8,9},{9,8},{10,11... | collective-permute-start | bytes 1277960 | tf_op jit(solution)/shard_map/ppermute | solution.py:388
  44.4 1.8 %collective-permute-start.15 = (bf16[4,32,1664]{2,1,0:T(8,128)(2,1)S(1)}, bf16[4,32,1664]{2,1,0:T(8,128)(2,1)S(1)}, u32[]{:S(2)}, u32[]{:S(2)}) collective-permute-start(bf16[4,32,1664]{2,1,0:T(8,128)(2,1)S(1)} %collective-permute-done.8.refs_3_), channel_id=1, source_target_pairs={{0,1},{1,0},{2,3},{3,2},{4,5},{5,4},{6,7},{7,6},{8,9},{9,8},{10,11... | collective-permute-start | bytes 1277960 | tf_op jit(solution)/shard_map/ppermute | solution.py:388
  44.4 11.3 %collective-permute-start.11 = (bf16[4,32,1664]{2,1,0:T(8,128)(2,1)S(1)}, bf16[4,32,1664]{2,1,0:T(8,128)(2,1)S(1)}, u32[]{:S(2)}, u32[]{:S(2)}) collective-permute-start(bf16[4,32,1664]{2,1,0:T(8,128)(2,1)S(1)} %collective-permute-done.9.refs_1_), channel_id=1, source_target_pairs={{0,4},{1,3},{2,6},{3,1},{4,0},{5,7},{6,2},{7,5},{8,12},{9,11},{10,... | collective-permute-start | bytes 1277960 | tf_op jit(solution)/shard_map/ppermute | solution.py:388
  44.9 11.0 %collective-permute-start.16 = (bf16[4,32,1664]{2,1,0:T(8,128)(2,1)S(1)}, bf16[4,32,1664]{2,1,0:T(8,128)(2,1)S(1)}, u32[]{:S(2)}, u32[]{:S(2)}) collective-permute-start(bf16[4,32,1664]{2,1,0:T(8,128)(2,1)S(1)} %shard_map.181.refs_0_), channel_id=1, source_target_pairs={{0,1},{1,0},{2,3},{3,2},{4,5},{5,4},{6,7},{7,6},{8,9},{9,8},{10,11... | collective-permute-start | bytes 1277960 | tf_op jit(solution)/shard_map/ppermute | solution.py:388
  45.2 10.7 %collective-permute-start.17 = (bf16[4,32,1664]{2,1,0:T(8,128)(2,1)S(1)}, bf16[4,32,1664]{2,1,0:T(8,128)(2,1)S(1)}, u32[]{:S(2)}, u32[]{:S(2)}) collective-permute-start(bf16[4,32,1664]{2,1,0:T(8,128)(2,1)S(1)} %collective-permute-done.9.refs_1_), channel_id=1, source_target_pairs={{0,1},{1,0},{2,3},{3,2},{4,5},{5,4},{6,7},{7,6},{8,9},{9,8},{10,11... | collective-permute-start | bytes 1277960 | tf_op jit(solution)/shard_map/ppermute | solution.py:388
  45.5 10.5 %collective-permute-start.18 = (bf16[4,32,1664]{2,1,0:T(8,128)(2,1)S(1)}, bf16[4,32,1664]{2,1,0:T(8,128)(2,1)S(1)}, u32[]{:S(2)}, u32[]{:S(2)}) collective-permute-start(bf16[4,32,1664]{2,1,0:T(8,128)(2,1)S(1)} %collective-permute-done.10.refs_2_), channel_id=1, source_target_pairs={{0,1},{1,0},{2,3},{3,2},{4,5},{5,4},{6,7},{7,6},{8,9},{9,8},{10,11... | collective-permute-start | bytes 1277960 | tf_op jit(solution)/shard_map/ppermute | solution.py:388
  55.7 1.8 %collective-permute-start.19 = (bf16[4,32,1664]{2,1,0:T(8,128)(2,1)S(1)}, bf16[4,32,1664]{2,1,0:T(8,128)(2,1)S(1)}, u32[]{:S(2)}, u32[]{:S(2)}) collective-permute-start(bf16[4,32,1664]{2,1,0:T(8,128)(2,1)S(1)} %collective-permute-done.11.refs_3_), channel_id=1, source_target_pairs={{0,1},{1,0},{2,3},{3,2},{4,5},{5,4},{6,7},{7,6},{8,9},{9,8},{10,11... | collective-permute-start | bytes 1277960 | tf_op jit(solution)/shard_map/ppermute | solution.py:388
  77.5 8.6 %collective-permute-start.20 = (bf16[2,2,4,32,1664]{4,3,2,1,0:T(8,128)(2,1)S(1)}, bf16[2,2,4,32,1664]{4,3,2,1,0:T(8,128)(2,1)S(1)}, u32[]{:S(2)}, u32[]{:S(2)}) collective-permute-start(bf16[2,2,4,32,1664]{4,3,2,1,0:T(8,128)(2,1)S(1)} %get-tuple-element.119), channel_id=1, source_target_pairs={{0,1},{1,0},{2,3},{3,2},{4,5},{5,4},{6,7},{7,6},{8,9},{9,8},{10,11... | collective-permute-start | bytes 5111816 | tf_op jit(solution)/shard_map/ppermute | solution.py:388
  86.5 12.8 %collective-permute-start.21 = (bf16[2,4,32,1664]{3,2,1,0:T(8,128)(2,1)S(1)}, bf16[2,4,32,1664]{3,2,1,0:T(8,128)(2,1)S(1)}, u32[]{:S(2)}, u32[]{:S(2)}) collective-permute-start(bf16[2,4,32,1664]{3,2,1,0:T(8,128)(2,1)S(1)} %get-tuple-element.127), channel_id=1, source_target_pairs={{0,2},{1,5},{2,0},{3,7},{4,6},{5,1},{6,4},{7,3},{8,10},{9,13},{10,... | collective-permute-start | bytes 2555912 | tf_op jit(solution)/shard_map/ppermute | solution.py:388
  99.3 3.6 %collective-permute-start.22 = (bf16[2,2,4,32,1664]{4,3,2,1,0:T(8,128)(2,1)S(1)}, bf16[2,2,4,32,1664]{4,3,2,1,0:T(8,128)(2,1)S(1)}, u32[]{:S(2)}, u32[]{:S(2)}) collective-permute-start(bf16[2,2,4,32,1664]{4,3,2,1,0:T(8,128)(2,1)S(1)} %get-tuple-element.128), channel_id=1, source_target_pairs={{0,1},{1,0},{2,3},{3,2},{4,5},{5,4},{6,7},{7,6},{8,9},{9,8},{10,11... | collective-permute-start | bytes 5111816 | tf_op jit(solution)/shard_map/ppermute | solution.py:388
  103.3 17.3 %collective-permute-start.23 = (bf16[2,4,32,1664]{3,2,1,0:T(8,128)(2,1)S(1)}, bf16[2,4,32,1664]{3,2,1,0:T(8,128)(2,1)S(1)}, u32[]{:S(2)}, u32[]{:S(2)}) collective-permute-start(bf16[2,4,32,1664]{3,2,1,0:T(8,128)(2,1)S(1)} %get-tuple-element.136), channel_id=1, source_target_pairs={{0,2},{1,5},{2,0},{3,7},{4,6},{5,1},{6,4},{7,3},{8,10},{9,13},{10,... | collective-permute-start | bytes 2555912 | tf_op jit(solution)/shard_map/ppermute | solution.py:388
  104.3 12.8 %collective-permute-start.24 = (bf16[4,32,1664]{2,1,0:T(8,128)(2,1)S(1)}, bf16[4,32,1664]{2,1,0:T(8,128)(2,1)S(1)}, u32[]{:S(2)}, u32[]{:S(2)}) collective-permute-start(bf16[4,32,1664]{2,1,0:T(8,128)(2,1)S(1)} %get-tuple-element.131), channel_id=1, source_target_pairs={{0,4},{1,3},{2,6},{3,1},{4,0},{5,7},{6,2},{7,5},{8,12},{9,11},{10,... | collective-permute-start | bytes 1277960 | tf_op jit(solution)/shard_map/ppermute | solution.py:388
  120.8 14.4 %collective-permute-start.25 = (bf16[4,32,1664]{2,1,0:T(8,128)(2,1)S(1)}, bf16[4,32,1664]{2,1,0:T(8,128)(2,1)S(1)}, u32[]{:S(2)}, u32[]{:S(2)}) collective-permute-start(bf16[4,32,1664]{2,1,0:T(8,128)(2,1)S(1)} %get-tuple-element.141), channel_id=1, source_target_pairs={{0,4},{1,3},{2,6},{3,1},{4,0},{5,7},{6,2},{7,5},{8,12},{9,11},{10,... | collective-permute-start | bytes 1277960 | tf_op jit(solution)/shard_map/ppermute | solution.py:388
  121.9 16.5 %collective-permute-start.29 = (bf16[32,1664]{1,0:T(8,128)(2,1)S(1)}, bf16[32,1664]{1,0:T(8,128)(2,1)S(1)}, u32[]{:S(2)}, u32[]{:S(2)}) collective-permute-start(bf16[32,1664]{1,0:T(8,128)(2,1)S(1)} %get-tuple-element.159), channel_id=1, source_target_pairs={{0,8},{1,9},{2,10},{3,11},{4,12},{5,13},{6,14},{7,15},{8,0},{9,1},... | collective-permute-start | bytes 319496 | tf_op jit(solution)/shard_map/ppermute | solution.py:388
  126.5 14.0 %collective-permute-start.30 = (bf16[32,1664]{1,0:T(8,128)(2,1)S(1)}, bf16[32,1664]{1,0:T(8,128)(2,1)S(1)}, u32[]{:S(2)}, u32[]{:S(2)}) collective-permute-start(bf16[32,1664]{1,0:T(8,128)(2,1)S(1)} %get-tuple-element.160), channel_id=1, source_target_pairs={{0,16},{1,17},{2,18},{3,19},{4,20},{5,21},{6,22},{7,23},{8,24},{9,... | collective-permute-start | bytes 319496 | tf_op jit(solution)/shard_map/ppermute | solution.py:388
  128.0 12.5 %collective-permute-start.31 = (bf16[32,1664]{1,0:T(8,128)(2,1)S(1)}, bf16[32,1664]{1,0:T(8,128)(2,1)S(1)}, u32[]{:S(2)}, u32[]{:S(2)}) collective-permute-start(bf16[32,1664]{1,0:T(8,128)(2,1)S(1)} %get-tuple-element.161), channel_id=1, source_target_pairs={{0,24},{1,25},{2,26},{3,27},{4,28},{5,29},{6,30},{7,31},{8,16},{9,... | collective-permute-start | bytes 319496 | tf_op jit(solution)/shard_map/ppermute | solution.py:388
  135.4 5.1 %collective-permute-start.26 = (bf16[32,1664]{1,0:T(8,128)(2,1)S(1)}, bf16[32,1664]{1,0:T(8,128)(2,1)S(1)}, u32[]{:S(2)}, u32[]{:S(2)}) collective-permute-start(bf16[32,1664]{1,0:T(8,128)(2,1)S(1)} %get-tuple-element.153), channel_id=1, source_target_pairs={{0,8},{1,9},{2,10},{3,11},{4,12},{5,13},{6,14},{7,15},{8,0},{9,1},... | collective-permute-start | bytes 319496 | tf_op jit(solution)/shard_map/ppermute | solution.py:388
  136.0 10.1 %collective-permute-start.27 = (bf16[32,1664]{1,0:T(8,128)(2,1)S(1)}, bf16[32,1664]{1,0:T(8,128)(2,1)S(1)}, u32[]{:S(2)}, u32[]{:S(2)}) collective-permute-start(bf16[32,1664]{1,0:T(8,128)(2,1)S(1)} %get-tuple-element.154), channel_id=1, source_target_pairs={{0,16},{1,17},{2,18},{3,19},{4,20},{5,21},{6,22},{7,23},{8,24},{9,... | collective-permute-start | bytes 319496 | tf_op jit(solution)/shard_map/ppermute | solution.py:388
  138.4 7.7 %collective-permute-start.28 = (bf16[32,1664]{1,0:T(8,128)(2,1)S(1)}, bf16[32,1664]{1,0:T(8,128)(2,1)S(1)}, u32[]{:S(2)}, u32[]{:S(2)}) collective-permute-start(bf16[32,1664]{1,0:T(8,128)(2,1)S(1)} %get-tuple-element.155), channel_id=1, source_target_pairs={{0,24},{1,25},{2,26},{3,27},{4,28},{5,29},{6,30},{7,31},{8,16},{9,... | collective-permute-start | bytes 319496 | tf_op jit(solution)/shard_map/ppermute | solution.py:388
  (1 other events, 0.7 us)

commit v7 on v6

--- a/solution.py
+++ b/solution.py
@@ -14,7 +14,7 @@
 PART = 256
 MIB = 1024 * 1024
 HINT = 4
-ROOM_0, ROOM_1, ROOM_2, ROOM_3, ROOM_4, ROOM_5, ROOM_SMALL = 8, 13, 6, 8, 8, 8, 12
+ROOM_0, ROOM_1, ROOM_2, ROOM_3, ROOM_4, ROOM_5, ROOM_SMALL = 6, 4, 5, 3, 6, 5, 10
 LOW = jnp.bfloat16
 FULL = jnp.float32
 
@@ -83,7 +83,7 @@
     return pl.ds(pl.multiple_of(step * rows, rows), rows)
 
 
-def prepare(size, info_ref, x_ref, go_ref, gs_ref, mel_ref, low0_ref, cond_ref, frames_ref, proj1_ref):
+def prepare(size, info_ref, x_ref, go_ref, gs_ref, mel_ref, low0_ref, place_ref, proj1_ref):
     step = pl.program_id(0)
     tile = rows_of(step, TILE)
     mask = mask_of(info_ref, step * TILE, TILE)
@@ -91,14 +91,14 @@
     proj1_ref[tile, : size.channels] = masked(go_ref[...], mask)
     proj1_ref[tile, size.channels :] = masked(gs_ref[...], mask)
     frames = frames_of(info_ref, step * TILE, TILE)
-    frames_ref[tile] = frames
-    cond_ref[tile] = dot(frames, mel_ref[...]).astype(LOW)
-
-
-def forward_0(size, wires, info_ref, low0_ref, cond_ref, *refs):
+    place_ref[tile, : size.extra_width] = dot(frames, mel_ref[...]).astype(LOW)
+    place_ref[tile, size.extra_width :] = frames
+
+
+def forward_0(size, wires, info_ref, low0_ref, place_ref, *refs):
     count = 8 if wires.direct else 1
     pieces, refs = refs[:count], refs[count:]
-    low1_ref, prev1_ref, gated_ref, slope_ref, w_ref, bias_s, carry_s = refs
+    taps1_ref, gated_ref, slope_ref, w_ref, bias_s, carry_s = refs
     step = pl.program_id(0)
     channels = size.channels
 
@@ -113,7 +113,7 @@
     low = low0_ref[tile]
     before = low0_ref[rows_of(jnp.maximum(step - 1, 0), TILE)]
     prev = jnp.where(step > 0, before, jnp.zeros_like(before))
-    taps = jnp.concatenate([prev, low, cond_ref[tile]], axis=1)
+    taps = jnp.concatenate([prev, low, place_ref[tile, : size.extra_width]], axis=1)
     for side in range(2):
         first, second, gated, slope_a, slope_b = gates(taps, w_ref, size, side)
         gated_ref[tile, first] = gated.astype(LOW)
@@ -121,14 +121,16 @@
         slope_ref[tile, second] = slope_b.astype(LOW)
     moved = dot_cols(gated_ref[tile], w_ref[:channels, :channels])
     low = ((low.astype(FULL) + moved + bias_s[...]) * mask).astype(LOW)
-    low1_ref[tile] = low
     wide = low.astype(FULL)
     place = lax.broadcasted_iota(jnp.int32, (TILE, 1), 0)
-    prev1_ref[tile] = jnp.where(place == 0, carry_s[7:8], pltpu.roll(wide, 1, 0)).astype(LOW)
+    prev = jnp.where(place == 0, carry_s[7:8], pltpu.roll(wide, 1, 0)).astype(LOW)
+    taps1_ref[tile, :channels] = prev
+    taps1_ref[tile, channels : 2 * channels] = low
+    taps1_ref[tile, 2 * channels :] = place_ref[tile]
     carry_s[...] = wide[TILE - 8 :]
 
 
-def layer_1(size, wires, steps, info_ref, low_ref, prev_ref, cond_ref, frames_ref, proj_ref, mel_ref, *refs):
+def layer_1(size, wires, steps, info_ref, taps_ref, proj_ref, *refs):
     count = 8 if wires.direct else 1
     pieces, refs = refs[:count], refs[count:]
     gated_ref, pre_ref, w_ref, here_ref, away_ref, melg_ref = refs
@@ -143,7 +145,7 @@
     @pl.when(step < steps)
     def _():
         tile = rows_of(step, TILE)
-        taps = jnp.concatenate([prev_ref[tile], low_ref[tile], cond_ref[tile]], axis=1)
+        taps = taps_ref[tile, : size.pack - channels]
         grad_gated = dot(proj_ref[tile], w_ref[:, :channels])
         for side in range(2):
             first, second, gated, slope_a, slope_b = gates(taps, w_ref, size, side)
@@ -156,11 +158,11 @@
         part = rows_of(step - steps, PART)
         pre = pre_ref[:, part]
         proj = proj_ref[:, part]
+        both = dot_rows(pre, taps_ref[...])
         grads = [
             dot_rows(proj, gated_ref[...]),
-            dot_rows(pre, prev_ref[...]),
-            dot_rows(pre, low_ref[...]),
-            extra_grads(size, pre, proj, frames_ref, mel_ref, w_ref[part, size.extra :], melg_ref),
+            both[:, : 2 * channels],
+            extra_grads(size, both[:, 2 * channels :], proj, w_ref[part, size.extra :], melg_ref),
         ]
         wires.put_apart(info_ref, step - steps, grads, here_ref, away_ref)
 
@@ -170,9 +172,8 @@
     return high, (value - high.astype(FULL)).astype(LOW)
 
 
-def extra_grads(size, pre, proj, frames_ref, mel_ref, cond_weight, melg_ref):
-    sums = in_two(dot_rows(pre, frames_ref[...]))
-    extra = sum(dot(half, mel_ref[...]) for half in sums)
+def extra_grads(size, both, proj, cond_weight, melg_ref):
+    extra, sums = both[:, : size.extra_width], in_two(both[:, size.extra_width :])
     melg_ref[...] += sum(dot_rows(half, cond_weight) for half in sums)
     total = jnp.sum(proj.astype(FULL), axis=0, keepdims=True)
     bias = jnp.broadcast_to(total, (LANES, total.shape[1])).T[:, 0:1]
@@ -180,16 +181,17 @@
     return jnp.where(column == size.mel + 1, bias, extra)
 
 
-def backward_0(size, info_ref, pre1_ref, w1_ref, w0_ref, proj1_ref, slope_ref, proj_ref, pre0_ref, carry_ref):
+def backward_0(size, last, info_ref, pre1_ref, w1_ref, w0_ref, proj1_ref, slope_ref, *refs):
+    before, (proj_ref, pre0_ref, carry_ref) = refs[:-3], refs[-3:]
     step = pl.program_id(0)
     channels = size.channels
-    index = pl.num_programs(0) - 1 - step
+    index = last - step
     tile = rows_of(index, TILE)
     mask = mask_of(info_ref, index * TILE, TILE)
 
     @pl.when(step == 0)
     def _():
-        carry_ref[...] = jnp.zeros_like(carry_ref)
+        carry_ref[...] = before[2][...] if before else jnp.zeros_like(carry_ref)
 
     pre1 = pre1_ref[tile]
     early = dot(pre1, w1_ref[:, size.early : size.now])
@@ -198,14 +200,25 @@
     carry_ref[...] = early[:8]
     now = dot(pre1, w1_ref[:, size.now : size.extra])
     res = ((proj1_ref[tile, :channels].astype(FULL) + now + later) * mask).astype(LOW)
-    proj = jnp.concatenate([res, proj1_ref[tile, channels:]], axis=1)
-    proj_ref[tile] = proj
-    grad_gated = dot(proj, w0_ref[:, :channels])
+    proj_ref[tile, :channels] = res
+    proj_ref[tile, channels:] = proj1_ref[tile, channels:]
+    grad_gated = dot(proj_ref[tile], w0_ref[:, :channels])
     for half in (slice(0, channels), slice(channels, 2 * channels)):
         pre0_ref[tile, half] = (grad_gated * slope_ref[tile, half].astype(FULL)).astype(LOW)
 
 
-def weights_0(size, wires, info_ref, pre_ref, proj_ref, x_ref, gated_ref, frames_ref, mel_ref, w_ref, here_ref, away_ref, melg_ref):
+def weights_0_early(size, wires, info_ref, pre_ref, proj_ref, x_ref, gated_ref, here_ref, away_ref):
+    step = pl.program_id(0)
+    part = rows_of(step, PART)
+    shift = FIRST_DILATION
+    grads = [
+        dot_rows(proj_ref[:, part], gated_ref[...]),
+        dot_rows(pre_ref[shift:, part], x_ref[: x_ref.shape[0] - shift]),
+    ]
+    wires.put_apart(info_ref, step, grads, here_ref, away_ref)
+
+
+def weights_0_now(size, wires, info_ref, pre_ref, proj_ref, x_ref, place_ref, w_ref, here_ref, away_ref, melg_ref):
     step = pl.program_id(0)
 
     @pl.when(step == 0)
@@ -214,13 +227,9 @@
 
     part = rows_of(step, PART)
     pre = pre_ref[:, part]
-    proj = proj_ref[:, part]
-    shift = FIRST_DILATION
     grads = [
-        dot_rows(proj, gated_ref[...]),
-        dot_rows(pre[shift:], x_ref[: x_ref.shape[0] - shift]),
         dot_rows(pre, x_ref[...]),
-        extra_grads(size, pre, proj, frames_ref, mel_ref, w_ref[part, size.extra :], melg_ref),
+        extra_grads(size, dot_rows(pre, place_ref[...]), proj_ref[:, part], w_ref[part, size.extra :], melg_ref),
     ]
     wires.put_apart(info_ref, step, grads, here_ref, away_ref)
 
@@ -235,7 +244,7 @@
     sg_ref[...] = grad * mask_of(info_ref, step * TILE, TILE)
 
 
-def forward_outputs(size, info_ref, low1_ref, gated0_ref, gated1_ref, w0_ref, w1_ref, res_ref, skip_ref, bias_s):
+def forward_outputs(size, info_ref, taps1_ref, gated0_ref, gated1_ref, w0_ref, w1_ref, res_ref, skip_ref, bias_s):
     step = pl.program_id(0)
     channels = size.channels
 
@@ -247,7 +256,7 @@
     tile = rows_of(step, TILE)
     mask = mask_of(info_ref, step * TILE, TILE)
     res = dot_cols(gated1_ref[tile], w1_ref[:channels, :channels]) + bias_s[:, :channels]
-    res_ref[...] = ((low1_ref[tile].astype(FULL) + res) * mask).astype(LOW)
+    res_ref[...] = ((taps1_ref[tile, channels : 2 * channels].astype(FULL) + res) * mask).astype(LOW)
     skip = dot_cols(gated0_ref[tile], w0_ref[channels:, :channels])
     skip = skip + dot_cols(gated1_ref[tile], w1_ref[channels:, :channels])
     skip_ref[...] = ((skip + bias_s[:, channels:]) * mask).astype(LOW)
@@ -264,6 +273,13 @@
     wide_s[:frames, :mel] = mel_ref[...].astype(FULL)
     wide_s[:frames, mel : mel + 1] = jnp.ones((frames, 1), FULL)
     table_ref[...] = wide_s[...].astype(LOW)
+
+
+def add_both(left_a, right_a, left_b, right_b, *refs):
+    cut = left_a.shape[-1]
+    for index, ref in enumerate(refs):
+        ref[..., :cut] = add_low(left_a[index], right_a[index])
+        ref[..., cut:] = add_low(left_b[index], right_b[index])
 
 
 def put_side_by_side(*refs):
@@ -327,7 +343,7 @@
     )(*operands)
 
 
-def call(kernel, grid, info, operands, outs, scratch, flops, room):
+def call(kernel, grid, info, operands, outs, scratch, flops, room, onto=None):
     arrays = [x if spec else pltpu.with_memory_space_constraint(x, pltpu.VMEM) for x, spec in operands]
     shapes = [x if spec else pltpu.VMEM(x.shape, x.dtype) for x, spec in outs]
     moved = sum(x.size * x.dtype.itemsize for x, spec in (*operands, *outs) if spec)
@@ -341,6 +357,7 @@
             scratch_shapes=scratch,
         ),
         out_shape=shapes,
+        input_output_aliases=onto or {},
         compiler_params=pltpu.CompilerParams(
             vmem_limit_bytes=room * MIB, dimension_semantics=("arbitrary",)
         ),
@@ -543,12 +560,12 @@
     near1 = wires.spread([own1] * wires.rest)
     mel_table, *near1 = lax.optimization_barrier((mel_table, *near1))
     mine1 = side_by_side(near1)
-    low0, cond, frames, proj1 = call(
+    low0, place, proj1 = call(
         functools.partial(prepare, size),
         steps,
         info,
         [*((at_home(value), tiled(channels)) for value in (x, go, gs)), (mel_table, table)],
-        kept(channels, LANES, LANES, gate),
+        kept(channels, size.extra_width + LANES, gate),
         [],
         macs,
         ROOM_0,
@@ -557,24 +574,23 @@
     far0 = wires.hop(one0, wires.second)
     one1, two1 = wires.hop(mine1, wires.first), wires.hop(mine1, wires.second)
     far0, one1, two1, low0 = lax.optimization_barrier((far0, one1, two1, low0))
-    low1, prev1, gated0, slope0, w0 = call(
+    taps1, gated0, slope0, w0 = call(
         functools.partial(forward_0, size, wires),
         steps,
         info,
-        keep(low0, cond, *wires.passed(mine0, one0, two0, far0)),
-        [*kept(channels, channels, channels, gate), whole_w],
+        keep(low0, place, *wires.passed(mine0, one0, two0, far0)),
+        [*kept(gate + size.extra_width + LANES, channels, gate), whole_w],
         [pltpu.VMEM((1, channels), FULL), pltpu.VMEM((8, channels), FULL)],
         10 * macs,
         ROOM_0,
     )
     far1 = wires.hop(one1, wires.second)
-    far1, low1 = lax.optimization_barrier((far1, low1))
+    far1, taps1 = lax.optimization_barrier((far1, taps1))
     gated1, pre1, w1, here1, away1, melg1 = call(
         functools.partial(layer_1, size, wires, steps),
         steps + parts,
         info,
-        [*keep(low1, prev1, cond, frames, proj1), (mel_table, table)]
-        + keep(*wires.passed(mine1, one1, two1, far1)),
+        keep(taps1, proj1, *wires.passed(mine1, one1, two1, far1)),
         [*kept(channels, gate), whole_w, *wires.apart(size.pack), melg],
         [],
         24 * macs,
@@ -584,40 +600,70 @@
         here1, away1 = wires.by_distance(here1)
     came1 = wires.hop(away1, wires.sibling)
 
-    proj0, pre0 = call(
-        functools.partial(backward_0, size),
-        steps,
+    carry = (shape_of(8, channels, dtype=FULL), None)
+    begun = call(
+        functools.partial(backward_0, size, steps - 1),
+        steps - steps // 2,
         info,
         keep(pre1, w1, w0, proj1, slope0),
-        kept(gate, gate),
-        [pltpu.VMEM((8, channels), FULL)],
-        12 * macs,
+        [*kept(gate, gate), carry],
+        [],
+        6 * macs,
         ROOM_2,
     )
     stay1, leave1 = plain(add_and_part, (here1, came1), [half_shape] * 2)
-    pre0, stay1, leave1 = lax.optimization_barrier((pre0, stay1, leave1))
+    begun, stay1, leave1 = lax.optimization_barrier((begun, stay1, leave1))
     came1 = wires.hop(leave1, wires.first)
-
-    here0, away0, melg0 = call(
-        functools.partial(weights_0, size, wires),
+    proj0, pre0, _ = call(
+        functools.partial(backward_0, size, steps // 2 - 1),
+        steps // 2,
+        info,
+        keep(pre1, w1, w0, proj1, slope0, *begun),
+        [*kept(gate, gate), carry],
+        [],
+        6 * macs,
+        ROOM_2,
+        {6: 0, 7: 1},
+    )
+
+    cut = lambda depth, *lead: shape_of(*lead, wires.rest, rows, depth)
+    depths = (size.now, size.pack - size.now)
+    here_a, away_a = call(
+        functools.partial(weights_0_early, size, wires),
         parts,
         info,
-        [*keep(pre0, proj0, low0, gated0, frames), (mel_table, table), (w0, None)],
-        [*wires.apart(size.pack), melg],
+        keep(pre0, proj0, low0, gated0),
+        wires.apart(depths[0]),
         [],
-        12 * macs,
+        7 * macs,
         ROOM_3,
     )
+    here_b, away_b, melg0 = call(
+        functools.partial(weights_0_now, size, wires),
+        parts,
+        info,
+        keep(pre0, proj0, low0, place, w0),
+        [*wires.apart(depths[1]), melg],
+        [],
+        5 * macs,
+        ROOM_3,
+    )
     if not wires.direct:
-        here0, away0 = wires.by_distance(here0)
-    away0, came1 = lax.optimization_barrier((away0, came1))
-    came0 = wires.hop(away0, wires.sibling)
+        here_a, away_a = wires.by_distance(here_a)
+        here_b, away_b = wires.by_distance(here_b)
+    came_a = wires.hop(away_a, wires.sibling)
+    came_a, here_b = lax.optimization_barrier((came_a, here_b))
+    away_b, came1 = lax.optimization_barrier((away_b, came1))
+    came_b = wires.hop(away_b, wires.sibling)
+    stay_a, leave_a = plain(add_and_part, (here_a, came_a), [cut(depths[0], 2)] * 2)
+    came_a = wires.hop(leave_a, wires.first)
+    stay1, leave_a = lax.optimization_barrier((stay1, leave_a))
     stay1, leave1 = plain(add_and_part, (stay1, came1), [last_shape] * 2)
     came1 = wires.hop(leave1, wires.second)
-    came0, leave1 = lax.optimization_barrier((came0, leave1))
-    stay0, leave0 = plain(add_and_part, (here0, came0), [half_shape] * 2)
-    pre0, stay0, leave0 = lax.optimization_barrier((pre0, stay0, leave0))
-    came0 = wires.hop(leave0, wires.first)
+    came_b, leave1 = lax.optimization_barrier((came_b, leave1))
+    stay_b, leave_b = plain(add_and_part, (here_b, came_b), [cut(depths[1], 2)] * 2)
+    came_b = wires.hop(leave_b, wires.first)
+    pre0, taps1, leave_b = lax.optimization_barrier((pre0, taps1, leave_b))
 
     (samples_grad,) = call(
         functools.partial(samples_gradient, size),
@@ -629,22 +675,22 @@
         8 * macs,
         ROOM_4,
     )
-    came0, came1, samples_grad = lax.optimization_barrier((came0, came1, samples_grad))
-    parts1 = wires.spread(plain(add_and_part, (stay1, came1), blocks_shape))
-    stay0, leave0 = plain(add_and_part, (stay0, came0), [last_shape] * 2)
-    low1, stay0, leave0 = lax.optimization_barrier((low1, stay0, leave0))
-    came0 = wires.hop(leave0, wires.second)
     residual_out, skip_output_sum = call(
         functools.partial(forward_outputs, size),
         steps,
         info,
-        keep(low1, gated0, gated1, w0, w1),
+        keep(taps1, gated0, gated1, w0, w1),
         [blocked, blocked],
         [pltpu.VMEM((1, gate), FULL)],
         8 * macs,
         ROOM_5,
     )
-    came0, residual_out = lax.optimization_barrier((came0, residual_out))
+    came_a, came_b, came1, samples_grad, residual_out = lax.optimization_barrier(
+        (came_a, came_b, came1, samples_grad, residual_out)
+    )
+    parts1 = wires.spread(plain(add_and_part, (stay1, came1), blocks_shape))
+    stay0, leave0 = plain(add_both, (stay_a, came_a, stay_b, came_b), [last_shape] * 2)
+    came0 = wires.hop(leave0, wires.second)
     parts0 = wires.spread(plain(add_and_part, (stay0, came0), blocks_shape))
     grads = plain(
         functools.partial(unpack_layers, layers, mel_count),

time: 147 us -> 143 us (0.973)
  waiting for transfers between devices: 41.1 us -> 36.3 us
  Pallas kernels: 68.8 us -> 70.6 us
    ppermute x32 -> x34, waiting for transfers between devices: 41.1 us -> 36.3 us  [hop(): return lax.ppermute(value, AXES, pairs)]
    pallas_call x7 -> x9, Pallas kernels: 65 us -> 66.8 us  [call(): pl.pallas_call(kernel, grid_spec=pltpu.PrefetchScalarGridSpec(num_scalar_...]
    ppermute x32 -> x34, starting transfers between devices: 33.8 us -> 32.4 us  [hop(): return lax.ppermute(value, AXES, pairs)]
  transfers between devices with their start and end apart: 32 -> 34, of which waited for: 12 -> 12; matrix products, arithmetic and copies ran while one was open for 0% -> 0% of each run, Pallas kernels for 31% -> 34%
where the time goes in v7:
time: 143 us
  Pallas kernels  70.6 us (49%)
  waiting for transfers between devices  36.3 us (25%)
  starting transfers between devices  32.4 us (23%)
  between operations  2.14 us (1%)
    pallas_call x9, Pallas kernels, call(): pl.pallas_call(kernel, grid_spec=pltpu.PrefetchScalarGridSpec(num_scalar_...  66.8 us
    ppermute x34, waiting for transfers between devices, hop(): return lax.ppermute(value, AXES, pairs)  36.3 us
    ppermute x34, starting transfers between devices, hop(): return lax.ppermute(value, AXES, pairs)  32.4 us
  transfers between devices with their start and end apart: 34, of which 12 were waited for; matrix products, arithmetic and copies ran while one was open for 0% of the time, Pallas kernels for 34%

profile of v7, /device:TPU:0, one launch (start us, length us, event | category | flops | bytes accessed | tf_op | source)
XLA Modules:
  0.0 142.8 jit_solution(17533400289468965430)
XLA Ops:
  0.6 1.2 shard_map.178
  1.8 5.1 %collective-permute-start.2 = (bf16[32,1664]{1,0:T(8,128)(2,1)S(1)}, bf16[32,1664]{1,0:T(8,128)(2,1)S(1)}, u32[]{:S(2)}, u32[]{:S(2)}) collective-permute-start(bf16[32,1664]{1,0:T(8,128)(2,1)S(1)} %get-tuple-element.94.refs_0_), channel_id=1, source_target_pairs={{0,24},{1,25},{2,26},{3,27},{4,28},{5,29},{6,30},{7,31},{8,16},{9,... | collective-permute-start | bytes 319496 | tf_op jit(solution)/shard_map/ppermute | solution.py:405
  7.6 3.3 %collective-permute-done.2.refs_3_ = bf16[32,1664]{1,0:T(8,128)(2,1)S(1)} collective-permute-done((bf16[32,1664]{1,0:T(8,128)(2,1)S(1)}, bf16[32,1664]{1,0:T(8,128)(2,1)S(1)}, u32[]{:S(2)}, u32[]{:S(2)}) %collective-permute-start.2) | collective-permute-done | bytes 106528 | tf_op jit(solution)/shard_map/ppermute | solution.py:405
  10.9 5.1 %collective-permute-done.1.refs_2_ = bf16[32,1664]{1,0:T(8,128)(2,1)S(1)} collective-permute-done((bf16[32,1664]{1,0:T(8,128)(2,1)S(1)}, bf16[32,1664]{1,0:T(8,128)(2,1)S(1)}, u32[]{:S(2)}, u32[]{:S(2)}) %collective-permute-start.1) | collective-permute-done | bytes 106528 | tf_op jit(solution)/shard_map/ppermute | solution.py:405
  16.0 1.6 %collective-permute-start.4 = (bf16[4,32,1664]{2,1,0:T(8,128)(2,1)S(1)}, bf16[4,32,1664]{2,1,0:T(8,128)(2,1)S(1)}, u32[]{:S(2)}, u32[]{:S(2)}) collective-permute-start(bf16[4,32,1664]{2,1,0:T(8,128)(2,1)S(1)} %shard_map.179.refs_0_), channel_id=1, source_target_pairs={{0,4},{1,3},{2,6},{3,1},{4,0},{5,7},{6,2},{7,5},{8,12},{9,11},{10,... | collective-permute-start | bytes 1277960 | tf_op jit(solution)/shard_map/ppermute | solution.py:405
  17.6 1.5 %collective-permute-start.3 = (bf16[4,32,1664]{2,1,0:T(8,128)(2,1)S(1)}, bf16[4,32,1664]{2,1,0:T(8,128)(2,1)S(1)}, u32[]{:S(2)}, u32[]{:S(2)}) collective-permute-start(bf16[4,32,1664]{2,1,0:T(8,128)(2,1)S(1)} %shard_map.179.refs_0_), channel_id=1, source_target_pairs={{0,2},{1,5},{2,0},{3,7},{4,6},{5,1},{6,4},{7,3},{8,10},{9,13},{10,... | collective-permute-start | bytes 1277960 | tf_op jit(solution)/shard_map/ppermute | solution.py:405
  19.7 2.5 %collective-permute-start.7 = (bf16[32,1664]{1,0:T(8,128)(2,1)S(1)}, bf16[32,1664]{1,0:T(8,128)(2,1)S(1)}, u32[]{:S(2)}, u32[]{:S(2)}) collective-permute-start(bf16[32,1664]{1,0:T(8,128)(2,1)S(1)} %get-tuple-element.99.refs_0_), channel_id=1, source_target_pairs={{0,24},{1,25},{2,26},{3,27},{4,28},{5,29},{6,30},{7,31},{8,16},{9,... | collective-permute-start | bytes 319496 | tf_op jit(solution)/shard_map/ppermute | solution.py:405
  22.3 1.9 %collective-permute-start.5 = (bf16[32,1664]{1,0:T(8,128)(2,1)S(1)}, bf16[32,1664]{1,0:T(8,128)(2,1)S(1)}, u32[]{:S(2)}, u32[]{:S(2)}) collective-permute-start(bf16[32,1664]{1,0:T(8,128)(2,1)S(1)} %get-tuple-element.99.refs_0_), channel_id=1, source_target_pairs={{0,8},{1,9},{2,10},{3,11},{4,12},{5,13},{6,14},{7,15},{8,0},{9,1},... | collective-permute-start | bytes 319496 | tf_op jit(solution)/shard_map/ppermute | solution.py:405
  24.2 3.2 %collective-permute-done.7.refs_3_ = bf16[32,1664]{1,0:T(8,128)(2,1)S(1)} collective-permute-done((bf16[32,1664]{1,0:T(8,128)(2,1)S(1)}, bf16[32,1664]{1,0:T(8,128)(2,1)S(1)}, u32[]{:S(2)}, u32[]{:S(2)}) %collective-permute-start.7) | collective-permute-done | bytes 106528 | tf_op jit(solution)/shard_map/ppermute | solution.py:405
  27.4 3.4 %collective-permute-done.6.refs_2_ = bf16[32,1664]{1,0:T(8,128)(2,1)S(1)} collective-permute-done((bf16[32,1664]{1,0:T(8,128)(2,1)S(1)}, bf16[32,1664]{1,0:T(8,128)(2,1)S(1)}, u32[]{:S(2)}, u32[]{:S(2)}) %collective-permute-start.6) | collective-permute-done | bytes 106528 | tf_op jit(solution)/shard_map/ppermute | solution.py:405
  31.4 1.5 %collective-permute-start.10 = (bf16[4,32,1664]{2,1,0:T(8,128)(2,1)S(1)}, bf16[4,32,1664]{2,1,0:T(8,128)(2,1)S(1)}, u32[]{:S(2)}, u32[]{:S(2)}) collective-permute-start(bf16[4,32,1664]{2,1,0:T(8,128)(2,1)S(1)} %shard_map.181.refs_0_), channel_id=1, source_target_pairs={{0,4},{1,3},{2,6},{3,1},{4,0},{5,7},{6,2},{7,5},{8,12},{9,11},{10,... | collective-permute-start | bytes 1277960 | tf_op jit(solution)/shard_map/ppermute | solution.py:405
  34.9 4.8 %shard_map.182 = (bf16[2048,512]{1,0:T(8,128)(2,1)S(1)}, bf16[2048,256]{1,0:T(8,128)(2,1)S(1)}, bf16[2048,1024]{1,0:T(8,128)(2,1)S(1)}) custom-call(s32[4]{0:T(128)S(1)} %pad_add_fusion.info_ref, bf16[2048,512]{1,0:T(8,128)(2,1)} %bitcast.19, bf16[2048,512]{1,0:T(8,128)(2,1)} %bitcast.20, bf16[2048,512]{1,0:T(8,128)(2,1)} %bitcast.21, ...), custom_call_target="tpu_custom_call" | custom-call | flops 134217728 | bytes 1581056 | tf_op jit(solution)/shard_map/pallas_call | solution.py:350
  40.2 2.9 %collective-permute-done.8.refs_3_ = bf16[4,32,1664]{2,1,0:T(8,128)(2,1)S(1)} collective-permute-done((bf16[4,32,1664]{2,1,0:T(8,128)(2,1)S(1)}, bf16[4,32,1664]{2,1,0:T(8,128)(2,1)S(1)}, u32[]{:S(2)}, u32[]{:S(2)}) %collective-permute-start.8) | collective-permute-done | bytes 426016 | tf_op jit(solution)/shard_map/ppermute | solution.py:405
  43.1 4.6 %collective-permute-done.10.refs_2_ = bf16[4,32,1664]{2,1,0:T(8,128)(2,1)S(1)} collective-permute-done((bf16[4,32,1664]{2,1,0:T(8,128)(2,1)S(1)}, bf16[4,32,1664]{2,1,0:T(8,128)(2,1)S(1)}, u32[]{:S(2)}, u32[]{:S(2)}) %collective-permute-start.10) | collective-permute-done | bytes 426016 | tf_op jit(solution)/shard_map/ppermute | solution.py:405
  49.4 9.5 %shard_map.183 = (bf16[2048,1280]{1,0:T(8,128)(2,1)S(1)}, bf16[2048,512]{1,0:T(8,128)(2,1)S(1)}, bf16[2048,1024]{1,0:T(8,128)(2,1)S(1)}, bf16[1024,1664]{1,0:T(8,128)(2,1)S(1)}) custom-call(s32[4]{0:T(128)S(1)} %pad_add_fusion.info_ref, bf16[2048,512]{1,0:T(8,128)(2,1)S(1)} %get-tuple-element.108.low0_ref.x_ref, ...), custom_call_target="tpu_custom_call" | custom-call | flops 1342177280 | tf_op jit(solution)/shard_map/pallas_call | solution.py:350
  59.2 1.6 %collective-permute-done.19.refs_7_ = bf16[4,32,1664]{2,1,0:T(8,128)(2,1)S(1)} collective-permute-done((bf16[4,32,1664]{2,1,0:T(8,128)(2,1)S(1)}, bf16[4,32,1664]{2,1,0:T(8,128)(2,1)S(1)}, u32[]{:S(2)}, u32[]{:S(2)}) %collective-permute-start.19) | collective-permute-done | bytes 426016 | tf_op jit(solution)/shard_map/ppermute | solution.py:405
  60.8 19.6 %shard_map.184 = (bf16[2048,512]{1,0:T(8,128)(2,1)S(1)}, bf16[2048,1024]{1,0:T(8,128)(2,1)S(1)}, bf16[1024,1664]{1,0:T(8,128)(2,1)S(1)}, bf16[2,2,4,32,1664]{4,3...) custom-call(s32[4]{0:T(128)S(1)} %pad_add_fusion.info_ref, ...), custom_call_target="tpu_custom_call" | custom-call | flops 3221225472 | bytes 16384 | tf_op jit(solution)/shard_map/pallas_call | solution.py:350
  80.6 4.4 %shard_map.185 = (bf16[2048,1024]{1,0:T(8,128)(2,1)S(1)}, bf16[2048,1024]{1,0:T(8,128)(2,1)S(1)}, f32[8,512]{1,0:T(8,128)S(1)}) custom-call(s32[4]{0:T(128)S(1)} %pad_add_fusion.info_ref, bf16[2048,1024]{1,0:T(8,128)(2,1)S(1)} %get-tuple-element.117.pre1_ref, bf16[1024,1664]{1,0:T(8,128)(2,1)S(1)} %get-tuple-element.118.w1_ref, ...), custom_call_target="tpu_custom_call" | custom-call | flops 805306368 | tf_op jit(solution)/shard_map/pallas_call | solution.py:350
  86.6 4.4 %shard_map.187 = (bf16[2048,1024]{1,0:T(8,128)(2,1)S(1)}, bf16[2048,1024]{1,0:T(8,128)(2,1)S(1)}, f32[8,512]{1,0:T(8,128)}) custom-call(s32[4]{0:T(128)S(1)} %pad_add_fusion.info_ref, bf16[2048,1024]{1,0:T(8,128)(2,1)S(1)} %get-tuple-element.117.pre1_ref, ...), custom_call_target="tpu_custom_call", output_to_operand_aliasing={{0}: (6, {}), {1}: (7, {})} | custom-call | flops 805306368 | tf_op jit(solution)/shard_map/pallas_call | solution.py:350
  91.0 5.3 %shard_map.188 = (bf16[2,2,4,32,1024]{4,3,2,1,0:T(8,128)(2,1)S(1)}, bf16[2,2,4,32,1024]{4,3,2,1,0:T(8,128)(2,1)S(1)}) custom-call(s32[4]{0:T(128)S(1)} %pad_add_fusion.info_ref, bf16[2048,1024]{1,0:T(8,128)(2,1)S(1)} %get-tuple-element.149.pre_ref, bf16[2048,1024]{1,0:T(8,128)(2,1)S(1)} %get-tuple-element.132.proj_ref, ...), custom_call_target="tpu_custom_call" | custom-call | flops 939524096 | tf_op jit(solution)/shard_map/pallas_call | solution.py:350
  96.4 6.0 %shard_map.189 = (bf16[2,2,4,32,640]{4,3,2,1,0:T(8,128)(2,1)S(1)}, bf16[2,2,4,32,640]{4,3,2,1,0:T(8,128)(2,1)S(1)}, f32[128,128]{1,0:T(8,128)S(1)}) custom-call(s32[4]{0:T(128)S(1)} %pad_add_fusion.info_ref, bf16[2048,1024]{1,0:T(8,128)(2,1)S(1)} %get-tuple-element.149.pre_ref, bf16[2048,1024]{1,0:T(8,128)(2,1)S(1)} %get-tuple-element.132.proj_ref, ...), custom_call_target="tpu_custom_call" | custom-call | flops 671088640 | bytes 16384 | tf_op jit(solution)/shard_map/pallas_call | solution.py:350
  104.6 1.2 collective-permute-start.26
  106.6 6.8 %shard_map.193 = f32[2048,512]{1,0:T(8,128)} custom-call(s32[4]{0:T(128)S(1)} %pad_add_fusion.info_ref, bf16[2048,1024]{1,0:T(8,128)(2,1)S(1)} %get-tuple-element.132.proj_ref, bf16[2048,1024]{1,0:T(8,128)(2,1)S(1)} %get-tuple-element.149.pre_ref, bf16[1024,1664]{1,0:T(8,128)(2,1)S(1)} %get-tuple-element.119.w0_ref.w_ref), custom_call_target="tpu_custom_call" | custom-call | flops 1073741824 | bytes 1048576 | tf_op jit(solution)/shard_map/pallas_call | solution.py:350
  113.4 5.9 %shard_map.194 = (bf16[2048,512]{1,0:T(8,128)(2,1)}, bf16[2048,512]{1,0:T(8,128)(2,1)}) custom-call(s32[4]{0:T(128)S(1)} %pad_add_fusion.info_ref, bf16[2048,1280]{1,0:T(8,128)(2,1)S(1)} %get-tuple-element.150.taps_ref.taps1_ref, bf16[2048,512]{1,0:T(8,128)(2,1)S(1)} %get-tuple-element.133.gated_ref.gated0_ref, ...), custom_call_target="tpu_custom_call" | custom-call | flops 1073741824 | bytes 1048576 | tf_op jit(solution)/shard_map/pallas_call | solution.py:350
  119.3 1.3 collective-permute-done.25.right_b
  121.8 2.6 %collective-permute-start.32 = (bf16[32,1664]{1,0:T(8,128)(2,1)S(1)}, bf16[32,1664]{1,0:T(8,128)(2,1)S(1)}, u32[]{:S(2)}, u32[]{:S(2)}) collective-permute-start(bf16[32,1664]{1,0:T(8,128)(2,1)S(1)} %get-tuple-element.172), channel_id=1, source_target_pairs={{0,16},{1,17},{2,18},{3,19},{4,20},{5,21},{6,22},{7,23},{8,24},{9,... | collective-permute-start | bytes 319496 | tf_op jit(solution)/shard_map/ppermute | solution.py:405
  124.4 1.8 %collective-permute-start.33 = (bf16[32,1664]{1,0:T(8,128)(2,1)S(1)}, bf16[32,1664]{1,0:T(8,128)(2,1)S(1)}, u32[]{:S(2)}, u32[]{:S(2)}) collective-permute-start(bf16[32,1664]{1,0:T(8,128)(2,1)S(1)} %get-tuple-element.173), channel_id=1, source_target_pairs={{0,24},{1,25},{2,26},{3,27},{4,28},{5,29},{6,30},{7,31},{8,16},{9,... | collective-permute-start | bytes 319496 | tf_op jit(solution)/shard_map/ppermute | solution.py:405
  126.1 2.9 %collective-permute-done.27.right_ref = bf16[4,32,1664]{2,1,0:T(8,128)(2,1)S(1)} collective-permute-done((bf16[4,32,1664]{2,1,0:T(8,128)(2,1)S(1)}, bf16[4,32,1664]{2,1,0:T(8,128)(2,1)S(1)}, u32[]{:S(2)}, u32[]{:S(2)}) %collective-permute-start.27) | collective-permute-done | bytes 426016 | tf_op jit(solution)/shard_map/ppermute | solution.py:405
  129.2 2.6 %collective-permute-start.29 = (bf16[32,1664]{1,0:T(8,128)(2,1)S(1)}, bf16[32,1664]{1,0:T(8,128)(2,1)S(1)}, u32[]{:S(2)}, u32[]{:S(2)}) collective-permute-start(bf16[32,1664]{1,0:T(8,128)(2,1)S(1)} %get-tuple-element.166), channel_id=1, source_target_pairs={{0,16},{1,17},{2,18},{3,19},{4,20},{5,21},{6,22},{7,23},{8,24},{9,... | collective-permute-start | bytes 319496 | tf_op jit(solution)/shard_map/ppermute | solution.py:405
  131.8 1.8 %collective-permute-start.30 = (bf16[32,1664]{1,0:T(8,128)(2,1)S(1)}, bf16[32,1664]{1,0:T(8,128)(2,1)S(1)}, u32[]{:S(2)}, u32[]{:S(2)}) collective-permute-start(bf16[32,1664]{1,0:T(8,128)(2,1)S(1)} %get-tuple-element.167), channel_id=1, source_target_pairs={{0,24},{1,25},{2,26},{3,27},{4,28},{5,29},{6,30},{7,31},{8,16},{9,... | collective-permute-start | bytes 319496 | tf_op jit(solution)/shard_map/ppermute | solution.py:405
  134.2 1.6 %collective-permute-done.28.refs_1_ = bf16[32,1664]{1,0:T(8,128)(2,1)S(1)} collective-permute-done((bf16[32,1664]{1,0:T(8,128)(2,1)S(1)}, bf16[32,1664]{1,0:T(8,128)(2,1)S(1)}, u32[]{:S(2)}, u32[]{:S(2)}) %collective-permute-start.28) | collective-permute-done | bytes 106528 | tf_op jit(solution)/shard_map/ppermute | solution.py:405
  135.8 5.9 %collective-permute-done.29.refs_2_ = bf16[32,1664]{1,0:T(8,128)(2,1)S(1)} collective-permute-done((bf16[32,1664]{1,0:T(8,128)(2,1)S(1)}, bf16[32,1664]{1,0:T(8,128)(2,1)S(1)}, u32[]{:S(2)}, u32[]{:S(2)}) %collective-permute-start.29) | collective-permute-done | bytes 106528 | tf_op jit(solution)/shard_map/ppermute | solution.py:405
  (62 shorter events, 12.8 us)
Async XLA Ops:
  1.8 9.0 %collective-permute-start.2 = (bf16[32,1664]{1,0:T(8,128)(2,1)S(1)}, bf16[32,1664]{1,0:T(8,128)(2,1)S(1)}, u32[]{:S(2)}, u32[]{:S(2)}) collective-permute-start(bf16[32,1664]{1,0:T(8,128)(2,1)S(1)} %get-tuple-element.94.refs_0_), channel_id=1, source_target_pairs={{0,24},{1,25},{2,26},{3,27},{4,28},{5,29},{6,30},{7,31},{8,16},{9,... | collective-permute-start | bytes 319496 | tf_op jit(solution)/shard_map/ppermute | solution.py:405
  7.0 9.0 %collective-permute-start.1 = (bf16[32,1664]{1,0:T(8,128)(2,1)S(1)}, bf16[32,1664]{1,0:T(8,128)(2,1)S(1)}, u32[]{:S(2)}, u32[]{:S(2)}) collective-permute-start(bf16[32,1664]{1,0:T(8,128)(2,1)S(1)} %get-tuple-element.94.refs_0_), channel_id=1, source_target_pairs={{0,16},{1,17},{2,18},{3,19},{4,20},{5,21},{6,22},{7,23},{8,24},{9,... | collective-permute-start | bytes 319496 | tf_op jit(solution)/shard_map/ppermute | solution.py:405
  7.0 9.0 %collective-permute-start = (bf16[32,1664]{1,0:T(8,128)(2,1)S(1)}, bf16[32,1664]{1,0:T(8,128)(2,1)S(1)}, u32[]{:S(2)}, u32[]{:S(2)}) collective-permute-start(bf16[32,1664]{1,0:T(8,128)(2,1)S(1)} %get-tuple-element.94.refs_0_), channel_id=1, source_target_pairs={{0,8},{1,9},{2,10},{3,11},{4,12},{5,13},{6,14},{7,15},{8,0},{9,1},... | collective-permute-start | bytes 319496 | tf_op jit(solution)/shard_map/ppermute | solution.py:405
  16.0 14.9 %collective-permute-start.4 = (bf16[4,32,1664]{2,1,0:T(8,128)(2,1)S(1)}, bf16[4,32,1664]{2,1,0:T(8,128)(2,1)S(1)}, u32[]{:S(2)}, u32[]{:S(2)}) collective-permute-start(bf16[4,32,1664]{2,1,0:T(8,128)(2,1)S(1)} %shard_map.179.refs_0_), channel_id=1, source_target_pairs={{0,4},{1,3},{2,6},{3,1},{4,0},{5,7},{6,2},{7,5},{8,12},{9,11},{10,... | collective-permute-start | bytes 1277960 | tf_op jit(solution)/shard_map/ppermute | solution.py:405
  17.6 13.3 %collective-permute-start.3 = (bf16[4,32,1664]{2,1,0:T(8,128)(2,1)S(1)}, bf16[4,32,1664]{2,1,0:T(8,128)(2,1)S(1)}, u32[]{:S(2)}, u32[]{:S(2)}) collective-permute-start(bf16[4,32,1664]{2,1,0:T(8,128)(2,1)S(1)} %shard_map.179.refs_0_), channel_id=1, source_target_pairs={{0,2},{1,5},{2,0},{3,7},{4,6},{5,1},{6,4},{7,3},{8,10},{9,13},{10,... | collective-permute-start | bytes 1277960 | tf_op jit(solution)/shard_map/ppermute | solution.py:405
  19.7 7.7 %collective-permute-start.7 = (bf16[32,1664]{1,0:T(8,128)(2,1)S(1)}, bf16[32,1664]{1,0:T(8,128)(2,1)S(1)}, u32[]{:S(2)}, u32[]{:S(2)}) collective-permute-start(bf16[32,1664]{1,0:T(8,128)(2,1)S(1)} %get-tuple-element.99.refs_0_), channel_id=1, source_target_pairs={{0,24},{1,25},{2,26},{3,27},{4,28},{5,29},{6,30},{7,31},{8,16},{9,... | collective-permute-start | bytes 319496 | tf_op jit(solution)/shard_map/ppermute | solution.py:405
  22.3 8.5 %collective-permute-start.6 = (bf16[32,1664]{1,0:T(8,128)(2,1)S(1)}, bf16[32,1664]{1,0:T(8,128)(2,1)S(1)}, u32[]{:S(2)}, u32[]{:S(2)}) collective-permute-start(bf16[32,1664]{1,0:T(8,128)(2,1)S(1)} %get-tuple-element.99.refs_0_), channel_id=1, source_target_pairs={{0,16},{1,17},{2,18},{3,19},{4,20},{5,21},{6,22},{7,23},{8,24},{9,... | collective-permute-start | bytes 319496 | tf_op jit(solution)/shard_map/ppermute | solution.py:405
  22.3 8.5 %collective-permute-start.5 = (bf16[32,1664]{1,0:T(8,128)(2,1)S(1)}, bf16[32,1664]{1,0:T(8,128)(2,1)S(1)}, u32[]{:S(2)}, u32[]{:S(2)}) collective-permute-start(bf16[32,1664]{1,0:T(8,128)(2,1)S(1)} %get-tuple-element.99.refs_0_), channel_id=1, source_target_pairs={{0,8},{1,9},{2,10},{3,11},{4,12},{5,13},{6,14},{7,15},{8,0},{9,1},... | collective-permute-start | bytes 319496 | tf_op jit(solution)/shard_map/ppermute | solution.py:405
  30.8 12.3 %collective-permute-start.8 = (bf16[4,32,1664]{2,1,0:T(8,128)(2,1)S(1)}, bf16[4,32,1664]{2,1,0:T(8,128)(2,1)S(1)}, u32[]{:S(2)}, u32[]{:S(2)}) collective-permute-start(bf16[4,32,1664]{2,1,0:T(8,128)(2,1)S(1)} %collective-permute-done.3.refs_1_), channel_id=1, source_target_pairs={{0,4},{1,3},{2,6},{3,1},{4,0},{5,7},{6,2},{7,5},{8,12},{9,11},{10,... | collective-permute-start | bytes 1277960 | tf_op jit(solution)/shard_map/ppermute | solution.py:405
  31.4 16.3 %collective-permute-start.10 = (bf16[4,32,1664]{2,1,0:T(8,128)(2,1)S(1)}, bf16[4,32,1664]{2,1,0:T(8,128)(2,1)S(1)}, u32[]{:S(2)}, u32[]{:S(2)}) collective-permute-start(bf16[4,32,1664]{2,1,0:T(8,128)(2,1)S(1)} %shard_map.181.refs_0_), channel_id=1, source_target_pairs={{0,4},{1,3},{2,6},{3,1},{4,0},{5,7},{6,2},{7,5},{8,12},{9,11},{10,... | collective-permute-start | bytes 1277960 | tf_op jit(solution)/shard_map/ppermute | solution.py:405
  32.9 14.7 %collective-permute-start.9 = (bf16[4,32,1664]{2,1,0:T(8,128)(2,1)S(1)}, bf16[4,32,1664]{2,1,0:T(8,128)(2,1)S(1)}, u32[]{:S(2)}, u32[]{:S(2)}) collective-permute-start(bf16[4,32,1664]{2,1,0:T(8,128)(2,1)S(1)} %shard_map.181.refs_0_), channel_id=1, source_target_pairs={{0,2},{1,5},{2,0},{3,7},{4,6},{5,1},{6,4},{7,3},{8,10},{9,13},{10,... | collective-permute-start | bytes 1277960 | tf_op jit(solution)/shard_map/ppermute | solution.py:405
  34.8 13.3 %collective-permute-start.12 = (bf16[4,32,1664]{2,1,0:T(8,128)(2,1)S(1)}, bf16[4,32,1664]{2,1,0:T(8,128)(2,1)S(1)}, u32[]{:S(2)}, u32[]{:S(2)}) collective-permute-start(bf16[4,32,1664]{2,1,0:T(8,128)(2,1)S(1)} %shard_map.179.refs_0_), channel_id=1, source_target_pairs={{0,1},{1,0},{2,3},{3,2},{4,5},{5,4},{6,7},{7,6},{8,9},{9,8},{10,11... | collective-permute-start | bytes 1277960 | tf_op jit(solution)/shard_map/ppermute | solution.py:405
  39.6 9.1 %collective-permute-start.13 = (bf16[4,32,1664]{2,1,0:T(8,128)(2,1)S(1)}, bf16[4,32,1664]{2,1,0:T(8,128)(2,1)S(1)}, u32[]{:S(2)}, u32[]{:S(2)}) collective-permute-start(bf16[4,32,1664]{2,1,0:T(8,128)(2,1)S(1)} %collective-permute-done.3.refs_1_), channel_id=1, source_target_pairs={{0,1},{1,0},{2,3},{3,2},{4,5},{5,4},{6,7},{7,6},{8,9},{9,8},{10,11... | collective-permute-start | bytes 1277960 | tf_op jit(solution)/shard_map/ppermute | solution.py:405
  43.1 5.3 %collective-permute-start.14 = (bf16[4,32,1664]{2,1,0:T(8,128)(2,1)S(1)}, bf16[4,32,1664]{2,1,0:T(8,128)(2,1)S(1)}, u32[]{:S(2)}, u32[]{:S(2)}) collective-permute-start(bf16[4,32,1664]{2,1,0:T(8,128)(2,1)S(1)} %collective-permute-done.4.refs_2_), channel_id=1, source_target_pairs={{0,1},{1,0},{2,3},{3,2},{4,5},{5,4},{6,7},{7,6},{8,9},{9,8},{10,11... | collective-permute-start | bytes 1277960 | tf_op jit(solution)/shard_map/ppermute | solution.py:405
  47.7 11.3 %collective-permute-start.11 = (bf16[4,32,1664]{2,1,0:T(8,128)(2,1)S(1)}, bf16[4,32,1664]{2,1,0:T(8,128)(2,1)S(1)}, u32[]{:S(2)}, u32[]{:S(2)}) collective-permute-start(bf16[4,32,1664]{2,1,0:T(8,128)(2,1)S(1)} %collective-permute-done.9.refs_1_), channel_id=1, source_target_pairs={{0,4},{1,3},{2,6},{3,1},{4,0},{5,7},{6,2},{7,5},{8,12},{9,11},{10,... | collective-permute-start | bytes 1277960 | tf_op jit(solution)/shard_map/ppermute | solution.py:405
  48.2 11.0 %collective-permute-start.16 = (bf16[4,32,1664]{2,1,0:T(8,128)(2,1)S(1)}, bf16[4,32,1664]{2,1,0:T(8,128)(2,1)S(1)}, u32[]{:S(2)}, u32[]{:S(2)}) collective-permute-start(bf16[4,32,1664]{2,1,0:T(8,128)(2,1)S(1)} %shard_map.181.refs_0_), channel_id=1, source_target_pairs={{0,1},{1,0},{2,3},{3,2},{4,5},{5,4},{6,7},{7,6},{8,9},{9,8},{10,11... | collective-permute-start | bytes 1277960 | tf_op jit(solution)/shard_map/ppermute | solution.py:405
  48.4 10.7 %collective-permute-start.17 = (bf16[4,32,1664]{2,1,0:T(8,128)(2,1)S(1)}, bf16[4,32,1664]{2,1,0:T(8,128)(2,1)S(1)}, u32[]{:S(2)}, u32[]{:S(2)}) collective-permute-start(bf16[4,32,1664]{2,1,0:T(8,128)(2,1)S(1)} %collective-permute-done.9.refs_1_), channel_id=1, source_target_pairs={{0,1},{1,0},{2,3},{3,2},{4,5},{5,4},{6,7},{7,6},{8,9},{9,8},{10,11... | collective-permute-start | bytes 1277960 | tf_op jit(solution)/shard_map/ppermute | solution.py:405
  48.7 10.5 %collective-permute-start.18 = (bf16[4,32,1664]{2,1,0:T(8,128)(2,1)S(1)}, bf16[4,32,1664]{2,1,0:T(8,128)(2,1)S(1)}, u32[]{:S(2)}, u32[]{:S(2)}) collective-permute-start(bf16[4,32,1664]{2,1,0:T(8,128)(2,1)S(1)} %collective-permute-done.10.refs_2_), channel_id=1, source_target_pairs={{0,1},{1,0},{2,3},{3,2},{4,5},{5,4},{6,7},{7,6},{8,9},{9,8},{10,11... | collective-permute-start | bytes 1277960 | tf_op jit(solution)/shard_map/ppermute | solution.py:405
  80.4 4.6 %collective-permute-start.20 = (bf16[2,2,4,32,1664]{4,3,2,1,0:T(8,128)(2,1)S(1)}, bf16[2,2,4,32,1664]{4,3,2,1,0:T(8,128)(2,1)S(1)}, u32[]{:S(2)}, u32[]{:S(2)}) collective-permute-start(bf16[2,2,4,32,1664]{4,3,2,1,0:T(8,128)(2,1)S(1)} %get-tuple-element.125), channel_id=1, source_target_pairs={{0,1},{1,0},{2,3},{3,2},{4,5},{5,4},{6,7},{7,6},{8,9},{9,8},{10,11... | collective-permute-start | bytes 5111816 | tf_op jit(solution)/shard_map/ppermute | solution.py:405
  85.5 16.9 %collective-permute-start.23 = (bf16[2,4,32,1664]{3,2,1,0:T(8,128)(2,1)S(1)}, bf16[2,4,32,1664]{3,2,1,0:T(8,128)(2,1)S(1)}, u32[]{:S(2)}, u32[]{:S(2)}) collective-permute-start(bf16[2,4,32,1664]{3,2,1,0:T(8,128)(2,1)S(1)} %get-tuple-element.141), channel_id=1, source_target_pairs={{0,2},{1,5},{2,0},{3,7},{4,6},{5,1},{6,4},{7,3},{8,10},{9,13},{10,... | collective-permute-start | bytes 2555912 | tf_op jit(solution)/shard_map/ppermute | solution.py:405
  96.3 6.7 %collective-permute-start.21 = (bf16[2,2,4,32,1024]{4,3,2,1,0:T(8,128)(2,1)S(1)}, bf16[2,2,4,32,1024]{4,3,2,1,0:T(8,128)(2,1)S(1)}, u32[]{:S(2)}, u32[]{:S(2)}) collective-permute-start(bf16[2,2,4,32,1024]{4,3,2,1,0:T(8,128)(2,1)S(1)} %get-tuple-element.135), channel_id=1, source_target_pairs={{0,1},{1,0},{2,3},{3,2},{4,5},{5,4},{6,7},{7,6},{8,9},{9,8},{10,11... | collective-permute-start | bytes 3145736 | tf_op jit(solution)/shard_map/ppermute | solution.py:405
  102.5 3.4 %collective-permute-start.24 = (bf16[2,2,4,32,640]{4,3,2,1,0:T(8,128)(2,1)S(1)}, bf16[2,2,4,32,640]{4,3,2,1,0:T(8,128)(2,1)S(1)}, u32[]{:S(2)}, u32[]{:S(2)}) collective-permute-start(bf16[2,2,4,32,640]{4,3,2,1,0:T(8,128)(2,1)S(1)} %get-tuple-element.142), channel_id=1, source_target_pairs={{0,1},{1,0},{2,3},{3,2},{4,5},{5,4},{6,7},{7,6},{8,9},{9,8},{10,11... | collective-permute-start | bytes 1966088 | tf_op jit(solution)/shard_map/ppermute | solution.py:405
  103.3 16.0 %collective-permute-start.22 = (bf16[2,4,32,1024]{3,2,1,0:T(8,128)(2,1)S(1)}, bf16[2,4,32,1024]{3,2,1,0:T(8,128)(2,1)S(1)}, u32[]{:S(2)}, u32[]{:S(2)}) collective-permute-start(bf16[2,4,32,1024]{3,2,1,0:T(8,128)(2,1)S(1)} %get-tuple-element.138), channel_id=1, source_target_pairs={{0,2},{1,5},{2,0},{3,7},{4,6},{5,1},{6,4},{7,3},{8,10},{9,13},{10,... | collective-permute-start | bytes 1572872 | tf_op jit(solution)/shard_map/ppermute | solution.py:405
  104.6 14.7 %collective-permute-start.26 = (bf16[4,32,1664]{2,1,0:T(8,128)(2,1)S(1)}, bf16[4,32,1664]{2,1,0:T(8,128)(2,1)S(1)}, u32[]{:S(2)}, u32[]{:S(2)}) collective-permute-start(bf16[4,32,1664]{2,1,0:T(8,128)(2,1)S(1)} %get-tuple-element.146), channel_id=1, source_target_pairs={{0,4},{1,3},{2,6},{3,1},{4,0},{5,7},{6,2},{7,5},{8,12},{9,11},{10,... | collective-permute-start | bytes 1277960 | tf_op jit(solution)/shard_map/ppermute | solution.py:405
  106.0 14.6 %collective-permute-start.25 = (bf16[2,4,32,640]{3,2,1,0:T(8,128)(2,1)S(1)}, bf16[2,4,32,640]{3,2,1,0:T(8,128)(2,1)S(1)}, u32[]{:S(2)}, u32[]{:S(2)}) collective-permute-start(bf16[2,4,32,640]{3,2,1,0:T(8,128)(2,1)S(1)} %get-tuple-element.148), channel_id=1, source_target_pairs={{0,2},{1,5},{2,0},{3,7},{4,6},{5,1},{6,4},{7,3},{8,10},{9,13},{10,... | collective-permute-start | bytes 983048 | tf_op jit(solution)/shard_map/ppermute | solution.py:405
  120.8 8.2 %collective-permute-start.27 = (bf16[4,32,1664]{2,1,0:T(8,128)(2,1)S(1)}, bf16[4,32,1664]{2,1,0:T(8,128)(2,1)S(1)}, u32[]{:S(2)}, u32[]{:S(2)}) collective-permute-start(bf16[4,32,1664]{2,1,0:T(8,128)(2,1)S(1)} %get-tuple-element.163), channel_id=1, source_target_pairs={{0,4},{1,3},{2,6},{3,1},{4,0},{5,7},{6,2},{7,5},{8,12},{9,11},{10,... | collective-permute-start | bytes 1277960 | tf_op jit(solution)/shard_map/ppermute | solution.py:405
  121.7 10.1 %collective-permute-start.31 = (bf16[32,1664]{1,0:T(8,128)(2,1)S(1)}, bf16[32,1664]{1,0:T(8,128)(2,1)S(1)}, u32[]{:S(2)}, u32[]{:S(2)}) collective-permute-start(bf16[32,1664]{1,0:T(8,128)(2,1)S(1)} %get-tuple-element.171), channel_id=1, source_target_pairs={{0,8},{1,9},{2,10},{3,11},{4,12},{5,13},{6,14},{7,15},{8,0},{9,1},... | collective-permute-start | bytes 319496 | tf_op jit(solution)/shard_map/ppermute | solution.py:405
  121.8 12.4 %collective-permute-start.32 = (bf16[32,1664]{1,0:T(8,128)(2,1)S(1)}, bf16[32,1664]{1,0:T(8,128)(2,1)S(1)}, u32[]{:S(2)}, u32[]{:S(2)}) collective-permute-start(bf16[32,1664]{1,0:T(8,128)(2,1)S(1)} %get-tuple-element.172), channel_id=1, source_target_pairs={{0,16},{1,17},{2,18},{3,19},{4,20},{5,21},{6,22},{7,23},{8,24},{9,... | collective-permute-start | bytes 319496 | tf_op jit(solution)/shard_map/ppermute | solution.py:405
  124.4 9.8 %collective-permute-start.33 = (bf16[32,1664]{1,0:T(8,128)(2,1)S(1)}, bf16[32,1664]{1,0:T(8,128)(2,1)S(1)}, u32[]{:S(2)}, u32[]{:S(2)}) collective-permute-start(bf16[32,1664]{1,0:T(8,128)(2,1)S(1)} %get-tuple-element.173), channel_id=1, source_target_pairs={{0,24},{1,25},{2,26},{3,27},{4,28},{5,29},{6,30},{7,31},{8,16},{9,... | collective-permute-start | bytes 319496 | tf_op jit(solution)/shard_map/ppermute | solution.py:405
  129.1 6.7 %collective-permute-start.28 = (bf16[32,1664]{1,0:T(8,128)(2,1)S(1)}, bf16[32,1664]{1,0:T(8,128)(2,1)S(1)}, u32[]{:S(2)}, u32[]{:S(2)}) collective-permute-start(bf16[32,1664]{1,0:T(8,128)(2,1)S(1)} %get-tuple-element.165), channel_id=1, source_target_pairs={{0,8},{1,9},{2,10},{3,11},{4,12},{5,13},{6,14},{7,15},{8,0},{9,1},... | collective-permute-start | bytes 319496 | tf_op jit(solution)/shard_map/ppermute | solution.py:405
  129.2 12.5 %collective-permute-start.29 = (bf16[32,1664]{1,0:T(8,128)(2,1)S(1)}, bf16[32,1664]{1,0:T(8,128)(2,1)S(1)}, u32[]{:S(2)}, u32[]{:S(2)}) collective-permute-start(bf16[32,1664]{1,0:T(8,128)(2,1)S(1)} %get-tuple-element.166), channel_id=1, source_target_pairs={{0,16},{1,17},{2,18},{3,19},{4,20},{5,21},{6,22},{7,23},{8,24},{9,... | collective-permute-start | bytes 319496 | tf_op jit(solution)/shard_map/ppermute | solution.py:405
  131.8 9.9 %collective-permute-start.30 = (bf16[32,1664]{1,0:T(8,128)(2,1)S(1)}, bf16[32,1664]{1,0:T(8,128)(2,1)S(1)}, u32[]{:S(2)}, u32[]{:S(2)}) collective-permute-start(bf16[32,1664]{1,0:T(8,128)(2,1)S(1)} %get-tuple-element.167), channel_id=1, source_target_pairs={{0,24},{1,25},{2,26},{3,27},{4,28},{5,29},{6,30},{7,31},{8,16},{9,... | collective-permute-start | bytes 319496 | tf_op jit(solution)/shard_map/ppermute | solution.py:405
  (3 other events, 4.3 us)

commit v8 on v7

--- a/solution.py
+++ b/solution.py
@@ -11,10 +11,12 @@
 AXES = ("dp", "group")
 LANES = 128
 TILE = 512
-PART = 256
+WIDE = 1024
+PART = 512
+PART_0 = 1024
 MIB = 1024 * 1024
 HINT = 4
-ROOM_0, ROOM_1, ROOM_2, ROOM_3, ROOM_4, ROOM_5, ROOM_SMALL = 6, 4, 5, 3, 6, 5, 10
+ROOM_0, ROOM_1, ROOM_2, ROOM_3, ROOM_4, ROOM_5, ROOM_SMALL = 7, 8, 6, 7, 6, 6, 6
 LOW = jnp.bfloat16
 FULL = jnp.float32
 
@@ -83,19 +85,31 @@
     return pl.ds(pl.multiple_of(step * rows, rows), rows)
 
 
-def prepare(size, info_ref, x_ref, go_ref, gs_ref, mel_ref, low0_ref, place_ref, proj1_ref):
+def prepare(size, info_ref, x_ref, go_ref, gs_ref, mel_ref, taps0_ref, proj1_ref):
     step = pl.program_id(0)
+    channels = size.channels
     tile = rows_of(step, TILE)
     mask = mask_of(info_ref, step * TILE, TILE)
-    low0_ref[tile] = masked(x_ref[...], mask)
-    proj1_ref[tile, : size.channels] = masked(go_ref[...], mask)
-    proj1_ref[tile, size.channels :] = masked(gs_ref[...], mask)
+    low = masked(x_ref[...], mask)
+    taps0_ref[tile, channels : 2 * channels] = low
+
+    @pl.when(step == 0)
+    def _():
+        taps0_ref[:TILE, :channels] = jnp.zeros((TILE, channels), LOW)
+
+    @pl.when(step < pl.num_programs(0) - 1)
+    def _():
+        taps0_ref[rows_of(step + 1, TILE), :channels] = low
+
+    proj1_ref[tile, :channels] = masked(go_ref[...], mask)
+    proj1_ref[tile, channels:] = masked(gs_ref[...], mask)
     frames = frames_of(info_ref, step * TILE, TILE)
-    place_ref[tile, : size.extra_width] = dot(frames, mel_ref[...]).astype(LOW)
-    place_ref[tile, size.extra_width :] = frames
-
-
-def forward_0(size, wires, info_ref, low0_ref, place_ref, *refs):
+    place = 2 * channels + size.extra_width
+    taps0_ref[tile, 2 * channels : place] = dot(frames, mel_ref[...]).astype(LOW)
+    taps0_ref[tile, place:] = frames
+
+
+def forward_0(size, wires, info_ref, taps0_ref, *refs):
     count = 8 if wires.direct else 1
     pieces, refs = refs[:count], refs[count:]
     taps1_ref, gated_ref, slope_ref, w_ref, bias_s, carry_s = refs
@@ -108,39 +122,36 @@
         bias_s[...] = out_bias_row(size, w_ref[:channels, size.extra :])
         carry_s[...] = jnp.zeros_like(carry_s)
 
-    tile = rows_of(step, TILE)
-    mask = mask_of(info_ref, step * TILE, TILE)
-    low = low0_ref[tile]
-    before = low0_ref[rows_of(jnp.maximum(step - 1, 0), TILE)]
-    prev = jnp.where(step > 0, before, jnp.zeros_like(before))
-    taps = jnp.concatenate([prev, low, place_ref[tile, : size.extra_width]], axis=1)
+    tile = rows_of(step, WIDE)
+    mask = mask_of(info_ref, step * WIDE, WIDE)
+    taps = taps0_ref[tile, : size.pack - channels]
     for side in range(2):
         first, second, gated, slope_a, slope_b = gates(taps, w_ref, size, side)
         gated_ref[tile, first] = gated.astype(LOW)
         slope_ref[tile, first] = slope_a.astype(LOW)
         slope_ref[tile, second] = slope_b.astype(LOW)
     moved = dot_cols(gated_ref[tile], w_ref[:channels, :channels])
-    low = ((low.astype(FULL) + moved + bias_s[...]) * mask).astype(LOW)
+    hidden = taps0_ref[tile, channels : 2 * channels].astype(FULL)
+    low = ((hidden + moved + bias_s[...]) * mask).astype(LOW)
     wide = low.astype(FULL)
-    place = lax.broadcasted_iota(jnp.int32, (TILE, 1), 0)
+    place = lax.broadcasted_iota(jnp.int32, (WIDE, 1), 0)
     prev = jnp.where(place == 0, carry_s[7:8], pltpu.roll(wide, 1, 0)).astype(LOW)
     taps1_ref[tile, :channels] = prev
     taps1_ref[tile, channels : 2 * channels] = low
-    taps1_ref[tile, 2 * channels :] = place_ref[tile]
-    carry_s[...] = wide[TILE - 8 :]
+    taps1_ref[tile, 2 * channels :] = taps0_ref[tile, 2 * channels :]
+    carry_s[...] = wide[WIDE - 8 :]
 
 
 def layer_1(size, wires, steps, info_ref, taps_ref, proj_ref, *refs):
     count = 8 if wires.direct else 1
     pieces, refs = refs[:count], refs[count:]
-    gated_ref, pre_ref, w_ref, here_ref, away_ref, melg_ref = refs
+    gated_ref, pre_ref, w_ref, sums_ref, here_ref, away_ref = refs
     step = pl.program_id(0)
     channels = size.channels
 
     @pl.when(step == 0)
     def _():
         wires.put_together(info_ref, pieces, w_ref)
-        melg_ref[...] = jnp.zeros_like(melg_ref)
 
     @pl.when(step < steps)
     def _():
@@ -156,13 +167,13 @@
     @pl.when(step >= steps)
     def _():
         part = rows_of(step - steps, PART)
-        pre = pre_ref[:, part]
         proj = proj_ref[:, part]
-        both = dot_rows(pre, taps_ref[...])
+        both = dot_rows(pre_ref[:, part], taps_ref[...])
+        sums_ref[part] = both[:, size.pack - channels :]
         grads = [
             dot_rows(proj, gated_ref[...]),
             both[:, : 2 * channels],
-            extra_grads(size, both[:, 2 * channels :], proj, w_ref[part, size.extra :], melg_ref),
+            extra_grads(size, both[:, 2 * channels : size.pack - channels], proj),
         ]
         wires.put_apart(info_ref, step - steps, grads, here_ref, away_ref)
 
@@ -172,9 +183,7 @@
     return high, (value - high.astype(FULL)).astype(LOW)
 
 
-def extra_grads(size, both, proj, cond_weight, melg_ref):
-    extra, sums = both[:, : size.extra_width], in_two(both[:, size.extra_width :])
-    melg_ref[...] += sum(dot_rows(half, cond_weight) for half in sums)
+def extra_grads(size, extra, proj):
     total = jnp.sum(proj.astype(FULL), axis=0, keepdims=True)
     bias = jnp.broadcast_to(total, (LANES, total.shape[1])).T[:, 0:1]
     column = lax.broadcasted_iota(jnp.int32, extra.shape, 1)
@@ -207,29 +216,27 @@
         pre0_ref[tile, half] = (grad_gated * slope_ref[tile, half].astype(FULL)).astype(LOW)
 
 
-def weights_0_early(size, wires, info_ref, pre_ref, proj_ref, x_ref, gated_ref, here_ref, away_ref):
+def weights_0_early(size, wires, info_ref, pre_ref, proj_ref, taps_ref, gated_ref, here_ref, away_ref):
     step = pl.program_id(0)
-    part = rows_of(step, PART)
+    now = slice(size.channels, 2 * size.channels)
+    part = rows_of(step, PART_0)
     shift = FIRST_DILATION
     grads = [
         dot_rows(proj_ref[:, part], gated_ref[...]),
-        dot_rows(pre_ref[shift:, part], x_ref[: x_ref.shape[0] - shift]),
+        dot_rows(pre_ref[shift:, part], taps_ref[: taps_ref.shape[0] - shift, now]),
     ]
     wires.put_apart(info_ref, step, grads, here_ref, away_ref)
 
 
-def weights_0_now(size, wires, info_ref, pre_ref, proj_ref, x_ref, place_ref, w_ref, here_ref, away_ref, melg_ref):
+def weights_0_now(size, wires, info_ref, pre_ref, proj_ref, taps_ref, sums_ref, here_ref, away_ref):
     step = pl.program_id(0)
-
-    @pl.when(step == 0)
-    def _():
-        melg_ref[...] = jnp.zeros_like(melg_ref)
-
-    part = rows_of(step, PART)
-    pre = pre_ref[:, part]
+    part = rows_of(step, PART_0)
+    channels = size.channels
+    both = dot_rows(pre_ref[:, part], taps_ref[:, channels:])
+    sums_ref[part] = both[:, channels + size.extra_width :]
     grads = [
-        dot_rows(pre, x_ref[...]),
-        extra_grads(size, dot_rows(pre, place_ref[...]), proj_ref[:, part], w_ref[part, size.extra :], melg_ref),
+        both[:, :channels],
+        extra_grads(size, both[:, channels : channels + size.extra_width], proj_ref[:, part]),
     ]
     wires.put_apart(info_ref, step, grads, here_ref, away_ref)
 
@@ -244,7 +251,7 @@
     sg_ref[...] = grad * mask_of(info_ref, step * TILE, TILE)
 
 
-def forward_outputs(size, info_ref, taps1_ref, gated0_ref, gated1_ref, w0_ref, w1_ref, res_ref, skip_ref, bias_s):
+def forward_outputs(size, info_ref, taps1_ref, gated0_ref, gated1_ref, w0_ref, w1_ref, sums0_ref, sums1_ref, res_ref, skip_ref, mel_ref, bias_s):
     step = pl.program_id(0)
     channels = size.channels
 
@@ -252,6 +259,11 @@
     def _():
         bias_s[...] = out_bias_row(size, w1_ref[:, size.extra :])
         bias_s[:, channels:] += out_bias_row(size, w0_ref[channels:, size.extra :])
+        mel_ref[...] = sum(
+            dot_rows(half, w_ref[:, size.extra :])
+            for sums_ref, w_ref in ((sums0_ref, w0_ref), (sums1_ref, w1_ref))
+            for half in in_two(sums_ref[...])
+        )
 
     tile = rows_of(step, TILE)
     mask = mask_of(info_ref, step * TILE, TILE)
@@ -282,14 +294,18 @@
         ref[..., cut:] = add_low(left_b[index], right_b[index])
 
 
+def hand_on(from_ref, to_ref):
+    to_ref[...] = from_ref[...]
+
+
 def put_side_by_side(*refs):
     for index, ref in enumerate(refs[:-1]):
         refs[-1][index] = ref[...]
 
 
 def pack_layers(layers, *refs):
-    sources, packs, kept = refs[:5], refs[5 : 5 + layers], refs[5 + layers : 10 + layers]
-    sems = refs[-1]
+    sources, packs, table_ref = refs[:6], refs[6 : 6 + layers], refs[6 + layers]
+    kept, wide_s, sems = refs[7 + layers : 13 + layers], refs[-2], refs[-1]
     copies = [
         pltpu.make_async_copy(source, to, sems.at[index])
         for index, (source, to) in enumerate(zip(sources, kept))
@@ -298,7 +314,8 @@
         copy.start()
     for copy in copies:
         copy.wait()
-    conv_ref, cond_ref, conv_b_ref, out_ref, out_b_ref = kept
+    conv_ref, cond_ref, conv_b_ref, out_ref, out_b_ref, mel_ref = kept
+    mel_rows(mel_ref, table_ref, wide_s)
     rows = conv_ref.shape[1]
     same = lax.broadcasted_iota(jnp.int32, (rows, rows), 0)
     same = (same == lax.broadcasted_iota(jnp.int32, (rows, rows), 1)).astype(FULL).astype(LOW)
@@ -335,16 +352,23 @@
         out_b_ref[layer : layer + 1] = biases[mel + 1 : mel + 2]
 
 
-def plain(kernel, operands, outs):
+def in_vmem(value):
+    return pltpu.with_memory_space_constraint(value, pltpu.VMEM)
+
+
+def plain(kernel, operands, outs, at_end=False):
+    shapes = outs if at_end else [pltpu.VMEM(x.shape, x.dtype) for x in outs]
     return pl.pallas_call(
         kernel,
-        out_shape=outs,
+        out_shape=shapes,
+        in_specs=[KEPT] * len(operands),
+        out_specs=[KEPT] * len(outs),
         compiler_params=pltpu.CompilerParams(vmem_limit_bytes=ROOM_SMALL * MIB),
-    )(*operands)
+    )(*map(in_vmem, operands))
 
 
 def call(kernel, grid, info, operands, outs, scratch, flops, room, onto=None):
-    arrays = [x if spec else pltpu.with_memory_space_constraint(x, pltpu.VMEM) for x, spec in operands]
+    arrays = [x if spec else in_vmem(x) for x, spec in operands]
     shapes = [x if spec else pltpu.VMEM(x.shape, x.dtype) for x, spec in outs]
     moved = sum(x.size * x.dtype.itemsize for x, spec in (*operands, *outs) if spec)
     return pl.pallas_call(
@@ -521,13 +545,13 @@
         w.swapaxes(1, 2) for w in (conv_weight, cond_weight, out_weight)
     )
     rows = conv_t.shape[1]
-    sources = (conv_t, cond_t, conv_bias, out_t, out_bias)
-    own = pl.pallas_call(
+    sources = (conv_t, cond_t, conv_bias, out_t, out_bias, mel[0])
+    own0, own1, mel_table = pl.pallas_call(
         functools.partial(pack_layers, layers),
         in_specs=[pl.BlockSpec(memory_space=pl.ANY)] * len(sources),
-        out_shape=[shape_of(rows, size.pack)] * layers,
+        out_shape=[shape_of(rows, size.pack)] * layers + [shape_of(LANES, size.extra_width)],
         scratch_shapes=[pltpu.VMEM(source.shape, LOW) for source in sources]
-        + [pltpu.SemaphoreType.DMA((len(sources),))],
+        + [pltpu.VMEM((LANES, size.extra_width), FULL), pltpu.SemaphoreType.DMA((len(sources),))],
         compiler_params=pltpu.CompilerParams(vmem_limit_bytes=ROOM_SMALL * MIB),
     )(*map(at_home, sources))
     last_shape = shape_of(wires.rest, rows, size.pack)
@@ -536,36 +560,31 @@
     side_by_side = lambda blocks: plain(put_side_by_side, blocks, [last_shape])[0]
     table = fixed(LANES, size.extra_width)
     macs = sample_count * channels * channels
-    assert gate % PART == 0
+    assert gate % PART == 0 and gate % PART_0 == 0 and sample_count % WIDE == 0
     kept = lambda *columns: [(shape_of(sample_count, c), None) for c in columns]
     whole_w = (shape_of(gate, size.pack), None)
     parts = gate // PART
-    melg = (shape_of(LANES, size.extra_width, dtype=FULL), table)
+    mel_sums = (shape_of(LANES, size.extra_width, dtype=FULL), table)
+    frame_sums = (shape_of(gate, LANES, dtype=FULL), None)
     scratch = lambda *shape: pltpu.VMEM(shape, LOW)
 
     blocked = (shape_of(sample_count, channels), tiled(channels))
     keep = lambda *values: [(value, None) for value in values]
 
-    near0 = wires.spread([own[0]] * wires.rest)
+    near0 = wires.spread([own0] * wires.rest)
     mine0 = side_by_side(near0)
     one0, two0 = wires.hop(mine0, wires.first), wires.hop(mine0, wires.second)
-    mel_late, _ = lax.optimization_barrier((mel[0], mine0))
-    mel_table = pl.pallas_call(
-        mel_rows,
-        out_shape=shape_of(LANES, size.extra_width),
-        scratch_shapes=[pltpu.VMEM((LANES, size.extra_width), FULL)],
-        compiler_params=pltpu.CompilerParams(vmem_limit_bytes=ROOM_SMALL * MIB),
-    )(mel_late)
-    own1, mel_table = lax.optimization_barrier((own[1], mel_table))
+    own1, _ = lax.optimization_barrier((own1, mine0))
+    (own1,) = plain(hand_on, (own1,), [shape_of(rows, size.pack)])
     near1 = wires.spread([own1] * wires.rest)
     mel_table, *near1 = lax.optimization_barrier((mel_table, *near1))
     mine1 = side_by_side(near1)
-    low0, place, proj1 = call(
+    taps0, proj1 = call(
         functools.partial(prepare, size),
         steps,
         info,
         [*((at_home(value), tiled(channels)) for value in (x, go, gs)), (mel_table, table)],
-        kept(channels, size.extra_width + LANES, gate),
+        kept(gate + size.extra_width + LANES, gate),
         [],
         macs,
         ROOM_0,
@@ -573,12 +592,12 @@
     one0, two0, mine1 = lax.optimization_barrier((one0, two0, mine1))
     far0 = wires.hop(one0, wires.second)
     one1, two1 = wires.hop(mine1, wires.first), wires.hop(mine1, wires.second)
-    far0, one1, two1, low0 = lax.optimization_barrier((far0, one1, two1, low0))
+    far0, one1, two1, taps0 = lax.optimization_barrier((far0, one1, two1, taps0))
     taps1, gated0, slope0, w0 = call(
         functools.partial(forward_0, size, wires),
-        steps,
-        info,
-        keep(low0, place, *wires.passed(mine0, one0, two0, far0)),
+        sample_count // WIDE,
+        info,
+        keep(taps0, *wires.passed(mine0, one0, two0, far0)),
         [*kept(gate + size.extra_width + LANES, channels, gate), whole_w],
         [pltpu.VMEM((1, channels), FULL), pltpu.VMEM((8, channels), FULL)],
         10 * macs,
@@ -586,12 +605,12 @@
     )
     far1 = wires.hop(one1, wires.second)
     far1, taps1 = lax.optimization_barrier((far1, taps1))
-    gated1, pre1, w1, here1, away1, melg1 = call(
+    gated1, pre1, w1, sums1, here1, away1 = call(
         functools.partial(layer_1, size, wires, steps),
         steps + parts,
         info,
         keep(taps1, proj1, *wires.passed(mine1, one1, two1, far1)),
-        [*kept(channels, gate), whole_w, *wires.apart(size.pack), melg],
+        [*kept(channels, gate), whole_w, frame_sums, *wires.apart(size.pack)],
         [],
         24 * macs,
         ROOM_1,
@@ -630,20 +649,20 @@
     depths = (size.now, size.pack - size.now)
     here_a, away_a = call(
         functools.partial(weights_0_early, size, wires),
-        parts,
-        info,
-        keep(pre0, proj0, low0, gated0),
+        gate // PART_0,
+        info,
+        keep(pre0, proj0, taps0, gated0),
         wires.apart(depths[0]),
         [],
         7 * macs,
         ROOM_3,
     )
-    here_b, away_b, melg0 = call(
+    sums0, here_b, away_b = call(
         functools.partial(weights_0_now, size, wires),
-        parts,
-        info,
-        keep(pre0, proj0, low0, place, w0),
-        [*wires.apart(depths[1]), melg],
+        gate // PART_0,
+        info,
+        keep(pre0, proj0, taps0),
+        [frame_sums, *wires.apart(depths[1])],
         [],
         5 * macs,
         ROOM_3,
@@ -675,12 +694,12 @@
         8 * macs,
         ROOM_4,
     )
-    residual_out, skip_output_sum = call(
+    residual_out, skip_output_sum, mel_grad = call(
         functools.partial(forward_outputs, size),
         steps,
         info,
-        keep(taps1, gated0, gated1, w0, w1),
-        [blocked, blocked],
+        keep(taps1, gated0, gated1, w0, w1, sums0, sums1),
+        [blocked, blocked, mel_sums],
         [pltpu.VMEM((1, gate), FULL)],
         8 * macs,
         ROOM_5,
@@ -702,14 +721,14 @@
             shape_of(layers, rows, channels, dtype=FULL),
             shape_of(layers, rows, dtype=FULL),
         ],
-    )
-    mel_grad = (melg0 + melg1)[:frame_count, :mel_count]
+        at_end=True,
+    )
     conv_grad, cond_grad, conv_b_grad, out_grad, out_b_grad = grads
     return (
         residual_out[None],
         skip_output_sum[None],
         samples_grad[None],
-        mel_grad[None],
+        mel_grad[:frame_count, :mel_count][None],
         conv_grad.swapaxes(1, 2),
         cond_grad.swapaxes(1, 2),
         conv_b_grad,

time: 143 us -> 138 us (0.965)
  Pallas kernels: 70.6 us -> 67.8 us
    pallas_call x9, Pallas kernels: 66.8 us -> 64.1 us  [call(): pl.pallas_call(kernel, grid_spec=pltpu.PrefetchScalarGridSpec(num_scalar_...]
  transfers between devices with their start and end apart: 34 -> 34, of which waited for: 12 -> 12; matrix products, arithmetic and copies ran while one was open for 0% -> 0% of each run, Pallas kernels for 34% -> 33%
where the time goes in v8:
time: 138 us
  Pallas kernels  67.8 us (49%)
  waiting for transfers between devices  35.2 us (26%)
  starting transfers between devices  32.4 us (23%)
  between operations  2.15 us (2%)
    pallas_call x9, Pallas kernels, call(): pl.pallas_call(kernel, grid_spec=pltpu.PrefetchScalarGridSpec(num_scalar_...  64.1 us
    ppermute x34, waiting for transfers between devices, hop(): return lax.ppermute(value, AXES, pairs)  35.2 us
    ppermute x34, starting transfers between devices, hop(): return lax.ppermute(value, AXES, pairs)  32.4 us
  transfers between devices with their start and end apart: 34, of which 12 were waited for; matrix products, arithmetic and copies ran while one was open for 0% of the time, Pallas kernels for 33%

profile of v8, /device:TPU:0, one launch (start us, length us, event | category | flops | bytes accessed | tf_op | source)
XLA Modules:
  0.0 138.3 jit_solution(8233741078735693728)
XLA Ops:
  0.6 1.2 shard_map.178
  1.9 5.1 %collective-permute-start.2 = (bf16[32,1664]{1,0:T(8,128)(2,1)S(1)}, bf16[32,1664]{1,0:T(8,128)(2,1)S(1)}, u32[]{:S(2)}, u32[]{:S(2)}) collective-permute-start(bf16[32,1664]{1,0:T(8,128)(2,1)S(1)} %get-tuple-element.93.refs_0_), channel_id=1, source_target_pairs={{0,24},{1,25},{2,26},{3,27},{4,28},{5,29},{6,30},{7,31},{8,16},{9,... | collective-permute-start | bytes 319496 | tf_op jit(solution)/shard_map/ppermute | solution.py:429
  7.6 3.3 %collective-permute-done.2.refs_3_ = bf16[32,1664]{1,0:T(8,128)(2,1)S(1)} collective-permute-done((bf16[32,1664]{1,0:T(8,128)(2,1)S(1)}, bf16[32,1664]{1,0:T(8,128)(2,1)S(1)}, u32[]{:S(2)}, u32[]{:S(2)}) %collective-permute-start.2) | collective-permute-done | bytes 106528 | tf_op jit(solution)/shard_map/ppermute | solution.py:429
  10.9 5.1 %collective-permute-done.1.refs_2_ = bf16[32,1664]{1,0:T(8,128)(2,1)S(1)} collective-permute-done((bf16[32,1664]{1,0:T(8,128)(2,1)S(1)}, bf16[32,1664]{1,0:T(8,128)(2,1)S(1)}, u32[]{:S(2)}, u32[]{:S(2)}) %collective-permute-start.1) | collective-permute-done | bytes 106528 | tf_op jit(solution)/shard_map/ppermute | solution.py:429
  16.0 1.6 %collective-permute-start.4 = (bf16[4,32,1664]{2,1,0:T(8,128)(2,1)S(1)}, bf16[4,32,1664]{2,1,0:T(8,128)(2,1)S(1)}, u32[]{:S(2)}, u32[]{:S(2)}) collective-permute-start(bf16[4,32,1664]{2,1,0:T(8,128)(2,1)S(1)} %shard_map.179.refs_0_), channel_id=1, source_target_pairs={{0,4},{1,3},{2,6},{3,1},{4,0},{5,7},{6,2},{7,5},{8,12},{9,11},{10,... | collective-permute-start | bytes 1277960 | tf_op jit(solution)/shard_map/ppermute | solution.py:429
  17.6 1.5 %collective-permute-start.3 = (bf16[4,32,1664]{2,1,0:T(8,128)(2,1)S(1)}, bf16[4,32,1664]{2,1,0:T(8,128)(2,1)S(1)}, u32[]{:S(2)}, u32[]{:S(2)}) collective-permute-start(bf16[4,32,1664]{2,1,0:T(8,128)(2,1)S(1)} %shard_map.179.refs_0_), channel_id=1, source_target_pairs={{0,2},{1,5},{2,0},{3,7},{4,6},{5,1},{6,4},{7,3},{8,10},{9,13},{10,... | collective-permute-start | bytes 1277960 | tf_op jit(solution)/shard_map/ppermute | solution.py:429
  19.1 2.5 %collective-permute-start.7 = (bf16[32,1664]{1,0:T(8,128)(2,1)S(1)}, bf16[32,1664]{1,0:T(8,128)(2,1)S(1)}, u32[]{:S(2)}, u32[]{:S(2)}) collective-permute-start(bf16[32,1664]{1,0:T(8,128)(2,1)S(1)} %shard_map.180.refs_0_), channel_id=1, source_target_pairs={{0,24},{1,25},{2,26},{3,27},{4,28},{5,29},{6,30},{7,31},{8,16},{9,... | collective-permute-start | bytes 319496 | tf_op jit(solution)/shard_map/ppermute | solution.py:429
  21.6 1.9 %collective-permute-start.5 = (bf16[32,1664]{1,0:T(8,128)(2,1)S(1)}, bf16[32,1664]{1,0:T(8,128)(2,1)S(1)}, u32[]{:S(2)}, u32[]{:S(2)}) collective-permute-start(bf16[32,1664]{1,0:T(8,128)(2,1)S(1)} %shard_map.180.refs_0_), channel_id=1, source_target_pairs={{0,8},{1,9},{2,10},{3,11},{4,12},{5,13},{6,14},{7,15},{8,0},{9,1},... | collective-permute-start | bytes 319496 | tf_op jit(solution)/shard_map/ppermute | solution.py:429
  23.5 3.2 %collective-permute-done.7.refs_3_ = bf16[32,1664]{1,0:T(8,128)(2,1)S(1)} collective-permute-done((bf16[32,1664]{1,0:T(8,128)(2,1)S(1)}, bf16[32,1664]{1,0:T(8,128)(2,1)S(1)}, u32[]{:S(2)}, u32[]{:S(2)}) %collective-permute-start.7) | collective-permute-done | bytes 106528 | tf_op jit(solution)/shard_map/ppermute | solution.py:429
  26.7 3.4 %collective-permute-done.6.refs_2_ = bf16[32,1664]{1,0:T(8,128)(2,1)S(1)} collective-permute-done((bf16[32,1664]{1,0:T(8,128)(2,1)S(1)}, bf16[32,1664]{1,0:T(8,128)(2,1)S(1)}, u32[]{:S(2)}, u32[]{:S(2)}) %collective-permute-start.6) | collective-permute-done | bytes 106528 | tf_op jit(solution)/shard_map/ppermute | solution.py:429
  30.7 1.5 %collective-permute-start.10 = (bf16[4,32,1664]{2,1,0:T(8,128)(2,1)S(1)}, bf16[4,32,1664]{2,1,0:T(8,128)(2,1)S(1)}, u32[]{:S(2)}, u32[]{:S(2)}) collective-permute-start(bf16[4,32,1664]{2,1,0:T(8,128)(2,1)S(1)} %shard_map.181.refs_0_), channel_id=1, source_target_pairs={{0,4},{1,3},{2,6},{3,1},{4,0},{5,7},{6,2},{7,5},{8,12},{9,11},{10,... | collective-permute-start | bytes 1277960 | tf_op jit(solution)/shard_map/ppermute | solution.py:429
  34.2 5.4 %shard_map.182 = (bf16[2048,1280]{1,0:T(8,128)(2,1)S(1)}, bf16[2048,1024]{1,0:T(8,128)(2,1)S(1)}) custom-call(s32[4]{0:T(128)S(1)} %pad_add_fusion.info_ref, bf16[2048,512]{1,0:T(8,128)(2,1)} %bitcast.18, bf16[2048,512]{1,0:T(8,128)(2,1)} %bitcast.19, bf16[2048,512]{1,0:T(8,128)(2,1)} %bitcast.20, bf16[128,128]{1,0:T(8,128)(2,1)S(1)} %get-tuple-element.103.mel_ref), custom_call_target="tpu_custom_call" | custom-call | flops 134217728 | bytes 1581056 | tf_op jit(solution)/shard_map/pallas_call | solution.py:374
  40.2 2.3 %collective-permute-done.8.refs_3_ = bf16[4,32,1664]{2,1,0:T(8,128)(2,1)S(1)} collective-permute-done((bf16[4,32,1664]{2,1,0:T(8,128)(2,1)S(1)}, bf16[4,32,1664]{2,1,0:T(8,128)(2,1)S(1)}, u32[]{:S(2)}, u32[]{:S(2)}) %collective-permute-start.8) | collective-permute-done | bytes 426016 | tf_op jit(solution)/shard_map/ppermute | solution.py:429
  42.4 4.6 %collective-permute-done.10.refs_2_ = bf16[4,32,1664]{2,1,0:T(8,128)(2,1)S(1)} collective-permute-done((bf16[4,32,1664]{2,1,0:T(8,128)(2,1)S(1)}, bf16[4,32,1664]{2,1,0:T(8,128)(2,1)S(1)}, u32[]{:S(2)}, u32[]{:S(2)}) %collective-permute-start.10) | collective-permute-done | bytes 426016 | tf_op jit(solution)/shard_map/ppermute | solution.py:429
  48.8 8.9 %shard_map.183 = (bf16[2048,1280]{1,0:T(8,128)(2,1)S(1)}, bf16[2048,512]{1,0:T(8,128)(2,1)S(1)}, bf16[2048,1024]{1,0:T(8,128)(2,1)S(1)}, bf16[1024,1664]{1,0:T(8,128)(2,1)S(1)}) custom-call(s32[4]{0:T(128)S(1)} %pad_add_fusion.info_ref, bf16[2048,1280]{1,0:T(8,128)(2,1)S(1)} %get-tuple-element.106.taps0_ref.taps_ref, ...), custom_call_target="tpu_custom_call" | custom-call | flops 1342177280 | tf_op jit(solution)/shard_map/pallas_call | solution.py:374
  57.9 1.6 %collective-permute-done.19.refs_7_ = bf16[4,32,1664]{2,1,0:T(8,128)(2,1)S(1)} collective-permute-done((bf16[4,32,1664]{2,1,0:T(8,128)(2,1)S(1)}, bf16[4,32,1664]{2,1,0:T(8,128)(2,1)S(1)}, u32[]{:S(2)}, u32[]{:S(2)}) %collective-permute-start.19) | collective-permute-done | bytes 426016 | tf_op jit(solution)/shard_map/ppermute | solution.py:429
  59.5 18.9 %shard_map.184 = (bf16[2048,512]{1,0:T(8,128)(2,1)S(1)}, bf16[2048,1024]{1,0:T(8,128)(2,1)S(1)}, bf16[1024,1664]{1,0:T(8,128)(2,1)S(1)}, f32[1024,128]{1,0:T(8,1...) custom-call(s32[4]{0:T(128)S(1)} %pad_add_fusion.info_ref, ...), custom_call_target="tpu_custom_call" | custom-call | flops 3221225472 | tf_op jit(solution)/shard_map/pallas_call | solution.py:374
  78.6 4.4 %shard_map.185 = (bf16[2048,1024]{1,0:T(8,128)(2,1)S(1)}, bf16[2048,1024]{1,0:T(8,128)(2,1)S(1)}, f32[8,512]{1,0:T(8,128)S(1)}) custom-call(s32[4]{0:T(128)S(1)} %pad_add_fusion.info_ref, bf16[2048,1024]{1,0:T(8,128)(2,1)S(1)} %get-tuple-element.114.pre1_ref, bf16[1024,1664]{1,0:T(8,128)(2,1)S(1)} %get-tuple-element.115.w1_ref, ...), custom_call_target="tpu_custom_call" | custom-call | flops 805306368 | tf_op jit(solution)/shard_map/pallas_call | solution.py:374
  83.4 1.1 collective-permute-start.23
  84.5 4.6 %shard_map.187 = (bf16[2048,1024]{1,0:T(8,128)(2,1)S(1)}, bf16[2048,1024]{1,0:T(8,128)(2,1)S(1)}, f32[8,512]{1,0:T(8,128)}) custom-call(s32[4]{0:T(128)S(1)} %pad_add_fusion.info_ref, bf16[2048,1024]{1,0:T(8,128)(2,1)S(1)} %get-tuple-element.114.pre1_ref, ...), custom_call_target="tpu_custom_call", output_to_operand_aliasing={{0}: (6, {}), {1}: (7, {})} | custom-call | flops 805306368 | tf_op jit(solution)/shard_map/pallas_call | solution.py:374
  89.2 4.5 %shard_map.188 = (bf16[2,2,4,32,1024]{4,3,2,1,0:T(8,128)(2,1)S(1)}, bf16[2,2,4,32,1024]{4,3,2,1,0:T(8,128)(2,1)S(1)}) custom-call(s32[4]{0:T(128)S(1)} %pad_add_fusion.info_ref, bf16[2048,1024]{1,0:T(8,128)(2,1)S(1)} %get-tuple-element.146.pre_ref, bf16[2048,1024]{1,0:T(8,128)(2,1)S(1)} %get-tuple-element.129.proj_ref, ...), custom_call_target="tpu_custom_call" | custom-call | flops 939524096 | tf_op jit(solution)/shard_map/pallas_call | solution.py:374
  93.8 4.2 %shard_map.189 = (f32[1024,128]{1,0:T(8,128)S(1)}, bf16[2,2,4,32,640]{4,3,2,1,0:T(8,128)(2,1)S(1)}, bf16[2,2,4,32,640]{4,3,2,1,0:T(8,128)(2,1)S(1)}) custom-call(s32[4]{0:T(128)S(1)} %pad_add_fusion.info_ref, bf16[2048,1024]{1,0:T(8,128)(2,1)S(1)} %get-tuple-element.146.pre_ref, bf16[2048,1024]{1,0:T(8,128)(2,1)S(1)} %get-tuple-element.129.proj_ref, ...), custom_call_target="tpu_custom_call" | custom-call | flops 671088640 | tf_op jit(solution)/shard_map/pallas_call | solution.py:374
  100.1 1.2 collective-permute-start.26
  102.1 6.8 %shard_map.193 = f32[2048,512]{1,0:T(8,128)} custom-call(s32[4]{0:T(128)S(1)} %pad_add_fusion.info_ref, bf16[2048,1024]{1,0:T(8,128)(2,1)S(1)} %get-tuple-element.129.proj_ref, bf16[2048,1024]{1,0:T(8,128)(2,1)S(1)} %get-tuple-element.146.pre_ref, bf16[1024,1664]{1,0:T(8,128)(2,1)S(1)} %get-tuple-element.116.w0_ref), custom_call_target="tpu_custom_call" | custom-call | flops 1073741824 | bytes 1048576 | tf_op jit(solution)/shard_map/pallas_call | solution.py:374
  108.9 6.3 %shard_map.194 = (bf16[2048,512]{1,0:T(8,128)(2,1)}, bf16[2048,512]{1,0:T(8,128)(2,1)}, f32[128,128]{1,0:T(8,128)S(1)}) custom-call(s32[4]{0:T(128)S(1)} %pad_add_fusion.info_ref, bf16[2048,1280]{1,0:T(8,128)(2,1)S(1)} %get-tuple-element.147.taps_ref.taps1_ref, bf16[2048,512]{1,0:T(8,128)(2,1)S(1)} %get-tuple-element.130.gated_ref.gated0_ref, ...), custom_call_target="tpu_custom_call" | custom-call | flops 1073741824 | bytes 1064960 | tf_op jit(solution)/shard_map/pallas_call | solution.py:374
  117.3 2.6 %collective-permute-start.32 = (bf16[32,1664]{1,0:T(8,128)(2,1)S(1)}, bf16[32,1664]{1,0:T(8,128)(2,1)S(1)}, u32[]{:S(2)}, u32[]{:S(2)}) collective-permute-start(bf16[32,1664]{1,0:T(8,128)(2,1)S(1)} %get-tuple-element.170), channel_id=1, source_target_pairs={{0,16},{1,17},{2,18},{3,19},{4,20},{5,21},{6,22},{7,23},{8,24},{9,... | collective-permute-start | bytes 319496 | tf_op jit(solution)/shard_map/ppermute | solution.py:429
  119.9 1.8 %collective-permute-start.33 = (bf16[32,1664]{1,0:T(8,128)(2,1)S(1)}, bf16[32,1664]{1,0:T(8,128)(2,1)S(1)}, u32[]{:S(2)}, u32[]{:S(2)}) collective-permute-start(bf16[32,1664]{1,0:T(8,128)(2,1)S(1)} %get-tuple-element.171), channel_id=1, source_target_pairs={{0,24},{1,25},{2,26},{3,27},{4,28},{5,29},{6,30},{7,31},{8,16},{9,... | collective-permute-start | bytes 319496 | tf_op jit(solution)/shard_map/ppermute | solution.py:429
  121.6 2.9 %collective-permute-done.27.right_ref = bf16[4,32,1664]{2,1,0:T(8,128)(2,1)S(1)} collective-permute-done((bf16[4,32,1664]{2,1,0:T(8,128)(2,1)S(1)}, bf16[4,32,1664]{2,1,0:T(8,128)(2,1)S(1)}, u32[]{:S(2)}, u32[]{:S(2)}) %collective-permute-start.27) | collective-permute-done | bytes 426016 | tf_op jit(solution)/shard_map/ppermute | solution.py:429
  124.7 2.6 %collective-permute-start.29 = (bf16[32,1664]{1,0:T(8,128)(2,1)S(1)}, bf16[32,1664]{1,0:T(8,128)(2,1)S(1)}, u32[]{:S(2)}, u32[]{:S(2)}) collective-permute-start(bf16[32,1664]{1,0:T(8,128)(2,1)S(1)} %get-tuple-element.164), channel_id=1, source_target_pairs={{0,16},{1,17},{2,18},{3,19},{4,20},{5,21},{6,22},{7,23},{8,24},{9,... | collective-permute-start | bytes 319496 | tf_op jit(solution)/shard_map/ppermute | solution.py:429
  127.3 1.8 %collective-permute-start.30 = (bf16[32,1664]{1,0:T(8,128)(2,1)S(1)}, bf16[32,1664]{1,0:T(8,128)(2,1)S(1)}, u32[]{:S(2)}, u32[]{:S(2)}) collective-permute-start(bf16[32,1664]{1,0:T(8,128)(2,1)S(1)} %get-tuple-element.165), channel_id=1, source_target_pairs={{0,24},{1,25},{2,26},{3,27},{4,28},{5,29},{6,30},{7,31},{8,16},{9,... | collective-permute-start | bytes 319496 | tf_op jit(solution)/shard_map/ppermute | solution.py:429
  129.7 1.6 %collective-permute-done.28.refs_1_ = bf16[32,1664]{1,0:T(8,128)(2,1)S(1)} collective-permute-done((bf16[32,1664]{1,0:T(8,128)(2,1)S(1)}, bf16[32,1664]{1,0:T(8,128)(2,1)S(1)}, u32[]{:S(2)}, u32[]{:S(2)}) %collective-permute-start.28) | collective-permute-done | bytes 106528 | tf_op jit(solution)/shard_map/ppermute | solution.py:429
  131.3 5.9 %collective-permute-done.29.refs_2_ = bf16[32,1664]{1,0:T(8,128)(2,1)S(1)} collective-permute-done((bf16[32,1664]{1,0:T(8,128)(2,1)S(1)}, bf16[32,1664]{1,0:T(8,128)(2,1)S(1)}, u32[]{:S(2)}, u32[]{:S(2)}) %collective-permute-start.29) | collective-permute-done | bytes 106528 | tf_op jit(solution)/shard_map/ppermute | solution.py:429
  (60 shorter events, 11.9 us)
Async XLA Ops:
  1.9 9.0 %collective-permute-start.2 = (bf16[32,1664]{1,0:T(8,128)(2,1)S(1)}, bf16[32,1664]{1,0:T(8,128)(2,1)S(1)}, u32[]{:S(2)}, u32[]{:S(2)}) collective-permute-start(bf16[32,1664]{1,0:T(8,128)(2,1)S(1)} %get-tuple-element.93.refs_0_), channel_id=1, source_target_pairs={{0,24},{1,25},{2,26},{3,27},{4,28},{5,29},{6,30},{7,31},{8,16},{9,... | collective-permute-start | bytes 319496 | tf_op jit(solution)/shard_map/ppermute | solution.py:429
  7.0 9.0 %collective-permute-start.1 = (bf16[32,1664]{1,0:T(8,128)(2,1)S(1)}, bf16[32,1664]{1,0:T(8,128)(2,1)S(1)}, u32[]{:S(2)}, u32[]{:S(2)}) collective-permute-start(bf16[32,1664]{1,0:T(8,128)(2,1)S(1)} %get-tuple-element.93.refs_0_), channel_id=1, source_target_pairs={{0,16},{1,17},{2,18},{3,19},{4,20},{5,21},{6,22},{7,23},{8,24},{9,... | collective-permute-start | bytes 319496 | tf_op jit(solution)/shard_map/ppermute | solution.py:429
  7.0 9.0 %collective-permute-start = (bf16[32,1664]{1,0:T(8,128)(2,1)S(1)}, bf16[32,1664]{1,0:T(8,128)(2,1)S(1)}, u32[]{:S(2)}, u32[]{:S(2)}) collective-permute-start(bf16[32,1664]{1,0:T(8,128)(2,1)S(1)} %get-tuple-element.93.refs_0_), channel_id=1, source_target_pairs={{0,8},{1,9},{2,10},{3,11},{4,12},{5,13},{6,14},{7,15},{8,0},{9,1},... | collective-permute-start | bytes 319496 | tf_op jit(solution)/shard_map/ppermute | solution.py:429
  16.0 14.2 %collective-permute-start.4 = (bf16[4,32,1664]{2,1,0:T(8,128)(2,1)S(1)}, bf16[4,32,1664]{2,1,0:T(8,128)(2,1)S(1)}, u32[]{:S(2)}, u32[]{:S(2)}) collective-permute-start(bf16[4,32,1664]{2,1,0:T(8,128)(2,1)S(1)} %shard_map.179.refs_0_), channel_id=1, source_target_pairs={{0,4},{1,3},{2,6},{3,1},{4,0},{5,7},{6,2},{7,5},{8,12},{9,11},{10,... | collective-permute-start | bytes 1277960 | tf_op jit(solution)/shard_map/ppermute | solution.py:429
  17.6 12.6 %collective-permute-start.3 = (bf16[4,32,1664]{2,1,0:T(8,128)(2,1)S(1)}, bf16[4,32,1664]{2,1,0:T(8,128)(2,1)S(1)}, u32[]{:S(2)}, u32[]{:S(2)}) collective-permute-start(bf16[4,32,1664]{2,1,0:T(8,128)(2,1)S(1)} %shard_map.179.refs_0_), channel_id=1, source_target_pairs={{0,2},{1,5},{2,0},{3,7},{4,6},{5,1},{6,4},{7,3},{8,10},{9,13},{10,... | collective-permute-start | bytes 1277960 | tf_op jit(solution)/shard_map/ppermute | solution.py:429
  19.1 7.7 %collective-permute-start.7 = (bf16[32,1664]{1,0:T(8,128)(2,1)S(1)}, bf16[32,1664]{1,0:T(8,128)(2,1)S(1)}, u32[]{:S(2)}, u32[]{:S(2)}) collective-permute-start(bf16[32,1664]{1,0:T(8,128)(2,1)S(1)} %shard_map.180.refs_0_), channel_id=1, source_target_pairs={{0,24},{1,25},{2,26},{3,27},{4,28},{5,29},{6,30},{7,31},{8,16},{9,... | collective-permute-start | bytes 319496 | tf_op jit(solution)/shard_map/ppermute | solution.py:429
  21.6 8.5 %collective-permute-start.6 = (bf16[32,1664]{1,0:T(8,128)(2,1)S(1)}, bf16[32,1664]{1,0:T(8,128)(2,1)S(1)}, u32[]{:S(2)}, u32[]{:S(2)}) collective-permute-start(bf16[32,1664]{1,0:T(8,128)(2,1)S(1)} %shard_map.180.refs_0_), channel_id=1, source_target_pairs={{0,16},{1,17},{2,18},{3,19},{4,20},{5,21},{6,22},{7,23},{8,24},{9,... | collective-permute-start | bytes 319496 | tf_op jit(solution)/shard_map/ppermute | solution.py:429
  21.6 8.5 %collective-permute-start.5 = (bf16[32,1664]{1,0:T(8,128)(2,1)S(1)}, bf16[32,1664]{1,0:T(8,128)(2,1)S(1)}, u32[]{:S(2)}, u32[]{:S(2)}) collective-permute-start(bf16[32,1664]{1,0:T(8,128)(2,1)S(1)} %shard_map.180.refs_0_), channel_id=1, source_target_pairs={{0,8},{1,9},{2,10},{3,11},{4,12},{5,13},{6,14},{7,15},{8,0},{9,1},... | collective-permute-start | bytes 319496 | tf_op jit(solution)/shard_map/ppermute | solution.py:429
  30.2 12.3 %collective-permute-start.8 = (bf16[4,32,1664]{2,1,0:T(8,128)(2,1)S(1)}, bf16[4,32,1664]{2,1,0:T(8,128)(2,1)S(1)}, u32[]{:S(2)}, u32[]{:S(2)}) collective-permute-start(bf16[4,32,1664]{2,1,0:T(8,128)(2,1)S(1)} %collective-permute-done.3.refs_1_), channel_id=1, source_target_pairs={{0,4},{1,3},{2,6},{3,1},{4,0},{5,7},{6,2},{7,5},{8,12},{9,11},{10,... | collective-permute-start | bytes 1277960 | tf_op jit(solution)/shard_map/ppermute | solution.py:429
  30.7 16.3 %collective-permute-start.10 = (bf16[4,32,1664]{2,1,0:T(8,128)(2,1)S(1)}, bf16[4,32,1664]{2,1,0:T(8,128)(2,1)S(1)}, u32[]{:S(2)}, u32[]{:S(2)}) collective-permute-start(bf16[4,32,1664]{2,1,0:T(8,128)(2,1)S(1)} %shard_map.181.refs_0_), channel_id=1, source_target_pairs={{0,4},{1,3},{2,6},{3,1},{4,0},{5,7},{6,2},{7,5},{8,12},{9,11},{10,... | collective-permute-start | bytes 1277960 | tf_op jit(solution)/shard_map/ppermute | solution.py:429
  32.3 14.7 %collective-permute-start.9 = (bf16[4,32,1664]{2,1,0:T(8,128)(2,1)S(1)}, bf16[4,32,1664]{2,1,0:T(8,128)(2,1)S(1)}, u32[]{:S(2)}, u32[]{:S(2)}) collective-permute-start(bf16[4,32,1664]{2,1,0:T(8,128)(2,1)S(1)} %shard_map.181.refs_0_), channel_id=1, source_target_pairs={{0,2},{1,5},{2,0},{3,7},{4,6},{5,1},{6,4},{7,3},{8,10},{9,13},{10,... | collective-permute-start | bytes 1277960 | tf_op jit(solution)/shard_map/ppermute | solution.py:429
  34.2 13.3 %collective-permute-start.12 = (bf16[4,32,1664]{2,1,0:T(8,128)(2,1)S(1)}, bf16[4,32,1664]{2,1,0:T(8,128)(2,1)S(1)}, u32[]{:S(2)}, u32[]{:S(2)}) collective-permute-start(bf16[4,32,1664]{2,1,0:T(8,128)(2,1)S(1)} %shard_map.179.refs_0_), channel_id=1, source_target_pairs={{0,1},{1,0},{2,3},{3,2},{4,5},{5,4},{6,7},{7,6},{8,9},{9,8},{10,11... | collective-permute-start | bytes 1277960 | tf_op jit(solution)/shard_map/ppermute | solution.py:429
  39.6 8.4 %collective-permute-start.13 = (bf16[4,32,1664]{2,1,0:T(8,128)(2,1)S(1)}, bf16[4,32,1664]{2,1,0:T(8,128)(2,1)S(1)}, u32[]{:S(2)}, u32[]{:S(2)}) collective-permute-start(bf16[4,32,1664]{2,1,0:T(8,128)(2,1)S(1)} %collective-permute-done.3.refs_1_), channel_id=1, source_target_pairs={{0,1},{1,0},{2,3},{3,2},{4,5},{5,4},{6,7},{7,6},{8,9},{9,8},{10,11... | collective-permute-start | bytes 1277960 | tf_op jit(solution)/shard_map/ppermute | solution.py:429
  42.4 5.3 %collective-permute-start.14 = (bf16[4,32,1664]{2,1,0:T(8,128)(2,1)S(1)}, bf16[4,32,1664]{2,1,0:T(8,128)(2,1)S(1)}, u32[]{:S(2)}, u32[]{:S(2)}) collective-permute-start(bf16[4,32,1664]{2,1,0:T(8,128)(2,1)S(1)} %collective-permute-done.4.refs_2_), channel_id=1, source_target_pairs={{0,1},{1,0},{2,3},{3,2},{4,5},{5,4},{6,7},{7,6},{8,9},{9,8},{10,11... | collective-permute-start | bytes 1277960 | tf_op jit(solution)/shard_map/ppermute | solution.py:429
  47.0 10.6 %collective-permute-start.11 = (bf16[4,32,1664]{2,1,0:T(8,128)(2,1)S(1)}, bf16[4,32,1664]{2,1,0:T(8,128)(2,1)S(1)}, u32[]{:S(2)}, u32[]{:S(2)}) collective-permute-start(bf16[4,32,1664]{2,1,0:T(8,128)(2,1)S(1)} %collective-permute-done.9.refs_1_), channel_id=1, source_target_pairs={{0,4},{1,3},{2,6},{3,1},{4,0},{5,7},{6,2},{7,5},{8,12},{9,11},{10,... | collective-permute-start | bytes 1277960 | tf_op jit(solution)/shard_map/ppermute | solution.py:429
  47.5 10.4 %collective-permute-start.16 = (bf16[4,32,1664]{2,1,0:T(8,128)(2,1)S(1)}, bf16[4,32,1664]{2,1,0:T(8,128)(2,1)S(1)}, u32[]{:S(2)}, u32[]{:S(2)}) collective-permute-start(bf16[4,32,1664]{2,1,0:T(8,128)(2,1)S(1)} %shard_map.181.refs_0_), channel_id=1, source_target_pairs={{0,1},{1,0},{2,3},{3,2},{4,5},{5,4},{6,7},{7,6},{8,9},{9,8},{10,11... | collective-permute-start | bytes 1277960 | tf_op jit(solution)/shard_map/ppermute | solution.py:429
  47.8 10.1 %collective-permute-start.17 = (bf16[4,32,1664]{2,1,0:T(8,128)(2,1)S(1)}, bf16[4,32,1664]{2,1,0:T(8,128)(2,1)S(1)}, u32[]{:S(2)}, u32[]{:S(2)}) collective-permute-start(bf16[4,32,1664]{2,1,0:T(8,128)(2,1)S(1)} %collective-permute-done.9.refs_1_), channel_id=1, source_target_pairs={{0,1},{1,0},{2,3},{3,2},{4,5},{5,4},{6,7},{7,6},{8,9},{9,8},{10,11... | collective-permute-start | bytes 1277960 | tf_op jit(solution)/shard_map/ppermute | solution.py:429
  48.0 9.8 %collective-permute-start.18 = (bf16[4,32,1664]{2,1,0:T(8,128)(2,1)S(1)}, bf16[4,32,1664]{2,1,0:T(8,128)(2,1)S(1)}, u32[]{:S(2)}, u32[]{:S(2)}) collective-permute-start(bf16[4,32,1664]{2,1,0:T(8,128)(2,1)S(1)} %collective-permute-done.10.refs_2_), channel_id=1, source_target_pairs={{0,1},{1,0},{2,3},{3,2},{4,5},{5,4},{6,7},{7,6},{8,9},{9,8},{10,11... | collective-permute-start | bytes 1277960 | tf_op jit(solution)/shard_map/ppermute | solution.py:429
  78.4 4.7 %collective-permute-start.20 = (bf16[2,2,4,32,1664]{4,3,2,1,0:T(8,128)(2,1)S(1)}, bf16[2,2,4,32,1664]{4,3,2,1,0:T(8,128)(2,1)S(1)}, u32[]{:S(2)}, u32[]{:S(2)}) collective-permute-start(bf16[2,2,4,32,1664]{4,3,2,1,0:T(8,128)(2,1)S(1)} %get-tuple-element.122), channel_id=1, source_target_pairs={{0,1},{1,0},{2,3},{3,2},{4,5},{5,4},{6,7},{7,6},{8,9},{9,8},{10,11... | collective-permute-start | bytes 5111816 | tf_op jit(solution)/shard_map/ppermute | solution.py:429
  83.4 14.6 %collective-permute-start.23 = (bf16[2,4,32,1664]{3,2,1,0:T(8,128)(2,1)S(1)}, bf16[2,4,32,1664]{3,2,1,0:T(8,128)(2,1)S(1)}, u32[]{:S(2)}, u32[]{:S(2)}) collective-permute-start(bf16[2,4,32,1664]{3,2,1,0:T(8,128)(2,1)S(1)} %get-tuple-element.138), channel_id=1, source_target_pairs={{0,2},{1,5},{2,0},{3,7},{4,6},{5,1},{6,4},{7,3},{8,10},{9,13},{10,... | collective-permute-start | bytes 2555912 | tf_op jit(solution)/shard_map/ppermute | solution.py:429
  93.7 4.9 %collective-permute-start.21 = (bf16[2,2,4,32,1024]{4,3,2,1,0:T(8,128)(2,1)S(1)}, bf16[2,2,4,32,1024]{4,3,2,1,0:T(8,128)(2,1)S(1)}, u32[]{:S(2)}, u32[]{:S(2)}) collective-permute-start(bf16[2,2,4,32,1024]{4,3,2,1,0:T(8,128)(2,1)S(1)} %get-tuple-element.132), channel_id=1, source_target_pairs={{0,1},{1,0},{2,3},{3,2},{4,5},{5,4},{6,7},{7,6},{8,9},{9,8},{10,11... | collective-permute-start | bytes 3145736 | tf_op jit(solution)/shard_map/ppermute | solution.py:429
  98.0 3.3 %collective-permute-start.24 = (bf16[2,2,4,32,640]{4,3,2,1,0:T(8,128)(2,1)S(1)}, bf16[2,2,4,32,640]{4,3,2,1,0:T(8,128)(2,1)S(1)}, u32[]{:S(2)}, u32[]{:S(2)}) collective-permute-start(bf16[2,2,4,32,640]{4,3,2,1,0:T(8,128)(2,1)S(1)} %get-tuple-element.139), channel_id=1, source_target_pairs={{0,1},{1,0},{2,3},{3,2},{4,5},{5,4},{6,7},{7,6},{8,9},{9,8},{10,11... | collective-permute-start | bytes 1966088 | tf_op jit(solution)/shard_map/ppermute | solution.py:429
  98.8 16.4 %collective-permute-start.22 = (bf16[2,4,32,1024]{3,2,1,0:T(8,128)(2,1)S(1)}, bf16[2,4,32,1024]{3,2,1,0:T(8,128)(2,1)S(1)}, u32[]{:S(2)}, u32[]{:S(2)}) collective-permute-start(bf16[2,4,32,1024]{3,2,1,0:T(8,128)(2,1)S(1)} %get-tuple-element.135), channel_id=1, source_target_pairs={{0,2},{1,5},{2,0},{3,7},{4,6},{5,1},{6,4},{7,3},{8,10},{9,13},{10,... | collective-permute-start | bytes 1572872 | tf_op jit(solution)/shard_map/ppermute | solution.py:429
  100.1 15.1 %collective-permute-start.26 = (bf16[4,32,1664]{2,1,0:T(8,128)(2,1)S(1)}, bf16[4,32,1664]{2,1,0:T(8,128)(2,1)S(1)}, u32[]{:S(2)}, u32[]{:S(2)}) collective-permute-start(bf16[4,32,1664]{2,1,0:T(8,128)(2,1)S(1)} %get-tuple-element.143), channel_id=1, source_target_pairs={{0,4},{1,3},{2,6},{3,1},{4,0},{5,7},{6,2},{7,5},{8,12},{9,11},{10,... | collective-permute-start | bytes 1277960 | tf_op jit(solution)/shard_map/ppermute | solution.py:429
  101.5 14.7 %collective-permute-start.25 = (bf16[2,4,32,640]{3,2,1,0:T(8,128)(2,1)S(1)}, bf16[2,4,32,640]{3,2,1,0:T(8,128)(2,1)S(1)}, u32[]{:S(2)}, u32[]{:S(2)}) collective-permute-start(bf16[2,4,32,640]{3,2,1,0:T(8,128)(2,1)S(1)} %get-tuple-element.145), channel_id=1, source_target_pairs={{0,2},{1,5},{2,0},{3,7},{4,6},{5,1},{6,4},{7,3},{8,10},{9,13},{10,... | collective-permute-start | bytes 983048 | tf_op jit(solution)/shard_map/ppermute | solution.py:429
  116.3 8.2 %collective-permute-start.27 = (bf16[4,32,1664]{2,1,0:T(8,128)(2,1)S(1)}, bf16[4,32,1664]{2,1,0:T(8,128)(2,1)S(1)}, u32[]{:S(2)}, u32[]{:S(2)}) collective-permute-start(bf16[4,32,1664]{2,1,0:T(8,128)(2,1)S(1)} %get-tuple-element.161), channel_id=1, source_target_pairs={{0,4},{1,3},{2,6},{3,1},{4,0},{5,7},{6,2},{7,5},{8,12},{9,11},{10,... | collective-permute-start | bytes 1277960 | tf_op jit(solution)/shard_map/ppermute | solution.py:429
  117.2 10.1 %collective-permute-start.31 = (bf16[32,1664]{1,0:T(8,128)(2,1)S(1)}, bf16[32,1664]{1,0:T(8,128)(2,1)S(1)}, u32[]{:S(2)}, u32[]{:S(2)}) collective-permute-start(bf16[32,1664]{1,0:T(8,128)(2,1)S(1)} %get-tuple-element.169), channel_id=1, source_target_pairs={{0,8},{1,9},{2,10},{3,11},{4,12},{5,13},{6,14},{7,15},{8,0},{9,1},... | collective-permute-start | bytes 319496 | tf_op jit(solution)/shard_map/ppermute | solution.py:429
  117.3 12.4 %collective-permute-start.32 = (bf16[32,1664]{1,0:T(8,128)(2,1)S(1)}, bf16[32,1664]{1,0:T(8,128)(2,1)S(1)}, u32[]{:S(2)}, u32[]{:S(2)}) collective-permute-start(bf16[32,1664]{1,0:T(8,128)(2,1)S(1)} %get-tuple-element.170), channel_id=1, source_target_pairs={{0,16},{1,17},{2,18},{3,19},{4,20},{5,21},{6,22},{7,23},{8,24},{9,... | collective-permute-start | bytes 319496 | tf_op jit(solution)/shard_map/ppermute | solution.py:429
  119.9 9.8 %collective-permute-start.33 = (bf16[32,1664]{1,0:T(8,128)(2,1)S(1)}, bf16[32,1664]{1,0:T(8,128)(2,1)S(1)}, u32[]{:S(2)}, u32[]{:S(2)}) collective-permute-start(bf16[32,1664]{1,0:T(8,128)(2,1)S(1)} %get-tuple-element.171), channel_id=1, source_target_pairs={{0,24},{1,25},{2,26},{3,27},{4,28},{5,29},{6,30},{7,31},{8,16},{9,... | collective-permute-start | bytes 319496 | tf_op jit(solution)/shard_map/ppermute | solution.py:429
  124.6 6.7 %collective-permute-start.28 = (bf16[32,1664]{1,0:T(8,128)(2,1)S(1)}, bf16[32,1664]{1,0:T(8,128)(2,1)S(1)}, u32[]{:S(2)}, u32[]{:S(2)}) collective-permute-start(bf16[32,1664]{1,0:T(8,128)(2,1)S(1)} %get-tuple-element.163), channel_id=1, source_target_pairs={{0,8},{1,9},{2,10},{3,11},{4,12},{5,13},{6,14},{7,15},{8,0},{9,1},... | collective-permute-start | bytes 319496 | tf_op jit(solution)/shard_map/ppermute | solution.py:429
  124.7 12.5 %collective-permute-start.29 = (bf16[32,1664]{1,0:T(8,128)(2,1)S(1)}, bf16[32,1664]{1,0:T(8,128)(2,1)S(1)}, u32[]{:S(2)}, u32[]{:S(2)}) collective-permute-start(bf16[32,1664]{1,0:T(8,128)(2,1)S(1)} %get-tuple-element.164), channel_id=1, source_target_pairs={{0,16},{1,17},{2,18},{3,19},{4,20},{5,21},{6,22},{7,23},{8,24},{9,... | collective-permute-start | bytes 319496 | tf_op jit(solution)/shard_map/ppermute | solution.py:429
  127.3 9.9 %collective-permute-start.30 = (bf16[32,1664]{1,0:T(8,128)(2,1)S(1)}, bf16[32,1664]{1,0:T(8,128)(2,1)S(1)}, u32[]{:S(2)}, u32[]{:S(2)}) collective-permute-start(bf16[32,1664]{1,0:T(8,128)(2,1)S(1)} %get-tuple-element.165), channel_id=1, source_target_pairs={{0,24},{1,25},{2,26},{3,27},{4,28},{5,29},{6,30},{7,31},{8,16},{9,... | collective-permute-start | bytes 319496 | tf_op jit(solution)/shard_map/ppermute | solution.py:429
  (2 other events, 3.6 us)

commit v9 on v8

--- a/solution.py
+++ b/solution.py
@@ -572,32 +572,34 @@
     keep = lambda *values: [(value, None) for value in values]
 
     near0 = wires.spread([own0] * wires.rest)
+    taps0, proj1 = call(
+        functools.partial(prepare, size),
+        steps,
+        info,
+        [*((at_home(value), tiled(channels)) for value in (x, go, gs)), (mel_table, table)],
+        kept(gate + size.extra_width + LANES, gate),
+        [],
+        macs,
+        ROOM_0,
+    )
+    taps0, proj1, *near0 = lax.optimization_barrier((taps0, proj1, *near0))
     mine0 = side_by_side(near0)
     one0, two0 = wires.hop(mine0, wires.first), wires.hop(mine0, wires.second)
     own1, _ = lax.optimization_barrier((own1, mine0))
     (own1,) = plain(hand_on, (own1,), [shape_of(rows, size.pack)])
     near1 = wires.spread([own1] * wires.rest)
-    mel_table, *near1 = lax.optimization_barrier((mel_table, *near1))
+    near1 = lax.optimization_barrier(near1[::-1])[::-1]
     mine1 = side_by_side(near1)
-    taps0, proj1 = call(
-        functools.partial(prepare, size),
-        steps,
-        info,
-        [*((at_home(value), tiled(channels)) for value in (x, go, gs)), (mel_table, table)],
-        kept(gate + size.extra_width + LANES, gate),
-        [],
-        macs,
-        ROOM_0,
-    )
-    one0, two0, mine1 = lax.optimization_barrier((one0, two0, mine1))
+    mine1, two0, one0 = lax.optimization_barrier((mine1, two0, one0))
     far0 = wires.hop(one0, wires.second)
     one1, two1 = wires.hop(mine1, wires.first), wires.hop(mine1, wires.second)
-    far0, one1, two1, taps0 = lax.optimization_barrier((far0, one1, two1, taps0))
+    two1, one1, far0 = lax.optimization_barrier((two1, one1, far0))
+    pieces0 = wires.passed(mine0, one0, two0, far0)
     taps1, gated0, slope0, w0 = call(
         functools.partial(forward_0, size, wires),
         sample_count // WIDE,
         info,
-        keep(taps0, *wires.passed(mine0, one0, two0, far0)),
+        keep(taps0, *pieces0),
         [*kept(gate + size.extra_width + LANES, channels, gate), whole_w],
         [pltpu.VMEM((1, channels), FULL), pltpu.VMEM((8, channels), FULL)],
         10 * macs,
@@ -707,7 +709,7 @@
     came_a, came_b, came1, samples_grad, residual_out = lax.optimization_barrier(
         (came_a, came_b, came1, samples_grad, residual_out)
     )
-    parts1 = wires.spread(plain(add_and_part, (stay1, came1), blocks_shape))
+    parts1 = lax.optimization_barrier(wires.spread(plain(add_and_part, (stay1, came1), blocks_shape))[::-1])[::-1]
     stay0, leave0 = plain(add_both, (stay_a, came_a, stay_b, came_b), [last_shape] * 2)
     came0 = wires.hop(leave0, wires.second)
     parts0 = wires.spread(plain(add_and_part, (stay0, came0), blocks_shape))

time: 138 us -> 136 us (0.986)
  waiting for transfers between devices: 35.2 us -> 33.2 us
    ppermute x34, waiting for transfers between devices: 35.2 us -> 33.2 us  [hop(): return lax.ppermute(value, AXES, pairs)]
  transfers between devices with their start and end apart: 34 -> 34, of which waited for: 12 -> 12; matrix products, arithmetic and copies ran while one was open for 0% -> 0% of each run, Pallas kernels for 33% -> 34%
where the time goes in v9:
time: 136 us
  Pallas kernels  67.8 us (50%)
  waiting for transfers between devices  33.2 us (24%)
  starting transfers between devices  32.3 us (24%)
  between operations  2.14 us (2%)
    pallas_call x9, Pallas kernels, call(): pl.pallas_call(kernel, grid_spec=pltpu.PrefetchScalarGridSpec(num_scalar_...  64.1 us
    ppermute x34, waiting for transfers between devices, hop(): return lax.ppermute(value, AXES, pairs)  33.2 us
    ppermute x34, starting transfers between devices, hop(): return lax.ppermute(value, AXES, pairs)  32.3 us
  transfers between devices with their start and end apart: 34, of which 12 were waited for; matrix products, arithmetic and copies ran while one was open for 0% of the time, Pallas kernels for 34%

profile of v9, /device:TPU:0, one launch (start us, length us, event | category | flops | bytes accessed | tf_op | source)
XLA Modules:
  0.0 136.1 jit_solution(5183893239268738194)
XLA Ops:
  0.6 1.2 shard_map.178
  1.9 5.1 %collective-permute-start.2 = (bf16[32,1664]{1,0:T(8,128)(2,1)S(1)}, bf16[32,1664]{1,0:T(8,128)(2,1)S(1)}, u32[]{:S(2)}, u32[]{:S(2)}) collective-permute-start(bf16[32,1664]{1,0:T(8,128)(2,1)S(1)} %get-tuple-element.106.refs_0_), channel_id=1, source_target_pairs={{0,24},{1,25},{2,26},{3,27},{4,28},{5,29},{6,30},{7,31},{8,16},{9,... | collective-permute-start | bytes 319496 | tf_op jit(solution)/shard_map/ppermute | solution.py:429
  9.0 5.4 %shard_map.179 = (bf16[2048,1280]{1,0:T(8,128)(2,1)S(1)}, bf16[2048,1024]{1,0:T(8,128)(2,1)S(1)}) custom-call(s32[4]{0:T(128)S(1)} %pad_add_fusion.info_ref, bf16[2048,512]{1,0:T(8,128)(2,1)} %bitcast.18, bf16[2048,512]{1,0:T(8,128)(2,1)} %bitcast.19, bf16[2048,512]{1,0:T(8,128)(2,1)} %bitcast.20, bf16[128,128]{1,0:T(8,128)(2,1)S(1)} %get-tuple-element.102.mel_ref), custom_call_target="tpu_custom_call" | custom-call | flops 134217728 | bytes 1581056 | tf_op jit(solution)/shard_map/pallas_call | solution.py:374
  14.4 1.5 %collective-permute-done.1.refs_2_ = bf16[32,1664]{1,0:T(8,128)(2,1)S(1)} collective-permute-done((bf16[32,1664]{1,0:T(8,128)(2,1)S(1)}, bf16[32,1664]{1,0:T(8,128)(2,1)S(1)}, u32[]{:S(2)}, u32[]{:S(2)}) %collective-permute-start.1) | collective-permute-done | bytes 106528 | tf_op jit(solution)/shard_map/ppermute | solution.py:429
  16.0 1.6 %collective-permute-start.7 = (bf16[4,32,1664]{2,1,0:T(8,128)(2,1)S(1)}, bf16[4,32,1664]{2,1,0:T(8,128)(2,1)S(1)}, u32[]{:S(2)}, u32[]{:S(2)}) collective-permute-start(bf16[4,32,1664]{2,1,0:T(8,128)(2,1)S(1)} %shard_map.180.refs_0_), channel_id=1, source_target_pairs={{0,2},{1,5},{2,0},{3,7},{4,6},{5,1},{6,4},{7,3},{8,10},{9,13},{10,... | collective-permute-start | bytes 1277960 | tf_op jit(solution)/shard_map/ppermute | solution.py:429
  17.6 1.5 %collective-permute-start.6 = (bf16[4,32,1664]{2,1,0:T(8,128)(2,1)S(1)}, bf16[4,32,1664]{2,1,0:T(8,128)(2,1)S(1)}, u32[]{:S(2)}, u32[]{:S(2)}) collective-permute-start(bf16[4,32,1664]{2,1,0:T(8,128)(2,1)S(1)} %shard_map.180.refs_0_), channel_id=1, source_target_pairs={{0,4},{1,3},{2,6},{3,1},{4,0},{5,7},{6,2},{7,5},{8,12},{9,11},{10,... | collective-permute-start | bytes 1277960 | tf_op jit(solution)/shard_map/ppermute | solution.py:429
  19.5 2.7 %collective-permute-start.4 = (bf16[32,1664]{1,0:T(8,128)(2,1)S(1)}, bf16[32,1664]{1,0:T(8,128)(2,1)S(1)}, u32[]{:S(2)}, u32[]{:S(2)}) collective-permute-start(bf16[32,1664]{1,0:T(8,128)(2,1)S(1)} %shard_map.181.refs_0_), channel_id=1, source_target_pairs={{0,16},{1,17},{2,18},{3,19},{4,20},{5,21},{6,22},{7,23},{8,24},{9,... | collective-permute-start | bytes 319496 | tf_op jit(solution)/shard_map/ppermute | solution.py:429
  22.2 1.3 collective-permute-start.3
  23.8 5.5 %collective-permute-done.4.refs_2_ = bf16[32,1664]{1,0:T(8,128)(2,1)S(1)} collective-permute-done((bf16[32,1664]{1,0:T(8,128)(2,1)S(1)}, bf16[32,1664]{1,0:T(8,128)(2,1)S(1)}, u32[]{:S(2)}, u32[]{:S(2)}) %collective-permute-start.4) | collective-permute-done | bytes 106528 | tf_op jit(solution)/shard_map/ppermute | solution.py:429
  30.5 1.5 %collective-permute-start.8 = (bf16[4,32,1664]{2,1,0:T(8,128)(2,1)S(1)}, bf16[4,32,1664]{2,1,0:T(8,128)(2,1)S(1)}, u32[]{:S(2)}, u32[]{:S(2)}) collective-permute-start(bf16[4,32,1664]{2,1,0:T(8,128)(2,1)S(1)} %shard_map.182.refs_0_), channel_id=1, source_target_pairs={{0,4},{1,3},{2,6},{3,1},{4,0},{5,7},{6,2},{7,5},{8,12},{9,11},{10,... | collective-permute-start | bytes 1277960 | tf_op jit(solution)/shard_map/ppermute | solution.py:429
  32.5 8.1 %collective-permute-done.10.refs_3_ = bf16[4,32,1664]{2,1,0:T(8,128)(2,1)S(1)} collective-permute-done((bf16[4,32,1664]{2,1,0:T(8,128)(2,1)S(1)}, bf16[4,32,1664]{2,1,0:T(8,128)(2,1)S(1)}, u32[]{:S(2)}, u32[]{:S(2)}) %collective-permute-start.10) | collective-permute-done | bytes 426016 | tf_op jit(solution)/shard_map/ppermute | solution.py:429
  40.7 2.1 %collective-permute-done.9.refs_1_ = bf16[4,32,1664]{2,1,0:T(8,128)(2,1)S(1)} collective-permute-done((bf16[4,32,1664]{2,1,0:T(8,128)(2,1)S(1)}, bf16[4,32,1664]{2,1,0:T(8,128)(2,1)S(1)}, u32[]{:S(2)}, u32[]{:S(2)}) %collective-permute-start.9) | collective-permute-done | bytes 426016 | tf_op jit(solution)/shard_map/ppermute | solution.py:429
  42.7 2.5 %collective-permute-done.8.refs_2_ = bf16[4,32,1664]{2,1,0:T(8,128)(2,1)S(1)} collective-permute-done((bf16[4,32,1664]{2,1,0:T(8,128)(2,1)S(1)}, bf16[4,32,1664]{2,1,0:T(8,128)(2,1)S(1)}, u32[]{:S(2)}, u32[]{:S(2)}) %collective-permute-start.8) | collective-permute-done | bytes 426016 | tf_op jit(solution)/shard_map/ppermute | solution.py:429
  47.0 8.9 %shard_map.183 = (bf16[2048,1280]{1,0:T(8,128)(2,1)S(1)}, bf16[2048,512]{1,0:T(8,128)(2,1)S(1)}, bf16[2048,1024]{1,0:T(8,128)(2,1)S(1)}, bf16[1024,1664]{1,0:T(8,128)(2,1)S(1)}) custom-call(s32[4]{0:T(128)S(1)} %pad_add_fusion.info_ref, bf16[2048,1280]{1,0:T(8,128)(2,1)S(1)} %get-tuple-element.118.taps0_ref.taps_ref, ...), custom_call_target="tpu_custom_call" | custom-call | flops 1342177280 | tf_op jit(solution)/shard_map/pallas_call | solution.py:374
  56.1 1.6 %collective-permute-done.19.refs_7_ = bf16[4,32,1664]{2,1,0:T(8,128)(2,1)S(1)} collective-permute-done((bf16[4,32,1664]{2,1,0:T(8,128)(2,1)S(1)}, bf16[4,32,1664]{2,1,0:T(8,128)(2,1)S(1)}, u32[]{:S(2)}, u32[]{:S(2)}) %collective-permute-start.19) | collective-permute-done | bytes 426016 | tf_op jit(solution)/shard_map/ppermute | solution.py:429
  57.7 18.9 %shard_map.184 = (bf16[2048,512]{1,0:T(8,128)(2,1)S(1)}, bf16[2048,1024]{1,0:T(8,128)(2,1)S(1)}, bf16[1024,1664]{1,0:T(8,128)(2,1)S(1)}, f32[1024,128]{1,0:T(8,1...) custom-call(s32[4]{0:T(128)S(1)} %pad_add_fusion.info_ref, ...), custom_call_target="tpu_custom_call" | custom-call | flops 3221225472 | tf_op jit(solution)/shard_map/pallas_call | solution.py:374
  76.8 4.6 %shard_map.185 = (bf16[2048,1024]{1,0:T(8,128)(2,1)S(1)}, bf16[2048,1024]{1,0:T(8,128)(2,1)S(1)}, f32[8,512]{1,0:T(8,128)S(1)}) custom-call(s32[4]{0:T(128)S(1)} %pad_add_fusion.info_ref, bf16[2048,1024]{1,0:T(8,128)(2,1)S(1)} %get-tuple-element.126.pre1_ref, bf16[1024,1664]{1,0:T(8,128)(2,1)S(1)} %get-tuple-element.127.w1_ref, ...), custom_call_target="tpu_custom_call" | custom-call | flops 805306368 | tf_op jit(solution)/shard_map/pallas_call | solution.py:374
  82.9 4.4 %shard_map.187 = (bf16[2048,1024]{1,0:T(8,128)(2,1)S(1)}, bf16[2048,1024]{1,0:T(8,128)(2,1)S(1)}, f32[8,512]{1,0:T(8,128)}) custom-call(s32[4]{0:T(128)S(1)} %pad_add_fusion.info_ref, bf16[2048,1024]{1,0:T(8,128)(2,1)S(1)} %get-tuple-element.126.pre1_ref, ...), custom_call_target="tpu_custom_call", output_to_operand_aliasing={{0}: (6, {}), {1}: (7, {})} | custom-call | flops 805306368 | tf_op jit(solution)/shard_map/pallas_call | solution.py:374
  87.4 4.5 %shard_map.188 = (bf16[2,2,4,32,1024]{4,3,2,1,0:T(8,128)(2,1)S(1)}, bf16[2,2,4,32,1024]{4,3,2,1,0:T(8,128)(2,1)S(1)}) custom-call(s32[4]{0:T(128)S(1)} %pad_add_fusion.info_ref, bf16[2048,1024]{1,0:T(8,128)(2,1)S(1)} %get-tuple-element.158.pre_ref, bf16[2048,1024]{1,0:T(8,128)(2,1)S(1)} %get-tuple-element.141.proj_ref, ...), custom_call_target="tpu_custom_call" | custom-call | flops 939524096 | tf_op jit(solution)/shard_map/pallas_call | solution.py:374
  92.0 4.2 %shard_map.189 = (f32[1024,128]{1,0:T(8,128)S(1)}, bf16[2,2,4,32,640]{4,3,2,1,0:T(8,128)(2,1)S(1)}, bf16[2,2,4,32,640]{4,3,2,1,0:T(8,128)(2,1)S(1)}) custom-call(s32[4]{0:T(128)S(1)} %pad_add_fusion.info_ref, bf16[2048,1024]{1,0:T(8,128)(2,1)S(1)} %get-tuple-element.158.pre_ref, bf16[2048,1024]{1,0:T(8,128)(2,1)S(1)} %get-tuple-element.141.proj_ref, ...), custom_call_target="tpu_custom_call" | custom-call | flops 671088640 | tf_op jit(solution)/shard_map/pallas_call | solution.py:374
  97.0 1.1 collective-permute-start.22
  98.3 1.2 collective-permute-start.26
  100.3 6.8 %shard_map.193 = f32[2048,512]{1,0:T(8,128)} custom-call(s32[4]{0:T(128)S(1)} %pad_add_fusion.info_ref, bf16[2048,1024]{1,0:T(8,128)(2,1)S(1)} %get-tuple-element.141.proj_ref, bf16[2048,1024]{1,0:T(8,128)(2,1)S(1)} %get-tuple-element.158.pre_ref, bf16[1024,1664]{1,0:T(8,128)(2,1)S(1)} %get-tuple-element.128.w0_ref), custom_call_target="tpu_custom_call" | custom-call | flops 1073741824 | bytes 1048576 | tf_op jit(solution)/shard_map/pallas_call | solution.py:374
  107.1 6.3 %shard_map.194 = (bf16[2048,512]{1,0:T(8,128)(2,1)}, bf16[2048,512]{1,0:T(8,128)(2,1)}, f32[128,128]{1,0:T(8,128)S(1)}) custom-call(s32[4]{0:T(128)S(1)} %pad_add_fusion.info_ref, bf16[2048,1280]{1,0:T(8,128)(2,1)S(1)} %get-tuple-element.159.taps_ref.taps1_ref, bf16[2048,512]{1,0:T(8,128)(2,1)S(1)} %get-tuple-element.142.gated_ref.gated0_ref, ...), custom_call_target="tpu_custom_call" | custom-call | flops 1073741824 | bytes 1064960 | tf_op jit(solution)/shard_map/pallas_call | solution.py:374
  115.4 1.7 %collective-permute-start.31 = (bf16[32,1664]{1,0:T(8,128)(2,1)S(1)}, bf16[32,1664]{1,0:T(8,128)(2,1)S(1)}, u32[]{:S(2)}, u32[]{:S(2)}) collective-permute-start(bf16[32,1664]{1,0:T(8,128)(2,1)S(1)} %get-tuple-element.180), channel_id=1, source_target_pairs={{0,24},{1,25},{2,26},{3,27},{4,28},{5,29},{6,30},{7,31},{8,16},{9,... | collective-permute-start | bytes 319496 | tf_op jit(solution)/shard_map/ppermute | solution.py:429
  117.1 1.4 %collective-permute-start.32 = (bf16[32,1664]{1,0:T(8,128)(2,1)S(1)}, bf16[32,1664]{1,0:T(8,128)(2,1)S(1)}, u32[]{:S(2)}, u32[]{:S(2)}) collective-permute-start(bf16[32,1664]{1,0:T(8,128)(2,1)S(1)} %get-tuple-element.181), channel_id=1, source_target_pairs={{0,16},{1,17},{2,18},{3,19},{4,20},{5,21},{6,22},{7,23},{8,24},{9,... | collective-permute-start | bytes 319496 | tf_op jit(solution)/shard_map/ppermute | solution.py:429
  118.6 1.3 collective-permute-start.33
  119.8 2.9 %collective-permute-done.27.right_ref = bf16[4,32,1664]{2,1,0:T(8,128)(2,1)S(1)} collective-permute-done((bf16[4,32,1664]{2,1,0:T(8,128)(2,1)S(1)}, bf16[4,32,1664]{2,1,0:T(8,128)(2,1)S(1)}, u32[]{:S(2)}, u32[]{:S(2)}) %collective-permute-start.27) | collective-permute-done | bytes 426016 | tf_op jit(solution)/shard_map/ppermute | solution.py:429
  122.8 1.3 collective-permute-start.28
  125.1 2.2 %collective-permute-start.30 = (bf16[32,1664]{1,0:T(8,128)(2,1)S(1)}, bf16[32,1664]{1,0:T(8,128)(2,1)S(1)}, u32[]{:S(2)}, u32[]{:S(2)}) collective-permute-start(bf16[32,1664]{1,0:T(8,128)(2,1)S(1)} %get-tuple-element.177), channel_id=1, source_target_pairs={{0,24},{1,25},{2,26},{3,27},{4,28},{5,29},{6,30},{7,31},{8,16},{9,... | collective-permute-start | bytes 319496 | tf_op jit(solution)/shard_map/ppermute | solution.py:429
  127.9 4.9 %collective-permute-done.32.refs_6_ = bf16[32,1664]{1,0:T(8,128)(2,1)S(1)} collective-permute-done((bf16[32,1664]{1,0:T(8,128)(2,1)S(1)}, bf16[32,1664]{1,0:T(8,128)(2,1)S(1)}, u32[]{:S(2)}, u32[]{:S(2)}) %collective-permute-start.32) | collective-permute-done | bytes 106528 | tf_op jit(solution)/shard_map/ppermute | solution.py:429
  132.8 2.2 %collective-permute-done.29.refs_2_ = bf16[32,1664]{1,0:T(8,128)(2,1)S(1)} collective-permute-done((bf16[32,1664]{1,0:T(8,128)(2,1)S(1)}, bf16[32,1664]{1,0:T(8,128)(2,1)S(1)}, u32[]{:S(2)}, u32[]{:S(2)}) %collective-permute-start.29) | collective-permute-done | bytes 106528 | tf_op jit(solution)/shard_map/ppermute | solution.py:429
  (60 shorter events, 13.4 us)
Async XLA Ops:
  1.9 12.5 %collective-permute-start.2 = (bf16[32,1664]{1,0:T(8,128)(2,1)S(1)}, bf16[32,1664]{1,0:T(8,128)(2,1)S(1)}, u32[]{:S(2)}, u32[]{:S(2)}) collective-permute-start(bf16[32,1664]{1,0:T(8,128)(2,1)S(1)} %get-tuple-element.106.refs_0_), channel_id=1, source_target_pairs={{0,24},{1,25},{2,26},{3,27},{4,28},{5,29},{6,30},{7,31},{8,16},{9,... | collective-permute-start | bytes 319496 | tf_op jit(solution)/shard_map/ppermute | solution.py:429
  7.0 9.0 %collective-permute-start.1 = (bf16[32,1664]{1,0:T(8,128)(2,1)S(1)}, bf16[32,1664]{1,0:T(8,128)(2,1)S(1)}, u32[]{:S(2)}, u32[]{:S(2)}) collective-permute-start(bf16[32,1664]{1,0:T(8,128)(2,1)S(1)} %get-tuple-element.106.refs_0_), channel_id=1, source_target_pairs={{0,16},{1,17},{2,18},{3,19},{4,20},{5,21},{6,22},{7,23},{8,24},{9,... | collective-permute-start | bytes 319496 | tf_op jit(solution)/shard_map/ppermute | solution.py:429
  7.0 9.0 %collective-permute-start = (bf16[32,1664]{1,0:T(8,128)(2,1)S(1)}, bf16[32,1664]{1,0:T(8,128)(2,1)S(1)}, u32[]{:S(2)}, u32[]{:S(2)}) collective-permute-start(bf16[32,1664]{1,0:T(8,128)(2,1)S(1)} %get-tuple-element.106.refs_0_), channel_id=1, source_target_pairs={{0,8},{1,9},{2,10},{3,11},{4,12},{5,13},{6,14},{7,15},{8,0},{9,1},... | collective-permute-start | bytes 319496 | tf_op jit(solution)/shard_map/ppermute | solution.py:429
  16.0 13.4 %collective-permute-start.7 = (bf16[4,32,1664]{2,1,0:T(8,128)(2,1)S(1)}, bf16[4,32,1664]{2,1,0:T(8,128)(2,1)S(1)}, u32[]{:S(2)}, u32[]{:S(2)}) collective-permute-start(bf16[4,32,1664]{2,1,0:T(8,128)(2,1)S(1)} %shard_map.180.refs_0_), channel_id=1, source_target_pairs={{0,2},{1,5},{2,0},{3,7},{4,6},{5,1},{6,4},{7,3},{8,10},{9,13},{10,... | collective-permute-start | bytes 1277960 | tf_op jit(solution)/shard_map/ppermute | solution.py:429
  17.6 11.8 %collective-permute-start.6 = (bf16[4,32,1664]{2,1,0:T(8,128)(2,1)S(1)}, bf16[4,32,1664]{2,1,0:T(8,128)(2,1)S(1)}, u32[]{:S(2)}, u32[]{:S(2)}) collective-permute-start(bf16[4,32,1664]{2,1,0:T(8,128)(2,1)S(1)} %shard_map.180.refs_0_), channel_id=1, source_target_pairs={{0,4},{1,3},{2,6},{3,1},{4,0},{5,7},{6,2},{7,5},{8,12},{9,11},{10,... | collective-permute-start | bytes 1277960 | tf_op jit(solution)/shard_map/ppermute | solution.py:429
  19.1 4.8 %collective-permute-start.5 = (bf16[32,1664]{1,0:T(8,128)(2,1)S(1)}, bf16[32,1664]{1,0:T(8,128)(2,1)S(1)}, u32[]{:S(2)}, u32[]{:S(2)}) collective-permute-start(bf16[32,1664]{1,0:T(8,128)(2,1)S(1)} %shard_map.181.refs_0_), channel_id=1, source_target_pairs={{0,8},{1,9},{2,10},{3,11},{4,12},{5,13},{6,14},{7,15},{8,0},{9,1},... | collective-permute-start | bytes 319496 | tf_op jit(solution)/shard_map/ppermute | solution.py:429
  19.5 9.8 %collective-permute-start.4 = (bf16[32,1664]{1,0:T(8,128)(2,1)S(1)}, bf16[32,1664]{1,0:T(8,128)(2,1)S(1)}, u32[]{:S(2)}, u32[]{:S(2)}) collective-permute-start(bf16[32,1664]{1,0:T(8,128)(2,1)S(1)} %shard_map.181.refs_0_), channel_id=1, source_target_pairs={{0,16},{1,17},{2,18},{3,19},{4,20},{5,21},{6,22},{7,23},{8,24},{9,... | collective-permute-start | bytes 319496 | tf_op jit(solution)/shard_map/ppermute | solution.py:429
  22.2 7.2 %collective-permute-start.3 = (bf16[32,1664]{1,0:T(8,128)(2,1)S(1)}, bf16[32,1664]{1,0:T(8,128)(2,1)S(1)}, u32[]{:S(2)}, u32[]{:S(2)}) collective-permute-start(bf16[32,1664]{1,0:T(8,128)(2,1)S(1)} %shard_map.181.refs_0_), channel_id=1, source_target_pairs={{0,24},{1,25},{2,26},{3,27},{4,28},{5,29},{6,30},{7,31},{8,16},{9,... | collective-permute-start | bytes 319496 | tf_op jit(solution)/shard_map/ppermute | solution.py:429
  29.4 11.3 %collective-permute-start.10 = (bf16[4,32,1664]{2,1,0:T(8,128)(2,1)S(1)}, bf16[4,32,1664]{2,1,0:T(8,128)(2,1)S(1)}, u32[]{:S(2)}, u32[]{:S(2)}) collective-permute-start(bf16[4,32,1664]{2,1,0:T(8,128)(2,1)S(1)} %collective-permute-done.7.refs_1_), channel_id=1, source_target_pairs={{0,4},{1,3},{2,6},{3,1},{4,0},{5,7},{6,2},{7,5},{8,12},{9,11},{10,... | collective-permute-start | bytes 1277960 | tf_op jit(solution)/shard_map/ppermute | solution.py:429
  30.0 12.8 %collective-permute-start.9 = (bf16[4,32,1664]{2,1,0:T(8,128)(2,1)S(1)}, bf16[4,32,1664]{2,1,0:T(8,128)(2,1)S(1)}, u32[]{:S(2)}, u32[]{:S(2)}) collective-permute-start(bf16[4,32,1664]{2,1,0:T(8,128)(2,1)S(1)} %shard_map.182.refs_0_), channel_id=1, source_target_pairs={{0,2},{1,5},{2,0},{3,7},{4,6},{5,1},{6,4},{7,3},{8,10},{9,13},{10,... | collective-permute-start | bytes 1277960 | tf_op jit(solution)/shard_map/ppermute | solution.py:429
  30.5 14.7 %collective-permute-start.8 = (bf16[4,32,1664]{2,1,0:T(8,128)(2,1)S(1)}, bf16[4,32,1664]{2,1,0:T(8,128)(2,1)S(1)}, u32[]{:S(2)}, u32[]{:S(2)}) collective-permute-start(bf16[4,32,1664]{2,1,0:T(8,128)(2,1)S(1)} %shard_map.182.refs_0_), channel_id=1, source_target_pairs={{0,4},{1,3},{2,6},{3,1},{4,0},{5,7},{6,2},{7,5},{8,12},{9,11},{10,... | collective-permute-start | bytes 1277960 | tf_op jit(solution)/shard_map/ppermute | solution.py:429
  32.0 13.5 %collective-permute-start.12 = (bf16[4,32,1664]{2,1,0:T(8,128)(2,1)S(1)}, bf16[4,32,1664]{2,1,0:T(8,128)(2,1)S(1)}, u32[]{:S(2)}, u32[]{:S(2)}) collective-permute-start(bf16[4,32,1664]{2,1,0:T(8,128)(2,1)S(1)} %shard_map.180.refs_0_), channel_id=1, source_target_pairs={{0,1},{1,0},{2,3},{3,2},{4,5},{5,4},{6,7},{7,6},{8,9},{9,8},{10,11... | collective-permute-start | bytes 1277960 | tf_op jit(solution)/shard_map/ppermute | solution.py:429
  32.0 14.0 %collective-permute-start.13 = (bf16[4,32,1664]{2,1,0:T(8,128)(2,1)S(1)}, bf16[4,32,1664]{2,1,0:T(8,128)(2,1)S(1)}, u32[]{:S(2)}, u32[]{:S(2)}) collective-permute-start(bf16[4,32,1664]{2,1,0:T(8,128)(2,1)S(1)} %collective-permute-done.7.refs_1_), channel_id=1, source_target_pairs={{0,1},{1,0},{2,3},{3,2},{4,5},{5,4},{6,7},{7,6},{8,9},{9,8},{10,11... | collective-permute-start | bytes 1277960 | tf_op jit(solution)/shard_map/ppermute | solution.py:429
  40.7 5.3 %collective-permute-start.14 = (bf16[4,32,1664]{2,1,0:T(8,128)(2,1)S(1)}, bf16[4,32,1664]{2,1,0:T(8,128)(2,1)S(1)}, u32[]{:S(2)}, u32[]{:S(2)}) collective-permute-start(bf16[4,32,1664]{2,1,0:T(8,128)(2,1)S(1)} %collective-permute-done.6.refs_2_), channel_id=1, source_target_pairs={{0,1},{1,0},{2,3},{3,2},{4,5},{5,4},{6,7},{7,6},{8,9},{9,8},{10,11... | collective-permute-start | bytes 1277960 | tf_op jit(solution)/shard_map/ppermute | solution.py:429
  45.2 10.7 %collective-permute-start.11 = (bf16[4,32,1664]{2,1,0:T(8,128)(2,1)S(1)}, bf16[4,32,1664]{2,1,0:T(8,128)(2,1)S(1)}, u32[]{:S(2)}, u32[]{:S(2)}) collective-permute-start(bf16[4,32,1664]{2,1,0:T(8,128)(2,1)S(1)} %collective-permute-done.9.refs_1_), channel_id=1, source_target_pairs={{0,4},{1,3},{2,6},{3,1},{4,0},{5,7},{6,2},{7,5},{8,12},{9,11},{10,... | collective-permute-start | bytes 1277960 | tf_op jit(solution)/shard_map/ppermute | solution.py:429
  45.5 10.6 %collective-permute-start.16 = (bf16[4,32,1664]{2,1,0:T(8,128)(2,1)S(1)}, bf16[4,32,1664]{2,1,0:T(8,128)(2,1)S(1)}, u32[]{:S(2)}, u32[]{:S(2)}) collective-permute-start(bf16[4,32,1664]{2,1,0:T(8,128)(2,1)S(1)} %shard_map.182.refs_0_), channel_id=1, source_target_pairs={{0,1},{1,0},{2,3},{3,2},{4,5},{5,4},{6,7},{7,6},{8,9},{9,8},{10,11... | collective-permute-start | bytes 1277960 | tf_op jit(solution)/shard_map/ppermute | solution.py:429
  46.0 10.1 %collective-permute-start.17 = (bf16[4,32,1664]{2,1,0:T(8,128)(2,1)S(1)}, bf16[4,32,1664]{2,1,0:T(8,128)(2,1)S(1)}, u32[]{:S(2)}, u32[]{:S(2)}) collective-permute-start(bf16[4,32,1664]{2,1,0:T(8,128)(2,1)S(1)} %collective-permute-done.9.refs_1_), channel_id=1, source_target_pairs={{0,1},{1,0},{2,3},{3,2},{4,5},{5,4},{6,7},{7,6},{8,9},{9,8},{10,11... | collective-permute-start | bytes 1277960 | tf_op jit(solution)/shard_map/ppermute | solution.py:429
  46.1 10.0 %collective-permute-start.18 = (bf16[4,32,1664]{2,1,0:T(8,128)(2,1)S(1)}, bf16[4,32,1664]{2,1,0:T(8,128)(2,1)S(1)}, u32[]{:S(2)}, u32[]{:S(2)}) collective-permute-start(bf16[4,32,1664]{2,1,0:T(8,128)(2,1)S(1)} %collective-permute-done.8.refs_2_), channel_id=1, source_target_pairs={{0,1},{1,0},{2,3},{3,2},{4,5},{5,4},{6,7},{7,6},{8,9},{9,8},{10,11... | collective-permute-start | bytes 1277960 | tf_op jit(solution)/shard_map/ppermute | solution.py:429
  76.6 4.8 %collective-permute-start.20 = (bf16[2,2,4,32,1664]{4,3,2,1,0:T(8,128)(2,1)S(1)}, bf16[2,2,4,32,1664]{4,3,2,1,0:T(8,128)(2,1)S(1)}, u32[]{:S(2)}, u32[]{:S(2)}) collective-permute-start(bf16[2,2,4,32,1664]{4,3,2,1,0:T(8,128)(2,1)S(1)} %get-tuple-element.134), channel_id=1, source_target_pairs={{0,1},{1,0},{2,3},{3,2},{4,5},{5,4},{6,7},{7,6},{8,9},{9,8},{10,11... | collective-permute-start | bytes 5111816 | tf_op jit(solution)/shard_map/ppermute | solution.py:429
  81.8 14.4 %collective-permute-start.23 = (bf16[2,4,32,1664]{3,2,1,0:T(8,128)(2,1)S(1)}, bf16[2,4,32,1664]{3,2,1,0:T(8,128)(2,1)S(1)}, u32[]{:S(2)}, u32[]{:S(2)}) collective-permute-start(bf16[2,4,32,1664]{3,2,1,0:T(8,128)(2,1)S(1)} %get-tuple-element.150), channel_id=1, source_target_pairs={{0,2},{1,5},{2,0},{3,7},{4,6},{5,1},{6,4},{7,3},{8,10},{9,13},{10,... | collective-permute-start | bytes 2555912 | tf_op jit(solution)/shard_map/ppermute | solution.py:429
  91.9 4.9 %collective-permute-start.21 = (bf16[2,2,4,32,1024]{4,3,2,1,0:T(8,128)(2,1)S(1)}, bf16[2,2,4,32,1024]{4,3,2,1,0:T(8,128)(2,1)S(1)}, u32[]{:S(2)}, u32[]{:S(2)}) collective-permute-start(bf16[2,2,4,32,1024]{4,3,2,1,0:T(8,128)(2,1)S(1)} %get-tuple-element.144), channel_id=1, source_target_pairs={{0,1},{1,0},{2,3},{3,2},{4,5},{5,4},{6,7},{7,6},{8,9},{9,8},{10,11... | collective-permute-start | bytes 3145736 | tf_op jit(solution)/shard_map/ppermute | solution.py:429
  96.2 3.3 %collective-permute-start.24 = (bf16[2,2,4,32,640]{4,3,2,1,0:T(8,128)(2,1)S(1)}, bf16[2,2,4,32,640]{4,3,2,1,0:T(8,128)(2,1)S(1)}, u32[]{:S(2)}, u32[]{:S(2)}) collective-permute-start(bf16[2,2,4,32,640]{4,3,2,1,0:T(8,128)(2,1)S(1)} %get-tuple-element.151), channel_id=1, source_target_pairs={{0,1},{1,0},{2,3},{3,2},{4,5},{5,4},{6,7},{7,6},{8,9},{9,8},{10,11... | collective-permute-start | bytes 1966088 | tf_op jit(solution)/shard_map/ppermute | solution.py:429
  97.0 16.4 %collective-permute-start.22 = (bf16[2,4,32,1024]{3,2,1,0:T(8,128)(2,1)S(1)}, bf16[2,4,32,1024]{3,2,1,0:T(8,128)(2,1)S(1)}, u32[]{:S(2)}, u32[]{:S(2)}) collective-permute-start(bf16[2,4,32,1024]{3,2,1,0:T(8,128)(2,1)S(1)} %get-tuple-element.147), channel_id=1, source_target_pairs={{0,2},{1,5},{2,0},{3,7},{4,6},{5,1},{6,4},{7,3},{8,10},{9,13},{10,... | collective-permute-start | bytes 1572872 | tf_op jit(solution)/shard_map/ppermute | solution.py:429
  98.3 15.1 %collective-permute-start.26 = (bf16[4,32,1664]{2,1,0:T(8,128)(2,1)S(1)}, bf16[4,32,1664]{2,1,0:T(8,128)(2,1)S(1)}, u32[]{:S(2)}, u32[]{:S(2)}) collective-permute-start(bf16[4,32,1664]{2,1,0:T(8,128)(2,1)S(1)} %get-tuple-element.155), channel_id=1, source_target_pairs={{0,4},{1,3},{2,6},{3,1},{4,0},{5,7},{6,2},{7,5},{8,12},{9,11},{10,... | collective-permute-start | bytes 1277960 | tf_op jit(solution)/shard_map/ppermute | solution.py:429
  99.7 14.7 %collective-permute-start.25 = (bf16[2,4,32,640]{3,2,1,0:T(8,128)(2,1)S(1)}, bf16[2,4,32,640]{3,2,1,0:T(8,128)(2,1)S(1)}, u32[]{:S(2)}, u32[]{:S(2)}) collective-permute-start(bf16[2,4,32,640]{3,2,1,0:T(8,128)(2,1)S(1)} %get-tuple-element.157), channel_id=1, source_target_pairs={{0,2},{1,5},{2,0},{3,7},{4,6},{5,1},{6,4},{7,3},{8,10},{9,13},{10,... | collective-permute-start | bytes 983048 | tf_op jit(solution)/shard_map/ppermute | solution.py:429
  114.5 8.2 %collective-permute-start.27 = (bf16[4,32,1664]{2,1,0:T(8,128)(2,1)S(1)}, bf16[4,32,1664]{2,1,0:T(8,128)(2,1)S(1)}, u32[]{:S(2)}, u32[]{:S(2)}) collective-permute-start(bf16[4,32,1664]{2,1,0:T(8,128)(2,1)S(1)} %get-tuple-element.173), channel_id=1, source_target_pairs={{0,4},{1,3},{2,6},{3,1},{4,0},{5,7},{6,2},{7,5},{8,12},{9,11},{10,... | collective-permute-start | bytes 1277960 | tf_op jit(solution)/shard_map/ppermute | solution.py:429
  115.4 9.8 %collective-permute-start.31 = (bf16[32,1664]{1,0:T(8,128)(2,1)S(1)}, bf16[32,1664]{1,0:T(8,128)(2,1)S(1)}, u32[]{:S(2)}, u32[]{:S(2)}) collective-permute-start(bf16[32,1664]{1,0:T(8,128)(2,1)S(1)} %get-tuple-element.180), channel_id=1, source_target_pairs={{0,24},{1,25},{2,26},{3,27},{4,28},{5,29},{6,30},{7,31},{8,16},{9,... | collective-permute-start | bytes 319496 | tf_op jit(solution)/shard_map/ppermute | solution.py:429
  117.1 15.7 %collective-permute-start.32 = (bf16[32,1664]{1,0:T(8,128)(2,1)S(1)}, bf16[32,1664]{1,0:T(8,128)(2,1)S(1)}, u32[]{:S(2)}, u32[]{:S(2)}) collective-permute-start(bf16[32,1664]{1,0:T(8,128)(2,1)S(1)} %get-tuple-element.181), channel_id=1, source_target_pairs={{0,16},{1,17},{2,18},{3,19},{4,20},{5,21},{6,22},{7,23},{8,24},{9,... | collective-permute-start | bytes 319496 | tf_op jit(solution)/shard_map/ppermute | solution.py:429
  118.6 14.3 %collective-permute-start.33 = (bf16[32,1664]{1,0:T(8,128)(2,1)S(1)}, bf16[32,1664]{1,0:T(8,128)(2,1)S(1)}, u32[]{:S(2)}, u32[]{:S(2)}) collective-permute-start(bf16[32,1664]{1,0:T(8,128)(2,1)S(1)} %get-tuple-element.182), channel_id=1, source_target_pairs={{0,8},{1,9},{2,10},{3,11},{4,12},{5,13},{6,14},{7,15},{8,0},{9,1},... | collective-permute-start | bytes 319496 | tf_op jit(solution)/shard_map/ppermute | solution.py:429
  122.8 10.0 %collective-permute-start.28 = (bf16[32,1664]{1,0:T(8,128)(2,1)S(1)}, bf16[32,1664]{1,0:T(8,128)(2,1)S(1)}, u32[]{:S(2)}, u32[]{:S(2)}) collective-permute-start(bf16[32,1664]{1,0:T(8,128)(2,1)S(1)} %get-tuple-element.175), channel_id=1, source_target_pairs={{0,8},{1,9},{2,10},{3,11},{4,12},{5,13},{6,14},{7,15},{8,0},{9,1},... | collective-permute-start | bytes 319496 | tf_op jit(solution)/shard_map/ppermute | solution.py:429
  124.2 10.9 %collective-permute-start.29 = (bf16[32,1664]{1,0:T(8,128)(2,1)S(1)}, bf16[32,1664]{1,0:T(8,128)(2,1)S(1)}, u32[]{:S(2)}, u32[]{:S(2)}) collective-permute-start(bf16[32,1664]{1,0:T(8,128)(2,1)S(1)} %get-tuple-element.176), channel_id=1, source_target_pairs={{0,16},{1,17},{2,18},{3,19},{4,20},{5,21},{6,22},{7,23},{8,24},{9,... | collective-permute-start | bytes 319496 | tf_op jit(solution)/shard_map/ppermute | solution.py:429
  125.1 9.9 %collective-permute-start.30 = (bf16[32,1664]{1,0:T(8,128)(2,1)S(1)}, bf16[32,1664]{1,0:T(8,128)(2,1)S(1)}, u32[]{:S(2)}, u32[]{:S(2)}) collective-permute-start(bf16[32,1664]{1,0:T(8,128)(2,1)S(1)} %get-tuple-element.177), channel_id=1, source_target_pairs={{0,24},{1,25},{2,26},{3,27},{4,28},{5,29},{6,30},{7,31},{8,16},{9,... | collective-permute-start | bytes 319496 | tf_op jit(solution)/shard_map/ppermute | solution.py:429
  (2 other events, 3.6 us)

commit v10 on v9

--- a/solution.py
+++ b/solution.py
@@ -16,7 +16,7 @@
 PART_0 = 1024
 MIB = 1024 * 1024
 HINT = 4
-ROOM_0, ROOM_1, ROOM_2, ROOM_3, ROOM_4, ROOM_5, ROOM_SMALL = 7, 8, 6, 7, 6, 6, 6
+ROOM_0, ROOM_1, ROOM_2, ROOM_3, ROOM_4, ROOM_5, ROOM_SMALL = 7, 8, 8, 7, 6, 6, 6
 LOW = jnp.bfloat16
 FULL = jnp.float32
 
@@ -195,8 +195,8 @@
     step = pl.program_id(0)
     channels = size.channels
     index = last - step
-    tile = rows_of(index, TILE)
-    mask = mask_of(info_ref, index * TILE, TILE)
+    tile = rows_of(index, WIDE)
+    mask = mask_of(info_ref, index * WIDE, WIDE)
 
     @pl.when(step == 0)
     def _():
@@ -204,8 +204,8 @@
 
     pre1 = pre1_ref[tile]
     early = dot(pre1, w1_ref[:, size.early : size.now])
-    place = lax.broadcasted_iota(jnp.int32, (TILE, 1), 0)
-    later = jnp.where(place == TILE - 1, carry_ref[0:1], pltpu.roll(early, TILE - 1, 0))
+    place = lax.broadcasted_iota(jnp.int32, (WIDE, 1), 0)
+    later = jnp.where(place == WIDE - 1, carry_ref[0:1], pltpu.roll(early, WIDE - 1, 0))
     carry_ref[...] = early[:8]
     now = dot(pre1, w1_ref[:, size.now : size.extra])
     res = ((proj1_ref[tile, :channels].astype(FULL) + now + later) * mask).astype(LOW)
@@ -537,7 +537,7 @@
     gate = size.gate
     wires = Wires(dp, cores, gate)
     assert layers == 2 and sample_count % TILE == 0 and TILE == FIRST_DILATION
-    steps = sample_count // TILE
+    steps, wide_steps = sample_count // TILE, sample_count // WIDE
     where = jnp.stack([wires.dp, wires.core]).astype(jnp.int32)
     info = jnp.concatenate([lengths, hops, where])
     x, go, gs = samples[0], grad_out[0], grad_skip[0]
@@ -606,7 +606,7 @@
         ROOM_0,
     )
     far1 = wires.hop(one1, wires.second)
-    far1, taps1 = lax.optimization_barrier((far1, taps1))
+    taps1, far1 = lax.optimization_barrier((taps1, far1))
     gated1, pre1, w1, sums1, here1, away1 = call(
         functools.partial(layer_1, size, wires, steps),
         steps + parts,
@@ -623,8 +623,8 @@
 
     carry = (shape_of(8, channels, dtype=FULL), None)
     begun = call(
-        functools.partial(backward_0, size, steps - 1),
-        steps - steps // 2,
+        functools.partial(backward_0, size, wide_steps - 1),
+        wide_steps - wide_steps // 2,
         info,
         keep(pre1, w1, w0, proj1, slope0),
         [*kept(gate, gate), carry],
@@ -636,8 +636,8 @@
     begun, stay1, leave1 = lax.optimization_barrier((begun, stay1, leave1))
     came1 = wires.hop(leave1, wires.first)
     proj0, pre0, _ = call(
-        functools.partial(backward_0, size, steps // 2 - 1),
-        steps // 2,
+        functools.partial(backward_0, size, wide_steps // 2 - 1),
+        wide_steps // 2,
         info,
         keep(pre1, w1, w0, proj1, slope0, *begun),
         [*kept(gate, gate), carry],

time: 136 us -> 136 us (level)
  transfers between devices with their start and end apart: 34 -> 34, of which waited for: 12 -> 12; matrix products, arithmetic and copies ran while one was open for 0% -> 1% of each run, Pallas kernels for 34% -> 34%
where the time goes in v10:
time: 136 us
  Pallas kernels  67.6 us (50%)
  waiting for transfers between devices  33 us (24%)
  starting transfers between devices  32.4 us (24%)
  between operations  2.14 us (2%)
    pallas_call x9, Pallas kernels, call(): pl.pallas_call(kernel, grid_spec=pltpu.PrefetchScalarGridSpec(num_scalar_...  63.6 us
    ppermute x34, waiting for transfers between devices, hop(): return lax.ppermute(value, AXES, pairs)  33 us
    ppermute x34, starting transfers between devices, hop(): return lax.ppermute(value, AXES, pairs)  32.4 us
    pallas_call x11, Pallas kernels, plain(): pl.pallas_call(kernel, out_shape=shapes, in_specs=[KEPT] * len(operands),...  2.73 us
  transfers between devices with their start and end apart: 34, of which 12 were waited for; matrix products, arithmetic and copies ran while one was open for 1% of the time, Pallas kernels for 34%

profile of v10, /device:TPU:0, one launch (start us, length us, event | category | flops | bytes accessed | tf_op | source)
XLA Modules:
  0.0 135.7 jit_solution(9576482996335272571)
XLA Ops:
  0.6 1.2 shard_map.178
  1.9 5.1 %collective-permute-start.2 = (bf16[32,1664]{1,0:T(8,128)(2,1)S(1)}, bf16[32,1664]{1,0:T(8,128)(2,1)S(1)}, u32[]{:S(2)}, u32[]{:S(2)}) collective-permute-start(bf16[32,1664]{1,0:T(8,128)(2,1)S(1)} %get-tuple-element.106.refs_0_), channel_id=1, source_target_pairs={{0,24},{1,25},{2,26},{3,27},{4,28},{5,29},{6,30},{7,31},{8,16},{9,... | collective-permute-start | bytes 319496 | tf_op jit(solution)/shard_map/ppermute | solution.py:429
  9.0 5.4 %shard_map.179 = (bf16[2048,1280]{1,0:T(8,128)(2,1)S(1)}, bf16[2048,1024]{1,0:T(8,128)(2,1)S(1)}) custom-call(s32[4]{0:T(128)S(1)} %pad_add_fusion.info_ref, bf16[2048,512]{1,0:T(8,128)(2,1)} %bitcast.18, bf16[2048,512]{1,0:T(8,128)(2,1)} %bitcast.19, bf16[2048,512]{1,0:T(8,128)(2,1)} %bitcast.20, bf16[128,128]{1,0:T(8,128)(2,1)S(1)} %get-tuple-element.101.mel_ref), custom_call_target="tpu_custom_call" | custom-call | flops 134217728 | bytes 1581056 | tf_op jit(solution)/shard_map/pallas_call | solution.py:374
  14.4 1.5 %collective-permute-done.1.refs_2_ = bf16[32,1664]{1,0:T(8,128)(2,1)S(1)} collective-permute-done((bf16[32,1664]{1,0:T(8,128)(2,1)S(1)}, bf16[32,1664]{1,0:T(8,128)(2,1)S(1)}, u32[]{:S(2)}, u32[]{:S(2)}) %collective-permute-start.1) | collective-permute-done | bytes 106528 | tf_op jit(solution)/shard_map/ppermute | solution.py:429
  16.0 1.6 %collective-permute-start.7 = (bf16[4,32,1664]{2,1,0:T(8,128)(2,1)S(1)}, bf16[4,32,1664]{2,1,0:T(8,128)(2,1)S(1)}, u32[]{:S(2)}, u32[]{:S(2)}) collective-permute-start(bf16[4,32,1664]{2,1,0:T(8,128)(2,1)S(1)} %shard_map.180.refs_0_), channel_id=1, source_target_pairs={{0,2},{1,5},{2,0},{3,7},{4,6},{5,1},{6,4},{7,3},{8,10},{9,13},{10,... | collective-permute-start | bytes 1277960 | tf_op jit(solution)/shard_map/ppermute | solution.py:429
  17.6 1.5 %collective-permute-start.6 = (bf16[4,32,1664]{2,1,0:T(8,128)(2,1)S(1)}, bf16[4,32,1664]{2,1,0:T(8,128)(2,1)S(1)}, u32[]{:S(2)}, u32[]{:S(2)}) collective-permute-start(bf16[4,32,1664]{2,1,0:T(8,128)(2,1)S(1)} %shard_map.180.refs_0_), channel_id=1, source_target_pairs={{0,4},{1,3},{2,6},{3,1},{4,0},{5,7},{6,2},{7,5},{8,12},{9,11},{10,... | collective-permute-start | bytes 1277960 | tf_op jit(solution)/shard_map/ppermute | solution.py:429
  19.5 2.7 %collective-permute-start.4 = (bf16[32,1664]{1,0:T(8,128)(2,1)S(1)}, bf16[32,1664]{1,0:T(8,128)(2,1)S(1)}, u32[]{:S(2)}, u32[]{:S(2)}) collective-permute-start(bf16[32,1664]{1,0:T(8,128)(2,1)S(1)} %shard_map.181.refs_0_), channel_id=1, source_target_pairs={{0,16},{1,17},{2,18},{3,19},{4,20},{5,21},{6,22},{7,23},{8,24},{9,... | collective-permute-start | bytes 319496 | tf_op jit(solution)/shard_map/ppermute | solution.py:429
  22.2 1.3 collective-permute-start.3
  23.8 5.5 %collective-permute-done.4.refs_2_ = bf16[32,1664]{1,0:T(8,128)(2,1)S(1)} collective-permute-done((bf16[32,1664]{1,0:T(8,128)(2,1)S(1)}, bf16[32,1664]{1,0:T(8,128)(2,1)S(1)}, u32[]{:S(2)}, u32[]{:S(2)}) %collective-permute-start.4) | collective-permute-done | bytes 106528 | tf_op jit(solution)/shard_map/ppermute | solution.py:429
  30.5 1.5 %collective-permute-start.8 = (bf16[4,32,1664]{2,1,0:T(8,128)(2,1)S(1)}, bf16[4,32,1664]{2,1,0:T(8,128)(2,1)S(1)}, u32[]{:S(2)}, u32[]{:S(2)}) collective-permute-start(bf16[4,32,1664]{2,1,0:T(8,128)(2,1)S(1)} %shard_map.182.refs_0_), channel_id=1, source_target_pairs={{0,4},{1,3},{2,6},{3,1},{4,0},{5,7},{6,2},{7,5},{8,12},{9,11},{10,... | collective-permute-start | bytes 1277960 | tf_op jit(solution)/shard_map/ppermute | solution.py:429
  32.5 8.1 %collective-permute-done.10.refs_3_ = bf16[4,32,1664]{2,1,0:T(8,128)(2,1)S(1)} collective-permute-done((bf16[4,32,1664]{2,1,0:T(8,128)(2,1)S(1)}, bf16[4,32,1664]{2,1,0:T(8,128)(2,1)S(1)}, u32[]{:S(2)}, u32[]{:S(2)}) %collective-permute-start.10) | collective-permute-done | bytes 426016 | tf_op jit(solution)/shard_map/ppermute | solution.py:429
  40.7 2.1 %collective-permute-done.9.refs_1_ = bf16[4,32,1664]{2,1,0:T(8,128)(2,1)S(1)} collective-permute-done((bf16[4,32,1664]{2,1,0:T(8,128)(2,1)S(1)}, bf16[4,32,1664]{2,1,0:T(8,128)(2,1)S(1)}, u32[]{:S(2)}, u32[]{:S(2)}) %collective-permute-start.9) | collective-permute-done | bytes 426016 | tf_op jit(solution)/shard_map/ppermute | solution.py:429
  42.7 2.5 %collective-permute-done.8.refs_2_ = bf16[4,32,1664]{2,1,0:T(8,128)(2,1)S(1)} collective-permute-done((bf16[4,32,1664]{2,1,0:T(8,128)(2,1)S(1)}, bf16[4,32,1664]{2,1,0:T(8,128)(2,1)S(1)}, u32[]{:S(2)}, u32[]{:S(2)}) %collective-permute-start.8) | collective-permute-done | bytes 426016 | tf_op jit(solution)/shard_map/ppermute | solution.py:429
  47.0 8.9 %shard_map.183 = (bf16[2048,1280]{1,0:T(8,128)(2,1)S(1)}, bf16[2048,512]{1,0:T(8,128)(2,1)S(1)}, bf16[2048,1024]{1,0:T(8,128)(2,1)S(1)}, bf16[1024,1664]{1,0:T(8,128)(2,1)S(1)}) custom-call(s32[4]{0:T(128)S(1)} %pad_add_fusion.info_ref, bf16[2048,1280]{1,0:T(8,128)(2,1)S(1)} %get-tuple-element.105.taps0_ref.taps_ref, ...), custom_call_target="tpu_custom_call" | custom-call | flops 1342177280 | tf_op jit(solution)/shard_map/pallas_call | solution.py:374
  56.1 1.6 %collective-permute-done.19.refs_7_ = bf16[4,32,1664]{2,1,0:T(8,128)(2,1)S(1)} collective-permute-done((bf16[4,32,1664]{2,1,0:T(8,128)(2,1)S(1)}, bf16[4,32,1664]{2,1,0:T(8,128)(2,1)S(1)}, u32[]{:S(2)}, u32[]{:S(2)}) %collective-permute-start.19) | collective-permute-done | bytes 426016 | tf_op jit(solution)/shard_map/ppermute | solution.py:429
  57.7 19.0 %shard_map.184 = (bf16[2048,512]{1,0:T(8,128)(2,1)S(1)}, bf16[2048,1024]{1,0:T(8,128)(2,1)S(1)}, bf16[1024,1664]{1,0:T(8,128)(2,1)S(1)}, f32[1024,128]{1,0:T(8,1...) custom-call(s32[4]{0:T(128)S(1)} %pad_add_fusion.info_ref, ...), custom_call_target="tpu_custom_call" | custom-call | flops 3221225472 | tf_op jit(solution)/shard_map/pallas_call | solution.py:374
  77.0 4.2 %shard_map.185 = (bf16[2048,1024]{1,0:T(8,128)(2,1)S(1)}, bf16[2048,1024]{1,0:T(8,128)(2,1)S(1)}, f32[8,512]{1,0:T(8,128)S(1)}) custom-call(s32[4]{0:T(128)S(1)} %pad_add_fusion.info_ref, bf16[2048,1024]{1,0:T(8,128)(2,1)S(1)} %get-tuple-element.126.pre1_ref, bf16[1024,1664]{1,0:T(8,128)(2,1)S(1)} %get-tuple-element.127.w1_ref, ...), custom_call_target="tpu_custom_call" | custom-call | flops 805306368 | tf_op jit(solution)/shard_map/pallas_call | solution.py:374
  82.7 4.2 %shard_map.187 = (bf16[2048,1024]{1,0:T(8,128)(2,1)S(1)}, bf16[2048,1024]{1,0:T(8,128)(2,1)S(1)}, f32[8,512]{1,0:T(8,128)}) custom-call(s32[4]{0:T(128)S(1)} %pad_add_fusion.info_ref, bf16[2048,1024]{1,0:T(8,128)(2,1)S(1)} %get-tuple-element.126.pre1_ref, ...), custom_call_target="tpu_custom_call", output_to_operand_aliasing={{0}: (6, {}), {1}: (7, {})} | custom-call | flops 805306368 | tf_op jit(solution)/shard_map/pallas_call | solution.py:374
  86.9 4.5 %shard_map.188 = (bf16[2,2,4,32,1024]{4,3,2,1,0:T(8,128)(2,1)S(1)}, bf16[2,2,4,32,1024]{4,3,2,1,0:T(8,128)(2,1)S(1)}) custom-call(s32[4]{0:T(128)S(1)} %pad_add_fusion.info_ref, bf16[2048,1024]{1,0:T(8,128)(2,1)S(1)} %get-tuple-element.158.pre_ref, bf16[2048,1024]{1,0:T(8,128)(2,1)S(1)} %get-tuple-element.141.proj_ref, ...), custom_call_target="tpu_custom_call" | custom-call | flops 939524096 | tf_op jit(solution)/shard_map/pallas_call | solution.py:374
  91.5 4.2 %shard_map.189 = (f32[1024,128]{1,0:T(8,128)S(1)}, bf16[2,2,4,32,640]{4,3,2,1,0:T(8,128)(2,1)S(1)}, bf16[2,2,4,32,640]{4,3,2,1,0:T(8,128)(2,1)S(1)}) custom-call(s32[4]{0:T(128)S(1)} %pad_add_fusion.info_ref, bf16[2048,1024]{1,0:T(8,128)(2,1)S(1)} %get-tuple-element.158.pre_ref, bf16[2048,1024]{1,0:T(8,128)(2,1)S(1)} %get-tuple-element.141.proj_ref, ...), custom_call_target="tpu_custom_call" | custom-call | flops 671088640 | tf_op jit(solution)/shard_map/pallas_call | solution.py:374
  96.6 1.1 collective-permute-start.22
  98.1 1.2 collective-permute-start.26
  100.1 6.8 %shard_map.193 = f32[2048,512]{1,0:T(8,128)} custom-call(s32[4]{0:T(128)S(1)} %pad_add_fusion.info_ref, bf16[2048,1024]{1,0:T(8,128)(2,1)S(1)} %get-tuple-element.141.proj_ref, bf16[2048,1024]{1,0:T(8,128)(2,1)S(1)} %get-tuple-element.158.pre_ref, bf16[1024,1664]{1,0:T(8,128)(2,1)S(1)} %get-tuple-element.128.w0_ref), custom_call_target="tpu_custom_call" | custom-call | flops 1073741824 | bytes 1048576 | tf_op jit(solution)/shard_map/pallas_call | solution.py:374
  106.9 6.3 %shard_map.194 = (bf16[2048,512]{1,0:T(8,128)(2,1)}, bf16[2048,512]{1,0:T(8,128)(2,1)}, f32[128,128]{1,0:T(8,128)S(1)}) custom-call(s32[4]{0:T(128)S(1)} %pad_add_fusion.info_ref, bf16[2048,1280]{1,0:T(8,128)(2,1)S(1)} %get-tuple-element.159.taps_ref.taps1_ref, bf16[2048,512]{1,0:T(8,128)(2,1)S(1)} %get-tuple-element.142.gated_ref.gated0_ref, ...), custom_call_target="tpu_custom_call" | custom-call | flops 1073741824 | bytes 1064960 | tf_op jit(solution)/shard_map/pallas_call | solution.py:374
  114.9 1.7 %collective-permute-start.31 = (bf16[32,1664]{1,0:T(8,128)(2,1)S(1)}, bf16[32,1664]{1,0:T(8,128)(2,1)S(1)}, u32[]{:S(2)}, u32[]{:S(2)}) collective-permute-start(bf16[32,1664]{1,0:T(8,128)(2,1)S(1)} %get-tuple-element.180), channel_id=1, source_target_pairs={{0,24},{1,25},{2,26},{3,27},{4,28},{5,29},{6,30},{7,31},{8,16},{9,... | collective-permute-start | bytes 319496 | tf_op jit(solution)/shard_map/ppermute | solution.py:429
  116.7 1.5 %collective-permute-start.32 = (bf16[32,1664]{1,0:T(8,128)(2,1)S(1)}, bf16[32,1664]{1,0:T(8,128)(2,1)S(1)}, u32[]{:S(2)}, u32[]{:S(2)}) collective-permute-start(bf16[32,1664]{1,0:T(8,128)(2,1)S(1)} %get-tuple-element.181), channel_id=1, source_target_pairs={{0,16},{1,17},{2,18},{3,19},{4,20},{5,21},{6,22},{7,23},{8,24},{9,... | collective-permute-start | bytes 319496 | tf_op jit(solution)/shard_map/ppermute | solution.py:429
  118.2 1.2 collective-permute-start.33
  119.4 2.9 %collective-permute-done.27.right_ref = bf16[4,32,1664]{2,1,0:T(8,128)(2,1)S(1)} collective-permute-done((bf16[4,32,1664]{2,1,0:T(8,128)(2,1)S(1)}, bf16[4,32,1664]{2,1,0:T(8,128)(2,1)S(1)}, u32[]{:S(2)}, u32[]{:S(2)}) %collective-permute-start.27) | collective-permute-done | bytes 426016 | tf_op jit(solution)/shard_map/ppermute | solution.py:429
  122.4 1.3 collective-permute-start.28
  124.7 2.2 %collective-permute-start.30 = (bf16[32,1664]{1,0:T(8,128)(2,1)S(1)}, bf16[32,1664]{1,0:T(8,128)(2,1)S(1)}, u32[]{:S(2)}, u32[]{:S(2)}) collective-permute-start(bf16[32,1664]{1,0:T(8,128)(2,1)S(1)} %get-tuple-element.177), channel_id=1, source_target_pairs={{0,24},{1,25},{2,26},{3,27},{4,28},{5,29},{6,30},{7,31},{8,16},{9,... | collective-permute-start | bytes 319496 | tf_op jit(solution)/shard_map/ppermute | solution.py:429
  127.5 4.9 %collective-permute-done.32.refs_6_ = bf16[32,1664]{1,0:T(8,128)(2,1)S(1)} collective-permute-done((bf16[32,1664]{1,0:T(8,128)(2,1)S(1)}, bf16[32,1664]{1,0:T(8,128)(2,1)S(1)}, u32[]{:S(2)}, u32[]{:S(2)}) %collective-permute-start.32) | collective-permute-done | bytes 106528 | tf_op jit(solution)/shard_map/ppermute | solution.py:429
  132.4 2.2 %collective-permute-done.29.refs_2_ = bf16[32,1664]{1,0:T(8,128)(2,1)S(1)} collective-permute-done((bf16[32,1664]{1,0:T(8,128)(2,1)S(1)}, bf16[32,1664]{1,0:T(8,128)(2,1)S(1)}, u32[]{:S(2)}, u32[]{:S(2)}) %collective-permute-start.29) | collective-permute-done | bytes 106528 | tf_op jit(solution)/shard_map/ppermute | solution.py:429
  (60 shorter events, 13.4 us)
Async XLA Ops:
  1.9 12.5 %collective-permute-start.2 = (bf16[32,1664]{1,0:T(8,128)(2,1)S(1)}, bf16[32,1664]{1,0:T(8,128)(2,1)S(1)}, u32[]{:S(2)}, u32[]{:S(2)}) collective-permute-start(bf16[32,1664]{1,0:T(8,128)(2,1)S(1)} %get-tuple-element.106.refs_0_), channel_id=1, source_target_pairs={{0,24},{1,25},{2,26},{3,27},{4,28},{5,29},{6,30},{7,31},{8,16},{9,... | collective-permute-start | bytes 319496 | tf_op jit(solution)/shard_map/ppermute | solution.py:429
  7.0 9.0 %collective-permute-start.1 = (bf16[32,1664]{1,0:T(8,128)(2,1)S(1)}, bf16[32,1664]{1,0:T(8,128)(2,1)S(1)}, u32[]{:S(2)}, u32[]{:S(2)}) collective-permute-start(bf16[32,1664]{1,0:T(8,128)(2,1)S(1)} %get-tuple-element.106.refs_0_), channel_id=1, source_target_pairs={{0,16},{1,17},{2,18},{3,19},{4,20},{5,21},{6,22},{7,23},{8,24},{9,... | collective-permute-start | bytes 319496 | tf_op jit(solution)/shard_map/ppermute | solution.py:429
  7.0 9.0 %collective-permute-start = (bf16[32,1664]{1,0:T(8,128)(2,1)S(1)}, bf16[32,1664]{1,0:T(8,128)(2,1)S(1)}, u32[]{:S(2)}, u32[]{:S(2)}) collective-permute-start(bf16[32,1664]{1,0:T(8,128)(2,1)S(1)} %get-tuple-element.106.refs_0_), channel_id=1, source_target_pairs={{0,8},{1,9},{2,10},{3,11},{4,12},{5,13},{6,14},{7,15},{8,0},{9,1},... | collective-permute-start | bytes 319496 | tf_op jit(solution)/shard_map/ppermute | solution.py:429
  16.0 13.4 %collective-permute-start.7 = (bf16[4,32,1664]{2,1,0:T(8,128)(2,1)S(1)}, bf16[4,32,1664]{2,1,0:T(8,128)(2,1)S(1)}, u32[]{:S(2)}, u32[]{:S(2)}) collective-permute-start(bf16[4,32,1664]{2,1,0:T(8,128)(2,1)S(1)} %shard_map.180.refs_0_), channel_id=1, source_target_pairs={{0,2},{1,5},{2,0},{3,7},{4,6},{5,1},{6,4},{7,3},{8,10},{9,13},{10,... | collective-permute-start | bytes 1277960 | tf_op jit(solution)/shard_map/ppermute | solution.py:429
  17.6 11.8 %collective-permute-start.6 = (bf16[4,32,1664]{2,1,0:T(8,128)(2,1)S(1)}, bf16[4,32,1664]{2,1,0:T(8,128)(2,1)S(1)}, u32[]{:S(2)}, u32[]{:S(2)}) collective-permute-start(bf16[4,32,1664]{2,1,0:T(8,128)(2,1)S(1)} %shard_map.180.refs_0_), channel_id=1, source_target_pairs={{0,4},{1,3},{2,6},{3,1},{4,0},{5,7},{6,2},{7,5},{8,12},{9,11},{10,... | collective-permute-start | bytes 1277960 | tf_op jit(solution)/shard_map/ppermute | solution.py:429
  19.1 4.8 %collective-permute-start.5 = (bf16[32,1664]{1,0:T(8,128)(2,1)S(1)}, bf16[32,1664]{1,0:T(8,128)(2,1)S(1)}, u32[]{:S(2)}, u32[]{:S(2)}) collective-permute-start(bf16[32,1664]{1,0:T(8,128)(2,1)S(1)} %shard_map.181.refs_0_), channel_id=1, source_target_pairs={{0,8},{1,9},{2,10},{3,11},{4,12},{5,13},{6,14},{7,15},{8,0},{9,1},... | collective-permute-start | bytes 319496 | tf_op jit(solution)/shard_map/ppermute | solution.py:429
  19.5 9.8 %collective-permute-start.4 = (bf16[32,1664]{1,0:T(8,128)(2,1)S(1)}, bf16[32,1664]{1,0:T(8,128)(2,1)S(1)}, u32[]{:S(2)}, u32[]{:S(2)}) collective-permute-start(bf16[32,1664]{1,0:T(8,128)(2,1)S(1)} %shard_map.181.refs_0_), channel_id=1, source_target_pairs={{0,16},{1,17},{2,18},{3,19},{4,20},{5,21},{6,22},{7,23},{8,24},{9,... | collective-permute-start | bytes 319496 | tf_op jit(solution)/shard_map/ppermute | solution.py:429
  22.2 7.2 %collective-permute-start.3 = (bf16[32,1664]{1,0:T(8,128)(2,1)S(1)}, bf16[32,1664]{1,0:T(8,128)(2,1)S(1)}, u32[]{:S(2)}, u32[]{:S(2)}) collective-permute-start(bf16[32,1664]{1,0:T(8,128)(2,1)S(1)} %shard_map.181.refs_0_), channel_id=1, source_target_pairs={{0,24},{1,25},{2,26},{3,27},{4,28},{5,29},{6,30},{7,31},{8,16},{9,... | collective-permute-start | bytes 319496 | tf_op jit(solution)/shard_map/ppermute | solution.py:429
  29.4 11.3 %collective-permute-start.10 = (bf16[4,32,1664]{2,1,0:T(8,128)(2,1)S(1)}, bf16[4,32,1664]{2,1,0:T(8,128)(2,1)S(1)}, u32[]{:S(2)}, u32[]{:S(2)}) collective-permute-start(bf16[4,32,1664]{2,1,0:T(8,128)(2,1)S(1)} %collective-permute-done.7.refs_1_), channel_id=1, source_target_pairs={{0,4},{1,3},{2,6},{3,1},{4,0},{5,7},{6,2},{7,5},{8,12},{9,11},{10,... | collective-permute-start | bytes 1277960 | tf_op jit(solution)/shard_map/ppermute | solution.py:429
  30.0 12.8 %collective-permute-start.9 = (bf16[4,32,1664]{2,1,0:T(8,128)(2,1)S(1)}, bf16[4,32,1664]{2,1,0:T(8,128)(2,1)S(1)}, u32[]{:S(2)}, u32[]{:S(2)}) collective-permute-start(bf16[4,32,1664]{2,1,0:T(8,128)(2,1)S(1)} %shard_map.182.refs_0_), channel_id=1, source_target_pairs={{0,2},{1,5},{2,0},{3,7},{4,6},{5,1},{6,4},{7,3},{8,10},{9,13},{10,... | collective-permute-start | bytes 1277960 | tf_op jit(solution)/shard_map/ppermute | solution.py:429
  30.5 14.7 %collective-permute-start.8 = (bf16[4,32,1664]{2,1,0:T(8,128)(2,1)S(1)}, bf16[4,32,1664]{2,1,0:T(8,128)(2,1)S(1)}, u32[]{:S(2)}, u32[]{:S(2)}) collective-permute-start(bf16[4,32,1664]{2,1,0:T(8,128)(2,1)S(1)} %shard_map.182.refs_0_), channel_id=1, source_target_pairs={{0,4},{1,3},{2,6},{3,1},{4,0},{5,7},{6,2},{7,5},{8,12},{9,11},{10,... | collective-permute-start | bytes 1277960 | tf_op jit(solution)/shard_map/ppermute | solution.py:429
  32.0 13.5 %collective-permute-start.11 = (bf16[4,32,1664]{2,1,0:T(8,128)(2,1)S(1)}, bf16[4,32,1664]{2,1,0:T(8,128)(2,1)S(1)}, u32[]{:S(2)}, u32[]{:S(2)}) collective-permute-start(bf16[4,32,1664]{2,1,0:T(8,128)(2,1)S(1)} %shard_map.180.refs_0_), channel_id=1, source_target_pairs={{0,1},{1,0},{2,3},{3,2},{4,5},{5,4},{6,7},{7,6},{8,9},{9,8},{10,11... | collective-permute-start | bytes 1277960 | tf_op jit(solution)/shard_map/ppermute | solution.py:429
  32.0 14.0 %collective-permute-start.12 = (bf16[4,32,1664]{2,1,0:T(8,128)(2,1)S(1)}, bf16[4,32,1664]{2,1,0:T(8,128)(2,1)S(1)}, u32[]{:S(2)}, u32[]{:S(2)}) collective-permute-start(bf16[4,32,1664]{2,1,0:T(8,128)(2,1)S(1)} %collective-permute-done.7.refs_1_), channel_id=1, source_target_pairs={{0,1},{1,0},{2,3},{3,2},{4,5},{5,4},{6,7},{7,6},{8,9},{9,8},{10,11... | collective-permute-start | bytes 1277960 | tf_op jit(solution)/shard_map/ppermute | solution.py:429
  40.7 5.3 %collective-permute-start.13 = (bf16[4,32,1664]{2,1,0:T(8,128)(2,1)S(1)}, bf16[4,32,1664]{2,1,0:T(8,128)(2,1)S(1)}, u32[]{:S(2)}, u32[]{:S(2)}) collective-permute-start(bf16[4,32,1664]{2,1,0:T(8,128)(2,1)S(1)} %collective-permute-done.6.refs_2_), channel_id=1, source_target_pairs={{0,1},{1,0},{2,3},{3,2},{4,5},{5,4},{6,7},{7,6},{8,9},{9,8},{10,11... | collective-permute-start | bytes 1277960 | tf_op jit(solution)/shard_map/ppermute | solution.py:429
  45.2 10.7 %collective-permute-start.15 = (bf16[4,32,1664]{2,1,0:T(8,128)(2,1)S(1)}, bf16[4,32,1664]{2,1,0:T(8,128)(2,1)S(1)}, u32[]{:S(2)}, u32[]{:S(2)}) collective-permute-start(bf16[4,32,1664]{2,1,0:T(8,128)(2,1)S(1)} %collective-permute-done.9.refs_1_), channel_id=1, source_target_pairs={{0,4},{1,3},{2,6},{3,1},{4,0},{5,7},{6,2},{7,5},{8,12},{9,11},{10,... | collective-permute-start | bytes 1277960 | tf_op jit(solution)/shard_map/ppermute | solution.py:429
  45.5 10.6 %collective-permute-start.16 = (bf16[4,32,1664]{2,1,0:T(8,128)(2,1)S(1)}, bf16[4,32,1664]{2,1,0:T(8,128)(2,1)S(1)}, u32[]{:S(2)}, u32[]{:S(2)}) collective-permute-start(bf16[4,32,1664]{2,1,0:T(8,128)(2,1)S(1)} %shard_map.182.refs_0_), channel_id=1, source_target_pairs={{0,1},{1,0},{2,3},{3,2},{4,5},{5,4},{6,7},{7,6},{8,9},{9,8},{10,11... | collective-permute-start | bytes 1277960 | tf_op jit(solution)/shard_map/ppermute | solution.py:429
  46.0 10.1 %collective-permute-start.17 = (bf16[4,32,1664]{2,1,0:T(8,128)(2,1)S(1)}, bf16[4,32,1664]{2,1,0:T(8,128)(2,1)S(1)}, u32[]{:S(2)}, u32[]{:S(2)}) collective-permute-start(bf16[4,32,1664]{2,1,0:T(8,128)(2,1)S(1)} %collective-permute-done.9.refs_1_), channel_id=1, source_target_pairs={{0,1},{1,0},{2,3},{3,2},{4,5},{5,4},{6,7},{7,6},{8,9},{9,8},{10,11... | collective-permute-start | bytes 1277960 | tf_op jit(solution)/shard_map/ppermute | solution.py:429
  46.1 10.0 %collective-permute-start.18 = (bf16[4,32,1664]{2,1,0:T(8,128)(2,1)S(1)}, bf16[4,32,1664]{2,1,0:T(8,128)(2,1)S(1)}, u32[]{:S(2)}, u32[]{:S(2)}) collective-permute-start(bf16[4,32,1664]{2,1,0:T(8,128)(2,1)S(1)} %collective-permute-done.8.refs_2_), channel_id=1, source_target_pairs={{0,1},{1,0},{2,3},{3,2},{4,5},{5,4},{6,7},{7,6},{8,9},{9,8},{10,11... | collective-permute-start | bytes 1277960 | tf_op jit(solution)/shard_map/ppermute | solution.py:429
  76.8 4.4 %collective-permute-start.20 = (bf16[2,2,4,32,1664]{4,3,2,1,0:T(8,128)(2,1)S(1)}, bf16[2,2,4,32,1664]{4,3,2,1,0:T(8,128)(2,1)S(1)}, u32[]{:S(2)}, u32[]{:S(2)}) collective-permute-start(bf16[2,2,4,32,1664]{4,3,2,1,0:T(8,128)(2,1)S(1)} %get-tuple-element.134), channel_id=1, source_target_pairs={{0,1},{1,0},{2,3},{3,2},{4,5},{5,4},{6,7},{7,6},{8,9},{9,8},{10,11... | collective-permute-start | bytes 5111816 | tf_op jit(solution)/shard_map/ppermute | solution.py:429
  81.6 14.1 %collective-permute-start.23 = (bf16[2,4,32,1664]{3,2,1,0:T(8,128)(2,1)S(1)}, bf16[2,4,32,1664]{3,2,1,0:T(8,128)(2,1)S(1)}, u32[]{:S(2)}, u32[]{:S(2)}) collective-permute-start(bf16[2,4,32,1664]{3,2,1,0:T(8,128)(2,1)S(1)} %get-tuple-element.150), channel_id=1, source_target_pairs={{0,2},{1,5},{2,0},{3,7},{4,6},{5,1},{6,4},{7,3},{8,10},{9,13},{10,... | collective-permute-start | bytes 2555912 | tf_op jit(solution)/shard_map/ppermute | solution.py:429
  91.4 4.9 %collective-permute-start.21 = (bf16[2,2,4,32,1024]{4,3,2,1,0:T(8,128)(2,1)S(1)}, bf16[2,2,4,32,1024]{4,3,2,1,0:T(8,128)(2,1)S(1)}, u32[]{:S(2)}, u32[]{:S(2)}) collective-permute-start(bf16[2,2,4,32,1024]{4,3,2,1,0:T(8,128)(2,1)S(1)} %get-tuple-element.144), channel_id=1, source_target_pairs={{0,1},{1,0},{2,3},{3,2},{4,5},{5,4},{6,7},{7,6},{8,9},{9,8},{10,11... | collective-permute-start | bytes 3145736 | tf_op jit(solution)/shard_map/ppermute | solution.py:429
  95.8 3.5 %collective-permute-start.24 = (bf16[2,2,4,32,640]{4,3,2,1,0:T(8,128)(2,1)S(1)}, bf16[2,2,4,32,640]{4,3,2,1,0:T(8,128)(2,1)S(1)}, u32[]{:S(2)}, u32[]{:S(2)}) collective-permute-start(bf16[2,2,4,32,640]{4,3,2,1,0:T(8,128)(2,1)S(1)} %get-tuple-element.151), channel_id=1, source_target_pairs={{0,1},{1,0},{2,3},{3,2},{4,5},{5,4},{6,7},{7,6},{8,9},{9,8},{10,11... | collective-permute-start | bytes 1966088 | tf_op jit(solution)/shard_map/ppermute | solution.py:429
  96.6 16.6 %collective-permute-start.22 = (bf16[2,4,32,1024]{3,2,1,0:T(8,128)(2,1)S(1)}, bf16[2,4,32,1024]{3,2,1,0:T(8,128)(2,1)S(1)}, u32[]{:S(2)}, u32[]{:S(2)}) collective-permute-start(bf16[2,4,32,1024]{3,2,1,0:T(8,128)(2,1)S(1)} %get-tuple-element.147), channel_id=1, source_target_pairs={{0,2},{1,5},{2,0},{3,7},{4,6},{5,1},{6,4},{7,3},{8,10},{9,13},{10,... | collective-permute-start | bytes 1572872 | tf_op jit(solution)/shard_map/ppermute | solution.py:429
  98.1 15.1 %collective-permute-start.26 = (bf16[4,32,1664]{2,1,0:T(8,128)(2,1)S(1)}, bf16[4,32,1664]{2,1,0:T(8,128)(2,1)S(1)}, u32[]{:S(2)}, u32[]{:S(2)}) collective-permute-start(bf16[4,32,1664]{2,1,0:T(8,128)(2,1)S(1)} %get-tuple-element.155), channel_id=1, source_target_pairs={{0,4},{1,3},{2,6},{3,1},{4,0},{5,7},{6,2},{7,5},{8,12},{9,11},{10,... | collective-permute-start | bytes 1277960 | tf_op jit(solution)/shard_map/ppermute | solution.py:429
  99.5 14.4 %collective-permute-start.25 = (bf16[2,4,32,640]{3,2,1,0:T(8,128)(2,1)S(1)}, bf16[2,4,32,640]{3,2,1,0:T(8,128)(2,1)S(1)}, u32[]{:S(2)}, u32[]{:S(2)}) collective-permute-start(bf16[2,4,32,640]{3,2,1,0:T(8,128)(2,1)S(1)} %get-tuple-element.157), channel_id=1, source_target_pairs={{0,2},{1,5},{2,0},{3,7},{4,6},{5,1},{6,4},{7,3},{8,10},{9,13},{10,... | collective-permute-start | bytes 983048 | tf_op jit(solution)/shard_map/ppermute | solution.py:429
  114.1 8.2 %collective-permute-start.27 = (bf16[4,32,1664]{2,1,0:T(8,128)(2,1)S(1)}, bf16[4,32,1664]{2,1,0:T(8,128)(2,1)S(1)}, u32[]{:S(2)}, u32[]{:S(2)}) collective-permute-start(bf16[4,32,1664]{2,1,0:T(8,128)(2,1)S(1)} %get-tuple-element.173), channel_id=1, source_target_pairs={{0,4},{1,3},{2,6},{3,1},{4,0},{5,7},{6,2},{7,5},{8,12},{9,11},{10,... | collective-permute-start | bytes 1277960 | tf_op jit(solution)/shard_map/ppermute | solution.py:429
  114.9 9.8 %collective-permute-start.31 = (bf16[32,1664]{1,0:T(8,128)(2,1)S(1)}, bf16[32,1664]{1,0:T(8,128)(2,1)S(1)}, u32[]{:S(2)}, u32[]{:S(2)}) collective-permute-start(bf16[32,1664]{1,0:T(8,128)(2,1)S(1)} %get-tuple-element.180), channel_id=1, source_target_pairs={{0,24},{1,25},{2,26},{3,27},{4,28},{5,29},{6,30},{7,31},{8,16},{9,... | collective-permute-start | bytes 319496 | tf_op jit(solution)/shard_map/ppermute | solution.py:429
  116.7 15.7 %collective-permute-start.32 = (bf16[32,1664]{1,0:T(8,128)(2,1)S(1)}, bf16[32,1664]{1,0:T(8,128)(2,1)S(1)}, u32[]{:S(2)}, u32[]{:S(2)}) collective-permute-start(bf16[32,1664]{1,0:T(8,128)(2,1)S(1)} %get-tuple-element.181), channel_id=1, source_target_pairs={{0,16},{1,17},{2,18},{3,19},{4,20},{5,21},{6,22},{7,23},{8,24},{9,... | collective-permute-start | bytes 319496 | tf_op jit(solution)/shard_map/ppermute | solution.py:429
  118.2 14.2 %collective-permute-start.33 = (bf16[32,1664]{1,0:T(8,128)(2,1)S(1)}, bf16[32,1664]{1,0:T(8,128)(2,1)S(1)}, u32[]{:S(2)}, u32[]{:S(2)}) collective-permute-start(bf16[32,1664]{1,0:T(8,128)(2,1)S(1)} %get-tuple-element.182), channel_id=1, source_target_pairs={{0,8},{1,9},{2,10},{3,11},{4,12},{5,13},{6,14},{7,15},{8,0},{9,1},... | collective-permute-start | bytes 319496 | tf_op jit(solution)/shard_map/ppermute | solution.py:429
  122.4 10.0 %collective-permute-start.28 = (bf16[32,1664]{1,0:T(8,128)(2,1)S(1)}, bf16[32,1664]{1,0:T(8,128)(2,1)S(1)}, u32[]{:S(2)}, u32[]{:S(2)}) collective-permute-start(bf16[32,1664]{1,0:T(8,128)(2,1)S(1)} %get-tuple-element.175), channel_id=1, source_target_pairs={{0,8},{1,9},{2,10},{3,11},{4,12},{5,13},{6,14},{7,15},{8,0},{9,1},... | collective-permute-start | bytes 319496 | tf_op jit(solution)/shard_map/ppermute | solution.py:429
  123.7 10.9 %collective-permute-start.29 = (bf16[32,1664]{1,0:T(8,128)(2,1)S(1)}, bf16[32,1664]{1,0:T(8,128)(2,1)S(1)}, u32[]{:S(2)}, u32[]{:S(2)}) collective-permute-start(bf16[32,1664]{1,0:T(8,128)(2,1)S(1)} %get-tuple-element.176), channel_id=1, source_target_pairs={{0,16},{1,17},{2,18},{3,19},{4,20},{5,21},{6,22},{7,23},{8,24},{9,... | collective-permute-start | bytes 319496 | tf_op jit(solution)/shard_map/ppermute | solution.py:429
  124.7 9.9 %collective-permute-start.30 = (bf16[32,1664]{1,0:T(8,128)(2,1)S(1)}, bf16[32,1664]{1,0:T(8,128)(2,1)S(1)}, u32[]{:S(2)}, u32[]{:S(2)}) collective-permute-start(bf16[32,1664]{1,0:T(8,128)(2,1)S(1)} %get-tuple-element.177), channel_id=1, source_target_pairs={{0,24},{1,25},{2,26},{3,27},{4,28},{5,29},{6,30},{7,31},{8,16},{9,... | collective-permute-start | bytes 319496 | tf_op jit(solution)/shard_map/ppermute | solution.py:429
  (2 other events, 3.6 us)

commit v11 on v10

--- a/solution.py
+++ b/solution.py
@@ -582,7 +582,9 @@
         macs,
         ROOM_0,
     )
-    taps0, proj1, *near0 = lax.optimization_barrier((taps0, proj1, *near0))
+    near0 = near0[::-1]
+    *near0, taps0, proj1 = lax.optimization_barrier((*near0, taps0, proj1))
+    near0 = near0[::-1]
     mine0 = side_by_side(near0)
     one0, two0 = wires.hop(mine0, wires.first), wires.hop(mine0, wires.second)
     own1, _ = lax.optimization_barrier((own1, mine0))

time: 136 us -> 136 us (level)
  waiting for transfers between devices: 33 us -> 26.5 us
  starting transfers between devices: 32.4 us -> 38.8 us
    ppermute x34, starting transfers between devices: 32.4 us -> 38.8 us  [hop(): return lax.ppermute(value, AXES, pairs)]
    ppermute x34, waiting for transfers between devices: 33 us -> 26.5 us  [hop(): return lax.ppermute(value, AXES, pairs)]
  transfers between devices with their start and end apart: 34 -> 34, of which waited for: 12 -> 11; matrix products, arithmetic and copies ran while one was open for 1% -> 1% of each run, Pallas kernels for 34% -> 34%
where the time goes in v11:
time: 136 us
  Pallas kernels  67.6 us (50%)
  starting transfers between devices  38.8 us (29%)
  waiting for transfers between devices  26.5 us (19%)
  between operations  2.14 us (2%)
    pallas_call x9, Pallas kernels, call(): pl.pallas_call(kernel, grid_spec=pltpu.PrefetchScalarGridSpec(num_scalar_...  63.6 us
    ppermute x34, starting transfers between devices, hop(): return lax.ppermute(value, AXES, pairs)  38.8 us
    ppermute x34, waiting for transfers between devices, hop(): return lax.ppermute(value, AXES, pairs)  26.5 us
    pallas_call x11, Pallas kernels, plain(): pl.pallas_call(kernel, out_shape=shapes, in_specs=[KEPT] * len(operands),...  2.74 us
  transfers between devices with their start and end apart: 34, of which 11 were waited for; matrix products, arithmetic and copies ran while one was open for 1% of the time, Pallas kernels for 34%

profile of v11, /device:TPU:0, one launch (start us, length us, event | category | flops | bytes accessed | tf_op | source)
XLA Modules:
  0.0 135.7 jit_solution(15292638147210056753)
XLA Ops:
  0.6 1.2 shard_map.178
  1.9 3.1 %collective-permute-start.2 = (bf16[32,1664]{1,0:T(8,128)(2,1)S(1)}, bf16[32,1664]{1,0:T(8,128)(2,1)S(1)}, u32[]{:S(2)}, u32[]{:S(2)}) collective-permute-start(bf16[32,1664]{1,0:T(8,128)(2,1)S(1)} %get-tuple-element.106.refs_0_), channel_id=1, source_target_pairs={{0,8},{1,9},{2,10},{3,11},{4,12},{5,13},{6,14},{7,15},{8,0},{9,1},... | collective-permute-start | bytes 319496 | tf_op jit(solution)/shard_map/ppermute | solution.py:429
  4.9 2.6 %collective-permute-start.1 = (bf16[32,1664]{1,0:T(8,128)(2,1)S(1)}, bf16[32,1664]{1,0:T(8,128)(2,1)S(1)}, u32[]{:S(2)}, u32[]{:S(2)}) collective-permute-start(bf16[32,1664]{1,0:T(8,128)(2,1)S(1)} %get-tuple-element.106.refs_0_), channel_id=1, source_target_pairs={{0,16},{1,17},{2,18},{3,19},{4,20},{5,21},{6,22},{7,23},{8,24},{9,... | collective-permute-start | bytes 319496 | tf_op jit(solution)/shard_map/ppermute | solution.py:429
  8.9 5.4 %shard_map.179 = (bf16[2048,1280]{1,0:T(8,128)(2,1)S(1)}, bf16[2048,1024]{1,0:T(8,128)(2,1)S(1)}) custom-call(s32[4]{0:T(128)S(1)} %pad_add_fusion.info_ref, bf16[2048,512]{1,0:T(8,128)(2,1)} %bitcast.18, bf16[2048,512]{1,0:T(8,128)(2,1)} %bitcast.19, bf16[2048,512]{1,0:T(8,128)(2,1)} %bitcast.20, bf16[128,128]{1,0:T(8,128)(2,1)S(1)} %get-tuple-element.102.mel_ref), custom_call_target="tpu_custom_call" | custom-call | flops 134217728 | bytes 1581056 | tf_op jit(solution)/shard_map/pallas_call | solution.py:374
  14.3 1.6 %collective-permute-done.1.refs_2_ = bf16[32,1664]{1,0:T(8,128)(2,1)S(1)} collective-permute-done((bf16[32,1664]{1,0:T(8,128)(2,1)S(1)}, bf16[32,1664]{1,0:T(8,128)(2,1)S(1)}, u32[]{:S(2)}, u32[]{:S(2)}) %collective-permute-start.1) | collective-permute-done | bytes 106528 | tf_op jit(solution)/shard_map/ppermute | solution.py:429
  16.0 1.6 %collective-permute-start.7 = (bf16[4,32,1664]{2,1,0:T(8,128)(2,1)S(1)}, bf16[4,32,1664]{2,1,0:T(8,128)(2,1)S(1)}, u32[]{:S(2)}, u32[]{:S(2)}) collective-permute-start(bf16[4,32,1664]{2,1,0:T(8,128)(2,1)S(1)} %shard_map.180.refs_0_), channel_id=1, source_target_pairs={{0,2},{1,5},{2,0},{3,7},{4,6},{5,1},{6,4},{7,3},{8,10},{9,13},{10,... | collective-permute-start | bytes 1277960 | tf_op jit(solution)/shard_map/ppermute | solution.py:429
  17.6 1.5 %collective-permute-start.6 = (bf16[4,32,1664]{2,1,0:T(8,128)(2,1)S(1)}, bf16[4,32,1664]{2,1,0:T(8,128)(2,1)S(1)}, u32[]{:S(2)}, u32[]{:S(2)}) collective-permute-start(bf16[4,32,1664]{2,1,0:T(8,128)(2,1)S(1)} %shard_map.180.refs_0_), channel_id=1, source_target_pairs={{0,4},{1,3},{2,6},{3,1},{4,0},{5,7},{6,2},{7,5},{8,12},{9,11},{10,... | collective-permute-start | bytes 1277960 | tf_op jit(solution)/shard_map/ppermute | solution.py:429
  19.1 1.8 %collective-permute-start.5 = (bf16[32,1664]{1,0:T(8,128)(2,1)S(1)}, bf16[32,1664]{1,0:T(8,128)(2,1)S(1)}, u32[]{:S(2)}, u32[]{:S(2)}) collective-permute-start(bf16[32,1664]{1,0:T(8,128)(2,1)S(1)} %shard_map.181.refs_0_), channel_id=1, source_target_pairs={{0,8},{1,9},{2,10},{3,11},{4,12},{5,13},{6,14},{7,15},{8,0},{9,1},... | collective-permute-start | bytes 319496 | tf_op jit(solution)/shard_map/ppermute | solution.py:429
  20.9 1.3 collective-permute-start.4
  22.2 1.3 collective-permute-start.3
  24.4 5.7 %collective-permute-done.4.refs_2_ = bf16[32,1664]{1,0:T(8,128)(2,1)S(1)} collective-permute-done((bf16[32,1664]{1,0:T(8,128)(2,1)S(1)}, bf16[32,1664]{1,0:T(8,128)(2,1)S(1)}, u32[]{:S(2)}, u32[]{:S(2)}) %collective-permute-start.4) | collective-permute-done | bytes 106528 | tf_op jit(solution)/shard_map/ppermute | solution.py:429
  31.3 1.5 %collective-permute-start.8 = (bf16[4,32,1664]{2,1,0:T(8,128)(2,1)S(1)}, bf16[4,32,1664]{2,1,0:T(8,128)(2,1)S(1)}, u32[]{:S(2)}, u32[]{:S(2)}) collective-permute-start(bf16[4,32,1664]{2,1,0:T(8,128)(2,1)S(1)} %shard_map.182.refs_0_), channel_id=1, source_target_pairs={{0,4},{1,3},{2,6},{3,1},{4,0},{5,7},{6,2},{7,5},{8,12},{9,11},{10,... | collective-permute-start | bytes 1277960 | tf_op jit(solution)/shard_map/ppermute | solution.py:429
  33.3 5.1 %collective-permute-done.10.refs_3_ = bf16[4,32,1664]{2,1,0:T(8,128)(2,1)S(1)} collective-permute-done((bf16[4,32,1664]{2,1,0:T(8,128)(2,1)S(1)}, bf16[4,32,1664]{2,1,0:T(8,128)(2,1)S(1)}, u32[]{:S(2)}, u32[]{:S(2)}) %collective-permute-start.10) | collective-permute-done | bytes 426016 | tf_op jit(solution)/shard_map/ppermute | solution.py:429
  38.4 3.9 %collective-permute-done.9.refs_1_ = bf16[4,32,1664]{2,1,0:T(8,128)(2,1)S(1)} collective-permute-done((bf16[4,32,1664]{2,1,0:T(8,128)(2,1)S(1)}, bf16[4,32,1664]{2,1,0:T(8,128)(2,1)S(1)}, u32[]{:S(2)}, u32[]{:S(2)}) %collective-permute-start.9) | collective-permute-done | bytes 426016 | tf_op jit(solution)/shard_map/ppermute | solution.py:429
  44.8 8.9 %shard_map.183 = (bf16[2048,1280]{1,0:T(8,128)(2,1)S(1)}, bf16[2048,512]{1,0:T(8,128)(2,1)S(1)}, bf16[2048,1024]{1,0:T(8,128)(2,1)S(1)}, bf16[1024,1664]{1,0:T(8,128)(2,1)S(1)}) custom-call(s32[4]{0:T(128)S(1)} %pad_add_fusion.info_ref, bf16[2048,1280]{1,0:T(8,128)(2,1)S(1)} %get-tuple-element.105.taps0_ref.taps_ref, ...), custom_call_target="tpu_custom_call" | custom-call | flops 1342177280 | tf_op jit(solution)/shard_map/pallas_call | solution.py:374
  53.8 1.7 %collective-permute-done.19.refs_7_ = bf16[4,32,1664]{2,1,0:T(8,128)(2,1)S(1)} collective-permute-done((bf16[4,32,1664]{2,1,0:T(8,128)(2,1)S(1)}, bf16[4,32,1664]{2,1,0:T(8,128)(2,1)S(1)}, u32[]{:S(2)}, u32[]{:S(2)}) %collective-permute-start.19) | collective-permute-done | bytes 426016 | tf_op jit(solution)/shard_map/ppermute | solution.py:429
  55.5 19.0 %shard_map.184 = (bf16[2048,512]{1,0:T(8,128)(2,1)S(1)}, bf16[2048,1024]{1,0:T(8,128)(2,1)S(1)}, bf16[1024,1664]{1,0:T(8,128)(2,1)S(1)}, f32[1024,128]{1,0:T(8,1...) custom-call(s32[4]{0:T(128)S(1)} %pad_add_fusion.info_ref, ...), custom_call_target="tpu_custom_call" | custom-call | flops 3221225472 | tf_op jit(solution)/shard_map/pallas_call | solution.py:374
  74.8 4.2 %shard_map.185 = (bf16[2048,1024]{1,0:T(8,128)(2,1)S(1)}, bf16[2048,1024]{1,0:T(8,128)(2,1)S(1)}, f32[8,512]{1,0:T(8,128)S(1)}) custom-call(s32[4]{0:T(128)S(1)} %pad_add_fusion.info_ref, bf16[2048,1024]{1,0:T(8,128)(2,1)S(1)} %get-tuple-element.126.pre1_ref, bf16[1024,1664]{1,0:T(8,128)(2,1)S(1)} %get-tuple-element.127.w1_ref, ...), custom_call_target="tpu_custom_call" | custom-call | flops 805306368 | tf_op jit(solution)/shard_map/pallas_call | solution.py:374
  80.5 4.2 %shard_map.187 = (bf16[2048,1024]{1,0:T(8,128)(2,1)S(1)}, bf16[2048,1024]{1,0:T(8,128)(2,1)S(1)}, f32[8,512]{1,0:T(8,128)}) custom-call(s32[4]{0:T(128)S(1)} %pad_add_fusion.info_ref, bf16[2048,1024]{1,0:T(8,128)(2,1)S(1)} %get-tuple-element.126.pre1_ref, ...), custom_call_target="tpu_custom_call", output_to_operand_aliasing={{0}: (6, {}), {1}: (7, {})} | custom-call | flops 805306368 | tf_op jit(solution)/shard_map/pallas_call | solution.py:374
  84.7 4.5 %shard_map.188 = (bf16[2,2,4,32,1024]{4,3,2,1,0:T(8,128)(2,1)S(1)}, bf16[2,2,4,32,1024]{4,3,2,1,0:T(8,128)(2,1)S(1)}) custom-call(s32[4]{0:T(128)S(1)} %pad_add_fusion.info_ref, bf16[2048,1024]{1,0:T(8,128)(2,1)S(1)} %get-tuple-element.158.pre_ref, bf16[2048,1024]{1,0:T(8,128)(2,1)S(1)} %get-tuple-element.141.proj_ref, ...), custom_call_target="tpu_custom_call" | custom-call | flops 939524096 | tf_op jit(solution)/shard_map/pallas_call | solution.py:374
  89.3 4.2 %shard_map.189 = (f32[1024,128]{1,0:T(8,128)S(1)}, bf16[2,2,4,32,640]{4,3,2,1,0:T(8,128)(2,1)S(1)}, bf16[2,2,4,32,640]{4,3,2,1,0:T(8,128)(2,1)S(1)}) custom-call(s32[4]{0:T(128)S(1)} %pad_add_fusion.info_ref, bf16[2048,1024]{1,0:T(8,128)(2,1)S(1)} %get-tuple-element.158.pre_ref, bf16[2048,1024]{1,0:T(8,128)(2,1)S(1)} %get-tuple-element.141.proj_ref, ...), custom_call_target="tpu_custom_call" | custom-call | flops 671088640 | tf_op jit(solution)/shard_map/pallas_call | solution.py:374
  97.2 1.1 collective-permute-start.25
  98.3 6.8 %shard_map.193 = f32[2048,512]{1,0:T(8,128)} custom-call(s32[4]{0:T(128)S(1)} %pad_add_fusion.info_ref, bf16[2048,1024]{1,0:T(8,128)(2,1)S(1)} %get-tuple-element.141.proj_ref, bf16[2048,1024]{1,0:T(8,128)(2,1)S(1)} %get-tuple-element.158.pre_ref, bf16[1024,1664]{1,0:T(8,128)(2,1)S(1)} %get-tuple-element.128.w0_ref), custom_call_target="tpu_custom_call" | custom-call | flops 1073741824 | bytes 1048576 | tf_op jit(solution)/shard_map/pallas_call | solution.py:374
  105.1 6.3 %shard_map.194 = (bf16[2048,512]{1,0:T(8,128)(2,1)}, bf16[2048,512]{1,0:T(8,128)(2,1)}, f32[128,128]{1,0:T(8,128)S(1)}) custom-call(s32[4]{0:T(128)S(1)} %pad_add_fusion.info_ref, bf16[2048,1280]{1,0:T(8,128)(2,1)S(1)} %get-tuple-element.159.taps_ref.taps1_ref, bf16[2048,512]{1,0:T(8,128)(2,1)S(1)} %get-tuple-element.142.gated_ref.gated0_ref, ...), custom_call_target="tpu_custom_call" | custom-call | flops 1073741824 | bytes 1064960 | tf_op jit(solution)/shard_map/pallas_call | solution.py:374
  111.9 1.2 collective-permute-start.27
  113.2 3.4 %collective-permute-start.31 = (bf16[32,1664]{1,0:T(8,128)(2,1)S(1)}, bf16[32,1664]{1,0:T(8,128)(2,1)S(1)}, u32[]{:S(2)}, u32[]{:S(2)}) collective-permute-start(bf16[32,1664]{1,0:T(8,128)(2,1)S(1)} %get-tuple-element.180), channel_id=1, source_target_pairs={{0,24},{1,25},{2,26},{3,27},{4,28},{5,29},{6,30},{7,31},{8,16},{9,... | collective-permute-start | bytes 319496 | tf_op jit(solution)/shard_map/ppermute | solution.py:429
  116.6 2.7 %collective-permute-start.32 = (bf16[32,1664]{1,0:T(8,128)(2,1)S(1)}, bf16[32,1664]{1,0:T(8,128)(2,1)S(1)}, u32[]{:S(2)}, u32[]{:S(2)}) collective-permute-start(bf16[32,1664]{1,0:T(8,128)(2,1)S(1)} %get-tuple-element.181), channel_id=1, source_target_pairs={{0,16},{1,17},{2,18},{3,19},{4,20},{5,21},{6,22},{7,23},{8,24},{9,... | collective-permute-start | bytes 319496 | tf_op jit(solution)/shard_map/ppermute | solution.py:429
  120.2 4.5 %collective-permute-start.28 = (bf16[32,1664]{1,0:T(8,128)(2,1)S(1)}, bf16[32,1664]{1,0:T(8,128)(2,1)S(1)}, u32[]{:S(2)}, u32[]{:S(2)}) collective-permute-start(bf16[32,1664]{1,0:T(8,128)(2,1)S(1)} %get-tuple-element.175), channel_id=1, source_target_pairs={{0,8},{1,9},{2,10},{3,11},{4,12},{5,13},{6,14},{7,15},{8,0},{9,1},... | collective-permute-start | bytes 319496 | tf_op jit(solution)/shard_map/ppermute | solution.py:429
  124.7 1.5 %collective-permute-start.29 = (bf16[32,1664]{1,0:T(8,128)(2,1)S(1)}, bf16[32,1664]{1,0:T(8,128)(2,1)S(1)}, u32[]{:S(2)}, u32[]{:S(2)}) collective-permute-start(bf16[32,1664]{1,0:T(8,128)(2,1)S(1)} %get-tuple-element.176), channel_id=1, source_target_pairs={{0,16},{1,17},{2,18},{3,19},{4,20},{5,21},{6,22},{7,23},{8,24},{9,... | collective-permute-start | bytes 319496 | tf_op jit(solution)/shard_map/ppermute | solution.py:429
  126.2 1.4 %collective-permute-start.30 = (bf16[32,1664]{1,0:T(8,128)(2,1)S(1)}, bf16[32,1664]{1,0:T(8,128)(2,1)S(1)}, u32[]{:S(2)}, u32[]{:S(2)}) collective-permute-start(bf16[32,1664]{1,0:T(8,128)(2,1)S(1)} %get-tuple-element.177), channel_id=1, source_target_pairs={{0,24},{1,25},{2,26},{3,27},{4,28},{5,29},{6,30},{7,31},{8,16},{9,... | collective-permute-start | bytes 319496 | tf_op jit(solution)/shard_map/ppermute | solution.py:429
  128.2 2.6 %collective-permute-done.28.refs_1_ = bf16[32,1664]{1,0:T(8,128)(2,1)S(1)} collective-permute-done((bf16[32,1664]{1,0:T(8,128)(2,1)S(1)}, bf16[32,1664]{1,0:T(8,128)(2,1)S(1)}, u32[]{:S(2)}, u32[]{:S(2)}) %collective-permute-start.28) | collective-permute-done | bytes 106528 | tf_op jit(solution)/shard_map/ppermute | solution.py:429
  130.9 3.8 %collective-permute-done.29.refs_2_ = bf16[32,1664]{1,0:T(8,128)(2,1)S(1)} collective-permute-done((bf16[32,1664]{1,0:T(8,128)(2,1)S(1)}, bf16[32,1664]{1,0:T(8,128)(2,1)S(1)}, u32[]{:S(2)}, u32[]{:S(2)}) %collective-permute-start.29) | collective-permute-done | bytes 106528 | tf_op jit(solution)/shard_map/ppermute | solution.py:429
  (60 shorter events, 13.7 us)
Async XLA Ops:
  1.9 12.5 %collective-permute-start.2 = (bf16[32,1664]{1,0:T(8,128)(2,1)S(1)}, bf16[32,1664]{1,0:T(8,128)(2,1)S(1)}, u32[]{:S(2)}, u32[]{:S(2)}) collective-permute-start(bf16[32,1664]{1,0:T(8,128)(2,1)S(1)} %get-tuple-element.106.refs_0_), channel_id=1, source_target_pairs={{0,8},{1,9},{2,10},{3,11},{4,12},{5,13},{6,14},{7,15},{8,0},{9,1},... | collective-permute-start | bytes 319496 | tf_op jit(solution)/shard_map/ppermute | solution.py:429
  4.9 11.0 %collective-permute-start.1 = (bf16[32,1664]{1,0:T(8,128)(2,1)S(1)}, bf16[32,1664]{1,0:T(8,128)(2,1)S(1)}, u32[]{:S(2)}, u32[]{:S(2)}) collective-permute-start(bf16[32,1664]{1,0:T(8,128)(2,1)S(1)} %get-tuple-element.106.refs_0_), channel_id=1, source_target_pairs={{0,16},{1,17},{2,18},{3,19},{4,20},{5,21},{6,22},{7,23},{8,24},{9,... | collective-permute-start | bytes 319496 | tf_op jit(solution)/shard_map/ppermute | solution.py:429
  7.5 8.4 %collective-permute-start = (bf16[32,1664]{1,0:T(8,128)(2,1)S(1)}, bf16[32,1664]{1,0:T(8,128)(2,1)S(1)}, u32[]{:S(2)}, u32[]{:S(2)}) collective-permute-start(bf16[32,1664]{1,0:T(8,128)(2,1)S(1)} %get-tuple-element.106.refs_0_), channel_id=1, source_target_pairs={{0,24},{1,25},{2,26},{3,27},{4,28},{5,29},{6,30},{7,31},{8,16},{9,... | collective-permute-start | bytes 319496 | tf_op jit(solution)/shard_map/ppermute | solution.py:429
  16.0 14.1 %collective-permute-start.7 = (bf16[4,32,1664]{2,1,0:T(8,128)(2,1)S(1)}, bf16[4,32,1664]{2,1,0:T(8,128)(2,1)S(1)}, u32[]{:S(2)}, u32[]{:S(2)}) collective-permute-start(bf16[4,32,1664]{2,1,0:T(8,128)(2,1)S(1)} %shard_map.180.refs_0_), channel_id=1, source_target_pairs={{0,2},{1,5},{2,0},{3,7},{4,6},{5,1},{6,4},{7,3},{8,10},{9,13},{10,... | collective-permute-start | bytes 1277960 | tf_op jit(solution)/shard_map/ppermute | solution.py:429
  17.6 12.6 %collective-permute-start.6 = (bf16[4,32,1664]{2,1,0:T(8,128)(2,1)S(1)}, bf16[4,32,1664]{2,1,0:T(8,128)(2,1)S(1)}, u32[]{:S(2)}, u32[]{:S(2)}) collective-permute-start(bf16[4,32,1664]{2,1,0:T(8,128)(2,1)S(1)} %shard_map.180.refs_0_), channel_id=1, source_target_pairs={{0,4},{1,3},{2,6},{3,1},{4,0},{5,7},{6,2},{7,5},{8,12},{9,11},{10,... | collective-permute-start | bytes 1277960 | tf_op jit(solution)/shard_map/ppermute | solution.py:429
  19.1 5.3 %collective-permute-start.5 = (bf16[32,1664]{1,0:T(8,128)(2,1)S(1)}, bf16[32,1664]{1,0:T(8,128)(2,1)S(1)}, u32[]{:S(2)}, u32[]{:S(2)}) collective-permute-start(bf16[32,1664]{1,0:T(8,128)(2,1)S(1)} %shard_map.181.refs_0_), channel_id=1, source_target_pairs={{0,8},{1,9},{2,10},{3,11},{4,12},{5,13},{6,14},{7,15},{8,0},{9,1},... | collective-permute-start | bytes 319496 | tf_op jit(solution)/shard_map/ppermute | solution.py:429
  20.9 9.2 %collective-permute-start.4 = (bf16[32,1664]{1,0:T(8,128)(2,1)S(1)}, bf16[32,1664]{1,0:T(8,128)(2,1)S(1)}, u32[]{:S(2)}, u32[]{:S(2)}) collective-permute-start(bf16[32,1664]{1,0:T(8,128)(2,1)S(1)} %shard_map.181.refs_0_), channel_id=1, source_target_pairs={{0,16},{1,17},{2,18},{3,19},{4,20},{5,21},{6,22},{7,23},{8,24},{9,... | collective-permute-start | bytes 319496 | tf_op jit(solution)/shard_map/ppermute | solution.py:429
  22.2 7.9 %collective-permute-start.3 = (bf16[32,1664]{1,0:T(8,128)(2,1)S(1)}, bf16[32,1664]{1,0:T(8,128)(2,1)S(1)}, u32[]{:S(2)}, u32[]{:S(2)}) collective-permute-start(bf16[32,1664]{1,0:T(8,128)(2,1)S(1)} %shard_map.181.refs_0_), channel_id=1, source_target_pairs={{0,24},{1,25},{2,26},{3,27},{4,28},{5,29},{6,30},{7,31},{8,16},{9,... | collective-permute-start | bytes 319496 | tf_op jit(solution)/shard_map/ppermute | solution.py:429
  30.2 8.2 %collective-permute-start.10 = (bf16[4,32,1664]{2,1,0:T(8,128)(2,1)S(1)}, bf16[4,32,1664]{2,1,0:T(8,128)(2,1)S(1)}, u32[]{:S(2)}, u32[]{:S(2)}) collective-permute-start(bf16[4,32,1664]{2,1,0:T(8,128)(2,1)S(1)} %collective-permute-done.7.refs_1_), channel_id=1, source_target_pairs={{0,4},{1,3},{2,6},{3,1},{4,0},{5,7},{6,2},{7,5},{8,12},{9,11},{10,... | collective-permute-start | bytes 1277960 | tf_op jit(solution)/shard_map/ppermute | solution.py:429
  30.7 11.5 %collective-permute-start.9 = (bf16[4,32,1664]{2,1,0:T(8,128)(2,1)S(1)}, bf16[4,32,1664]{2,1,0:T(8,128)(2,1)S(1)}, u32[]{:S(2)}, u32[]{:S(2)}) collective-permute-start(bf16[4,32,1664]{2,1,0:T(8,128)(2,1)S(1)} %shard_map.182.refs_0_), channel_id=1, source_target_pairs={{0,2},{1,5},{2,0},{3,7},{4,6},{5,1},{6,4},{7,3},{8,10},{9,13},{10,... | collective-permute-start | bytes 1277960 | tf_op jit(solution)/shard_map/ppermute | solution.py:429
  31.3 11.7 %collective-permute-start.8 = (bf16[4,32,1664]{2,1,0:T(8,128)(2,1)S(1)}, bf16[4,32,1664]{2,1,0:T(8,128)(2,1)S(1)}, u32[]{:S(2)}, u32[]{:S(2)}) collective-permute-start(bf16[4,32,1664]{2,1,0:T(8,128)(2,1)S(1)} %shard_map.182.refs_0_), channel_id=1, source_target_pairs={{0,4},{1,3},{2,6},{3,1},{4,0},{5,7},{6,2},{7,5},{8,12},{9,11},{10,... | collective-permute-start | bytes 1277960 | tf_op jit(solution)/shard_map/ppermute | solution.py:429
  32.8 10.6 %collective-permute-start.11 = (bf16[4,32,1664]{2,1,0:T(8,128)(2,1)S(1)}, bf16[4,32,1664]{2,1,0:T(8,128)(2,1)S(1)}, u32[]{:S(2)}, u32[]{:S(2)}) collective-permute-start(bf16[4,32,1664]{2,1,0:T(8,128)(2,1)S(1)} %shard_map.180.refs_0_), channel_id=1, source_target_pairs={{0,1},{1,0},{2,3},{3,2},{4,5},{5,4},{6,7},{7,6},{8,9},{9,8},{10,11... | collective-permute-start | bytes 1277960 | tf_op jit(solution)/shard_map/ppermute | solution.py:429
  32.8 11.5 %collective-permute-start.12 = (bf16[4,32,1664]{2,1,0:T(8,128)(2,1)S(1)}, bf16[4,32,1664]{2,1,0:T(8,128)(2,1)S(1)}, u32[]{:S(2)}, u32[]{:S(2)}) collective-permute-start(bf16[4,32,1664]{2,1,0:T(8,128)(2,1)S(1)} %collective-permute-done.7.refs_1_), channel_id=1, source_target_pairs={{0,1},{1,0},{2,3},{3,2},{4,5},{5,4},{6,7},{7,6},{8,9},{9,8},{10,11... | collective-permute-start | bytes 1277960 | tf_op jit(solution)/shard_map/ppermute | solution.py:429
  38.4 5.9 %collective-permute-start.13 = (bf16[4,32,1664]{2,1,0:T(8,128)(2,1)S(1)}, bf16[4,32,1664]{2,1,0:T(8,128)(2,1)S(1)}, u32[]{:S(2)}, u32[]{:S(2)}) collective-permute-start(bf16[4,32,1664]{2,1,0:T(8,128)(2,1)S(1)} %collective-permute-done.6.refs_2_), channel_id=1, source_target_pairs={{0,1},{1,0},{2,3},{3,2},{4,5},{5,4},{6,7},{7,6},{8,9},{9,8},{10,11... | collective-permute-start | bytes 1277960 | tf_op jit(solution)/shard_map/ppermute | solution.py:429
  42.9 10.7 %collective-permute-start.15 = (bf16[4,32,1664]{2,1,0:T(8,128)(2,1)S(1)}, bf16[4,32,1664]{2,1,0:T(8,128)(2,1)S(1)}, u32[]{:S(2)}, u32[]{:S(2)}) collective-permute-start(bf16[4,32,1664]{2,1,0:T(8,128)(2,1)S(1)} %collective-permute-done.9.refs_1_), channel_id=1, source_target_pairs={{0,4},{1,3},{2,6},{3,1},{4,0},{5,7},{6,2},{7,5},{8,12},{9,11},{10,... | collective-permute-start | bytes 1277960 | tf_op jit(solution)/shard_map/ppermute | solution.py:429
  43.4 10.4 %collective-permute-start.16 = (bf16[4,32,1664]{2,1,0:T(8,128)(2,1)S(1)}, bf16[4,32,1664]{2,1,0:T(8,128)(2,1)S(1)}, u32[]{:S(2)}, u32[]{:S(2)}) collective-permute-start(bf16[4,32,1664]{2,1,0:T(8,128)(2,1)S(1)} %shard_map.182.refs_0_), channel_id=1, source_target_pairs={{0,1},{1,0},{2,3},{3,2},{4,5},{5,4},{6,7},{7,6},{8,9},{9,8},{10,11... | collective-permute-start | bytes 1277960 | tf_op jit(solution)/shard_map/ppermute | solution.py:429
  44.3 9.6 %collective-permute-start.17 = (bf16[4,32,1664]{2,1,0:T(8,128)(2,1)S(1)}, bf16[4,32,1664]{2,1,0:T(8,128)(2,1)S(1)}, u32[]{:S(2)}, u32[]{:S(2)}) collective-permute-start(bf16[4,32,1664]{2,1,0:T(8,128)(2,1)S(1)} %collective-permute-done.9.refs_1_), channel_id=1, source_target_pairs={{0,1},{1,0},{2,3},{3,2},{4,5},{5,4},{6,7},{7,6},{8,9},{9,8},{10,11... | collective-permute-start | bytes 1277960 | tf_op jit(solution)/shard_map/ppermute | solution.py:429
  44.3 9.5 %collective-permute-start.18 = (bf16[4,32,1664]{2,1,0:T(8,128)(2,1)S(1)}, bf16[4,32,1664]{2,1,0:T(8,128)(2,1)S(1)}, u32[]{:S(2)}, u32[]{:S(2)}) collective-permute-start(bf16[4,32,1664]{2,1,0:T(8,128)(2,1)S(1)} %collective-permute-done.8.refs_2_), channel_id=1, source_target_pairs={{0,1},{1,0},{2,3},{3,2},{4,5},{5,4},{6,7},{7,6},{8,9},{9,8},{10,11... | collective-permute-start | bytes 1277960 | tf_op jit(solution)/shard_map/ppermute | solution.py:429
  74.6 4.4 %collective-permute-start.20 = (bf16[2,2,4,32,1664]{4,3,2,1,0:T(8,128)(2,1)S(1)}, bf16[2,2,4,32,1664]{4,3,2,1,0:T(8,128)(2,1)S(1)}, u32[]{:S(2)}, u32[]{:S(2)}) collective-permute-start(bf16[2,2,4,32,1664]{4,3,2,1,0:T(8,128)(2,1)S(1)} %get-tuple-element.134), channel_id=1, source_target_pairs={{0,1},{1,0},{2,3},{3,2},{4,5},{5,4},{6,7},{7,6},{8,9},{9,8},{10,11... | collective-permute-start | bytes 5111816 | tf_op jit(solution)/shard_map/ppermute | solution.py:429
  79.4 14.1 %collective-permute-start.23 = (bf16[2,4,32,1664]{3,2,1,0:T(8,128)(2,1)S(1)}, bf16[2,4,32,1664]{3,2,1,0:T(8,128)(2,1)S(1)}, u32[]{:S(2)}, u32[]{:S(2)}) collective-permute-start(bf16[2,4,32,1664]{3,2,1,0:T(8,128)(2,1)S(1)} %get-tuple-element.150), channel_id=1, source_target_pairs={{0,2},{1,5},{2,0},{3,7},{4,6},{5,1},{6,4},{7,3},{8,10},{9,13},{10,... | collective-permute-start | bytes 2555912 | tf_op jit(solution)/shard_map/ppermute | solution.py:429
  89.2 4.9 %collective-permute-start.21 = (bf16[2,2,4,32,1024]{4,3,2,1,0:T(8,128)(2,1)S(1)}, bf16[2,2,4,32,1024]{4,3,2,1,0:T(8,128)(2,1)S(1)}, u32[]{:S(2)}, u32[]{:S(2)}) collective-permute-start(bf16[2,2,4,32,1024]{4,3,2,1,0:T(8,128)(2,1)S(1)} %get-tuple-element.144), channel_id=1, source_target_pairs={{0,1},{1,0},{2,3},{3,2},{4,5},{5,4},{6,7},{7,6},{8,9},{9,8},{10,11... | collective-permute-start | bytes 3145736 | tf_op jit(solution)/shard_map/ppermute | solution.py:429
  93.6 3.5 %collective-permute-start.24 = (bf16[2,2,4,32,640]{4,3,2,1,0:T(8,128)(2,1)S(1)}, bf16[2,2,4,32,640]{4,3,2,1,0:T(8,128)(2,1)S(1)}, u32[]{:S(2)}, u32[]{:S(2)}) collective-permute-start(bf16[2,2,4,32,640]{4,3,2,1,0:T(8,128)(2,1)S(1)} %get-tuple-element.151), channel_id=1, source_target_pairs={{0,1},{1,0},{2,3},{3,2},{4,5},{5,4},{6,7},{7,6},{8,9},{9,8},{10,11... | collective-permute-start | bytes 1966088 | tf_op jit(solution)/shard_map/ppermute | solution.py:429
  94.4 17.1 %collective-permute-start.22 = (bf16[2,4,32,1024]{3,2,1,0:T(8,128)(2,1)S(1)}, bf16[2,4,32,1024]{3,2,1,0:T(8,128)(2,1)S(1)}, u32[]{:S(2)}, u32[]{:S(2)}) collective-permute-start(bf16[2,4,32,1024]{3,2,1,0:T(8,128)(2,1)S(1)} %get-tuple-element.147), channel_id=1, source_target_pairs={{0,2},{1,5},{2,0},{3,7},{4,6},{5,1},{6,4},{7,3},{8,10},{9,13},{10,... | collective-permute-start | bytes 1572872 | tf_op jit(solution)/shard_map/ppermute | solution.py:429
  95.9 15.6 %collective-permute-start.26 = (bf16[4,32,1664]{2,1,0:T(8,128)(2,1)S(1)}, bf16[4,32,1664]{2,1,0:T(8,128)(2,1)S(1)}, u32[]{:S(2)}, u32[]{:S(2)}) collective-permute-start(bf16[4,32,1664]{2,1,0:T(8,128)(2,1)S(1)} %get-tuple-element.155), channel_id=1, source_target_pairs={{0,4},{1,3},{2,6},{3,1},{4,0},{5,7},{6,2},{7,5},{8,12},{9,11},{10,... | collective-permute-start | bytes 1277960 | tf_op jit(solution)/shard_map/ppermute | solution.py:429
  97.2 14.5 %collective-permute-start.25 = (bf16[2,4,32,640]{3,2,1,0:T(8,128)(2,1)S(1)}, bf16[2,4,32,640]{3,2,1,0:T(8,128)(2,1)S(1)}, u32[]{:S(2)}, u32[]{:S(2)}) collective-permute-start(bf16[2,4,32,640]{3,2,1,0:T(8,128)(2,1)S(1)} %get-tuple-element.157), channel_id=1, source_target_pairs={{0,2},{1,5},{2,0},{3,7},{4,6},{5,1},{6,4},{7,3},{8,10},{9,13},{10,... | collective-permute-start | bytes 983048 | tf_op jit(solution)/shard_map/ppermute | solution.py:429
  111.9 8.2 %collective-permute-start.27 = (bf16[4,32,1664]{2,1,0:T(8,128)(2,1)S(1)}, bf16[4,32,1664]{2,1,0:T(8,128)(2,1)S(1)}, u32[]{:S(2)}, u32[]{:S(2)}) collective-permute-start(bf16[4,32,1664]{2,1,0:T(8,128)(2,1)S(1)} %get-tuple-element.173), channel_id=1, source_target_pairs={{0,4},{1,3},{2,6},{3,1},{4,0},{5,7},{6,2},{7,5},{8,12},{9,11},{10,... | collective-permute-start | bytes 1277960 | tf_op jit(solution)/shard_map/ppermute | solution.py:429
  113.2 13.0 %collective-permute-start.31 = (bf16[32,1664]{1,0:T(8,128)(2,1)S(1)}, bf16[32,1664]{1,0:T(8,128)(2,1)S(1)}, u32[]{:S(2)}, u32[]{:S(2)}) collective-permute-start(bf16[32,1664]{1,0:T(8,128)(2,1)S(1)} %get-tuple-element.180), channel_id=1, source_target_pairs={{0,24},{1,25},{2,26},{3,27},{4,28},{5,29},{6,30},{7,31},{8,16},{9,... | collective-permute-start | bytes 319496 | tf_op jit(solution)/shard_map/ppermute | solution.py:429
  116.6 11.6 %collective-permute-start.32 = (bf16[32,1664]{1,0:T(8,128)(2,1)S(1)}, bf16[32,1664]{1,0:T(8,128)(2,1)S(1)}, u32[]{:S(2)}, u32[]{:S(2)}) collective-permute-start(bf16[32,1664]{1,0:T(8,128)(2,1)S(1)} %get-tuple-element.181), channel_id=1, source_target_pairs={{0,16},{1,17},{2,18},{3,19},{4,20},{5,21},{6,22},{7,23},{8,24},{9,... | collective-permute-start | bytes 319496 | tf_op jit(solution)/shard_map/ppermute | solution.py:429
  119.3 9.0 %collective-permute-start.33 = (bf16[32,1664]{1,0:T(8,128)(2,1)S(1)}, bf16[32,1664]{1,0:T(8,128)(2,1)S(1)}, u32[]{:S(2)}, u32[]{:S(2)}) collective-permute-start(bf16[32,1664]{1,0:T(8,128)(2,1)S(1)} %get-tuple-element.182), channel_id=1, source_target_pairs={{0,8},{1,9},{2,10},{3,11},{4,12},{5,13},{6,14},{7,15},{8,0},{9,1},... | collective-permute-start | bytes 319496 | tf_op jit(solution)/shard_map/ppermute | solution.py:429
  120.2 10.7 %collective-permute-start.28 = (bf16[32,1664]{1,0:T(8,128)(2,1)S(1)}, bf16[32,1664]{1,0:T(8,128)(2,1)S(1)}, u32[]{:S(2)}, u32[]{:S(2)}) collective-permute-start(bf16[32,1664]{1,0:T(8,128)(2,1)S(1)} %get-tuple-element.175), channel_id=1, source_target_pairs={{0,8},{1,9},{2,10},{3,11},{4,12},{5,13},{6,14},{7,15},{8,0},{9,1},... | collective-permute-start | bytes 319496 | tf_op jit(solution)/shard_map/ppermute | solution.py:429
  124.7 9.9 %collective-permute-start.29 = (bf16[32,1664]{1,0:T(8,128)(2,1)S(1)}, bf16[32,1664]{1,0:T(8,128)(2,1)S(1)}, u32[]{:S(2)}, u32[]{:S(2)}) collective-permute-start(bf16[32,1664]{1,0:T(8,128)(2,1)S(1)} %get-tuple-element.176), channel_id=1, source_target_pairs={{0,16},{1,17},{2,18},{3,19},{4,20},{5,21},{6,22},{7,23},{8,24},{9,... | collective-permute-start | bytes 319496 | tf_op jit(solution)/shard_map/ppermute | solution.py:429
  126.2 8.4 %collective-permute-start.30 = (bf16[32,1664]{1,0:T(8,128)(2,1)S(1)}, bf16[32,1664]{1,0:T(8,128)(2,1)S(1)}, u32[]{:S(2)}, u32[]{:S(2)}) collective-permute-start(bf16[32,1664]{1,0:T(8,128)(2,1)S(1)} %get-tuple-element.177), channel_id=1, source_target_pairs={{0,24},{1,25},{2,26},{3,27},{4,28},{5,29},{6,30},{7,31},{8,16},{9,... | collective-permute-start | bytes 319496 | tf_op jit(solution)/shard_map/ppermute | solution.py:429
  (2 other events, 3.7 us)
